TPU v7x, 32 devices: a whole 2x2x4 slice. The times are simulated.
32 devices in a mesh: grp: 4 (over y, x), shard: 8 (over z, core).
Axes of the slice: x: 2, y: 2, z: 4, core: 2. Of those that a mesh axis runs over, the one named last changes fastest.
Arguments:
- tokens: bfloat16 [32, 1024, 1024], P(('grp', 'shard')), may hold values from -6 to 6
- segment_ids: int32 [32, 1024], P(('grp', 'shard')), may hold values from 0 to 17, as said below
- keep_flag: int32 [32, 1024], P(('grp', 'shard')), may hold values from 0 to 1, as said below
- cotangent: bfloat16 [32, 1024, 1024], P(('grp', 'shard')), may hold values from -6 to 6
- w_qkv: bfloat16 [1024, 3072], P('shard', 'grp'), may hold values from -0.25 to 0.25
- b_query: bfloat16 [1024], P('shard'), may hold values from -3 to 3
- b_value: bfloat16 [1024], P('shard'), may hold values from -3 to 3
- w_attn_out: bfloat16 [1024, 1024], P('shard', 'grp'), may hold values from -0.75 to 0.75
- b_attn_out: bfloat16 [1024], P('shard'), may hold values from -3 to 3
- norm1_gain: bfloat16 [1024], P('shard'), may hold values from 0.5 to 1.5
- norm1_bias: bfloat16 [1024], P('shard'), may hold values from -3 to 3
- w_in: bfloat16 [1024, 4096], P('shard', 'grp'), may hold values from -0.1875 to 0.1875
- b_in: bfloat16 [4096], P('shard'), may hold values from -3 to 3
- w_out: bfloat16 [4096, 1024], P('shard', 'grp'), may hold values from -0.09375 to 0.09375
- b_out: bfloat16 [1024], P('shard'), may hold values from -3 to 3
- norm2_gain: bfloat16 [1024], P('shard'), may hold values from 0.5 to 1.5
- norm2_bias: bfloat16 [1024], P('shard'), may hold values from -3 to 3
Outputs:
- layer_out: bfloat16 [32, 1024, 1024], P(('grp', 'shard'))
- input_grad: float32 [32, 1024, 1024], P(('grp', 'shard'))
- grad_w_qkv: float32 [1024, 3072], P('shard')
- grad_b_query: float32 [1024], P('shard')
- grad_b_value: float32 [1024], P('shard')
- grad_w_attn_out: float32 [1024, 1024], P('shard')
- grad_b_attn_out: float32 [1024], P('shard')
- grad_norm1_gain: float32 [1024], P('shard')
- grad_norm1_bias: float32 [1024], P('shard')
- grad_w_in: float32 [1024, 4096], P('shard')
- grad_b_in: float32 [4096], P('shard')
- grad_w_out: float32 [4096, 1024], P('shard')
- grad_b_out: float32 [1024], P('shard')
- grad_norm2_gain: float32 [1024], P('shard')
- grad_norm2_bias: float32 [1024], P('shard')
Inputs may be any that keep to these rules, and one draw needn't show every extreme that they name: `segment_ids`: along each sequence the ids start at 0 and rise by one at the first token of each document; every document but the last of its sequence has 60 to 800 tokens, the last one is cut by the sequence's end. `keep_flag`: 0 exactly on the tokens of the last document of each sequence.
All inputs are finite; a program needn't handle non-finite values.
Results may differ from a plain program's by a relative error of at most 0.02.
Values may be sent and summed in bfloat16 or wider, within the bound.
No kernel may reach another device: no remote copies, remote signals or barrier semaphores. Data moves between devices by JAX's collectives and lax.ppermute only.
A program may use at most 256 MiB of HBM per device.

v0:
```python
import functools
import math

import jax
import jax.numpy as jnp
from jax import lax
from jax.experimental import pallas as pl
from jax.experimental.pallas import tpu as pltpu
from jax.sharding import PartitionSpec as P

H = 16
HD = 64


masked_score = -1e30
epsilon = 1e-05


def norm_layer(rows, gain_row, shift_row):
    row_mean = jnp.mean(rows, -1, keepdims=True)
    centered = rows - row_mean
    row_var = jnp.mean(centered * centered, -1, keepdims=True)
    return centered * lax.rsqrt(row_var + epsilon) * gain_row + shift_row


def gelu_exact(values):
    return 0.5 * values * (1.0 + lax.erf(values * (1.0 / math.sqrt(2.0))))


def contract_rows(left, right):
    return lax.dot_general(
        left, right, (((0,), (0,)), ((), ())), preferred_element_type=jnp.float32
    )


def contract_cols(left, right):
    return lax.dot_general(
        left, right, (((1,), (1,)), ((), ())), preferred_element_type=jnp.float32
    )


def attend_forward(queries, key_rows, value_rows, segment_row, block_rows):
    length, model_width = queries.shape
    scaling = 1.0 / math.sqrt(HD)
    key_heads = key_rows.reshape(length, H, HD)
    value_heads = value_rows.reshape(length, H, HD)
    query_blocks = queries.reshape(length // block_rows, block_rows, H, HD)
    segment_blocks = segment_row.reshape(length // block_rows, block_rows)

    def one_block(pieces):
        query_part, segment_part = pieces
        scores = (
            jnp.einsum("qhd,khd->hqk", query_part, key_heads, preferred_element_type=jnp.float32)
            * scaling
        )
        allowed = segment_part[:, None] == segment_row[None, :]
        scores = jnp.where(allowed[None], scores, masked_score)
        row_max = jnp.max(scores, -1, keepdims=True)
        powers = jnp.exp(scores - row_max)
        totals = jnp.sum(powers, -1, keepdims=True)
        attn_probs = (powers / totals).astype(jnp.bfloat16)
        context = jnp.einsum(
            "hqk,khd->qhd", attn_probs, value_heads, preferred_element_type=jnp.float32
        )
        return (
            context.reshape(block_rows, model_width).astype(jnp.bfloat16),
            (row_max + jnp.log(totals))[:, :, 0],
        )

    contexts, log_sums = lax.map(one_block, (query_blocks, segment_blocks))
    return (contexts.reshape(length, model_width), log_sums)


def attend_backward(queries, key_rows, value_rows, segment_row, log_sums, context_grad, block_rows):
    length, model_width = queries.shape
    scaling = 1.0 / math.sqrt(HD)
    key_heads = key_rows.reshape(length, H, HD)
    value_heads = value_rows.reshape(length, H, HD)
    query_blocks = queries.reshape(length // block_rows, block_rows, H, HD)
    segment_blocks = segment_row.reshape(length // block_rows, block_rows)
    grad_blocks = context_grad.reshape(length // block_rows, block_rows, H, HD)

    def one_block(running, pieces):
        key_acc, value_acc = running
        query_part, segment_part, lse_part, grad_part = pieces
        scores = (
            jnp.einsum("qhd,khd->hqk", query_part, key_heads, preferred_element_type=jnp.float32)
            * scaling
        )
        allowed = segment_part[:, None] == segment_row[None, :]
        scores = jnp.where(allowed[None], scores, masked_score)
        probs = jnp.exp(scores - lse_part[:, :, None])
        prob_low = probs.astype(jnp.bfloat16)
        prob_grad = jnp.einsum(
            "qhd,khd->hqk", grad_part, value_heads, preferred_element_type=jnp.float32
        )
        row_dot = jnp.sum(prob_grad * probs, -1, keepdims=True)
        score_grad = (probs * (prob_grad - row_dot)).astype(jnp.bfloat16)
        query_grad = (
            jnp.einsum("hqk,khd->qhd", score_grad, key_heads, preferred_element_type=jnp.float32)
            * scaling
        )
        key_acc = (
            key_acc
            + jnp.einsum("hqk,qhd->khd", score_grad, query_part, preferred_element_type=jnp.float32)
            * scaling
        )
        value_acc = value_acc + jnp.einsum(
            "hqk,qhd->khd", prob_low, grad_part, preferred_element_type=jnp.float32
        )
        return ((key_acc, value_acc), query_grad.reshape(block_rows, model_width))

    empty_acc = jnp.zeros((length, H, HD), jnp.float32)
    (key_grad, value_grad), query_grads = lax.scan(
        one_block, (empty_acc, empty_acc), (query_blocks, segment_blocks, log_sums, grad_blocks)
    )
    return (
        query_grads.reshape(length, model_width),
        key_grad.reshape(length, model_width),
        value_grad.reshape(length, model_width),
    )


def on_device(
    tokens,
    segment_ids,
    keep_flag,
    cotangent,
    w_qkv,
    b_query,
    b_value,
    w_attn_out,
    b_attn_out,
    norm1_gain,
    norm1_bias,
    w_in,
    b_in,
    w_out,
    b_out,
    norm2_gain,
    norm2_bias,
):
    seq_count, length, model_width = tokens.shape
    block_rows = min(512, length)
    within = (
        lax.all_gather(w_qkv, "shard", axis=0, tiled=True),
        lax.all_gather(w_attn_out, "shard", axis=0, tiled=True),
        lax.all_gather(w_in, "shard", axis=0, tiled=True),
        lax.all_gather(w_out, "shard", axis=0, tiled=True),
        lax.all_gather(b_query, "shard", axis=0, tiled=True),
        lax.all_gather(b_value, "shard", axis=0, tiled=True),
        lax.all_gather(b_attn_out, "shard", axis=0, tiled=True),
        lax.all_gather(norm1_gain, "shard", axis=0, tiled=True),
        lax.all_gather(norm1_bias, "shard", axis=0, tiled=True),
        lax.all_gather(b_in, "shard", axis=0, tiled=True),
        lax.all_gather(b_out, "shard", axis=0, tiled=True),
        lax.all_gather(norm2_gain, "shard", axis=0, tiled=True),
        lax.all_gather(norm2_bias, "shard", axis=0, tiled=True),
    )
    full_qkv, full_attn, full_in, full_out = (
        lax.all_gather(within[0], "grp", axis=1, tiled=True),
        lax.all_gather(within[1], "grp", axis=1, tiled=True),
        lax.all_gather(within[2], "grp", axis=1, tiled=True),
        lax.all_gather(within[3], "grp", axis=1, tiled=True),
    )
    (
        bias_query,
        bias_value,
        bias_attn,
        gain_one,
        shift_one,
        bias_in,
        bias_out,
        gain_two,
        shift_two,
    ) = [piece.astype(jnp.float32) for piece in within[4:]]
    flat_rows = tokens.reshape(seq_count * length, model_width)
    mixed_qkv = jnp.dot(flat_rows, full_qkv, preferred_element_type=jnp.float32)
    queries = (mixed_qkv[:, :model_width] + bias_query).astype(jnp.bfloat16)
    key_rows = mixed_qkv[:, model_width : 2 * model_width].astype(jnp.bfloat16)
    value_rows = (mixed_qkv[:, 2 * model_width :] + bias_value).astype(jnp.bfloat16)
    query_seqs = queries.reshape(seq_count, length, model_width)
    key_seqs = key_rows.reshape(seq_count, length, model_width)
    value_seqs = value_rows.reshape(seq_count, length, model_width)

    def forward_sequence(pieces):
        return attend_forward(pieces[0], pieces[1], pieces[2], pieces[3], block_rows)

    contexts, log_sums = lax.map(forward_sequence, (query_seqs, key_seqs, value_seqs, segment_ids))
    contexts = contexts.reshape(seq_count * length, model_width)
    attended = jnp.dot(contexts, full_attn, preferred_element_type=jnp.float32) + bias_attn
    first_sum = flat_rows.astype(jnp.float32) + attended
    normed_one, norm_one_back = jax.vjp(norm_layer, first_sum, gain_one, shift_one)
    normed_low = normed_one.astype(jnp.bfloat16)
    hidden_pre = jnp.dot(normed_low, full_in, preferred_element_type=jnp.float32) + bias_in
    hidden, gelu_back = jax.vjp(gelu_exact, hidden_pre)
    hidden_low = hidden.astype(jnp.bfloat16)
    second_sum = normed_one + (
        jnp.dot(hidden_low, full_out, preferred_element_type=jnp.float32) + bias_out
    )
    result, norm_two_back = jax.vjp(norm_layer, second_sum, gain_two, shift_two)
    layer_out = result.astype(jnp.bfloat16).reshape(seq_count, length, model_width)
    again = (
        lax.all_gather(w_qkv, "shard", axis=0, tiled=True),
        lax.all_gather(w_attn_out, "shard", axis=0, tiled=True),
        lax.all_gather(w_in, "shard", axis=0, tiled=True),
        lax.all_gather(w_out, "shard", axis=0, tiled=True),
    )
    back_qkv, back_attn, back_in, back_out = (
        lax.all_gather(again[0], "grp", axis=1, tiled=True),
        lax.all_gather(again[1], "grp", axis=1, tiled=True),
        lax.all_gather(again[2], "grp", axis=1, tiled=True),
        lax.all_gather(again[3], "grp", axis=1, tiled=True),
    )
    masked_cot = cotangent.astype(jnp.float32).reshape(
        seq_count * length, model_width
    ) * keep_flag.reshape(seq_count * length, 1).astype(jnp.float32)
    second_grad, gain_two_grad, shift_two_grad = norm_two_back(masked_cot)
    bias_out_grad = jnp.sum(second_grad, 0)
    out_low = second_grad.astype(jnp.bfloat16)
    w_out_grad = contract_rows(hidden_low, out_low)
    hidden_grad = contract_cols(out_low, back_out)
    (pre_grad,) = gelu_back(hidden_grad)
    bias_in_grad = jnp.sum(pre_grad, 0)
    pre_low = pre_grad.astype(jnp.bfloat16)
    w_in_grad = contract_rows(normed_low, pre_low)
    normed_grad = second_grad + contract_cols(pre_low, back_in)
    first_grad, gain_one_grad, shift_one_grad = norm_one_back(normed_grad)
    bias_attn_grad = jnp.sum(first_grad, 0)
    attn_low = first_grad.astype(jnp.bfloat16)
    w_attn_grad = contract_rows(contexts, attn_low)
    context_grad = contract_cols(attn_low, back_attn).astype(jnp.bfloat16)

    def backward_sequence(pieces):
        return attend_backward(
            pieces[0], pieces[1], pieces[2], pieces[3], pieces[4], pieces[5], block_rows
        )

    query_grad, key_grad, value_grad = lax.map(
        backward_sequence,
        (
            query_seqs,
            key_seqs,
            value_seqs,
            segment_ids,
            log_sums,
            context_grad.reshape(seq_count, length, model_width),
        ),
    )
    query_grad = query_grad.reshape(seq_count * length, model_width)
    key_grad = key_grad.reshape(seq_count * length, model_width)
    value_grad = value_grad.reshape(seq_count * length, model_width)
    bias_query_grad = jnp.sum(query_grad, 0)
    bias_value_grad = jnp.sum(value_grad, 0)
    qkv_low = jnp.concatenate([query_grad, key_grad, value_grad], 1).astype(jnp.bfloat16)
    w_qkv_grad = contract_rows(flat_rows, qkv_low)
    input_grad = first_grad + contract_cols(qkv_low, back_qkv)
    reduced = (
        lax.psum_scatter(
            w_qkv_grad.astype(jnp.bfloat16), "shard", scatter_dimension=0, tiled=True
        ).astype(jnp.float32),
        lax.psum_scatter(
            bias_query_grad.astype(jnp.bfloat16), "shard", scatter_dimension=0, tiled=True
        ).astype(jnp.float32),
        lax.psum_scatter(
            bias_value_grad.astype(jnp.bfloat16), "shard", scatter_dimension=0, tiled=True
        ).astype(jnp.float32),
        lax.psum_scatter(
            w_attn_grad.astype(jnp.bfloat16), "shard", scatter_dimension=0, tiled=True
        ).astype(jnp.float32),
        lax.psum_scatter(
            bias_attn_grad.astype(jnp.bfloat16), "shard", scatter_dimension=0, tiled=True
        ).astype(jnp.float32),
        lax.psum_scatter(
            gain_one_grad.astype(jnp.bfloat16), "shard", scatter_dimension=0, tiled=True
        ).astype(jnp.float32),
        lax.psum_scatter(
            shift_one_grad.astype(jnp.bfloat16), "shard", scatter_dimension=0, tiled=True
        ).astype(jnp.float32),
        lax.psum_scatter(
            w_in_grad.astype(jnp.bfloat16), "shard", scatter_dimension=0, tiled=True
        ).astype(jnp.float32),
        lax.psum_scatter(
            bias_in_grad.astype(jnp.bfloat16), "shard", scatter_dimension=0, tiled=True
        ).astype(jnp.float32),
        lax.psum_scatter(
            w_out_grad.astype(jnp.bfloat16), "shard", scatter_dimension=0, tiled=True
        ).astype(jnp.float32),
        lax.psum_scatter(
            bias_out_grad.astype(jnp.bfloat16), "shard", scatter_dimension=0, tiled=True
        ).astype(jnp.float32),
        lax.psum_scatter(
            gain_two_grad.astype(jnp.bfloat16), "shard", scatter_dimension=0, tiled=True
        ).astype(jnp.float32),
        lax.psum_scatter(
            shift_two_grad.astype(jnp.bfloat16), "shard", scatter_dimension=0, tiled=True
        ).astype(jnp.float32),
    )
    summed = (
        lax.psum(reduced[0].astype(jnp.bfloat16), "grp").astype(jnp.float32),
        lax.psum(reduced[1].astype(jnp.bfloat16), "grp").astype(jnp.float32),
        lax.psum(reduced[2].astype(jnp.bfloat16), "grp").astype(jnp.float32),
        lax.psum(reduced[3].astype(jnp.bfloat16), "grp").astype(jnp.float32),
        lax.psum(reduced[4].astype(jnp.bfloat16), "grp").astype(jnp.float32),
        lax.psum(reduced[5].astype(jnp.bfloat16), "grp").astype(jnp.float32),
        lax.psum(reduced[6].astype(jnp.bfloat16), "grp").astype(jnp.float32),
        lax.psum(reduced[7].astype(jnp.bfloat16), "grp").astype(jnp.float32),
        lax.psum(reduced[8].astype(jnp.bfloat16), "grp").astype(jnp.float32),
        lax.psum(reduced[9].astype(jnp.bfloat16), "grp").astype(jnp.float32),
        lax.psum(reduced[10].astype(jnp.bfloat16), "grp").astype(jnp.float32),
        lax.psum(reduced[11].astype(jnp.bfloat16), "grp").astype(jnp.float32),
        lax.psum(reduced[12].astype(jnp.bfloat16), "grp").astype(jnp.float32),
    )
    return (
        layer_out,
        input_grad.reshape(seq_count, length, model_width),
        summed[0],
        summed[1],
        summed[2],
        summed[3],
        summed[4],
        summed[5],
        summed[6],
        summed[7],
        summed[8],
        summed[9],
        summed[10],
        summed[11],
        summed[12],
    )


NT = (((1,), (1,)), ((), ()))
NN = (((1,), (0,)), ((), ()))
TN = (((0,), (0,)), ((), ()))
LANES = 128
AXES = ("grp", "shard")


def mxu(left, right, dims):
    return lax.dot_general(left, right, dims, preferred_element_type=jnp.float32)


def cost(flops):
    return pl.CostEstimate(flops=2 * flops, bytes_accessed=0, transcendentals=0)


def params(megabytes=60):
    return pltpu.CompilerParams(vmem_limit_bytes=megabytes << 20)


def attention_forward_kernel(q_ref, k_ref, v_ref, seg_col, seg_row, out_ref, probs_ref, *, rows):
    length = q_ref.shape[0]
    first = lax.broadcasted_iota(jnp.int32, (1, LANES), 1) < HD
    keys = k_ref[...]
    values = v_ref[...]
    zero = jnp.zeros_like(keys)
    head_keys = (jnp.where(first, keys, zero), jnp.where(first, zero, keys))
    key_segments = seg_col[...]
    for block in range(length // rows):
        here = pl.ds(block * rows, rows)
        q = q_ref[here, :]
        allowed = key_segments == seg_row[:, here]
        outs = []
        for head in range(2):
            scores = mxu(head_keys[head], q, NT)
            scores = jnp.where(allowed, scores, masked_score)
            powers = jnp.exp(scores - jnp.max(scores, 0, keepdims=True))
            probs = powers * (1.0 / jnp.sum(powers, 0, keepdims=True))
            probs = probs.astype(jnp.bfloat16)
            probs_ref[head, :, here] = probs
            outs.append(mxu(probs, values, TN))
        out_ref[here, :] = jnp.where(first, outs[0], outs[1]).astype(jnp.bfloat16)


def attention_forward(qkv, seg_col, seg_row, start, pairs, before=None):
    length, width = qkv.shape[0], qkv.shape[1] // 3
    total = width // LANES
    rows = min(512, length)
    more = () if before is None else before

    def pair(part):
        return pl.BlockSpec((length, LANES), lambda j: (0, part * total + start + j))

    def body(q_ref, k_ref, v_ref, seg_c, seg_r, *refs):
        attention_forward_kernel(q_ref, k_ref, v_ref, seg_c, seg_r, *refs[-2:], rows=rows)

    return pl.pallas_call(
        body,
        grid=(pairs,),
        in_specs=[
            pair(0),
            pair(1),
            pair(2),
            pl.BlockSpec((length, 1), lambda j: (0, 0)),
            pl.BlockSpec((1, length), lambda j: (0, 0)),
        ]
        + [pl.BlockSpec(memory_space=pl.ANY)] * len(more),
        out_specs=[
            pl.BlockSpec((length, LANES), lambda j: (0, start + j)),
            pl.BlockSpec((2, length, length), lambda j: (start + j, 0, 0)),
        ],
        out_shape=[
            jax.ShapeDtypeStruct((length, width), jnp.bfloat16),
            jax.ShapeDtypeStruct((2 * total, length, length), jnp.bfloat16),
        ],
        input_output_aliases={} if before is None else {5: 0, 6: 1},
        compiler_params=params(60),
        cost_estimate=cost(16 * length * length * pairs * LANES),
        name="attn_fwd",
    )(qkv, qkv, qkv, seg_col, seg_row, *more)


def attention_backward_kernel(q_ref, k_ref, v_ref, o_ref, do_ref, probs_ref, grad_ref, sum_ref):
    first = lax.broadcasted_iota(jnp.int32, (1, LANES), 1) < HD
    pick = (
        lax.broadcasted_iota(jnp.int32, (8, LANES), 0)
        == lax.broadcasted_iota(jnp.int32, (8, LANES), 1) // HD
    ).astype(jnp.float32)
    q = q_ref[...]
    do = do_ref[...]
    keys = k_ref[...]
    values = v_ref[...]
    zero = jnp.zeros_like(values)
    head_values = (jnp.where(first, values, zero), jnp.where(first, zero, values))
    dots = lax.dot_general(
        pick,
        do.astype(jnp.float32) * o_ref[...].astype(jnp.float32),
        NT,
        precision=lax.Precision.HIGHEST,
        preferred_element_type=jnp.float32,
    )
    query_parts, key_parts, value_parts = [], [], []
    for head in range(2):
        probs = probs_ref[head]
        prob_grad = mxu(head_values[head], do, NT)
        score_grad = probs.astype(jnp.float32) * (prob_grad - dots[head : head + 1, :])
        score_grad = score_grad.astype(jnp.bfloat16)
        value_parts.append(mxu(probs, do, NN))
        key_parts.append(mxu(score_grad, q, NN))
        query_parts.append(mxu(score_grad, keys, TN))
    query_grad = jnp.where(first, *query_parts) * (1.0 / math.sqrt(HD))
    value_grad = jnp.where(first, *value_parts)
    grad_ref[0] = query_grad.astype(jnp.bfloat16)
    grad_ref[1] = jnp.where(first, *key_parts).astype(jnp.bfloat16)
    grad_ref[2] = value_grad.astype(jnp.bfloat16)
    sum_ref[0:1, :] = jnp.sum(query_grad, 0, keepdims=True)
    sum_ref[1:2, :] = jnp.sum(value_grad, 0, keepdims=True)


def attention_backward(qkv, out, out_grad, probs, start, pairs, at, size, before=None):
    length, width = out.shape
    total = width // LANES
    more = () if before is None else before

    def pair(part):
        return pl.BlockSpec((length, LANES), lambda j: (0, part * total + start + j))

    def body(*refs):
        attention_backward_kernel(*refs[:6], *refs[-2:])

    return pl.pallas_call(
        body,
        grid=(pairs,),
        in_specs=[
            pair(0),
            pair(1),
            pair(2),
            pair(0),
            pair(0),
            pl.BlockSpec((2, length, length), lambda j: (start + j, 0, 0)),
        ]
        + [pl.BlockSpec(memory_space=pl.ANY)] * len(more),
        out_specs=[
            pl.BlockSpec((3, length, LANES), lambda j: (0, 0, j + at)),
            pl.BlockSpec((2, LANES), lambda j: (0, j + at)),
        ],
        out_shape=[
            jax.ShapeDtypeStruct((3, length, size * LANES), jnp.bfloat16),
            jax.ShapeDtypeStruct((2, size * LANES), jnp.float32),
        ],
        input_output_aliases={} if before is None else {6: 0, 7: 1},
        compiler_params=params(60),
        cost_estimate=cost(32 * length * length * pairs * LANES),
        name="attn_bwd",
    )(qkv, qkv, qkv, out, out_grad, probs, *more)


class Place:
    def __init__(self, groups, shards):
        self.groups = groups
        self.shards = shards
        self.chips = shards // 2
        self.grp = lax.axis_index("grp")
        self.shard = lax.axis_index("shard")
        self.core = self.shard % 2
        self.chip = self.shard // 2
        self.scalars = jnp.stack([self.core, self.chip, self.grp]).astype(jnp.int32)

    def permute(self, array, mask_of_core):
        pairs = [(i, i ^ mask_of_core[i % 2]) for i in range(self.groups * self.shards)]
        return lax.ppermute(array, AXES, pairs)

    def swap_core(self, array):
        return self.permute(array, (1, 1))

    def swap_grp(self, array, step):
        masks = (self.shards, 2 * self.shards)
        return self.permute(array, masks if step == 0 else masks[::-1])

    def swap_chip(self, array, step):
        masks = (2, 4)
        return self.permute(array, masks if step == 0 else masks[::-1])

    def slot_chip(self, slot):
        return self.chip ^ turn(slot, self.core)

    def slot_grp(self, slot):
        return self.grp ^ turn(slot, self.core)


def turn(slot, core):
    if isinstance(slot, int):
        return slot if slot in (0, 3) else jnp.where(core == 0, slot, 3 - slot)
    return jnp.where((core == 0) | (slot == 0) | (slot == 3), slot, 3 - slot)


def after(value, *others):
    return lax.optimization_barrier((value, *others))[0]


def meet(anchor, *flights):
    arrays = [f.flying for f in flights]
    _, *arrays = lax.optimization_barrier((anchor, *arrays))
    for f, array in zip(flights, arrays):
        f.flying = array


class Gather:
    def __init__(self, place, piece):
        self.place = place
        self.piece = piece
        self.held = [None] * 4
        self.crossed = [None] * 4

    def chips_near(self, *wait):
        self.piece = after(self.piece, *wait)
        self.flying = self.place.swap_chip(self.piece, 0)

    def chips_far(self):
        self.pair = jnp.stack([self.piece, self.flying])
        self.flying = self.place.swap_chip(self.pair, 1)
        return self.pair

    def join(self):
        self.held[0] = jnp.concatenate([self.pair, self.flying])
        return self.held[0]

    def near(self, *wait):
        self.held[0] = after(self.held[0], *wait)
        self.flying = (self.place.swap_grp(self.held[0], 0), self.place.swap_grp(self.held[0], 1))
        return self.held[0]

    def far(self, *wait):
        self.held[1:3] = self.flying
        first = after(self.held[1], *wait)
        self.flying = self.place.swap_grp(first, 1)

    def landed(self):
        self.held[3] = self.flying

    def cross(self, *which, wait=()):
        for n in which:
            self.crossed[n] = self.place.swap_core(after(self.held[n], *wait))

    def pieces(self):
        return self.held + self.crossed


class Window:
    def __init__(self, gather, start, cols):
        self.arrays = gather.pieces()
        self.start, self.cols = start, cols
        chips, rows, _ = self.arrays[0].shape
        self.chips, self.rows = chips, rows


def fetch(where, window, refs, whole, sem, by):
    rows, cols, chips = window.rows, window.cols, window.chips
    for slot in range(4):
        for side in range(2):
            core = where[0] ^ side
            ref = refs[4 * side + slot]
            distance = turn(slot, core)
            col = pl.multiple_of((where[2] ^ distance) * cols, LANES)
            for k in range(chips):
                row = ((where[1] ^ turn(k, core)) * 2 + core) * rows
                pltpu.make_async_copy(
                    ref.at[k, :, pl.ds(window.start, cols)],
                    whole.at[pl.ds(pl.multiple_of(row, rows), rows), pl.ds(col, cols)],
                    sem.at[distance if by == "grp" else 0],
                ).start()


def weight_call(place, kernel, window, inputs, in_specs, outs, out_specs, steps, by, name, flops, write=True):
    cols, groups = window.cols, place.groups
    pieces = window.arrays
    shape = (window.chips * 2 * window.rows, groups * cols)
    slots = {"grp": groups, "all": 1}[by]
    anywhere = pl.BlockSpec(memory_space=pl.ANY)

    def body(where, *refs):
        taken, refs = refs[: len(pieces)], refs[len(pieces) :]
        *refs, weight, sem, out_sem = refs
        if write:
            *refs, written = refs
        step = pl.program_id(0)

        @pl.when(step == 0)
        def _():
            fetch(where, window, taken, weight, sem, by)

        def ready():
            if by == "all":

                @pl.when(step == 0)
                def _():
                    pltpu.make_async_copy(weight, weight, sem.at[0]).wait()
                    if write:
                        pltpu.make_async_copy(weight, written, out_sem.at[0]).start()

            else:
                at = pl.ds(pl.multiple_of((where[2] ^ step) * cols, LANES), cols)
                view = weight.at[:, at]
                pltpu.make_async_copy(view, view, sem.at[step]).wait()
                pltpu.make_async_copy(view, written.at[:, at], out_sem.at[step]).start()

        kernel(where, ready, weight, *refs)

        @pl.when(step == (steps - 1 if write else -1))
        def _():
            for slot in range(slots if write else 0):
                width = shape[1] // slots
                view = weight.at[:, pl.ds(slot * width, width)]
                pltpu.make_async_copy(view, view, out_sem.at[slot]).wait()

    total = sum(math.prod(x.shape) * x.dtype.itemsize for x in list(inputs) + list(outs))
    return pl.pallas_call(
        body,
        grid_spec=pltpu.PrefetchScalarGridSpec(
            num_scalar_prefetch=1,
            grid=(steps,),
            in_specs=[anywhere] * len(pieces) + in_specs,
            out_specs=out_specs + [anywhere] * write,
            scratch_shapes=[
                pltpu.VMEM(shape, jnp.bfloat16),
                pltpu.SemaphoreType.DMA((slots,)),
                pltpu.SemaphoreType.DMA((slots,)),
            ],
        ),
        out_shape=outs + [shaped(shape, jnp.bfloat16)] * write,
        compiler_params=params(60),
        cost_estimate=cost(flops),
        name=name,
    )(place.scalars, *pieces, *inputs)


def plain_call(kernel, inputs, in_specs, outs, out_specs, steps, name, flops):
    total = sum(math.prod(x.shape) * x.dtype.itemsize for x in list(inputs) + list(outs))
    return pl.pallas_call(
        kernel,
        grid=(steps,),
        in_specs=in_specs,
        out_specs=out_specs,
        out_shape=outs,
        compiler_params=params(60),
        cost_estimate=cost(flops),
        name=name,
    )(*inputs)


TILE = 256


def row_tiles(width):
    return pl.BlockSpec((TILE, width), lambda i, *s: (i, 0))


def fixed(*shape):
    return pl.BlockSpec(shape, lambda i, *s: (0,) * len(shape))


def whole_once(shape):
    return pl.BlockSpec(shape, lambda i: (0,) * len(shape), pipeline_mode=pl.Buffered(1))


def shaped(shape, dtype):
    return jax.ShapeDtypeStruct(shape, dtype)


B_QUERY, B_VALUE, B_ATTN, GAIN_ONE, SHIFT_ONE, B_OUT, GAIN_TWO, SHIFT_TWO, B_IN = range(9)


def row(ref, n):
    return ref[n : n + 1, :]


class Vectors:
    def __init__(self, place, vectors):
        lines = [v.reshape(-1, LANES) for v in vectors]
        blank = jnp.zeros((-sum(x.shape[0] for x in lines) % 16, LANES), jnp.bfloat16)
        self.own = jnp.concatenate([*lines, blank])
        self.place = place
        self.flying = place.swap_core(self.own)

    def chips_near(self):
        self.own = jnp.stack([self.own, self.flying])
        self.flying = self.place.swap_chip(self.own, 0)

    def chips_far(self):
        self.own = jnp.stack([self.own, self.flying])
        self.flying = self.place.swap_chip(self.own, 1)

    def landed(self):
        self.slots = jnp.concatenate([self.own, self.flying])

    def unpack(self, seg_row, keep_row):
        place = self.place
        length = seg_row.shape[1]
        slots, sides, rows, lanes = self.slots.shape
        shards = place.shards

        def kernel(where, in_ref, seg_ref, keep_ref, *outs):
            rows_ref, inner_ref, qkv_ref, seg_col_ref, keep_col_ref = outs
            for line_ref, col_ref in ((seg_ref, seg_col_ref), (keep_ref, keep_col_ref)):
                line = jnp.broadcast_to(line_ref[...].astype(jnp.float32), (8, length))
                col_ref[...] = line.T[:, 0:1].astype(col_ref.dtype)
            width = shards * lanes
            qkv_ref[...] = jnp.zeros_like(qkv_ref)
            for slot in range(slots):
                for side in range(sides):
                    core = where[0] ^ side
                    shard = (where[1] ^ turn(slot, where[0])) * 2 + core
                    part = in_ref[slot, side].astype(jnp.float32)
                    at = pl.multiple_of(shard * lanes, lanes)
                    rows_ref[:, pl.ds(at, lanes)] = part
                    qkv_ref[:, pl.ds(at, lanes)] = part[B_QUERY : B_QUERY + 1]
                    qkv_ref[:, pl.ds(2 * width + at, lanes)] = part[B_VALUE : B_VALUE + 1]
                    for n in range(4):
                        start = pl.multiple_of((shard * 4 + n) * lanes, lanes)
                        inner_ref[:, pl.ds(start, lanes)] = part[B_IN + n : B_IN + n + 1]

        in_vmem = pl.BlockSpec(memory_space=pltpu.VMEM)
        return pl.pallas_call(
            kernel,
            in_specs=[pl.BlockSpec(memory_space=pltpu.SMEM)] + [in_vmem] * 3,
            out_specs=[in_vmem] * 5,
            out_shape=[
                shaped((rows, shards * lanes), jnp.float32),
                shaped((1, 4 * shards * lanes), jnp.float32),
                shaped((1, 3 * shards * lanes), jnp.float32),
                shaped((length, 1), jnp.int32),
                shaped((length, 1), jnp.float32),
            ],
            name="vectors",
        )(place.scalars, self.slots, seg_row, keep_row)


def pack_sums(late_a, late_b, first_sums, second_sums, inner_sums):
    width = first_sums.shape[1]
    half = late_a.shape[1]

    def kernel(a_ref, b_ref, one_ref, two_ref, inner_ref, out_ref):
        def place_of(n):
            return n // 3 * 8 + n % 3

        out_ref[...] = jnp.zeros_like(out_ref)
        for n in (B_QUERY, B_VALUE):
            at = place_of(n)
            out_ref[at : at + 1, 0:half] = a_ref[n : n + 1, :]
            out_ref[at : at + 1, half:width] = b_ref[n : n + 1, :]
        for n, source, line in (
            (GAIN_ONE, one_ref, 0),
            (SHIFT_ONE, one_ref, 1),
            (B_ATTN, one_ref, 2),
            (GAIN_TWO, two_ref, 0),
            (SHIFT_TWO, two_ref, 1),
            (B_OUT, two_ref, 2),
        ):
            at = place_of(n)
            out_ref[at : at + 1, :] = source[line : line + 1, :]
        for n in range(4):
            at = place_of(B_IN + n)
            for shard in range(width // LANES):
                start = (4 * shard + n) * LANES
                out_ref[at : at + 1, shard * LANES : (shard + 1) * LANES] = inner_ref[
                    :, start : start + LANES
                ]

    in_vmem = pl.BlockSpec(memory_space=pltpu.VMEM)
    return pl.pallas_call(
        kernel,
        in_specs=[in_vmem] * 5,
        out_specs=in_vmem,
        out_shape=shaped((32, width), jnp.float32),
        name="pack_sums",
    )(late_a, late_b, first_sums, second_sums, inner_sums)


def project_qkv(place, rows, window, bias, scale):
    length, width = rows.shape
    cols = window.cols

    def kernel(where, ready, weight, x_ref, bias_ref, scale_ref, out_ref):
        ready()
        at = pl.ds(pl.multiple_of((where[2] ^ pl.program_id(0)) * cols, LANES), cols)
        for tile in range(length // TILE):
            here = pl.ds(tile * TILE, TILE)
            mixed = mxu(x_ref[here, :], weight[:, at], NN) + bias_ref[:, at]
            mixed = mixed.astype(jnp.bfloat16).astype(jnp.float32) * scale_ref[:, at]
            out_ref[here, :] = mixed.astype(jnp.bfloat16)

    total = cols * place.groups
    return weight_call(
        place,
        kernel,
        window,
        (rows, bias, scale),
        [fixed(length, width), fixed(1, total), fixed(1, total)],
        [shaped((length, total), jnp.bfloat16)],
        [pl.BlockSpec((length, cols), lambda i, s: (0, i ^ s[2]))],
        place.groups,
        "grp",
        "qkv",
        2 * length * width * total,
    )


def norm_parts(rows):
    centered = rows - jnp.mean(rows, -1, keepdims=True)
    scale = lax.rsqrt(jnp.mean(centered * centered, -1, keepdims=True) + epsilon)
    return centered * scale, scale


def norm_back(grad, normed, scale):
    return scale * (
        grad
        - jnp.mean(grad, -1, keepdims=True)
        - normed * jnp.mean(grad * normed, -1, keepdims=True)
    )


def add_rows(sum_ref, *terms):
    @pl.when(pl.program_id(0) == 0)
    def _():
        sum_ref[...] = jnp.zeros_like(sum_ref)

    for n, term in enumerate(terms):
        sum_ref[n : n + 1, :] += jnp.sum(term, 0, keepdims=True)


def project_out(place, contexts, window, rows, vectors):
    length, width = rows.shape

    def kernel(where, ready, weight, c_ref, x_ref, v_ref, n_ref, r_ref, low_ref):
        ready()
        first_sum = mxu(c_ref[...], weight[...], NN) + row(v_ref, B_ATTN)
        first_sum = first_sum + x_ref[...].astype(jnp.float32)
        normed, scale = norm_parts(first_sum)
        n_ref[...] = normed
        r_ref[...] = jnp.broadcast_to(scale, r_ref.shape)
        low_ref[...] = (normed * row(v_ref, GAIN_ONE) + row(v_ref, SHIFT_ONE)).astype(jnp.bfloat16)

    return weight_call(
        place,
        kernel,
        window,
        (contexts, rows, vectors),
        [row_tiles(width), row_tiles(width), fixed(*vectors.shape)],
        [
            shaped((length, width), jnp.float32),
            shaped((length, LANES), jnp.float32),
            shaped((length, width), jnp.bfloat16),
        ],
        [row_tiles(width), row_tiles(LANES), row_tiles(width)],
        length // TILE,
        "all",
        "attn_out",
        2 * length * width * width,
    )


def feed_in(place, normed_low, window, bias):
    length, width = normed_low.shape
    cols = window.cols

    def kernel(where, ready, weight, x_ref, bias_ref, hid_ref, slope_ref):
        ready()
        at = pl.ds(pl.multiple_of((where[2] ^ pl.program_id(0)) * cols, LANES), cols)
        for tile in range(length // TILE):
            here = pl.ds(tile * TILE, TILE)
            pre = mxu(x_ref[here, :], weight[:, at], NN) + bias_ref[:, at]
            share = 0.5 + 0.5 * lax.erf(pre * (1.0 / math.sqrt(2.0)))
            bell = jnp.exp(-0.5 * pre * pre) * (1.0 / math.sqrt(2.0 * math.pi))
            hid_ref[here, :] = (pre * share).astype(jnp.bfloat16)
            slope_ref[here, :] = (share + pre * bell).astype(jnp.bfloat16)

    total = cols * place.groups
    block = pl.BlockSpec((length, cols), lambda i, s: (0, i ^ s[2]))
    return weight_call(
        place,
        kernel,
        window,
        (normed_low, bias),
        [fixed(length, width), fixed(1, total)],
        [shaped((length, total), jnp.bfloat16)] * 2,
        [block, block],
        place.groups,
        "grp",
        "feed_in",
        2 * length * width * total,
    )


def feed_out(place, hidden, window, normed, cot, keep, vectors, slope):
    length, inner = hidden.shape
    width = normed.shape[1]

    def kernel(where, ready, weight, h_ref, n_ref, cot_ref, keep_ref, v_ref, slope_ref, *outs):
        out_ref, grad_ref, low_ref, sum_ref, pre_ref, inner_ref = outs
        ready()
        fed = mxu(h_ref[...], weight[...], NN)
        normed_one = n_ref[...] * row(v_ref, GAIN_ONE) + row(v_ref, SHIFT_ONE)
        second_sum = normed_one + (fed + row(v_ref, B_OUT))
        second, scale = norm_parts(second_sum)
        out_ref[...] = (second * row(v_ref, GAIN_TWO) + row(v_ref, SHIFT_TWO)).astype(jnp.bfloat16)
        masked = cot_ref[...].astype(jnp.float32) * keep_ref[...]
        grad = norm_back(masked * row(v_ref, GAIN_TWO), second, scale)
        grad_ref[...] = grad
        low = grad.astype(jnp.bfloat16)
        low_ref[...] = low
        add_rows(sum_ref, masked * second, masked, grad)

        @pl.when(pl.program_id(0) == 0)
        def _():
            inner_ref[...] = jnp.zeros_like(inner_ref)

        size = min(1024, inner)
        for n in range(inner // size):
            at = slice(n * size, (n + 1) * size)
            pre = mxu(low, weight[at, :], NT) * slope_ref[:, at].astype(jnp.float32)
            pre_ref[:, at] = pre.astype(jnp.bfloat16)
            inner_ref[:, at] += jnp.sum(pre, 0, keepdims=True)

    return weight_call(
        place,
        kernel,
        window,
        (hidden, normed, cot, keep, vectors, slope),
        [
            row_tiles(inner),
            row_tiles(width),
            row_tiles(width),
            row_tiles(1),
            fixed(*vectors.shape),
            row_tiles(inner),
        ],
        [
            shaped((length, width), jnp.bfloat16),
            shaped((length, width), jnp.float32),
            shaped((length, width), jnp.bfloat16),
            shaped((8, width), jnp.float32),
            shaped((length, inner), jnp.bfloat16),
            shaped((1, inner), jnp.float32),
        ],
        [
            row_tiles(width),
            row_tiles(width),
            row_tiles(width),
            fixed(8, width),
            row_tiles(inner),
            fixed(1, inner),
        ],
        length // TILE,
        "all",
        "feed_out",
        4 * length * width * inner,
        write=False,
    )


def feed_in_back(pre_low, weight, second_grad, normed, scale, vectors, attn_weight):
    length, inner = pre_low.shape
    width = normed.shape[1]

    def kernel(p_ref, w_ref, g_ref, n_ref, r_ref, v_ref, a_ref, first_ref, low_ref, ctx_ref, sum_ref):
        grad = g_ref[...] + mxu(p_ref[...], w_ref[...], NT)
        first = norm_back(grad * row(v_ref, GAIN_ONE), n_ref[...], r_ref[:, :1])
        low = first.astype(jnp.bfloat16)
        first_ref[...] = first
        low_ref[...] = low
        ctx_ref[...] = mxu(low, a_ref[...], NT).astype(jnp.bfloat16)
        add_rows(sum_ref, grad * n_ref[...], grad, first)

    return plain_call(
        kernel,
        (pre_low, weight, second_grad, normed, scale, vectors, attn_weight),
        [
            row_tiles(inner),
            whole_once(weight.shape),
            row_tiles(width),
            row_tiles(width),
            row_tiles(LANES),
            fixed(*vectors.shape),
            whole_once(attn_weight.shape),
        ],
        [
            shaped((length, width), jnp.float32),
            shaped((length, width), jnp.bfloat16),
            shaped((length, width), jnp.bfloat16),
            shaped((8, width), jnp.float32),
        ],
        [row_tiles(width), row_tiles(width), row_tiles(width), fixed(8, width)],
        length // TILE,
        "feed_in_back",
        2 * length * width * (inner + width),
    )


def project_qkv_back(grads, weight, first_grad, start, tiles, before=None):
    length, width = first_grad.shape
    part = width // len(grads)

    def kernel(w_ref, *refs):
        grad_refs, first_ref, out_ref = refs[: len(grads)], refs[len(grads)], refs[-1]
        total = first_ref[...]
        for n in range(3):
            for m, grad_ref in enumerate(grad_refs):
                at = n * width + m * part
                total = total + mxu(grad_ref[n], w_ref[:, at : at + part], NT)
        out_ref[...] = total

    tile = pl.BlockSpec((TILE, width), lambda i: (start + i, 0))
    more = () if before is None else (before,)
    return pl.pallas_call(
        kernel,
        grid=(tiles,),
        in_specs=[whole_once(weight.shape)]
        + [pl.BlockSpec((3, TILE, part), lambda i: (0, start + i, 0))] * len(grads)
        + [tile]
        + [pl.BlockSpec(memory_space=pl.ANY)] * len(more),
        out_specs=tile,
        out_shape=shaped((length, width), jnp.float32),
        input_output_aliases={} if before is None else {len(grads) + 2: 0},
        compiler_params=params(60),
        cost_estimate=cost(6 * tiles * TILE * width * width),
        name="qkv_back",
    )(weight, *grads, first_grad, *more)


ORDER = (1, 3, 0, 2)


def ordered_slot(j):
    return jnp.where(j < 2, 2 * j + 1, 2 * j - 4)


def weight_grad_kernel(where, left_ref, right_ref, own, sent, kept, *, rows, groups, split):
    core = where[0]
    chips = left_ref.shape[1] // (2 * rows)

    @pl.when(pl.program_id(1) == 0)
    def _():
        keep_rows(core, left_ref, rows, kept)

    if split:
        size = min(512, right_ref.shape[1])
        for ref, side in ((sent, 1), (own, 0)):
            for n in range(right_ref.shape[1] // size):
                at = slice(n * size, (n + 1) * size)
                part = mxu(kept[side], right_ref[:, at], NN).astype(jnp.bfloat16)
                ref[0, :, :, at] = part.reshape(chips, rows, size)
    else:
        cols = right_ref.shape[1] // groups
        for ref, side in ((sent, 1), (own, 0)):
            for pos, slot in enumerate(ORDER):
                start = pl.multiple_of((where[2] ^ turn(slot, core ^ side)) * cols, LANES)
                part = mxu(kept[side], right_ref[:, pl.ds(start, cols)], NN)
                ref[pos] = part.astype(jnp.bfloat16).reshape(chips, rows, cols)


def keep_rows(core, left_ref, rows, kept):
    chips = left_ref.shape[1] // (2 * rows)
    for side in range(2):
        chosen = []
        for k in range(chips):
            even = left_ref[:, 2 * k * rows : (2 * k + 1) * rows]
            odd = left_ref[:, (2 * k + 1) * rows : (2 * k + 2) * rows]
            chosen.append(jnp.where(core == side, even, odd))
        left = chosen[0] if chips == 1 else jnp.concatenate(chosen, 1)
        kept[side] = left.T


def turned_rows(place, left):
    tokens, height = left.shape

    def kernel(where, left_ref, out_ref):
        keep_rows(where[0], left_ref, height // place.shards, out_ref)

    in_vmem = pl.BlockSpec(memory_space=pltpu.VMEM)
    return pl.pallas_call(
        kernel,
        in_specs=[pl.BlockSpec(memory_space=pltpu.SMEM), in_vmem],
        out_specs=in_vmem,
        out_shape=shaped((2, height // 2, tokens), jnp.bfloat16),
        compiler_params=params(40),
        name="turned_rows",
    )(place.scalars, left)


def attention_grads_kernel(where, *refs, rows, groups, extra):
    turned, right_ref, *refs = refs
    *more, own, sent, kept = refs
    core, grp = where[0], where[2]
    chips = turned.shape[1] // rows
    step = pl.program_id(0)

    def scatter(lefts, right, at, cols):
        for ref, side in ((sent, 1), (own, 0)):
            part = mxu(lefts[side], right, NN).astype(jnp.bfloat16)
            for g in range(groups):
                pos = position(grp ^ g, core ^ side)
                block = part[:, g * cols : (g + 1) * cols].reshape(chips, rows, cols)
                ref[pos, :, 0:rows, pl.ds(at, cols)] = block

    skip = 0
    if not extra:
        other_left, other_right = more
        skip = other_right.shape[1] // groups

        @pl.when(step == 0)
        def _():
            keep_rows(core, other_left, rows, kept)
            scatter(kept, other_right[...], 0, skip)

    cols = right_ref.shape[2] // groups
    scatter(turned, right_ref[0], pl.multiple_of(skip + step * cols, LANES), cols)

    if extra:
        (sums_ref,) = more

        @pl.when(step == 2)
        def _():
            blank = jnp.zeros((extra, own.shape[3]), jnp.bfloat16)
            for ref, side in ((sent, 1), (own, 0)):
                for g in range(groups):
                    pos = position(grp ^ g, core ^ side)
                    for k in range(chips):
                        start = pl.multiple_of((2 * k + (core ^ side)) * LANES, LANES)
                        ref[pos, k, rows : rows + extra, :] = blank
                        lines = sums_ref[8 * g : 8 * g + 8, pl.ds(start, LANES)]
                        for n in range(3):
                            ref[pos, k, rows : rows + 1, n * LANES : (n + 1) * LANES] = lines[
                                n : n + 1
                            ].astype(jnp.bfloat16)


def position(distance, core):
    slot = turn(distance, core)
    return jnp.where(slot == 0, 2, jnp.where(slot == 1, 0, jnp.where(slot == 3, 1, 3)))


def attention_grads(place, turned, right, more, name):
    height, tokens = 2 * turned.shape[1], turned.shape[2]
    groups, chips = place.groups, place.chips
    rows = height // place.shards
    extra = 16 if len(more) == 1 else 0
    size = right.shape[2]
    cols = 3 * size // groups + (0 if extra else more[1].shape[1] // groups)
    shape = (groups, chips, rows + extra, cols)
    once = [
        pl.BlockSpec(x.shape, lambda i, s: (0, 0), pipeline_mode=pl.Buffered(1)) for x in more
    ]
    return pl.pallas_call(
        functools.partial(attention_grads_kernel, rows=rows, groups=groups, extra=extra),
        grid_spec=pltpu.PrefetchScalarGridSpec(
            num_scalar_prefetch=1,
            grid=(3,),
            in_specs=[
                pl.BlockSpec(turned.shape, lambda i, s: (0, 0, 0), pipeline_mode=pl.Buffered(1)),
                pl.BlockSpec((1, tokens, size), lambda i, s: (i, 0, 0)),
            ]
            + once,
            out_specs=[pl.BlockSpec(shape, lambda i, s: (0, 0, 0, 0))] * 2,
            scratch_shapes=[pltpu.VMEM((8, LANES) if extra else turned.shape, jnp.bfloat16)],
        ),
        out_shape=[shaped(shape, jnp.bfloat16)] * 2,
        compiler_params=params(60),
        cost_estimate=cost(2 * tokens * height * cols * groups),
        name="wgrad_" + name,
    )(place.scalars, turned, right, *more)


def weight_grad(place, left, right, split, name):
    tokens, height = left.shape
    groups, chips = place.groups, place.chips
    rows = height // place.shards
    step_chips = chips if split else max(1, 1024 // (2 * rows))
    cols = right.shape[1] // groups
    if split:
        grid = (1, groups)
        block = lambda i, j, s: (0, s[2] ^ turn(ordered_slot(j), s[0]))
        right_spec = pl.BlockSpec((tokens, cols), block)
        one = (1, chips, rows, cols)
        other = lambda j: jnp.where(j == 0, 3, jnp.where(j == 3, 0, j))
        out_specs = [
            pl.BlockSpec(one, lambda i, j, s: (j, 0, 0, 0)),
            pl.BlockSpec(one, lambda i, j, s: (other(j), 0, 0, 0)),
        ]
    else:
        grid = (chips // step_chips, 1)
        right_spec = pl.BlockSpec(right.shape, lambda i, j, s: (0, 0))
        out_specs = [
            pl.BlockSpec((groups, step_chips, rows, cols), lambda i, j, s: (0, i, 0, 0))
        ] * 2
    return pl.pallas_call(
        functools.partial(weight_grad_kernel, rows=rows, groups=groups, split=split),
        grid_spec=pltpu.PrefetchScalarGridSpec(
            num_scalar_prefetch=1,
            grid=grid,
            in_specs=[
                pl.BlockSpec((tokens, step_chips * 2 * rows), lambda i, j, s: (0, i)),
                right_spec,
            ],
            out_specs=out_specs,
            scratch_shapes=[pltpu.VMEM((2, step_chips * rows, tokens), jnp.bfloat16)],
        ),
        out_shape=[shaped((groups, chips, rows, cols), jnp.bfloat16)] * 2,
        compiler_params=params(60),
        cost_estimate=cost(2 * tokens * height * cols * groups),
        name="wgrad_" + name,
    )(place.scalars, left, right)


def add(*terms):
    total = terms[0].astype(jnp.float32)
    for term in terms[1:]:
        total = total + term.astype(jnp.float32)
    return total.astype(jnp.bfloat16)


class Reduction:
    def __init__(self, place, made):
        self.place = place
        self.made, sent = made
        self.flying = place.swap_core(sent)

    def near(self):
        self.core = self.flying
        leave = add(self.made[:2], self.core[:2])
        self.flying = self.place.swap_grp(leave, 0)
        return leave

    def middle(self):
        self.first = self.flying
        second = add(self.made[3], self.core[3], self.first[1])
        self.flying = self.place.swap_grp(second, 1)
        return second

    def column(self):
        mine = add(self.made[2], self.core[2], self.first[0], self.flying)
        return mine, lambda chip: lax.dynamic_index_in_dim(mine, chip, 0, False)

    def along(self):
        place = self.place
        mine, at = self.column()
        self.mine = [at(place.slot_chip(slot)) for slot in range(4)]
        both = jnp.stack([self.mine[1], self.mine[3]])
        self.flying = place.swap_chip(both, 0)
        return both

    def along_far(self):
        self.first = self.flying
        second = add(self.mine[2], self.first[1])
        self.flying = self.place.swap_chip(second, 1)
        return second

    def share(self):
        return add(self.mine[0], self.first[0], self.flying)

    def along_direct(self):
        place = self.place
        mine, at = self.column()
        self.mine = at(place.chip)
        self.flying = tuple(
            place.permute(at(place.chip ^ k), (2 * k, 2 * k)) for k in range(place.chips - 1, 0, -1)
        )
        return mine

    def share_direct(self):
        return add(self.mine, *self.flying)


class Replication:
    def __init__(self, place, share, direct=False):
        self.place = place
        self.blocks = [share] + [None] * 3
        if direct:
            size = place.shards
            for mask in (3, 1, 2):
                self.blocks[mask] = place.permute(share, (mask * size, mask * size))
        else:
            self.flying = place.swap_grp(share, 0)

    def far(self):
        pair = jnp.stack([self.blocks[0], self.flying])
        self.blocks[1] = self.flying
        self.flying = self.place.swap_grp(pair, 1)
        return pair

    def landed(self):
        if self.blocks[2] is None:
            self.blocks[2:] = [self.flying[0], self.flying[1]]
        return self.blocks


def order_feed_forward(place, blocks, rows_in):
    groups = place.groups
    height, cols = blocks[0].shape
    rows_out = height - groups * rows_in

    def kernel(where, *refs):
        *blocks, out_ref, in_ref = refs
        for slot, ref in enumerate(blocks):
            g = where[2] ^ turn(slot, where[0])
            at = pl.multiple_of(g * cols, LANES)
            out_ref[:, pl.ds(at, cols)] = ref[0:rows_out, :].astype(jnp.float32)
            for n in range(groups):
                at = pl.multiple_of((g * groups + n) * cols, LANES)
                part = ref[rows_out + n * rows_in : rows_out + (n + 1) * rows_in, :]
                in_ref[:, pl.ds(at, cols)] = part.astype(jnp.float32)

    in_vmem = pl.BlockSpec(memory_space=pltpu.VMEM)
    return pl.pallas_call(
        kernel,
        in_specs=[pl.BlockSpec(memory_space=pltpu.SMEM)] + [in_vmem] * groups,
        out_specs=[in_vmem] * 2,
        out_shape=[
            shaped((rows_out, groups * cols), jnp.float32),
            shaped((rows_in, groups * groups * cols), jnp.float32),
        ],
        compiler_params=params(40),
        cost_estimate=cost(height * cols * 1024),
        name="order_feed_forward",
    )(place.scalars, *blocks)


def order_attention(place, blocks_a, blocks_b, rows):
    groups = place.groups
    size = blocks_b[0].shape[1] // 3
    skip = blocks_a[0].shape[1] - 3 * size
    width = groups * skip

    def kernel(where, *refs):
        *blocks, attn_ref, qkv_ref, small_ref = refs
        for n in range(groups):
            ref = blocks[n]
            g = where[2] ^ turn(n, where[0])
            attn_ref[:, pl.ds(pl.multiple_of(g * skip, LANES), skip)] = ref[:, 0:skip].astype(
                jnp.float32
            )
            for part in range(3):
                at = pl.multiple_of(part * width + g * size, LANES)
                block = ref[:, skip + part * size : skip + (part + 1) * size]
                qkv_ref[:, pl.ds(at, size)] = block.astype(jnp.float32)
        for n in range(groups):
            ref = blocks[groups + n]
            g = where[2] ^ n
            lines = []
            for part in range(3):
                at = pl.multiple_of(part * width + width // 2 + g * size, LANES)
                here = slice(part * size, (part + 1) * size)
                qkv_ref[:, pl.ds(at, size)] = ref[0:rows, here].astype(jnp.float32)
                lines.append(ref[rows : rows + 16, here].astype(jnp.float32)[0:1])
            lines.append(jnp.zeros((5, size), jnp.float32))
            small_ref[pl.ds(pl.multiple_of(g * 8, 8), 8), :] = jnp.concatenate(lines)

    in_vmem = pl.BlockSpec(memory_space=pltpu.VMEM)
    return pl.pallas_call(
        kernel,
        in_specs=[pl.BlockSpec(memory_space=pltpu.SMEM)] + [in_vmem] * (2 * groups),
        out_specs=[in_vmem] * 3,
        out_shape=[
            shaped((rows, width), jnp.float32),
            shaped((rows, 3 * width), jnp.float32),
            shaped((8 * groups, size), jnp.float32),
        ],
        compiler_params=params(40),
        name="order_attention",
    )(place.scalars, *blocks_a, *blocks_b)


def on_device_permutes(
    tokens,
    segment_ids,
    keep_flag,
    cotangent,
    w_qkv,
    b_query,
    b_value,
    w_attn_out,
    b_attn_out,
    norm1_gain,
    norm1_bias,
    w_in,
    b_in,
    w_out,
    b_out,
    norm2_gain,
    norm2_bias,
    *,
    groups,
    shards,
):
    place = Place(groups, shards)
    _, length, width = tokens.shape
    rows = tokens[0]
    seg_row = segment_ids.reshape(1, length)
    pairs = width // LANES

    c1 = Gather(place, w_qkv)
    c2 = Gather(place, jnp.concatenate([w_in, w_attn_out], 1))
    c3 = Gather(place, w_out)
    c1.chips_near()
    small = Vectors(
        place,
        (b_query, b_value, b_attn_out, norm1_gain, norm1_bias, b_out, norm2_gain, norm2_bias, b_in),
    )
    meet(rows, c1, small)
    pair = c1.chips_far()
    small.chips_near()
    meet(pair, c1, small)
    joined = c1.join()
    c1.near()
    small.chips_far()
    c2.chips_near(joined)
    meet(joined, c2, small)
    small.landed()
    pair = c2.chips_far()
    vectors, bias_in, qkv_bias, seg_col, keep = small.unpack(
        seg_row, keep_flag.reshape(1, length)
    )
    c1.flying = lax.optimization_barrier(c1.flying)
    turned = turned_rows(place, after(rows, vectors))
    c1.far(pair, vectors)
    c1.cross(0, 1, 2)
    joined = c2.join()
    meet((joined, turned), c1)
    c1.landed()
    c2.near(c1.held[3])
    c1.cross(3)
    c3.chips_near(c1.held[3])
    blank = jnp.ones((1, width), jnp.float32)
    qkv_scale = jnp.concatenate([blank / math.sqrt(HD), blank, blank], 1)

    mixed, full_qkv = project_qkv(place, rows, Window(c1, 0, w_qkv.shape[1]), qkv_bias, qkv_scale)
    meet(mixed, c3)
    pair = c3.chips_far()
    c2.cross(0, wait=(mixed,))
    first, second = pairs * 3 // 8, pairs * 3 // 4
    forward = attention_forward(after(mixed, pair), seg_col, seg_row, 0, first)
    meet(forward[0], c2, c3)
    c2.far()
    joined = c3.join()
    c3.near()
    c2.cross(1, 2)
    forward = attention_forward(
        after(mixed, joined), seg_col, seg_row, first, second - first, forward
    )
    meet(forward[0], c2)
    c2.landed()
    c2.cross(3)
    contexts, probs = attention_forward(
        after(mixed, c2.held[3]), seg_col, seg_row, second, pairs - second, forward
    )
    normed, scale_one, normed_low, full_attn = project_out(
        place, contexts, Window(c2, w_in.shape[1], w_attn_out.shape[1]), rows, vectors
    )
    meet(normed_low, c3)
    c3.far()
    c3.cross(0, 1, 2)
    hidden, slope, full_in = feed_in(
        place, after(normed_low, c3.held[1]), Window(c2, 0, w_in.shape[1]), bias_in
    )
    meet(hidden, c3)
    c3.landed()
    c3.cross(3)
    layer_out, second_grad, out_low, second_sums, pre_low, bias_in_grad = feed_out(
        place, hidden, Window(c3, 0, w_out.shape[1]), normed, cotangent[0], keep, vectors, slope
    )

    r_out = Reduction(place, weight_grad(place, hidden, out_low, False, "out"))
    r_in = Reduction(place, weight_grad(place, after(normed_low, r_out.made), pre_low, True, "in"))
    meet(r_in.made, r_out)
    step = r_out.near()
    first_grad, attn_low, context_grad, first_sums = feed_in_back(
        after(pre_low, r_in.made, step), full_in, second_grad, normed, scale_one, vectors, full_attn
    )
    meet(attn_low, r_in)
    step = r_in.near()
    half, quarter = pairs // 2, pairs // 4

    def back(wait, start, count, at, before=None):
        return attention_backward(
            mixed,
            contexts,
            after(context_grad, *wait),
            probs,
            start,
            count,
            at,
            half,
            before,
        )

    low_a, late_a = back((step,), 0, half, 0)
    meet(late_a, r_out, r_in)
    steps = (r_out.middle(), r_in.middle())
    r_a = Reduction(
        place, attention_grads(place, after(turned, *steps), low_a, (contexts, attn_low), "a")
    )
    meet(r_a.made, r_out)
    step = r_out.along()
    part = back((r_a.made, step), half, quarter, 0)
    meet(part[1], r_out, r_in, r_a)
    steps = (r_out.along_far(), r_in.along(), r_a.near())
    low_b, late_b = back(steps, half + quarter, quarter, quarter, part)
    meet(late_b, r_out, r_in, r_a)
    sums = pack_sums(late_a, late_b, first_sums, second_sums, bias_in_grad)
    share_out = r_out.share()
    steps = (r_in.along_far(), r_a.middle(), share_out)
    r_b = Reduction(place, attention_grads(place, after(turned, *steps), low_b, (sums,), "b"))
    meet(r_b.made, r_in, r_a)
    share_in = r_in.share()
    inner = share_in.shape[1] // groups
    joined = jnp.concatenate(
        [share_out] + [share_in[:, n * inner : (n + 1) * inner] for n in range(groups)]
    )
    all_ffn = Replication(place, joined)
    grads = (low_a, after(low_b, r_b.made, joined, r_a.along()))
    tiles = length // TILE // 2
    input_grad = project_qkv_back(grads, full_qkv, first_grad, 0, tiles)
    meet(input_grad, r_b, r_a, all_ffn)
    steps = (r_b.near(), r_a.along_far())
    input_grad = project_qkv_back(
        grads, full_qkv, after(first_grad, *steps), tiles, tiles, input_grad
    )
    meet(input_grad, r_b, r_a)
    middle = r_b.middle()
    r_a.flying = after(r_a.flying, middle)
    all_a = Replication(place, r_a.share())
    meet(all_a.blocks[0], r_b, all_a)
    along = r_b.along_direct()
    all_a.flying = after(all_a.flying, along)
    all_ffn.flying = after(all_ffn.flying, along)
    pairs_made = (all_a.far(), all_ffn.far())
    meet(pairs_made, r_b)
    share_b = r_b.share_direct()
    all_b = Replication(place, share_b, direct=True)
    meet(share_b, all_ffn)
    w_out_grad, w_in_grad = order_feed_forward(place, all_ffn.landed(), share_in.shape[0])
    all_a.flying = after(all_a.flying, w_out_grad)
    w_attn_grad, w_qkv_grad, small = order_attention(
        place, all_a.landed(), all_b.landed(), w_attn_out.shape[0]
    )
    small = [small[8 * (n // 3) + n % 3] for n in range(12)]
    return (
        layer_out[None],
        input_grad[None],
        w_qkv_grad,
        small[B_QUERY],
        small[B_VALUE],
        w_attn_grad,
        small[B_ATTN],
        small[GAIN_ONE],
        small[SHIFT_ONE],
        w_in_grad,
        jnp.concatenate(small[B_IN:]),
        w_out_grad,
        small[B_OUT],
        small[GAIN_TWO],
        small[SHIFT_TWO],
    )


def solution(mesh):
    groups, shards = mesh.shape["grp"], mesh.shape["shard"]
    if groups == 4 and shards == 8:
        body = functools.partial(on_device_permutes, groups=groups, shards=shards)
    else:
        body = on_device
    return jax.shard_map(
        body,
        mesh=mesh,
        in_specs=(
            P(("grp", "shard"), None, None),
            P(("grp", "shard"), None),
            P(("grp", "shard"), None),
            P(("grp", "shard"), None, None),
            P("shard", "grp"),
            P("shard"),
            P("shard"),
            P("shard", "grp"),
            P("shard"),
            P("shard"),
            P("shard"),
            P("shard", "grp"),
            P("shard"),
            P("shard", "grp"),
            P("shard"),
            P("shard"),
            P("shard"),
        ),
        out_specs=(
            P(("grp", "shard"), None, None),
            P(("grp", "shard"), None, None),
            P("shard", None),
            P("shard"),
            P("shard"),
            P("shard", None),
            P("shard"),
            P("shard"),
            P("shard"),
            P("shard", None),
            P("shard"),
            P("shard", None),
            P("shard"),
            P("shard"),
            P("shard"),
        ),
        check_vma=False,
    )
```

profile of v0, /device:TPU:0, one launch (start us, length us, event | category | flops | bytes accessed | tf_op | source)
XLA Modules:
  0.0 432.8 jit_solution(11291779297922249514)
XLA Ops:
  0.6 3.1 collective-permute-start
  3.7 1.5 concatenate.29
  6.7 2.7 collective-permute-done
  10.4 2.5 collective-permute-start.2
  12.9 2.5 collective-permute-start.3
  16.4 4.3 collective-permute-done.3
  22.9 2.7 collective-permute-start.4
  25.6 1.6 collective-permute-start.7
  27.2 1.5 collective-permute-start.8
  29.3 3.3 collective-permute-start.5
  32.6 2.0 collective-permute-done.5
  35.5 2.9 collective-permute-start.6
  40.4 2.1 vectors.1
  42.4 2.3 collective-permute-done.7.refs_1_
  49.0 5.3 %collective-permute-done.6 = bf16[2,128,1280]{2,1,0:T(8,128)(2,1)} collective-permute-done((bf16[2,128,1280]{2,1,0:T(8,128)(2,1)}, bf16[2,128,1280]{2,1,0:T(8,128)(2,1)}, u32[]{:S(2)}, u32[]{:S(2)}) %collective-permute-start.6) | collective-permute-done | bytes 655392 | tf_op jit(solution)/shard_map/ppermute | solution.py:502
  57.0 1.5 collective-permute-start.15
  61.7 12.8 %qkv.1 = (bf16[1024,3072]{1,0:T(8,128)(2,1)}, bf16[1024,3072]{1,0:T(8,128)(2,1)}) custom-call(s32[3]{0:T(128)} %pad_add_fusion.where, bf16[4,128,768]{2,1,0:T(8,128)(2,1)} %copy-done.7, bf16[4,128,768]{2,1,0:T(8,128)(2,1)} %collective-permute-done.7.refs_1_, bf16[4,128,768]{2,1,0:T(8,128)(2,1)} %collective-permute-done.8.refs_2_, ...), custom_call_target="tpu_custom_call" | custom-call | flops 12884901888 | tf_op jit(solution)/shard_map/qkv/pallas_call | solution.py:648
  74.6 2.5 collective-permute-start.17
  77.1 16.7 %attn_fwd.3 = (bf16[1024,1024]{1,0:T(8,128)(2,1)}, bf16[16,1024,1024]{2,1,0:T(8,128)(2,1)}) custom-call(bf16[1024,3072]{1,0:T(8,128)(2,1)} %get-tuple-element.157.q_ref.k_ref.v_ref.refs_0_.refs_1_.refs_2_, bf16[1024,3072]{1,0:T(8,128)(2,1)} %get-tuple-element.157.q_ref.k_ref.v_ref.refs_0_.refs_1_.refs_2_, ...), custom_call_target="tpu_custom_call" | custom-call | flops 12884901888 | tf_op jit(solution)/shard_map/attn_fwd/pallas_call | solution.py:388
  93.9 1.4 collective-permute-start.18
  96.0 16.7 %attn_fwd.4 = (bf16[1024,1024]{1,0:T(8,128)(2,1)}, bf16[16,1024,1024]{2,1,0:T(8,128)(2,1)}) custom-call(bf16[1024,3072]{1,0:T(8,128)(2,1)} %get-tuple-element.157.q_ref.k_ref.v_ref.refs_0_.refs_1_.refs_2_, bf16[1024,3072]{1,0:T(8,128)(2,1)} %get-tuple-element.157.q_ref.k_ref.v_ref.refs_0_.refs_1_.refs_2_, ...), custom_call_target="tpu_custom_call", output_to_operand_aliasing={{0}: (5, {}), {1}: (6, {})} | custom-call | flops 12884901888 | tf_op jit(solution)/shard_map/attn_fwd/pallas_call | solution.py:388
  115.0 12.3 %attn_fwd.5 = (bf16[1024,1024]{1,0:T(8,128)(2,1)}, bf16[16,1024,1024]{2,1,0:T(8,128)(2,1)}) custom-call(bf16[1024,3072]{1,0:T(8,128)(2,1)} %get-tuple-element.157.q_ref.k_ref.v_ref.refs_0_.refs_1_.refs_2_, bf16[1024,3072]{1,0:T(8,128)(2,1)} %get-tuple-element.157.q_ref.k_ref.v_ref.refs_0_.refs_1_.refs_2_, ...), custom_call_target="tpu_custom_call", output_to_operand_aliasing={{0}: (5, {}), {1}: (6, {})} | custom-call | flops 8589934592 | tf_op jit(solution)/shard_map/attn_fwd/pallas_call | solution.py:388
  128.5 9.6 %attn_out.1 = (f32[1024,1024]{1,0:T(8,128)}, f32[1024,128]{1,0:T(8,128)}, bf16[1024,1024]{1,0:T(8,128)(2,1)}, bf16[1024,1024]{1,0:T(8,128)(2,1)}) custom-call(s32[3]{0:T(128)} %pad_add_fusion.where, bf16[4,128,1280]{2,1,0:T(8,128)(2,1)} %copy-done.4, bf16[4,128,1280]{2,1,0:T(8,128)(2,1)} %collective-permute-done.15.refs_1_, ...), custom_call_target="tpu_custom_call" | custom-call | flops 4294967296 | tf_op jit(solution)/shard_map/attn_out/pallas_call | solution.py:648
  140.1 22.0 %feed_in.1 = (bf16[1024,4096]{1,0:T(8,128)(2,1)}, bf16[1024,4096]{1,0:T(8,128)(2,1)}, bf16[1024,4096]{1,0:T(8,128)(2,1)}) custom-call(s32[3]{0:T(128)} %pad_add_fusion.where, bf16[4,128,1280]{2,1,0:T(8,128)(2,1)} %copy-done.4, bf16[4,128,1280]{2,1,0:T(8,128)(2,1)} %collective-permute-done.15.refs_1_, bf16[4,128,1280]{2,1,0:T(8,128)(2,1)} %collective-permute-done.16.refs_2_, ...), custom_call_target="tpu_custom_call" | custom-call | flops 17179869184 | tf_op jit(solution)/shard_map/feed_in/pallas_call | solution.py:648
  162.2 2.6 collective-permute-done.29.refs_7_
  165.8 32.5 %feed_out.1 = (bf16[1024,1024]{1,0:T(8,128)(2,1)}, f32[1024,1024]{1,0:T(8,128)}, bf16[1024,1024]{1,0:T(8,128)(2,1)}, f32[8,1024]{1,0:T(8,128)}, bf16[1024,4096]{1,0:T(8,128)(2,1)}, /*index=5*/f32[1,4096]{1,0:T(1,128)}) custom-call(s32[3]{0:T(128)} %pad_add_fusion.where, bf16[4,512,256]{2,1,0:T(8,128)(2,1)} %copy-done.5, ...), custom_call_target="tpu_custom_call" | custom-call | flops 34359738368 | tf_op jit(solution)/shard_map/feed_out/pallas_call | solution.py:648
  198.4 14.0 %wgrad_out.1 = (bf16[4,4,512,256]{3,2,1,0:T(8,128)(2,1)}, bf16[4,4,512,256]{3,2,1,0:T(8,128)(2,1)}) custom-call(s32[3]{0:T(128)} %pad_add_fusion.where, bf16[1024,4096]{1,0:T(8,128)(2,1)} %get-tuple-element.165.refs_8_.left_ref, bf16[1024,1024]{1,0:T(8,128)(2,1)} %get-tuple-element.173.right_ref), custom_call_target="tpu_custom_call" | custom-call | flops 17179869184 | tf_op jit(solution)/shard_map/wgrad_out/pallas_call | solution.py:1226
  212.5 14.1 %wgrad_in.1 = (bf16[4,4,128,1024]{3,2,1,0:T(8,128)(2,1)}, bf16[4,4,128,1024]{3,2,1,0:T(8,128)(2,1)}) custom-call(s32[3]{0:T(128)} %pad_add_fusion.where, bf16[1024,1024]{1,0:T(8,128)(2,1)} %get-tuple-element.175.refs_8_.left_ref, bf16[1024,4096]{1,0:T(8,128)(2,1)} %get-tuple-element.179.right_ref.p_ref), custom_call_target="tpu_custom_call" | custom-call | flops 17179869184 | tf_op jit(solution)/shard_map/wgrad_in/pallas_call | solution.py:1226
  226.9 2.7 add_convert_fusion.1
  231.0 21.0 %feed_in_back.1 = (f32[1024,1024]{1,0:T(8,128)}, bf16[1024,1024]{1,0:T(8,128)(2,1)}, bf16[1024,1024]{1,0:T(8,128)(2,1)}, f32[8,1024]{1,0:T(8,128)}) custom-call(bf16[1024,4096]{1,0:T(8,128)(2,1)} %get-tuple-element.179.right_ref.p_ref, bf16[1024,4096]{1,0:T(8,128)(2,1)} %get-tuple-element.180.w_ref, f32[1024,1024]{1,0:T(8,128)} %get-tuple-element.181.g_ref, ...), custom_call_target="tpu_custom_call" | custom-call | flops 21474836480 | tf_op jit(solution)/shard_map/feed_in_back/pallas_call | solution.py:670
  252.1 4.6 %add_convert_fusion = bf16[2,4,128,1024]{3,2,1,0:T(8,128)(2,1)} fusion(bf16[4,4,128,1024]{3,2,1,0:T(8,128)(2,1)} %collective-permute-done.31, bf16[4,4,128,1024]{3,2,1,0:T(8,128)(2,1)} %get-tuple-element.176), kind=kLoop, calls=%fused_computation | loop fusion | flops 4194304 | bytes 6291456 | tf_op jit(solution)/shard_map/convert_element_type | solution.py:1249
  257.4 23.5 %attn_bwd.3 = (bf16[3,1024,512]{2,1,0:T(8,128)(2,1)}, f32[2,512]{1,0:T(2,128)}) custom-call(bf16[1024,3072]{1,0:T(8,128)(2,1)} %get-tuple-element.157.q_ref.k_ref.v_ref.refs_0_.refs_1_.refs_2_, bf16[1024,3072]{1,0:T(8,128)(2,1)} %get-tuple-element.157.q_ref.k_ref.v_ref.refs_0_.refs_1_.refs_2_, ...), custom_call_target="tpu_custom_call" | custom-call | flops 34359738368 | tf_op jit(solution)/shard_map/attn_bwd/pallas_call | solution.py:462
  280.9 2.1 collective-permute-done.33
  283.0 3.5 fusion.4
  286.5 2.2 fusion.3
  289.5 12.3 %wgrad_a.1 = (bf16[4,4,128,640]{3,2,1,0:T(8,128)(2,1)}, bf16[4,4,128,640]{3,2,1,0:T(8,128)(2,1)}) custom-call(s32[3]{0:T(128)} %pad_add_fusion.where, bf16[2,512,1024]{2,1,0:T(8,128)(2,1)} %copy-done.1, bf16[3,1024,512]{2,1,0:T(8,128)(2,1)} %get-tuple-element.190.refs_1_.refs_0_, bf16[1024,1024]{1,0:T(8,128)(2,1)} %get-tuple-element.159.refs_8_.refs_3_.refs_2_, ...), custom_call_target="tpu_custom_call" | custom-call | flops 10737418240 | tf_op jit(solution)/shard_map/wgrad_a/pallas_call | solution.py:1184
  303.6 2.4 fusion.1
  306.9 13.5 %attn_bwd.4 = (bf16[3,1024,512]{2,1,0:T(8,128)(2,1)}, f32[2,512]{1,0:T(2,128)}) custom-call(bf16[1024,3072]{1,0:T(8,128)(2,1)} %get-tuple-element.157.q_ref.k_ref.v_ref.refs_0_.refs_1_.refs_2_, bf16[1024,3072]{1,0:T(8,128)(2,1)} %get-tuple-element.157.q_ref.k_ref.v_ref.refs_0_.refs_1_.refs_2_, ...), custom_call_target="tpu_custom_call" | custom-call | flops 17179869184 | tf_op jit(solution)/shard_map/attn_bwd/pallas_call | solution.py:462
  320.8 3.3 add_convert_fusion.2
  324.1 3.1 fusion
  329.1 1.7 fusion.11
  331.1 13.8 %attn_bwd.5 = (bf16[3,1024,512]{2,1,0:T(8,128)(2,1)}, f32[2,512]{1,0:T(2,128)}) custom-call(bf16[1024,3072]{1,0:T(8,128)(2,1)} %get-tuple-element.157.q_ref.k_ref.v_ref.refs_0_.refs_1_.refs_2_, bf16[1024,3072]{1,0:T(8,128)(2,1)} %get-tuple-element.157.q_ref.k_ref.v_ref.refs_0_.refs_1_.refs_2_, ...), custom_call_target="tpu_custom_call", output_to_operand_aliasing={{0}: (6, {}), {1}: (7, {})} | custom-call | flops 17179869184 | tf_op jit(solution)/shard_map/attn_bwd/pallas_call | solution.py:462
  344.9 1.5 pack_sums.1.refs_2_
  346.4 1.8 collective-permute-done.39
  349.0 1.8 fusion.6
  351.6 1.6 collective-permute-start.42
  353.2 1.9 collective-permute-start.41
  355.2 8.6 %wgrad_b.1 = (bf16[4,4,144,384]{3,2,1,0:T(8,128)(2,1)}, bf16[4,4,144,384]{3,2,1,0:T(8,128)(2,1)}) custom-call(s32[3]{0:T(128)} %pad_add_fusion.where, bf16[2,512,1024]{2,1,0:T(8,128)(2,1)} %copy-done.1, bf16[3,1024,512]{2,1,0:T(8,128)(2,1)} %get-tuple-element.217.refs_1_, f32[32,1024]{1,0:T(8,128)} %pack_sums.1.refs_2_), custom_call_target="tpu_custom_call" | custom-call | flops 6442450944 | tf_op jit(solution)/shard_map/wgrad_b/pallas_call | solution.py:1184
  363.9 2.1 fusion.2
  368.7 8.2 %qkv_back.2.refs_3_ = f32[1024,1024]{1,0:T(8,128)} custom-call(bf16[1024,3072]{1,0:T(8,128)(2,1)} %get-tuple-element.171.w_ref, bf16[3,1024,512]{2,1,0:T(8,128)(2,1)} %get-tuple-element.190.refs_1_.refs_0_, bf16[3,1024,512]{2,1,0:T(8,128)(2,1)} %get-tuple-element.217.refs_1_, f32[1024,1024]{1,0:T(8,128)} %get-tuple-element.222.refs_2_), custom_call_target="tpu_custom_call" | custom-call | flops 6442450944 | tf_op jit(solution)/shard_map/qkv_back/pallas_call | solution.py:1045
  377.0 2.6 add_convert_fusion.5
  380.6 1.6 collective-permute-start.47
  382.2 8.2 %qkv_back.3 = f32[1024,1024]{1,0:T(8,128)} custom-call(bf16[1024,3072]{1,0:T(8,128)(2,1)} %get-tuple-element.171.w_ref, bf16[3,1024,512]{2,1,0:T(8,128)(2,1)} %get-tuple-element.190.refs_1_.refs_0_, bf16[3,1024,512]{2,1,0:T(8,128)(2,1)} %get-tuple-element.217.refs_1_, f32[1024,1024]{1,0:T(8,128)} %get-tuple-element.222.refs_2_, ...), custom_call_target="tpu_custom_call", output_to_operand_aliasing={{}: (4, {})} | custom-call | flops 6442450944 | tf_op jit(solution)/shard_map/qkv_back/pallas_call | solution.py:1045
  390.4 2.4 collective-permute-done.46
  396.3 6.1 %collective-permute-done.49.refs_1_ = bf16[128,640]{1,0:T(8,128)(2,1)S(1)} collective-permute-done((bf16[128,640]{1,0:T(8,128)(2,1)S(1)}, bf16[128,640]{1,0:T(8,128)(2,1)S(1)}, u32[]{:S(2)}, u32[]{:S(2)}) %collective-permute-start.49) | collective-permute-done | bytes 163872 | tf_op jit(solution)/shard_map/ppermute | solution.py:502
  406.7 2.5 collective-permute-start.51
  409.3 1.8 collective-permute-start.53
  411.2 1.5 collective-permute-start.50
  412.7 1.9 collective-permute-done.51
  414.6 4.3 collective-permute-done.52
  419.6 1.7 collective-permute-start.56
  422.6 2.8 order_feed_forward.1
  425.8 3.5 collective-permute-done.56.refs_6_
  429.4 2.1 order_attention.1
  (171 shorter events, 52.0 us)
Async XLA Ops:
  0.6 8.7 %collective-permute-start = (bf16[128,768]{1,0:T(8,128)(2,1)}, bf16[128,768]{1,0:T(8,128)(2,1)S(1)}, u32[]{:S(2)}, u32[]{:S(2)}) collective-permute-start(bf16[128,768]{1,0:T(8,128)(2,1)} %param.21), channel_id=1, source_target_pairs={{0,2},{1,5},{2,0},{3,7},{4,6},{5,1},{6,4},{7,3},{8,10},{9,13},{10,... | collective-permute-start | bytes 589832 | tf_op jit(solution)/shard_map/ppermute | solution.py:502
  5.2 1.4 collective-permute-start.1
  9.3 36.0 %copy-start = (bf16[1,1024,1024]{2,1,0:T(8,128)(2,1)S(1)}, bf16[1,1024,1024]{2,1,0:T(8,128)(2,1)}, u32[]{:S(2)}) copy-start(bf16[1,1024,1024]{2,1,0:T(8,128)(2,1)} %param.17) | copy-start | bytes 6291460
  10.4 11.5 %collective-permute-start.2 = (bf16[2,128,768]{2,1,0:T(8,128)(2,1)S(1)}, bf16[2,128,768]{2,1,0:T(8,128)(2,1)S(1)}, u32[]{:S(2)}, u32[]{:S(2)}) collective-permute-start(bf16[2,128,768]{2,1,0:T(8,128)(2,1)S(1)} %pad_maximum_fusion.8), channel_id=1, source_target_pairs={{0,4},{1,3},{2,6},{3,1},{4,0},{5,7},{6,2},{7,5},{8,12},{9,11},{10,... | collective-permute-start | bytes 1179656 | tf_op jit(solution)/shard_map/ppermute | solution.py:502
  12.9 7.8 %collective-permute-start.3 = (bf16[2,16,128]{2,1,0:T(8,128)(2,1)S(1)}, bf16[2,16,128]{2,1,0:T(8,128)(2,1)S(1)}, u32[]{:S(2)}, u32[]{:S(2)}) collective-permute-start(bf16[2,16,128]{2,1,0:T(8,128)(2,1)S(1)} %get-tuple-element.269), channel_id=1, source_target_pairs={{0,2},{1,5},{2,0},{3,7},{4,6},{5,1},{6,4},{7,3},{8,10},{9,13},{10,... | collective-permute-start | bytes 24584 | tf_op jit(solution)/shard_map/ppermute | solution.py:502
  22.9 24.2 %copy-start.7 = (bf16[4,128,768]{2,1,0:T(8,128)(2,1)}, bf16[4,128,768]{2,1,0:T(8,128)(2,1)S(1)}, u32[]{:S(2)}) copy-start(bf16[4,128,768]{2,1,0:T(8,128)(2,1)S(1)} %pad_maximum_fusion.3.refs_0_) | copy-start | bytes 2359300
  22.9 11.7 %collective-permute-start.4 = (bf16[128,1280]{1,0:T(8,128)(2,1)S(1)}, bf16[128,1280]{1,0:T(8,128)(2,1)S(1)}, u32[]{:S(2)}, u32[]{:S(2)}) collective-permute-start(bf16[128,1280]{1,0:T(8,128)(2,1)S(1)} %pad_maximum_fusion.9), channel_id=1, source_target_pairs={{0,2},{1,5},{2,0},{3,7},{4,6},{5,1},{6,4},{7,3},{8,10},{9,13},{10,... | collective-permute-start | bytes 983048 | tf_op jit(solution)/shard_map/ppermute | solution.py:502
  25.6 19.2 %collective-permute-start.7 = (bf16[4,128,768]{2,1,0:T(8,128)(2,1)S(1)}, bf16[4,128,768]{2,1,0:T(8,128)(2,1)}, u32[]{:S(2)}, u32[]{:S(2)}) collective-permute-start(bf16[4,128,768]{2,1,0:T(8,128)(2,1)S(1)} %pad_maximum_fusion.3.refs_0_), channel_id=1, source_target_pairs={{0,8},{1,17},{2,10},{3,19},{4,12},{5,21},{6,14},{7,23},{8,0},{9,25... | collective-permute-start | bytes 2359304 | tf_op jit(solution)/shard_map/ppermute | solution.py:502
  27.2 17.6 %collective-permute-start.8 = (bf16[4,128,768]{2,1,0:T(8,128)(2,1)S(1)}, bf16[4,128,768]{2,1,0:T(8,128)(2,1)}, u32[]{:S(2)}, u32[]{:S(2)}) collective-permute-start(bf16[4,128,768]{2,1,0:T(8,128)(2,1)S(1)} %pad_maximum_fusion.3.refs_0_), channel_id=1, source_target_pairs={{0,16},{1,9},{2,18},{3,11},{4,20},{5,13},{6,22},{7,15},{8,24},{9,1... | collective-permute-start | bytes 2359304 | tf_op jit(solution)/shard_map/ppermute | solution.py:502
  29.3 5.3 %collective-permute-start.5 = (bf16[2,2,16,128]{3,2,1,0:T(8,128)(2,1)}, bf16[2,2,16,128]{3,2,1,0:T(8,128)(2,1)}, u32[]{:S(2)}, u32[]{:S(2)}) collective-permute-start(bf16[2,2,16,128]{3,2,1,0:T(8,128)(2,1)} %pad_maximum_fusion.13), channel_id=1, source_target_pairs={{0,4},{1,3},{2,6},{3,1},{4,0},{5,7},{6,2},{7,5},{8,12},{9,11},{10,... | collective-permute-start | bytes 49160 | tf_op jit(solution)/shard_map/ppermute | solution.py:502
  35.5 18.8 %collective-permute-start.6 = (bf16[2,128,1280]{2,1,0:T(8,128)(2,1)}, bf16[2,128,1280]{2,1,0:T(8,128)(2,1)}, u32[]{:S(2)}, u32[]{:S(2)}) collective-permute-start(bf16[2,128,1280]{2,1,0:T(8,128)(2,1)} %pad_maximum_fusion.4), channel_id=1, source_target_pairs={{0,4},{1,3},{2,6},{3,1},{4,0},{5,7},{6,2},{7,5},{8,12},{9,11},{10,... | collective-permute-start | bytes 1966088 | tf_op jit(solution)/shard_map/ppermute | solution.py:502
  44.8 12.2 %collective-permute-start.9 = (bf16[4,128,768]{2,1,0:T(8,128)(2,1)}, bf16[4,128,768]{2,1,0:T(8,128)(2,1)S(1)}, u32[]{:S(2)}, u32[]{:S(2)}) collective-permute-start(bf16[4,128,768]{2,1,0:T(8,128)(2,1)} %collective-permute-done.7.refs_1_), channel_id=1, source_target_pairs={{0,16},{1,9},{2,18},{3,11},{4,20},{5,13},{6,22},{7,15},{8,24},{9,1... | collective-permute-start | bytes 2359304 | tf_op jit(solution)/shard_map/ppermute | solution.py:502
  45.3 13.2 %collective-permute-start.10 = (bf16[4,128,768]{2,1,0:T(8,128)(2,1)S(1)}, bf16[4,128,768]{2,1,0:T(8,128)(2,1)S(1)}, u32[]{:S(2)}, u32[]{:S(2)}) collective-permute-start(bf16[4,128,768]{2,1,0:T(8,128)(2,1)S(1)} %pad_maximum_fusion.3.refs_0_), channel_id=1, source_target_pairs={{0,1},{1,0},{2,3},{3,2},{4,5},{5,4},{6,7},{7,6},{8,9},{9,8},{10,11... | collective-permute-start | bytes 2359304 | tf_op jit(solution)/shard_map/ppermute | solution.py:502
  48.5 10.5 %collective-permute-start.11 = (bf16[4,128,768]{2,1,0:T(8,128)(2,1)}, bf16[4,128,768]{2,1,0:T(8,128)(2,1)S(1)}, u32[]{:S(2)}, u32[]{:S(2)}) collective-permute-start(bf16[4,128,768]{2,1,0:T(8,128)(2,1)} %collective-permute-done.7.refs_1_), channel_id=1, source_target_pairs={{0,1},{1,0},{2,3},{3,2},{4,5},{5,4},{6,7},{7,6},{8,9},{9,8},{10,11... | collective-permute-start | bytes 2359304 | tf_op jit(solution)/shard_map/ppermute | solution.py:502
  49.0 10.9 %collective-permute-start.12 = (bf16[4,128,768]{2,1,0:T(8,128)(2,1)}, bf16[4,128,768]{2,1,0:T(8,128)(2,1)S(1)}, u32[]{:S(2)}, u32[]{:S(2)}) collective-permute-start(bf16[4,128,768]{2,1,0:T(8,128)(2,1)} %collective-permute-done.8.refs_2_), channel_id=1, source_target_pairs={{0,1},{1,0},{2,3},{3,2},{4,5},{5,4},{6,7},{7,6},{8,9},{9,8},{10,11... | collective-permute-start | bytes 2359304 | tf_op jit(solution)/shard_map/ppermute | solution.py:502
  55.6 21.6 %copy-start.4 = (bf16[4,128,1280]{2,1,0:T(8,128)(2,1)}, bf16[4,128,1280]{2,1,0:T(8,128)(2,1)S(1)}, u32[]{:S(2)}) copy-start(bf16[4,128,1280]{2,1,0:T(8,128)(2,1)S(1)} %pad_maximum_fusion.refs_0_) | copy-start | bytes 3932164
  57.0 2.9 collective-permute-start.13
  57.0 36.9 %collective-permute-start.15 = (bf16[4,128,1280]{2,1,0:T(8,128)(2,1)S(1)}, bf16[4,128,1280]{2,1,0:T(8,128)(2,1)}, u32[]{:S(2)}, u32[]{:S(2)}) collective-permute-start(bf16[4,128,1280]{2,1,0:T(8,128)(2,1)S(1)} %pad_maximum_fusion.refs_0_), channel_id=1, source_target_pairs={{0,8},{1,17},{2,10},{3,19},{4,12},{5,21},{6,14},{7,23},{8,0},{9,25... | collective-permute-start | bytes 3932168 | tf_op jit(solution)/shard_map/ppermute | solution.py:502
  58.5 35.4 %collective-permute-start.16 = (bf16[4,128,1280]{2,1,0:T(8,128)(2,1)S(1)}, bf16[4,128,1280]{2,1,0:T(8,128)(2,1)}, u32[]{:S(2)}, u32[]{:S(2)}) collective-permute-start(bf16[4,128,1280]{2,1,0:T(8,128)(2,1)S(1)} %pad_maximum_fusion.refs_0_), channel_id=1, source_target_pairs={{0,16},{1,9},{2,18},{3,11},{4,20},{5,13},{6,22},{7,15},{8,24},{9,1... | collective-permute-start | bytes 3932168 | tf_op jit(solution)/shard_map/ppermute | solution.py:502
  59.0 15.5 %collective-permute-start.14 = (bf16[512,256]{1,0:T(8,128)(2,1)S(1)}, bf16[512,256]{1,0:T(8,128)(2,1)S(1)}, u32[]{:S(2)}, u32[]{:S(2)}) collective-permute-start(bf16[512,256]{1,0:T(8,128)(2,1)S(1)} %copy-done.6), channel_id=1, source_target_pairs={{0,2},{1,5},{2,0},{3,7},{4,6},{5,1},{6,4},{7,3},{8,10},{9,13},{10,... | collective-permute-start | bytes 786440 | tf_op jit(solution)/shard_map/ppermute | solution.py:502
  74.6 19.3 %collective-permute-start.17 = (bf16[2,512,256]{2,1,0:T(8,128)(2,1)S(1)}, bf16[2,512,256]{2,1,0:T(8,128)(2,1)S(1)}, u32[]{:S(2)}, u32[]{:S(2)}) collective-permute-start(bf16[2,512,256]{2,1,0:T(8,128)(2,1)S(1)} %pad_maximum_fusion.5), channel_id=1, source_target_pairs={{0,4},{1,3},{2,6},{3,1},{4,0},{5,7},{6,2},{7,5},{8,12},{9,11},{10,... | collective-permute-start | bytes 1572872 | tf_op jit(solution)/shard_map/ppermute | solution.py:502
  77.1 36.6 %collective-permute-start.19 = (bf16[4,128,1280]{2,1,0:T(8,128)(2,1)S(1)}, bf16[4,128,1280]{2,1,0:T(8,128)(2,1)}, u32[]{:S(2)}, u32[]{:S(2)}) collective-permute-start(bf16[4,128,1280]{2,1,0:T(8,128)(2,1)S(1)} %pad_maximum_fusion.refs_0_), channel_id=1, source_target_pairs={{0,1},{1,0},{2,3},{3,2},{4,5},{5,4},{6,7},{7,6},{8,9},{9,8},{10,11... | collective-permute-start | bytes 3932168 | tf_op jit(solution)/shard_map/ppermute | solution.py:502
  93.9 18.8 %collective-permute-start.18 = (bf16[4,128,1280]{2,1,0:T(8,128)(2,1)}, bf16[4,128,1280]{2,1,0:T(8,128)(2,1)}, u32[]{:S(2)}, u32[]{:S(2)}) collective-permute-start(bf16[4,128,1280]{2,1,0:T(8,128)(2,1)} %collective-permute-done.15.refs_1_), channel_id=1, source_target_pairs={{0,16},{1,9},{2,18},{3,11},{4,20},{5,13},{6,22},{7,15},{8,24},{9,1... | collective-permute-start | bytes 3932168 | tf_op jit(solution)/shard_map/ppermute | solution.py:502
  95.3 32.0 %collective-permute-start.20 = (bf16[4,128,1280]{2,1,0:T(8,128)(2,1)}, bf16[4,128,1280]{2,1,0:T(8,128)(2,1)}, u32[]{:S(2)}, u32[]{:S(2)}) collective-permute-start(bf16[4,128,1280]{2,1,0:T(8,128)(2,1)} %collective-permute-done.15.refs_1_), channel_id=1, source_target_pairs={{0,1},{1,0},{2,3},{3,2},{4,5},{5,4},{6,7},{7,6},{8,9},{9,8},{10,11... | collective-permute-start | bytes 3932168 | tf_op jit(solution)/shard_map/ppermute | solution.py:502
  95.4 31.9 %copy-start.5 = (bf16[4,512,256]{2,1,0:T(8,128)(2,1)}, bf16[4,512,256]{2,1,0:T(8,128)(2,1)S(1)}, u32[]{:S(2)}) copy-start(bf16[4,512,256]{2,1,0:T(8,128)(2,1)S(1)} %pad_maximum_fusion.1.refs_0_) | copy-start | bytes 3145732
  95.4 32.0 %collective-permute-start.21 = (bf16[4,128,1280]{2,1,0:T(8,128)(2,1)}, bf16[4,128,1280]{2,1,0:T(8,128)(2,1)S(1)}, u32[]{:S(2)}, u32[]{:S(2)}) collective-permute-start(bf16[4,128,1280]{2,1,0:T(8,128)(2,1)} %collective-permute-done.16.refs_2_), channel_id=1, source_target_pairs={{0,1},{1,0},{2,3},{3,2},{4,5},{5,4},{6,7},{7,6},{8,9},{9,8},{10,11... | collective-permute-start | bytes 3932168 | tf_op jit(solution)/shard_map/ppermute | solution.py:502
  112.7 14.7 %collective-permute-start.22 = (bf16[4,128,1280]{2,1,0:T(8,128)(2,1)}, bf16[4,128,1280]{2,1,0:T(8,128)(2,1)}, u32[]{:S(2)}, u32[]{:S(2)}) collective-permute-start(bf16[4,128,1280]{2,1,0:T(8,128)(2,1)} %collective-permute-done.18.refs_3_), channel_id=1, source_target_pairs={{0,1},{1,0},{2,3},{3,2},{4,5},{5,4},{6,7},{7,6},{8,9},{9,8},{10,11... | collective-permute-start | bytes 3932168 | tf_op jit(solution)/shard_map/ppermute | solution.py:502
  113.1 25.8 %collective-permute-start.23 = (bf16[4,512,256]{2,1,0:T(8,128)(2,1)S(1)}, bf16[4,512,256]{2,1,0:T(8,128)(2,1)}, u32[]{:S(2)}, u32[]{:S(2)}) collective-permute-start(bf16[4,512,256]{2,1,0:T(8,128)(2,1)S(1)} %pad_maximum_fusion.1.refs_0_), channel_id=1, source_target_pairs={{0,8},{1,17},{2,10},{3,19},{4,12},{5,21},{6,14},{7,23},{8,0},{9,25... | collective-permute-start | bytes 3145736 | tf_op jit(solution)/shard_map/ppermute | solution.py:502
  113.7 25.2 %collective-permute-start.24 = (bf16[4,512,256]{2,1,0:T(8,128)(2,1)S(1)}, bf16[4,512,256]{2,1,0:T(8,128)(2,1)S(1)}, u32[]{:S(2)}, u32[]{:S(2)}) collective-permute-start(bf16[4,512,256]{2,1,0:T(8,128)(2,1)S(1)} %pad_maximum_fusion.1.refs_0_), channel_id=1, source_target_pairs={{0,16},{1,9},{2,18},{3,11},{4,20},{5,13},{6,22},{7,15},{8,24},{9,1... | collective-permute-start | bytes 3145736 | tf_op jit(solution)/shard_map/ppermute | solution.py:502
  127.4 34.8 %collective-permute-start.26 = (bf16[4,512,256]{2,1,0:T(8,128)(2,1)S(1)}, bf16[4,512,256]{2,1,0:T(8,128)(2,1)}, u32[]{:S(2)}, u32[]{:S(2)}) collective-permute-start(bf16[4,512,256]{2,1,0:T(8,128)(2,1)S(1)} %pad_maximum_fusion.1.refs_0_), channel_id=1, source_target_pairs={{0,1},{1,0},{2,3},{3,2},{4,5},{5,4},{6,7},{7,6},{8,9},{9,8},{10,11... | collective-permute-start | bytes 3145736 | tf_op jit(solution)/shard_map/ppermute | solution.py:502
  138.9 23.2 %copy-start.16 = (bf16[4,512,256]{2,1,0:T(8,128)(2,1)}, bf16[4,512,256]{2,1,0:T(8,128)(2,1)S(1)}, u32[]{:S(2)}) copy-start(bf16[4,512,256]{2,1,0:T(8,128)(2,1)S(1)} %collective-permute-done.24.refs_2_) | copy-start | bytes 3145732
  138.9 23.2 %collective-permute-start.25 = (bf16[4,512,256]{2,1,0:T(8,128)(2,1)}, bf16[4,512,256]{2,1,0:T(8,128)(2,1)S(1)}, u32[]{:S(2)}, u32[]{:S(2)}) collective-permute-start(bf16[4,512,256]{2,1,0:T(8,128)(2,1)} %collective-permute-done.23.refs_1_), channel_id=1, source_target_pairs={{0,16},{1,9},{2,18},{3,11},{4,20},{5,13},{6,22},{7,15},{8,24},{9,1... | collective-permute-start | bytes 3145736 | tf_op jit(solution)/shard_map/ppermute | solution.py:502
  139.6 22.6 %collective-permute-start.27 = (bf16[4,512,256]{2,1,0:T(8,128)(2,1)}, bf16[4,512,256]{2,1,0:T(8,128)(2,1)}, u32[]{:S(2)}, u32[]{:S(2)}) collective-permute-start(bf16[4,512,256]{2,1,0:T(8,128)(2,1)} %collective-permute-done.23.refs_1_), channel_id=1, source_target_pairs={{0,1},{1,0},{2,3},{3,2},{4,5},{5,4},{6,7},{7,6},{8,9},{9,8},{10,11... | collective-permute-start | bytes 3145736 | tf_op jit(solution)/shard_map/ppermute | solution.py:502
  139.6 22.7 %collective-permute-start.28 = (bf16[4,512,256]{2,1,0:T(8,128)(2,1)S(1)}, bf16[4,512,256]{2,1,0:T(8,128)(2,1)}, u32[]{:S(2)}, u32[]{:S(2)}) collective-permute-start(bf16[4,512,256]{2,1,0:T(8,128)(2,1)S(1)} %collective-permute-done.24.refs_2_), channel_id=1, source_target_pairs={{0,1},{1,0},{2,3},{3,2},{4,5},{5,4},{6,7},{7,6},{8,9},{9,8},{10,11... | collective-permute-start | bytes 3145736 | tf_op jit(solution)/shard_map/ppermute | solution.py:502
  162.1 2.7 collective-permute-start.29
  212.3 14.6 %collective-permute-start.30 = (bf16[4,4,512,256]{3,2,1,0:T(8,128)(2,1)}, bf16[4,4,512,256]{3,2,1,0:T(8,128)(2,1)}, u32[]{:S(2)}, u32[]{:S(2)}) collective-permute-start(bf16[4,4,512,256]{3,2,1,0:T(8,128)(2,1)} %get-tuple-element.177), channel_id=1, source_target_pairs={{0,1},{1,0},{2,3},{3,2},{4,5},{5,4},{6,7},{7,6},{8,9},{9,8},{10,11... | collective-permute-start | bytes 12582920 | tf_op jit(solution)/shard_map/ppermute | solution.py:502
  226.6 25.5 %collective-permute-start.31 = (bf16[4,4,128,1024]{3,2,1,0:T(8,128)(2,1)}, bf16[4,4,128,1024]{3,2,1,0:T(8,128)(2,1)}, u32[]{:S(2)}, u32[]{:S(2)}) collective-permute-start(bf16[4,4,128,1024]{3,2,1,0:T(8,128)(2,1)} %get-tuple-element.186), channel_id=1, source_target_pairs={{0,1},{1,0},{2,3},{3,2},{4,5},{5,4},{6,7},{7,6},{8,9},{9,8},{10,11... | collective-permute-start | bytes 12582920 | tf_op jit(solution)/shard_map/ppermute | solution.py:502
  229.7 53.4 %collective-permute-start.32 = (bf16[2,4,512,256]{3,2,1,0:T(8,128)(2,1)S(1)}, bf16[2,4,512,256]{3,2,1,0:T(8,128)(2,1)}, u32[]{:S(2)}, u32[]{:S(2)}) collective-permute-start(bf16[2,4,512,256]{3,2,1,0:T(8,128)(2,1)S(1)} %add_convert_fusion.1), channel_id=1, source_target_pairs={{0,8},{1,17},{2,10},{3,19},{4,12},{5,21},{6,14},{7,23},{8,0},{9,25... | collective-permute-start | bytes 6291464 | tf_op jit(solution)/shard_map/ppermute | solution.py:502
  256.7 26.4 %collective-permute-start.33 = (bf16[2,4,128,1024]{3,2,1,0:T(8,128)(2,1)}, bf16[2,4,128,1024]{3,2,1,0:T(8,128)(2,1)}, u32[]{:S(2)}, u32[]{:S(2)}) collective-permute-start(bf16[2,4,128,1024]{3,2,1,0:T(8,128)(2,1)} %add_convert_fusion), channel_id=1, source_target_pairs={{0,8},{1,17},{2,10},{3,19},{4,12},{5,21},{6,14},{7,23},{8,0},{9,25... | collective-permute-start | bytes 6291464 | tf_op jit(solution)/shard_map/ppermute | solution.py:502
  288.7 14.9 %collective-permute-start.34 = (bf16[4,512,256]{2,1,0:T(8,128)(2,1)S(1)}, bf16[4,512,256]{2,1,0:T(8,128)(2,1)S(1)}, u32[]{:S(2)}, u32[]{:S(2)}) collective-permute-start(bf16[4,512,256]{2,1,0:T(8,128)(2,1)S(1)} %fusion.3), channel_id=1, source_target_pairs={{0,16},{1,9},{2,18},{3,11},{4,20},{5,13},{6,22},{7,15},{8,24},{9,1... | collective-permute-start | bytes 3145736 | tf_op jit(solution)/shard_map/ppermute | solution.py:502
  301.8 19.0 %collective-permute-start.37 = (bf16[4,4,128,640]{3,2,1,0:T(8,128)(2,1)}, bf16[4,4,128,640]{3,2,1,0:T(8,128)(2,1)}, u32[]{:S(2)}, u32[]{:S(2)}) collective-permute-start(bf16[4,4,128,640]{3,2,1,0:T(8,128)(2,1)} %get-tuple-element.199), channel_id=1, source_target_pairs={{0,1},{1,0},{2,3},{3,2},{4,5},{5,4},{6,7},{7,6},{8,9},{9,8},{10,11... | collective-permute-start | bytes 7864328 | tf_op jit(solution)/shard_map/ppermute | solution.py:502
  301.8 18.6 %collective-permute-start.36 = (bf16[4,128,1024]{2,1,0:T(8,128)(2,1)}, bf16[4,128,1024]{2,1,0:T(8,128)(2,1)}, u32[]{:S(2)}, u32[]{:S(2)}) collective-permute-start(bf16[4,128,1024]{2,1,0:T(8,128)(2,1)} %fusion.4), channel_id=1, source_target_pairs={{0,16},{1,9},{2,18},{3,11},{4,20},{5,13},{6,22},{7,15},{8,24},{9,1... | collective-permute-start | bytes 3145736 | tf_op jit(solution)/shard_map/ppermute | solution.py:502
  306.1 14.7 %collective-permute-start.35 = (bf16[2,512,256]{2,1,0:T(8,128)(2,1)S(1)}, bf16[2,512,256]{2,1,0:T(8,128)(2,1)S(1)}, u32[]{:S(2)}, u32[]{:S(2)}) collective-permute-start(bf16[2,512,256]{2,1,0:T(8,128)(2,1)S(1)} %pad_maximum_fusion.6), channel_id=1, source_target_pairs={{0,2},{1,5},{2,0},{3,7},{4,6},{5,1},{6,4},{7,3},{8,10},{9,13},{10,... | collective-permute-start | bytes 1572872 | tf_op jit(solution)/shard_map/ppermute | solution.py:502
  327.3 21.7 %collective-permute-start.40 = (bf16[2,4,128,640]{3,2,1,0:T(8,128)(2,1)}, bf16[2,4,128,640]{3,2,1,0:T(8,128)(2,1)}, u32[]{:S(2)}, u32[]{:S(2)}) collective-permute-start(bf16[2,4,128,640]{3,2,1,0:T(8,128)(2,1)} %add_convert_fusion.2), channel_id=1, source_target_pairs={{0,8},{1,17},{2,10},{3,19},{4,12},{5,21},{6,14},{7,23},{8,0},{9,25... | collective-permute-start | bytes 3932168 | tf_op jit(solution)/shard_map/ppermute | solution.py:502
  328.3 19.8 %collective-permute-start.39 = (bf16[2,128,1024]{2,1,0:T(8,128)(2,1)S(1)}, bf16[2,128,1024]{2,1,0:T(8,128)(2,1)S(1)}, u32[]{:S(2)}, u32[]{:S(2)}) collective-permute-start(bf16[2,128,1024]{2,1,0:T(8,128)(2,1)S(1)} %pad_maximum_fusion.7), channel_id=1, source_target_pairs={{0,2},{1,5},{2,0},{3,7},{4,6},{5,1},{6,4},{7,3},{8,10},{9,13},{10,... | collective-permute-start | bytes 1572872 | tf_op jit(solution)/shard_map/ppermute | solution.py:502
  330.8 15.6 %collective-permute-start.38 = (bf16[512,256]{1,0:T(8,128)(2,1)}, bf16[512,256]{1,0:T(8,128)(2,1)S(1)}, u32[]{:S(2)}, u32[]{:S(2)}) collective-permute-start(bf16[512,256]{1,0:T(8,128)(2,1)} %fusion.11), channel_id=1, source_target_pairs={{0,4},{1,3},{2,6},{3,1},{4,0},{5,7},{6,2},{7,5},{8,12},{9,11},{10,... | collective-permute-start | bytes 786440 | tf_op jit(solution)/shard_map/ppermute | solution.py:502
  351.6 12.3 %collective-permute-start.42 = (bf16[4,128,640]{2,1,0:T(8,128)(2,1)S(1)}, bf16[4,128,640]{2,1,0:T(8,128)(2,1)}, u32[]{:S(2)}, u32[]{:S(2)}) collective-permute-start(bf16[4,128,640]{2,1,0:T(8,128)(2,1)S(1)} %fusion.6), channel_id=1, source_target_pairs={{0,16},{1,9},{2,18},{3,11},{4,20},{5,13},{6,22},{7,15},{8,24},{9,1... | collective-permute-start | bytes 1966088 | tf_op jit(solution)/shard_map/ppermute | solution.py:502
  353.2 10.6 %collective-permute-start.41 = (bf16[128,1024]{1,0:T(8,128)(2,1)}, bf16[128,1024]{1,0:T(8,128)(2,1)S(1)}, u32[]{:S(2)}, u32[]{:S(2)}) collective-permute-start(bf16[128,1024]{1,0:T(8,128)(2,1)} %fusion.12), channel_id=1, source_target_pairs={{0,4},{1,3},{2,6},{3,1},{4,0},{5,7},{6,2},{7,5},{8,12},{9,11},{10,... | collective-permute-start | bytes 786440 | tf_op jit(solution)/shard_map/ppermute | solution.py:502
  363.8 13.1 %collective-permute-start.43 = (bf16[4,4,144,384]{3,2,1,0:T(8,128)(2,1)}, bf16[4,4,144,384]{3,2,1,0:T(8,128)(2,1)}, u32[]{:S(2)}, u32[]{:S(2)}) collective-permute-start(bf16[4,4,144,384]{3,2,1,0:T(8,128)(2,1)} %get-tuple-element.219), channel_id=1, source_target_pairs={{0,1},{1,0},{2,3},{3,2},{4,5},{5,4},{6,7},{7,6},{8,9},{9,8},{10,11... | collective-permute-start | bytes 5308424 | tf_op jit(solution)/shard_map/ppermute | solution.py:502
  366.1 10.9 %collective-permute-start.44 = (bf16[2,128,640]{2,1,0:T(8,128)(2,1)S(1)}, bf16[2,128,640]{2,1,0:T(8,128)(2,1)S(1)}, u32[]{:S(2)}, u32[]{:S(2)}) collective-permute-start(bf16[2,128,640]{2,1,0:T(8,128)(2,1)S(1)} %pad_maximum_fusion.10), channel_id=1, source_target_pairs={{0,2},{1,5},{2,0},{3,7},{4,6},{5,1},{6,4},{7,3},{8,10},{9,13},{10,... | collective-permute-start | bytes 983048 | tf_op jit(solution)/shard_map/ppermute | solution.py:502
  367.6 9.4 %collective-permute-start.45 = (bf16[1024,256]{1,0:T(8,128)(2,1)S(1)}, bf16[1024,256]{1,0:T(8,128)(2,1)S(1)}, u32[]{:S(2)}, u32[]{:S(2)}) collective-permute-start(bf16[1024,256]{1,0:T(8,128)(2,1)S(1)} %slice_dynamic-update-slice_fusion.refs_0_), channel_id=1, source_target_pairs={{0,8},{1,17},{2,10},{3,19},{4,12},{5,21},{6,14},{7,23},{8,0},{9,25... | collective-permute-start | bytes 1572872 | tf_op jit(solution)/shard_map/ppermute | solution.py:502
  379.5 13.3 %collective-permute-start.46 = (bf16[2,4,144,384]{3,2,1,0:T(8,128)(2,1)}, bf16[2,4,144,384]{3,2,1,0:T(8,128)(2,1)S(1)}, u32[]{:S(2)}, u32[]{:S(2)}) collective-permute-start(bf16[2,4,144,384]{3,2,1,0:T(8,128)(2,1)} %add_convert_fusion.5), channel_id=1, source_target_pairs={{0,8},{1,17},{2,10},{3,19},{4,12},{5,21},{6,14},{7,23},{8,0},{9,25... | collective-permute-start | bytes 2654216 | tf_op jit(solution)/shard_map/ppermute | solution.py:502
  380.6 9.8 %collective-permute-start.47 = (bf16[128,640]{1,0:T(8,128)(2,1)S(1)}, bf16[128,640]{1,0:T(8,128)(2,1)S(1)}, u32[]{:S(2)}, u32[]{:S(2)}) collective-permute-start(bf16[128,640]{1,0:T(8,128)(2,1)S(1)} %fusion.16), channel_id=1, source_target_pairs={{0,4},{1,3},{2,6},{3,1},{4,0},{5,7},{6,2},{7,5},{8,12},{9,11},{10,... | collective-permute-start | bytes 491528 | tf_op jit(solution)/shard_map/ppermute | solution.py:502
  394.1 9.5 %collective-permute-start.48 = (bf16[4,144,384]{2,1,0:T(8,128)(2,1)S(1)}, bf16[4,144,384]{2,1,0:T(8,128)(2,1)S(1)}, u32[]{:S(2)}, u32[]{:S(2)}) collective-permute-start(bf16[4,144,384]{2,1,0:T(8,128)(2,1)S(1)} %fusion.9), channel_id=1, source_target_pairs={{0,16},{1,9},{2,18},{3,11},{4,20},{5,13},{6,22},{7,15},{8,24},{9,1... | collective-permute-start | bytes 1327112 | tf_op jit(solution)/shard_map/ppermute | solution.py:502
  395.3 7.1 %collective-permute-start.49 = (bf16[128,640]{1,0:T(8,128)(2,1)S(1)}, bf16[128,640]{1,0:T(8,128)(2,1)S(1)}, u32[]{:S(2)}, u32[]{:S(2)}) collective-permute-start(bf16[128,640]{1,0:T(8,128)(2,1)S(1)} %fusion.10.refs_0_), channel_id=1, source_target_pairs={{0,8},{1,17},{2,10},{3,19},{4,12},{5,21},{6,14},{7,23},{8,0},{9,25... | collective-permute-start | bytes 491528 | tf_op jit(solution)/shard_map/ppermute | solution.py:502
  406.1 16.5 %copy-start.3 = (s32[3]{0:T(128)S(1)}, s32[3]{0:T(128)}, u32[]{:S(2)}) copy-start(s32[3]{0:T(128)} %pad_add_fusion.where) | copy-start | bytes 40
  406.1 16.4 %collective-permute-start.54 = (bf16[2,1024,256]{2,1,0:T(8,128)(2,1)}, bf16[2,1024,256]{2,1,0:T(8,128)(2,1)S(1)}, u32[]{:S(2)}, u32[]{:S(2)}) collective-permute-start(bf16[2,1024,256]{2,1,0:T(8,128)(2,1)} %pad_maximum_fusion.2), channel_id=1, source_target_pairs={{0,16},{1,9},{2,18},{3,11},{4,20},{5,13},{6,22},{7,15},{8,24},{9,1... | collective-permute-start | bytes 3145736 | tf_op jit(solution)/shard_map/ppermute | solution.py:502
  406.7 7.9 %collective-permute-start.51 = (bf16[144,384]{1,0:T(8,128)(2,1)S(1)}, bf16[144,384]{1,0:T(8,128)(2,1)S(1)}, u32[]{:S(2)}, u32[]{:S(2)}) collective-permute-start(bf16[144,384]{1,0:T(8,128)(2,1)S(1)} %get-tuple-element.253), channel_id=1, source_target_pairs={{0,6},{1,7},{2,4},{3,5},{4,2},{5,3},{6,0},{7,1},{8,14},{9,15},{10,... | collective-permute-start | bytes 331784 | tf_op jit(solution)/shard_map/ppermute | solution.py:502
  409.2 9.7 %collective-permute-start.52 = (bf16[144,384]{1,0:T(8,128)(2,1)S(1)}, bf16[144,384]{1,0:T(8,128)(2,1)S(1)}, u32[]{:S(2)}, u32[]{:S(2)}) collective-permute-start(bf16[144,384]{1,0:T(8,128)(2,1)S(1)} %get-tuple-element.252), channel_id=1, source_target_pairs={{0,4},{1,5},{2,6},{3,7},{4,0},{5,1},{6,2},{7,3},{8,12},{9,13},{10,... | collective-permute-start | bytes 331784 | tf_op jit(solution)/shard_map/ppermute | solution.py:502
  409.3 9.5 %collective-permute-start.53 = (bf16[144,384]{1,0:T(8,128)(2,1)S(1)}, bf16[144,384]{1,0:T(8,128)(2,1)S(1)}, u32[]{:S(2)}, u32[]{:S(2)}) collective-permute-start(bf16[144,384]{1,0:T(8,128)(2,1)S(1)} %get-tuple-element.251), channel_id=1, source_target_pairs={{0,2},{1,3},{2,0},{3,1},{4,6},{5,7},{6,4},{7,5},{8,10},{9,11},{10,... | collective-permute-start | bytes 331784 | tf_op jit(solution)/shard_map/ppermute | solution.py:502
  411.2 14.6 %collective-permute-start.50 = (bf16[2,128,640]{2,1,0:T(8,128)(2,1)S(1)}, bf16[2,128,640]{2,1,0:T(8,128)(2,1)S(1)}, u32[]{:S(2)}, u32[]{:S(2)}) collective-permute-start(bf16[2,128,640]{2,1,0:T(8,128)(2,1)S(1)} %pad_maximum_fusion.11), channel_id=1, source_target_pairs={{0,16},{1,9},{2,18},{3,11},{4,20},{5,13},{6,22},{7,15},{8,24},{9,1... | collective-permute-start | bytes 983048 | tf_op jit(solution)/shard_map/ppermute | solution.py:502
  418.9 6.9 %collective-permute-start.55 = (bf16[144,384]{1,0:T(8,128)(2,1)S(1)}, bf16[144,384]{1,0:T(8,128)(2,1)S(1)}, u32[]{:S(2)}, u32[]{:S(2)}) collective-permute-start(bf16[144,384]{1,0:T(8,128)(2,1)S(1)} %fusion.15.refs_4_), channel_id=1, source_target_pairs={{0,8},{1,9},{2,10},{3,11},{4,12},{5,13},{6,14},{7,15},{8,0},{9,1},... | collective-permute-start | bytes 331784 | tf_op jit(solution)/shard_map/ppermute | solution.py:502
  419.6 9.8 %collective-permute-start.56 = (bf16[144,384]{1,0:T(8,128)(2,1)S(1)}, bf16[144,384]{1,0:T(8,128)(2,1)S(1)}, u32[]{:S(2)}, u32[]{:S(2)}) collective-permute-start(bf16[144,384]{1,0:T(8,128)(2,1)S(1)} %fusion.15.refs_4_), channel_id=1, source_target_pairs={{0,16},{1,17},{2,18},{3,19},{4,20},{5,21},{6,22},{7,23},{8,24},{9,... | collective-permute-start | bytes 331784 | tf_op jit(solution)/shard_map/ppermute | solution.py:502
  421.3 8.1 %collective-permute-start.57 = (bf16[144,384]{1,0:T(8,128)(2,1)S(1)}, bf16[144,384]{1,0:T(8,128)(2,1)S(1)}, u32[]{:S(2)}, u32[]{:S(2)}) collective-permute-start(bf16[144,384]{1,0:T(8,128)(2,1)S(1)} %fusion.15.refs_4_), channel_id=1, source_target_pairs={{0,24},{1,25},{2,26},{3,27},{4,28},{5,29},{6,30},{7,31},{8,16},{9,... | collective-permute-start | bytes 331784 | tf_op jit(solution)/shard_map/ppermute | solution.py:502
  (18 other events, 54.0 us)
where the time goes:
time: 437 us; the launch traced here: 433 us
  Pallas kernels  270 us (62%)
  starting transfers between devices  60.1 us (14%)
  waiting for transfers between devices  48 us (11%)
  other arithmetic  44.5 us (10%)
  local copies, waits for them, and re-layouts  8.95 us (2%)
    pallas_call x4, Pallas kernels, weight_call(): pl.pallas_call(body, grid_spec=pltpu.PrefetchScalarGridSpec(num_scalar_pr...  77 us
    ppermute x58, starting transfers between devices, permute(): return lax.ppermute(array, AXES, pairs)  60.1 us
    pallas_call x3, Pallas kernels, attention_backward(): pl.pallas_call(body, grid=(pairs,), in_specs=[pair(0), pair(1), pair(2),...  50.8 us
    ppermute x58, waiting for transfers between devices, permute(): return lax.ppermute(array, AXES, pairs)  48 us
    pallas_call x3, Pallas kernels, attention_forward(): pl.pallas_call(body, grid=(pairs,), in_specs=[pair(0), pair(1), pair(2),...  45.8 us
    convert_element_type x18, other arithmetic, add(): return total.astype(jnp.bfloat16)  34.6 us
    pallas_call x2, Pallas kernels, weight_grad(): pl.pallas_call(functools.partial(weight_grad_kernel, rows=rows, groups=gr...  28.1 us
    pallas_call x1, Pallas kernels, plain_call(): pl.pallas_call(kernel, grid=(steps,), in_specs=in_specs, out_specs=out_sp...  21 us
  transfers between devices with their start and end apart: 58, of which 21 were waited for; matrix products, arithmetic and copies ran while one was open for 5% of the time, Pallas kernels for 51%

commit v1 on v0

--- a/solution.py
+++ b/solution.py
@@ -349,7 +349,7 @@
     return pltpu.CompilerParams(vmem_limit_bytes=megabytes << 20)
 
 
-def attention_forward_kernel(q_ref, k_ref, v_ref, seg_col, seg_row, out_ref, probs_ref, *, rows):
+def attention_forward_kernel(q_ref, k_ref, v_ref, seg_col, seg_row, out_ref, probs_ref, scale_ref, *, rows):
     length = q_ref.shape[0]
     first = lax.broadcasted_iota(jnp.int32, (1, LANES), 1) < HD
     keys = k_ref[...]
@@ -361,16 +361,19 @@
         here = pl.ds(block * rows, rows)
         q = q_ref[here, :]
         allowed = key_segments == seg_row[:, here]
-        outs = []
+        outs, scales = [], []
         for head in range(2):
             scores = mxu(head_keys[head], q, NT)
             scores = jnp.where(allowed, scores, masked_score)
             powers = jnp.exp(scores - jnp.max(scores, 0, keepdims=True))
-            probs = powers * (1.0 / jnp.sum(powers, 0, keepdims=True))
-            probs = probs.astype(jnp.bfloat16)
-            probs_ref[head, :, here] = probs
-            outs.append(mxu(probs, values, TN))
-        out_ref[here, :] = jnp.where(first, outs[0], outs[1]).astype(jnp.bfloat16)
+            scale = 1.0 / jnp.sum(powers, 0, keepdims=True)
+            scales.append(jnp.transpose(jnp.broadcast_to(scale, (LANES, rows))))
+            powers = powers.astype(jnp.bfloat16)
+            probs_ref[head, :, here] = powers
+            outs.append(mxu(powers, values, TN))
+        scale = jnp.where(first, scales[0], scales[1])
+        scale_ref[here, :] = scale
+        out_ref[here, :] = (jnp.where(first, outs[0], outs[1]) * scale).astype(jnp.bfloat16)
 
 
 def attention_forward(qkv, seg_col, seg_row, start, pairs, before=None):
@@ -383,7 +386,7 @@
         return pl.BlockSpec((length, LANES), lambda j: (0, part * total + start + j))
 
     def body(q_ref, k_ref, v_ref, seg_c, seg_r, *refs):
-        attention_forward_kernel(q_ref, k_ref, v_ref, seg_c, seg_r, *refs[-2:], rows=rows)
+        attention_forward_kernel(q_ref, k_ref, v_ref, seg_c, seg_r, *refs[-3:], rows=rows)
 
     return pl.pallas_call(
         body,
@@ -399,33 +402,38 @@
         out_specs=[
             pl.BlockSpec((length, LANES), lambda j: (0, start + j)),
             pl.BlockSpec((2, length, length), lambda j: (start + j, 0, 0)),
+            pl.BlockSpec((length, LANES), lambda j: (0, start + j)),
         ],
         out_shape=[
             jax.ShapeDtypeStruct((length, width), jnp.bfloat16),
             jax.ShapeDtypeStruct((2 * total, length, length), jnp.bfloat16),
+            jax.ShapeDtypeStruct((length, width), jnp.float32),
         ],
-        input_output_aliases={} if before is None else {5: 0, 6: 1},
+        input_output_aliases={} if before is None else {5: 0, 6: 1, 7: 2},
         compiler_params=params(60),
         cost_estimate=cost(16 * length * length * pairs * LANES),
         name="attn_fwd",
     )(qkv, qkv, qkv, seg_col, seg_row, *more)
 
 
-def attention_backward_kernel(q_ref, k_ref, v_ref, o_ref, do_ref, probs_ref, grad_ref, sum_ref):
+def attention_backward_kernel(
+    q_ref, k_ref, v_ref, o_ref, do_ref, probs_ref, scale_ref, grad_ref, sum_ref
+):
     first = lax.broadcasted_iota(jnp.int32, (1, LANES), 1) < HD
     pick = (
         lax.broadcasted_iota(jnp.int32, (8, LANES), 0)
         == lax.broadcasted_iota(jnp.int32, (8, LANES), 1) // HD
     ).astype(jnp.float32)
     q = q_ref[...]
-    do = do_ref[...]
+    scaled = do_ref[...].astype(jnp.float32) * scale_ref[...]
+    do = scaled.astype(jnp.bfloat16)
     keys = k_ref[...]
     values = v_ref[...]
     zero = jnp.zeros_like(values)
     head_values = (jnp.where(first, values, zero), jnp.where(first, zero, values))
     dots = lax.dot_general(
         pick,
-        do.astype(jnp.float32) * o_ref[...].astype(jnp.float32),
+        scaled * o_ref[...].astype(jnp.float32),
         NT,
         precision=lax.Precision.HIGHEST,
         preferred_element_type=jnp.float32,
@@ -448,7 +456,7 @@
     sum_ref[1:2, :] = jnp.sum(value_grad, 0, keepdims=True)
 
 
-def attention_backward(qkv, out, out_grad, probs, start, pairs, at, size, before=None):
+def attention_backward(qkv, out, out_grad, probs, scale, start, pairs, at, size, before=None):
     length, width = out.shape
     total = width // LANES
     more = () if before is None else before
@@ -457,7 +465,7 @@
         return pl.BlockSpec((length, LANES), lambda j: (0, part * total + start + j))
 
     def body(*refs):
-        attention_backward_kernel(*refs[:6], *refs[-2:])
+        attention_backward_kernel(*refs[:7], *refs[-2:])
 
     return pl.pallas_call(
         body,
@@ -469,6 +477,7 @@
             pair(0),
             pair(0),
             pl.BlockSpec((2, length, length), lambda j: (start + j, 0, 0)),
+            pair(0),
         ]
         + [pl.BlockSpec(memory_space=pl.ANY)] * len(more),
         out_specs=[
@@ -479,11 +488,11 @@
             jax.ShapeDtypeStruct((3, length, size * LANES), jnp.bfloat16),
             jax.ShapeDtypeStruct((2, size * LANES), jnp.float32),
         ],
-        input_output_aliases={} if before is None else {6: 0, 7: 1},
+        input_output_aliases={} if before is None else {7: 0, 8: 1},
         compiler_params=params(60),
         cost_estimate=cost(32 * length * length * pairs * LANES),
         name="attn_bwd",
-    )(qkv, qkv, qkv, out, out_grad, probs, *more)
+    )(qkv, qkv, qkv, out, out_grad, probs, scale, *more)
 
 
 class Place:
@@ -764,47 +773,6 @@
             ],
             name="vectors",
         )(place.scalars, self.slots, seg_row, keep_row)
-
-
-def pack_sums(late_a, late_b, first_sums, second_sums, inner_sums):
-    width = first_sums.shape[1]
-    half = late_a.shape[1]
-
-    def kernel(a_ref, b_ref, one_ref, two_ref, inner_ref, out_ref):
-        def place_of(n):
-            return n // 3 * 8 + n % 3
-
-        out_ref[...] = jnp.zeros_like(out_ref)
-        for n in (B_QUERY, B_VALUE):
-            at = place_of(n)
-            out_ref[at : at + 1, 0:half] = a_ref[n : n + 1, :]
-            out_ref[at : at + 1, half:width] = b_ref[n : n + 1, :]
-        for n, source, line in (
-            (GAIN_ONE, one_ref, 0),
-            (SHIFT_ONE, one_ref, 1),
-            (B_ATTN, one_ref, 2),
-            (GAIN_TWO, two_ref, 0),
-            (SHIFT_TWO, two_ref, 1),
-            (B_OUT, two_ref, 2),
-        ):
-            at = place_of(n)
-            out_ref[at : at + 1, :] = source[line : line + 1, :]
-        for n in range(4):
-            at = place_of(B_IN + n)
-            for shard in range(width // LANES):
-                start = (4 * shard + n) * LANES
-                out_ref[at : at + 1, shard * LANES : (shard + 1) * LANES] = inner_ref[
-                    :, start : start + LANES
-                ]
-
-    in_vmem = pl.BlockSpec(memory_space=pltpu.VMEM)
-    return pl.pallas_call(
-        kernel,
-        in_specs=[in_vmem] * 5,
-        out_specs=in_vmem,
-        out_shape=shaped((32, width), jnp.float32),
-        name="pack_sums",
-    )(late_a, late_b, first_sums, second_sums, inner_sums)
 
 
 def project_qkv(place, rows, window, bias, scale):
@@ -1147,22 +1115,42 @@
     scatter(turned, right_ref[0], pl.multiple_of(skip + step * cols, LANES), cols)
 
     if extra:
-        (sums_ref,) = more
 
         @pl.when(step == 2)
         def _():
             blank = jnp.zeros((extra, own.shape[3]), jnp.bfloat16)
             for ref, side in ((sent, 1), (own, 0)):
-                for g in range(groups):
-                    pos = position(grp ^ g, core ^ side)
-                    for k in range(chips):
-                        start = pl.multiple_of((2 * k + (core ^ side)) * LANES, LANES)
+                for k in range(chips):
+                    lines = vector_sums(2 * k + (core ^ side), *more)
+                    for g in range(groups):
+                        pos = position(grp ^ g, core ^ side)
                         ref[pos, k, rows : rows + extra, :] = blank
-                        lines = sums_ref[8 * g : 8 * g + 8, pl.ds(start, LANES)]
                         for n in range(3):
                             ref[pos, k, rows : rows + 1, n * LANES : (n + 1) * LANES] = lines[
-                                n : n + 1
+                                3 * g + n
                             ].astype(jnp.bfloat16)
+
+
+def vector_sums(shard, a_ref, b_ref, one_ref, two_ref, inner_ref):
+    half = a_ref.shape[1]
+    start = shard * LANES
+
+    def part(ref, start):
+        return ref[:, pl.ds(pl.multiple_of(start, LANES), LANES)]
+
+    late = jnp.where(
+        start < half,
+        part(a_ref, jnp.minimum(start, half - LANES)),
+        part(b_ref, jnp.maximum(start - half, 0)),
+    )
+    one, two = part(one_ref, start), part(two_ref, start)
+    lines = [None] * 12
+    lines[B_QUERY], lines[B_VALUE] = late[0:1], late[1:2]
+    lines[GAIN_ONE], lines[SHIFT_ONE], lines[B_ATTN] = one[0:1], one[1:2], one[2:3]
+    lines[GAIN_TWO], lines[SHIFT_TWO], lines[B_OUT] = two[0:1], two[1:2], two[2:3]
+    for n in range(4):
+        lines[B_IN + n] = part(inner_ref, (4 * shard + n) * LANES)
+    return lines
 
 
 def position(distance, core):
@@ -1174,7 +1162,7 @@
     height, tokens = 2 * turned.shape[1], turned.shape[2]
     groups, chips = place.groups, place.chips
     rows = height // place.shards
-    extra = 16 if len(more) == 1 else 0
+    extra = 16 if len(more) > 2 else 0
     size = right.shape[2]
     cols = 3 * size // groups + (0 if extra else more[1].shape[1] // groups)
     shape = (groups, chips, rows + extra, cols)
@@ -1249,6 +1237,26 @@
     return total.astype(jnp.bfloat16)
 
 
+def add_leading(left, right):
+    _, chips, rows, cols = left.shape
+
+    def kernel(left_ref, right_ref, out_ref):
+        total = left_ref[...].astype(jnp.float32) + right_ref[...].astype(jnp.float32)
+        out_ref[...] = total.astype(jnp.bfloat16)
+
+    block = pl.BlockSpec((1, chips, rows, cols), lambda i: (i, 0, 0, 0))
+    return pl.pallas_call(
+        kernel,
+        grid=(2,),
+        in_specs=[block, block],
+        out_specs=block,
+        out_shape=shaped((2, chips, rows, cols), jnp.bfloat16),
+        compiler_params=params(60),
+        cost_estimate=cost(512 * chips * rows * cols),
+        name="add_leading",
+    )(left, right)
+
+
 class Reduction:
     def __init__(self, place, made):
         self.place = place
@@ -1257,7 +1265,7 @@
 
     def near(self):
         self.core = self.flying
-        leave = add(self.made[:2], self.core[:2])
+        leave = add_leading(self.made, self.core)
         self.flying = self.place.swap_grp(leave, 0)
         return leave
 
@@ -1480,7 +1488,7 @@
     meet(forward[0], c2)
     c2.landed()
     c2.cross(3)
-    contexts, probs = attention_forward(
+    contexts, probs, probs_scale = attention_forward(
         after(mixed, c2.held[3]), seg_col, seg_row, second, pairs - second, forward
     )
     normed, scale_one, normed_low, full_attn = project_out(
@@ -1516,6 +1524,7 @@
             contexts,
             after(context_grad, *wait),
             probs,
+            probs_scale,
             start,
             count,
             at,
@@ -1536,10 +1545,10 @@
     steps = (r_out.along_far(), r_in.along(), r_a.near())
     low_b, late_b = back(steps, half + quarter, quarter, quarter, part)
     meet(late_b, r_out, r_in, r_a)
-    sums = pack_sums(late_a, late_b, first_sums, second_sums, bias_in_grad)
+    sums = (late_a, late_b, first_sums, second_sums, bias_in_grad)
     share_out = r_out.share()
     steps = (r_in.along_far(), r_a.middle(), share_out)
-    r_b = Reduction(place, attention_grads(place, after(turned, *steps), low_b, (sums,), "b"))
+    r_b = Reduction(place, attention_grads(place, after(turned, *steps), low_b, sums, "b"))
     meet(r_b.made, r_in, r_a)
     share_in = r_in.share()
     inner = share_in.shape[1] // groups

time: 437 us -> 443 us (1.014)
  Pallas kernels: 270 us -> 279 us
  other arithmetic: 44.5 us -> 38.9 us
    pallas_call x1 -> x4, Pallas kernels: 1.46 us -> 11.8 us  [add_leading(): pl.pallas_call(kernel, grid=(2,), in_specs=[block, block], out_specs=bloc...]
    convert_element_type x18 -> x14, other arithmetic: 34.6 us -> 27.3 us  [add(): return total.astype(jnp.bfloat16)]
  transfers between devices with their start and end apart: 58 -> 58, of which waited for: 21 -> 24; matrix products, arithmetic and copies ran while one was open for 5% -> 4% of each run, Pallas kernels for 51% -> 51%
where the time goes in v1:
time: 443 us; the launch traced here: 439 us
  Pallas kernels  279 us (63%)
  starting transfers between devices  58.6 us (13%)
  waiting for transfers between devices  49.7 us (11%)
  other arithmetic  38.9 us (9%)
  local copies, waits for them, and re-layouts  10.6 us (2%)
    pallas_call x4, Pallas kernels, weight_call(): pl.pallas_call(body, grid_spec=pltpu.PrefetchScalarGridSpec(num_scalar_pr...  77 us
    ppermute x58, starting transfers between devices, permute(): return lax.ppermute(array, AXES, pairs)  58.6 us
    pallas_call x3, Pallas kernels, attention_backward(): pl.pallas_call(body, grid=(pairs,), in_specs=[pair(0), pair(1), pair(2),...  51.2 us
    ppermute x58, waiting for transfers between devices, permute(): return lax.ppermute(array, AXES, pairs)  49.7 us
    pallas_call x3, Pallas kernels, attention_forward(): pl.pallas_call(body, grid=(pairs,), in_specs=[pair(0), pair(1), pair(2),...  44.4 us
    pallas_call x2, Pallas kernels, weight_grad(): pl.pallas_call(functools.partial(weight_grad_kernel, rows=rows, groups=gr...  28 us
    convert_element_type x14, other arithmetic, add(): return total.astype(jnp.bfloat16)  27.3 us
    pallas_call x2, Pallas kernels, attention_grads(): pl.pallas_call(functools.partial(attention_grads_kernel, rows=rows, group...  21.3 us
  transfers between devices with their start and end apart: 58, of which 24 were waited for; matrix products, arithmetic and copies ran while one was open for 4% of the time, Pallas kernels for 51%

profile of v1, /device:TPU:0, one launch (start us, length us, event | category | flops | bytes accessed | tf_op | source)
XLA Modules:
  0.0 438.6 jit_solution(13734685775094280549)
XLA Ops:
  0.6 3.1 collective-permute-start
  3.7 1.5 concatenate.29
  6.7 2.7 collective-permute-done
  10.4 2.5 collective-permute-start.2
  12.9 2.5 collective-permute-start.3
  16.4 4.3 collective-permute-done.3
  22.9 2.7 collective-permute-start.4
  25.6 1.6 collective-permute-start.7
  27.2 1.5 collective-permute-start.8
  29.3 3.3 collective-permute-start.5
  32.6 2.0 collective-permute-done.5
  35.5 2.9 collective-permute-start.6
  40.4 2.1 vectors.1
  42.4 2.3 collective-permute-done.7.refs_1_
  49.0 5.4 %collective-permute-done.6 = bf16[2,128,1280]{2,1,0:T(8,128)(2,1)} collective-permute-done((bf16[2,128,1280]{2,1,0:T(8,128)(2,1)}, bf16[2,128,1280]{2,1,0:T(8,128)(2,1)}, u32[]{:S(2)}, u32[]{:S(2)}) %collective-permute-start.6) | collective-permute-done | bytes 655392 | tf_op jit(solution)/shard_map/ppermute | solution.py:511
  55.6 1.4 collective-permute-done.9.refs_3_
  57.0 1.5 collective-permute-start.15
  61.7 12.8 %qkv.1 = (bf16[1024,3072]{1,0:T(8,128)(2,1)}, bf16[1024,3072]{1,0:T(8,128)(2,1)}) custom-call(s32[3]{0:T(128)} %pad_add_fusion.where, bf16[4,128,768]{2,1,0:T(8,128)(2,1)} %copy-done.15, bf16[4,128,768]{2,1,0:T(8,128)(2,1)} %collective-permute-done.7.refs_1_, bf16[4,128,768]{2,1,0:T(8,128)(2,1)} %collective-permute-done.8.refs_2_, ...), custom_call_target="tpu_custom_call" | custom-call | flops 12884901888 | tf_op jit(solution)/shard_map/qkv/pallas_call | solution.py:657
  74.6 2.5 collective-permute-start.17
  77.1 16.2 %attn_fwd.3 = (bf16[1024,1024]{1,0:T(8,128)(2,1)}, bf16[16,1024,1024]{2,1,0:T(8,128)(2,1)}, f32[1024,1024]{1,0:T(8,128)}) custom-call(bf16[1024,3072]{1,0:T(8,128)(2,1)} %get-tuple-element.161.q_ref.k_ref.v_ref.refs_0_.refs_1_.refs_2_, bf16[1024,3072]{1,0:T(8,128)(2,1)} %get-tuple-element.161.q_ref.k_ref.v_ref.refs_0_.refs_1_.refs_2_, ...), custom_call_target="tpu_custom_call" | custom-call | flops 12884901888 | tf_op jit(solution)/shard_map/attn_fwd/pallas_call | solution.py:391
  93.3 1.5 collective-permute-start.18
  95.5 16.2 %attn_fwd.4 = (bf16[1024,1024]{1,0:T(8,128)(2,1)}, bf16[16,1024,1024]{2,1,0:T(8,128)(2,1)}, f32[1024,1024]{1,0:T(8,128)}) custom-call(bf16[1024,3072]{1,0:T(8,128)(2,1)} %get-tuple-element.161.q_ref.k_ref.v_ref.refs_0_.refs_1_.refs_2_, ...), custom_call_target="tpu_custom_call", output_to_operand_aliasing={{0}: (5, {}), {1}: (6, {}), {2}: (7, {})} | custom-call | flops 12884901888 | tf_op jit(solution)/shard_map/attn_fwd/pallas_call | solution.py:391
  114.0 12.0 %attn_fwd.5 = (bf16[1024,1024]{1,0:T(8,128)(2,1)}, bf16[16,1024,1024]{2,1,0:T(8,128)(2,1)}, f32[1024,1024]{1,0:T(8,128)}) custom-call(bf16[1024,3072]{1,0:T(8,128)(2,1)} %get-tuple-element.161.q_ref.k_ref.v_ref.refs_0_.refs_1_.refs_2_, ...), custom_call_target="tpu_custom_call", output_to_operand_aliasing={{0}: (5, {}), {1}: (6, {}), {2}: (7, {})} | custom-call | flops 8589934592 | tf_op jit(solution)/shard_map/attn_fwd/pallas_call | solution.py:391
  127.2 9.6 %attn_out.1 = (f32[1024,1024]{1,0:T(8,128)}, f32[1024,128]{1,0:T(8,128)}, bf16[1024,1024]{1,0:T(8,128)(2,1)}, bf16[1024,1024]{1,0:T(8,128)(2,1)}) custom-call(s32[3]{0:T(128)} %pad_add_fusion.where, bf16[4,128,1280]{2,1,0:T(8,128)(2,1)} %copy-done.12, bf16[4,128,1280]{2,1,0:T(8,128)(2,1)} %collective-permute-done.15.refs_1_, ...), custom_call_target="tpu_custom_call" | custom-call | flops 4294967296 | tf_op jit(solution)/shard_map/attn_out/pallas_call | solution.py:657
  139.1 22.0 %feed_in.1 = (bf16[1024,4096]{1,0:T(8,128)(2,1)}, bf16[1024,4096]{1,0:T(8,128)(2,1)}, bf16[1024,4096]{1,0:T(8,128)(2,1)}) custom-call(s32[3]{0:T(128)} %pad_add_fusion.where, bf16[4,128,1280]{2,1,0:T(8,128)(2,1)} %copy-done.12, bf16[4,128,1280]{2,1,0:T(8,128)(2,1)} %collective-permute-done.15.refs_1_, bf16[4,128,1280]{2,1,0:T(8,128)(2,1)} %collective-permute-done.16.refs_2_, ...), custom_call_target="tpu_custom_call" | custom-call | flops 17179869184 | tf_op jit(solution)/shard_map/feed_in/pallas_call | solution.py:657
  161.2 2.6 collective-permute-done.29.refs_7_
  164.8 32.5 %feed_out.1 = (bf16[1024,1024]{1,0:T(8,128)(2,1)}, f32[1024,1024]{1,0:T(8,128)}, bf16[1024,1024]{1,0:T(8,128)(2,1)}, f32[8,1024]{1,0:T(8,128)}, bf16[1024,4096]{1,0:T(8,128)(2,1)}, /*index=5*/f32[1,4096]{1,0:T(1,128)}) custom-call(s32[3]{0:T(128)} %pad_add_fusion.where, bf16[4,512,256]{2,1,0:T(8,128)(2,1)} %copy-done.13, ...), custom_call_target="tpu_custom_call" | custom-call | flops 34359738368 | tf_op jit(solution)/shard_map/feed_out/pallas_call | solution.py:657
  197.4 13.9 %wgrad_out.1 = (bf16[4,4,512,256]{3,2,1,0:T(8,128)(2,1)}, bf16[4,4,512,256]{3,2,1,0:T(8,128)(2,1)}) custom-call(s32[3]{0:T(128)} %pad_add_fusion.where, bf16[1024,4096]{1,0:T(8,128)(2,1)} %get-tuple-element.170.refs_8_.left_ref, bf16[1024,1024]{1,0:T(8,128)(2,1)} %get-tuple-element.178.right_ref), custom_call_target="tpu_custom_call" | custom-call | flops 17179869184 | tf_op jit(solution)/shard_map/wgrad_out/pallas_call | solution.py:1214
  211.5 14.1 %wgrad_in.1 = (bf16[4,4,128,1024]{3,2,1,0:T(8,128)(2,1)}, bf16[4,4,128,1024]{3,2,1,0:T(8,128)(2,1)}) custom-call(s32[3]{0:T(128)} %pad_add_fusion.where, bf16[1024,1024]{1,0:T(8,128)(2,1)} %get-tuple-element.180.refs_8_.left_ref, bf16[1024,4096]{1,0:T(8,128)(2,1)} %get-tuple-element.184.right_ref.p_ref), custom_call_target="tpu_custom_call" | custom-call | flops 17179869184 | tf_op jit(solution)/shard_map/wgrad_in/pallas_call | solution.py:1214
  225.9 3.4 add_leading.4
  230.6 21.0 %feed_in_back.1 = (f32[1024,1024]{1,0:T(8,128)}, bf16[1024,1024]{1,0:T(8,128)(2,1)}, bf16[1024,1024]{1,0:T(8,128)(2,1)}, f32[8,1024]{1,0:T(8,128)}) custom-call(bf16[1024,4096]{1,0:T(8,128)(2,1)} %get-tuple-element.184.right_ref.p_ref, bf16[1024,4096]{1,0:T(8,128)(2,1)} %get-tuple-element.185.w_ref, f32[1024,1024]{1,0:T(8,128)} %get-tuple-element.186.g_ref, ...), custom_call_target="tpu_custom_call" | custom-call | flops 21474836480 | tf_op jit(solution)/shard_map/feed_in_back/pallas_call | solution.py:679
  251.6 3.4 add_leading.5
  255.8 23.7 %attn_bwd.3 = (bf16[3,1024,512]{2,1,0:T(8,128)(2,1)}, f32[2,512]{1,0:T(2,128)}) custom-call(bf16[1024,3072]{1,0:T(8,128)(2,1)} %get-tuple-element.161.q_ref.k_ref.v_ref.refs_0_.refs_1_.refs_2_, bf16[1024,3072]{1,0:T(8,128)(2,1)} %get-tuple-element.161.q_ref.k_ref.v_ref.refs_0_.refs_1_.refs_2_, ...), custom_call_target="tpu_custom_call" | custom-call | flops 34359738368 | tf_op jit(solution)/shard_map/attn_bwd/pallas_call | solution.py:470
  279.5 1.8 collective-permute-done.33
  281.2 3.9 fusion.4
  285.1 3.2 fusion.3
  289.1 12.3 %wgrad_a.1 = (bf16[4,4,128,640]{3,2,1,0:T(8,128)(2,1)}, bf16[4,4,128,640]{3,2,1,0:T(8,128)(2,1)}) custom-call(s32[3]{0:T(128)} %pad_add_fusion.where, bf16[2,512,1024]{2,1,0:T(8,128)(2,1)} %copy-done.1, bf16[3,1024,512]{2,1,0:T(8,128)(2,1)} %get-tuple-element.196.refs_1_.refs_0_, bf16[1024,1024]{1,0:T(8,128)(2,1)} %get-tuple-element.164.refs_8_.refs_3_.refs_2_, ...), custom_call_target="tpu_custom_call" | custom-call | flops 10737418240 | tf_op jit(solution)/shard_map/wgrad_a/pallas_call | solution.py:1172
  303.5 2.7 fusion.1
  307.8 13.7 %attn_bwd.4 = (bf16[3,1024,512]{2,1,0:T(8,128)(2,1)}, f32[2,512]{1,0:T(2,128)}) custom-call(bf16[1024,3072]{1,0:T(8,128)(2,1)} %get-tuple-element.161.q_ref.k_ref.v_ref.refs_0_.refs_1_.refs_2_, bf16[1024,3072]{1,0:T(8,128)(2,1)} %get-tuple-element.161.q_ref.k_ref.v_ref.refs_0_.refs_1_.refs_2_, ...), custom_call_target="tpu_custom_call" | custom-call | flops 17179869184 | tf_op jit(solution)/shard_map/attn_bwd/pallas_call | solution.py:470
  322.1 1.6 copy-done.5
  323.6 2.7 add_leading.6
  326.3 3.1 fusion
  332.1 1.7 fusion.11
  334.4 13.8 %attn_bwd.5 = (bf16[3,1024,512]{2,1,0:T(8,128)(2,1)}, f32[2,512]{1,0:T(2,128)}) custom-call(bf16[1024,3072]{1,0:T(8,128)(2,1)} %get-tuple-element.161.q_ref.k_ref.v_ref.refs_0_.refs_1_.refs_2_, bf16[1024,3072]{1,0:T(8,128)(2,1)} %get-tuple-element.161.q_ref.k_ref.v_ref.refs_0_.refs_1_.refs_2_, ...), custom_call_target="tpu_custom_call", output_to_operand_aliasing={{0}: (7, {}), {1}: (8, {})} | custom-call | flops 17179869184 | tf_op jit(solution)/shard_map/attn_bwd/pallas_call | solution.py:470
  349.4 2.4 collective-permute-done.39
  351.8 2.4 fusion.6
  354.1 1.7 fusion.12
  359.4 9.0 %wgrad_b.1 = (bf16[4,4,144,384]{3,2,1,0:T(8,128)(2,1)}, bf16[4,4,144,384]{3,2,1,0:T(8,128)(2,1)}) custom-call(s32[3]{0:T(128)} %pad_add_fusion.where, bf16[2,512,1024]{2,1,0:T(8,128)(2,1)} %copy-done.1, bf16[3,1024,512]{2,1,0:T(8,128)(2,1)} %get-tuple-element.223.refs_1_, f32[2,512]{1,0:T(2,128)} %get-tuple-element.197.refs_2_, ...), custom_call_target="tpu_custom_call" | custom-call | flops 6442450944 | tf_op jit(solution)/shard_map/wgrad_b/pallas_call | solution.py:1172
  368.4 1.9 fusion.2
  373.1 8.2 %qkv_back.2.refs_3_ = f32[1024,1024]{1,0:T(8,128)} custom-call(bf16[1024,3072]{1,0:T(8,128)(2,1)} %get-tuple-element.176.w_ref, bf16[3,1024,512]{2,1,0:T(8,128)(2,1)} %get-tuple-element.196.refs_1_.refs_0_, bf16[3,1024,512]{2,1,0:T(8,128)(2,1)} %get-tuple-element.223.refs_1_, f32[1024,1024]{1,0:T(8,128)} %get-tuple-element.228.refs_2_), custom_call_target="tpu_custom_call" | custom-call | flops 6442450944 | tf_op jit(solution)/shard_map/qkv_back/pallas_call | solution.py:1013
  381.6 2.3 add_leading.7
  387.4 8.2 %qkv_back.3 = f32[1024,1024]{1,0:T(8,128)} custom-call(bf16[1024,3072]{1,0:T(8,128)(2,1)} %get-tuple-element.176.w_ref, bf16[3,1024,512]{2,1,0:T(8,128)(2,1)} %get-tuple-element.196.refs_1_.refs_0_, bf16[3,1024,512]{2,1,0:T(8,128)(2,1)} %get-tuple-element.223.refs_1_, f32[1024,1024]{1,0:T(8,128)} %get-tuple-element.228.refs_2_, ...), custom_call_target="tpu_custom_call", output_to_operand_aliasing={{}: (4, {})} | custom-call | flops 6442450944 | tf_op jit(solution)/shard_map/qkv_back/pallas_call | solution.py:1013
  395.6 1.6 collective-permute-done.46
  401.5 6.2 %collective-permute-done.49.refs_1_ = bf16[128,640]{1,0:T(8,128)(2,1)S(1)} collective-permute-done((bf16[128,640]{1,0:T(8,128)(2,1)S(1)}, bf16[128,640]{1,0:T(8,128)(2,1)S(1)}, u32[]{:S(2)}, u32[]{:S(2)}) %collective-permute-start.49) | collective-permute-done | bytes 163872 | tf_op jit(solution)/shard_map/ppermute | solution.py:511
  408.7 2.1 fusion.5
  412.8 2.3 collective-permute-start.51
  415.6 1.7 collective-permute-start.53
  418.5 2.2 collective-permute-done.51
  420.7 3.3 collective-permute-done.52
  426.1 1.5 collective-permute-start.57
  428.2 2.8 order_feed_forward.1
  431.0 1.6 collective-permute-done.50
  432.6 2.5 collective-permute-done.56.refs_6_
  435.1 2.1 order_attention.1
  (178 shorter events, 60.1 us)
Async XLA Ops:
  0.6 8.7 %collective-permute-start = (bf16[128,768]{1,0:T(8,128)(2,1)}, bf16[128,768]{1,0:T(8,128)(2,1)S(1)}, u32[]{:S(2)}, u32[]{:S(2)}) collective-permute-start(bf16[128,768]{1,0:T(8,128)(2,1)} %param.21), channel_id=1, source_target_pairs={{0,2},{1,5},{2,0},{3,7},{4,6},{5,1},{6,4},{7,3},{8,10},{9,13},{10,... | collective-permute-start | bytes 589832 | tf_op jit(solution)/shard_map/ppermute | solution.py:511
  5.2 1.4 collective-permute-start.1
  9.3 36.0 %copy-start = (bf16[1,1024,1024]{2,1,0:T(8,128)(2,1)S(1)}, bf16[1,1024,1024]{2,1,0:T(8,128)(2,1)}, u32[]{:S(2)}) copy-start(bf16[1,1024,1024]{2,1,0:T(8,128)(2,1)} %param.17) | copy-start | bytes 6291460
  10.4 11.5 %collective-permute-start.2 = (bf16[2,128,768]{2,1,0:T(8,128)(2,1)S(1)}, bf16[2,128,768]{2,1,0:T(8,128)(2,1)S(1)}, u32[]{:S(2)}, u32[]{:S(2)}) collective-permute-start(bf16[2,128,768]{2,1,0:T(8,128)(2,1)S(1)} %pad_maximum_fusion.8), channel_id=1, source_target_pairs={{0,4},{1,3},{2,6},{3,1},{4,0},{5,7},{6,2},{7,5},{8,12},{9,11},{10,... | collective-permute-start | bytes 1179656 | tf_op jit(solution)/shard_map/ppermute | solution.py:511
  12.9 7.8 %collective-permute-start.3 = (bf16[2,16,128]{2,1,0:T(8,128)(2,1)S(1)}, bf16[2,16,128]{2,1,0:T(8,128)(2,1)S(1)}, u32[]{:S(2)}, u32[]{:S(2)}) collective-permute-start(bf16[2,16,128]{2,1,0:T(8,128)(2,1)S(1)} %get-tuple-element.275), channel_id=1, source_target_pairs={{0,2},{1,5},{2,0},{3,7},{4,6},{5,1},{6,4},{7,3},{8,10},{9,13},{10,... | collective-permute-start | bytes 24584 | tf_op jit(solution)/shard_map/ppermute | solution.py:511
  22.9 24.2 %copy-start.15 = (bf16[4,128,768]{2,1,0:T(8,128)(2,1)}, bf16[4,128,768]{2,1,0:T(8,128)(2,1)S(1)}, u32[]{:S(2)}) copy-start(bf16[4,128,768]{2,1,0:T(8,128)(2,1)S(1)} %pad_maximum_fusion.3.refs_0_) | copy-start | bytes 2359300
  22.9 11.7 %collective-permute-start.4 = (bf16[128,1280]{1,0:T(8,128)(2,1)S(1)}, bf16[128,1280]{1,0:T(8,128)(2,1)S(1)}, u32[]{:S(2)}, u32[]{:S(2)}) collective-permute-start(bf16[128,1280]{1,0:T(8,128)(2,1)S(1)} %pad_maximum_fusion.9), channel_id=1, source_target_pairs={{0,2},{1,5},{2,0},{3,7},{4,6},{5,1},{6,4},{7,3},{8,10},{9,13},{10,... | collective-permute-start | bytes 983048 | tf_op jit(solution)/shard_map/ppermute | solution.py:511
  25.6 19.2 %collective-permute-start.7 = (bf16[4,128,768]{2,1,0:T(8,128)(2,1)S(1)}, bf16[4,128,768]{2,1,0:T(8,128)(2,1)}, u32[]{:S(2)}, u32[]{:S(2)}) collective-permute-start(bf16[4,128,768]{2,1,0:T(8,128)(2,1)S(1)} %pad_maximum_fusion.3.refs_0_), channel_id=1, source_target_pairs={{0,8},{1,17},{2,10},{3,19},{4,12},{5,21},{6,14},{7,23},{8,0},{9,25... | collective-permute-start | bytes 2359304 | tf_op jit(solution)/shard_map/ppermute | solution.py:511
  27.2 17.6 %collective-permute-start.8 = (bf16[4,128,768]{2,1,0:T(8,128)(2,1)S(1)}, bf16[4,128,768]{2,1,0:T(8,128)(2,1)}, u32[]{:S(2)}, u32[]{:S(2)}) collective-permute-start(bf16[4,128,768]{2,1,0:T(8,128)(2,1)S(1)} %pad_maximum_fusion.3.refs_0_), channel_id=1, source_target_pairs={{0,16},{1,9},{2,18},{3,11},{4,20},{5,13},{6,22},{7,15},{8,24},{9,1... | collective-permute-start | bytes 2359304 | tf_op jit(solution)/shard_map/ppermute | solution.py:511
  29.3 5.3 %collective-permute-start.5 = (bf16[2,2,16,128]{3,2,1,0:T(8,128)(2,1)}, bf16[2,2,16,128]{3,2,1,0:T(8,128)(2,1)}, u32[]{:S(2)}, u32[]{:S(2)}) collective-permute-start(bf16[2,2,16,128]{3,2,1,0:T(8,128)(2,1)} %pad_maximum_fusion.13), channel_id=1, source_target_pairs={{0,4},{1,3},{2,6},{3,1},{4,0},{5,7},{6,2},{7,5},{8,12},{9,11},{10,... | collective-permute-start | bytes 49160 | tf_op jit(solution)/shard_map/ppermute | solution.py:511
  35.5 18.8 %collective-permute-start.6 = (bf16[2,128,1280]{2,1,0:T(8,128)(2,1)}, bf16[2,128,1280]{2,1,0:T(8,128)(2,1)}, u32[]{:S(2)}, u32[]{:S(2)}) collective-permute-start(bf16[2,128,1280]{2,1,0:T(8,128)(2,1)} %pad_maximum_fusion.4), channel_id=1, source_target_pairs={{0,4},{1,3},{2,6},{3,1},{4,0},{5,7},{6,2},{7,5},{8,12},{9,11},{10,... | collective-permute-start | bytes 1966088 | tf_op jit(solution)/shard_map/ppermute | solution.py:511
  44.8 12.2 %collective-permute-start.9 = (bf16[4,128,768]{2,1,0:T(8,128)(2,1)}, bf16[4,128,768]{2,1,0:T(8,128)(2,1)S(1)}, u32[]{:S(2)}, u32[]{:S(2)}) collective-permute-start(bf16[4,128,768]{2,1,0:T(8,128)(2,1)} %collective-permute-done.7.refs_1_), channel_id=1, source_target_pairs={{0,16},{1,9},{2,18},{3,11},{4,20},{5,13},{6,22},{7,15},{8,24},{9,1... | collective-permute-start | bytes 2359304 | tf_op jit(solution)/shard_map/ppermute | solution.py:511
  45.3 13.2 %collective-permute-start.10 = (bf16[4,128,768]{2,1,0:T(8,128)(2,1)S(1)}, bf16[4,128,768]{2,1,0:T(8,128)(2,1)S(1)}, u32[]{:S(2)}, u32[]{:S(2)}) collective-permute-start(bf16[4,128,768]{2,1,0:T(8,128)(2,1)S(1)} %pad_maximum_fusion.3.refs_0_), channel_id=1, source_target_pairs={{0,1},{1,0},{2,3},{3,2},{4,5},{5,4},{6,7},{7,6},{8,9},{9,8},{10,11... | collective-permute-start | bytes 2359304 | tf_op jit(solution)/shard_map/ppermute | solution.py:511
  48.5 10.6 %collective-permute-start.11 = (bf16[4,128,768]{2,1,0:T(8,128)(2,1)}, bf16[4,128,768]{2,1,0:T(8,128)(2,1)S(1)}, u32[]{:S(2)}, u32[]{:S(2)}) collective-permute-start(bf16[4,128,768]{2,1,0:T(8,128)(2,1)} %collective-permute-done.7.refs_1_), channel_id=1, source_target_pairs={{0,1},{1,0},{2,3},{3,2},{4,5},{5,4},{6,7},{7,6},{8,9},{9,8},{10,11... | collective-permute-start | bytes 2359304 | tf_op jit(solution)/shard_map/ppermute | solution.py:511
  49.0 11.0 %collective-permute-start.12 = (bf16[4,128,768]{2,1,0:T(8,128)(2,1)}, bf16[4,128,768]{2,1,0:T(8,128)(2,1)S(1)}, u32[]{:S(2)}, u32[]{:S(2)}) collective-permute-start(bf16[4,128,768]{2,1,0:T(8,128)(2,1)} %collective-permute-done.8.refs_2_), channel_id=1, source_target_pairs={{0,1},{1,0},{2,3},{3,2},{4,5},{5,4},{6,7},{7,6},{8,9},{9,8},{10,11... | collective-permute-start | bytes 2359304 | tf_op jit(solution)/shard_map/ppermute | solution.py:511
  55.6 21.5 %copy-start.12 = (bf16[4,128,1280]{2,1,0:T(8,128)(2,1)}, bf16[4,128,1280]{2,1,0:T(8,128)(2,1)S(1)}, u32[]{:S(2)}) copy-start(bf16[4,128,1280]{2,1,0:T(8,128)(2,1)S(1)} %pad_maximum_fusion.refs_0_) | copy-start | bytes 3932164
  57.0 2.9 collective-permute-start.13
  57.0 36.3 %collective-permute-start.15 = (bf16[4,128,1280]{2,1,0:T(8,128)(2,1)S(1)}, bf16[4,128,1280]{2,1,0:T(8,128)(2,1)}, u32[]{:S(2)}, u32[]{:S(2)}) collective-permute-start(bf16[4,128,1280]{2,1,0:T(8,128)(2,1)S(1)} %pad_maximum_fusion.refs_0_), channel_id=1, source_target_pairs={{0,8},{1,17},{2,10},{3,19},{4,12},{5,21},{6,14},{7,23},{8,0},{9,25... | collective-permute-start | bytes 3932168 | tf_op jit(solution)/shard_map/ppermute | solution.py:511
  58.5 34.8 %collective-permute-start.16 = (bf16[4,128,1280]{2,1,0:T(8,128)(2,1)S(1)}, bf16[4,128,1280]{2,1,0:T(8,128)(2,1)}, u32[]{:S(2)}, u32[]{:S(2)}) collective-permute-start(bf16[4,128,1280]{2,1,0:T(8,128)(2,1)S(1)} %pad_maximum_fusion.refs_0_), channel_id=1, source_target_pairs={{0,16},{1,9},{2,18},{3,11},{4,20},{5,13},{6,22},{7,15},{8,24},{9,1... | collective-permute-start | bytes 3932168 | tf_op jit(solution)/shard_map/ppermute | solution.py:511
  59.0 15.5 %collective-permute-start.14 = (bf16[512,256]{1,0:T(8,128)(2,1)S(1)}, bf16[512,256]{1,0:T(8,128)(2,1)S(1)}, u32[]{:S(2)}, u32[]{:S(2)}) collective-permute-start(bf16[512,256]{1,0:T(8,128)(2,1)S(1)} %copy-done.14), channel_id=1, source_target_pairs={{0,2},{1,5},{2,0},{3,7},{4,6},{5,1},{6,4},{7,3},{8,10},{9,13},{10,... | collective-permute-start | bytes 786440 | tf_op jit(solution)/shard_map/ppermute | solution.py:511
  74.6 18.7 %collective-permute-start.17 = (bf16[2,512,256]{2,1,0:T(8,128)(2,1)S(1)}, bf16[2,512,256]{2,1,0:T(8,128)(2,1)S(1)}, u32[]{:S(2)}, u32[]{:S(2)}) collective-permute-start(bf16[2,512,256]{2,1,0:T(8,128)(2,1)S(1)} %pad_maximum_fusion.5), channel_id=1, source_target_pairs={{0,4},{1,3},{2,6},{3,1},{4,0},{5,7},{6,2},{7,5},{8,12},{9,11},{10,... | collective-permute-start | bytes 1572872 | tf_op jit(solution)/shard_map/ppermute | solution.py:511
  77.1 35.5 %collective-permute-start.19 = (bf16[4,128,1280]{2,1,0:T(8,128)(2,1)S(1)}, bf16[4,128,1280]{2,1,0:T(8,128)(2,1)}, u32[]{:S(2)}, u32[]{:S(2)}) collective-permute-start(bf16[4,128,1280]{2,1,0:T(8,128)(2,1)S(1)} %pad_maximum_fusion.refs_0_), channel_id=1, source_target_pairs={{0,1},{1,0},{2,3},{3,2},{4,5},{5,4},{6,7},{7,6},{8,9},{9,8},{10,11... | collective-permute-start | bytes 3932168 | tf_op jit(solution)/shard_map/ppermute | solution.py:511
  93.3 18.4 %collective-permute-start.18 = (bf16[4,128,1280]{2,1,0:T(8,128)(2,1)}, bf16[4,128,1280]{2,1,0:T(8,128)(2,1)}, u32[]{:S(2)}, u32[]{:S(2)}) collective-permute-start(bf16[4,128,1280]{2,1,0:T(8,128)(2,1)} %collective-permute-done.15.refs_1_), channel_id=1, source_target_pairs={{0,16},{1,9},{2,18},{3,11},{4,20},{5,13},{6,22},{7,15},{8,24},{9,1... | collective-permute-start | bytes 3932168 | tf_op jit(solution)/shard_map/ppermute | solution.py:511
  94.8 31.2 %collective-permute-start.20 = (bf16[4,128,1280]{2,1,0:T(8,128)(2,1)}, bf16[4,128,1280]{2,1,0:T(8,128)(2,1)}, u32[]{:S(2)}, u32[]{:S(2)}) collective-permute-start(bf16[4,128,1280]{2,1,0:T(8,128)(2,1)} %collective-permute-done.15.refs_1_), channel_id=1, source_target_pairs={{0,1},{1,0},{2,3},{3,2},{4,5},{5,4},{6,7},{7,6},{8,9},{9,8},{10,11... | collective-permute-start | bytes 3932168 | tf_op jit(solution)/shard_map/ppermute | solution.py:511
  94.9 31.1 %copy-start.13 = (bf16[4,512,256]{2,1,0:T(8,128)(2,1)}, bf16[4,512,256]{2,1,0:T(8,128)(2,1)S(1)}, u32[]{:S(2)}) copy-start(bf16[4,512,256]{2,1,0:T(8,128)(2,1)S(1)} %pad_maximum_fusion.1.refs_0_) | copy-start | bytes 3145732
  94.9 31.2 %collective-permute-start.21 = (bf16[4,128,1280]{2,1,0:T(8,128)(2,1)}, bf16[4,128,1280]{2,1,0:T(8,128)(2,1)S(1)}, u32[]{:S(2)}, u32[]{:S(2)}) collective-permute-start(bf16[4,128,1280]{2,1,0:T(8,128)(2,1)} %collective-permute-done.16.refs_2_), channel_id=1, source_target_pairs={{0,1},{1,0},{2,3},{3,2},{4,5},{5,4},{6,7},{7,6},{8,9},{9,8},{10,11... | collective-permute-start | bytes 3932168 | tf_op jit(solution)/shard_map/ppermute | solution.py:511
  111.7 14.4 %collective-permute-start.22 = (bf16[4,128,1280]{2,1,0:T(8,128)(2,1)}, bf16[4,128,1280]{2,1,0:T(8,128)(2,1)}, u32[]{:S(2)}, u32[]{:S(2)}) collective-permute-start(bf16[4,128,1280]{2,1,0:T(8,128)(2,1)} %collective-permute-done.18.refs_3_), channel_id=1, source_target_pairs={{0,1},{1,0},{2,3},{3,2},{4,5},{5,4},{6,7},{7,6},{8,9},{9,8},{10,11... | collective-permute-start | bytes 3932168 | tf_op jit(solution)/shard_map/ppermute | solution.py:511
  112.1 26.1 %collective-permute-start.23 = (bf16[4,512,256]{2,1,0:T(8,128)(2,1)S(1)}, bf16[4,512,256]{2,1,0:T(8,128)(2,1)}, u32[]{:S(2)}, u32[]{:S(2)}) collective-permute-start(bf16[4,512,256]{2,1,0:T(8,128)(2,1)S(1)} %pad_maximum_fusion.1.refs_0_), channel_id=1, source_target_pairs={{0,8},{1,17},{2,10},{3,19},{4,12},{5,21},{6,14},{7,23},{8,0},{9,25... | collective-permute-start | bytes 3145736 | tf_op jit(solution)/shard_map/ppermute | solution.py:511
  112.6 25.5 %collective-permute-start.24 = (bf16[4,512,256]{2,1,0:T(8,128)(2,1)S(1)}, bf16[4,512,256]{2,1,0:T(8,128)(2,1)S(1)}, u32[]{:S(2)}, u32[]{:S(2)}) collective-permute-start(bf16[4,512,256]{2,1,0:T(8,128)(2,1)S(1)} %pad_maximum_fusion.1.refs_0_), channel_id=1, source_target_pairs={{0,16},{1,9},{2,18},{3,11},{4,20},{5,13},{6,22},{7,15},{8,24},{9,1... | collective-permute-start | bytes 3145736 | tf_op jit(solution)/shard_map/ppermute | solution.py:511
  126.0 35.2 %collective-permute-start.26 = (bf16[4,512,256]{2,1,0:T(8,128)(2,1)S(1)}, bf16[4,512,256]{2,1,0:T(8,128)(2,1)}, u32[]{:S(2)}, u32[]{:S(2)}) collective-permute-start(bf16[4,512,256]{2,1,0:T(8,128)(2,1)S(1)} %pad_maximum_fusion.1.refs_0_), channel_id=1, source_target_pairs={{0,1},{1,0},{2,3},{3,2},{4,5},{5,4},{6,7},{7,6},{8,9},{9,8},{10,11... | collective-permute-start | bytes 3145736 | tf_op jit(solution)/shard_map/ppermute | solution.py:511
  138.1 23.0 %copy-start.20 = (bf16[4,512,256]{2,1,0:T(8,128)(2,1)}, bf16[4,512,256]{2,1,0:T(8,128)(2,1)S(1)}, u32[]{:S(2)}) copy-start(bf16[4,512,256]{2,1,0:T(8,128)(2,1)S(1)} %collective-permute-done.24.refs_2_) | copy-start | bytes 3145732
  138.1 23.0 %collective-permute-start.25 = (bf16[4,512,256]{2,1,0:T(8,128)(2,1)}, bf16[4,512,256]{2,1,0:T(8,128)(2,1)S(1)}, u32[]{:S(2)}, u32[]{:S(2)}) collective-permute-start(bf16[4,512,256]{2,1,0:T(8,128)(2,1)} %collective-permute-done.23.refs_1_), channel_id=1, source_target_pairs={{0,16},{1,9},{2,18},{3,11},{4,20},{5,13},{6,22},{7,15},{8,24},{9,1... | collective-permute-start | bytes 3145736 | tf_op jit(solution)/shard_map/ppermute | solution.py:511
  138.6 22.7 %collective-permute-start.27 = (bf16[4,512,256]{2,1,0:T(8,128)(2,1)}, bf16[4,512,256]{2,1,0:T(8,128)(2,1)}, u32[]{:S(2)}, u32[]{:S(2)}) collective-permute-start(bf16[4,512,256]{2,1,0:T(8,128)(2,1)} %collective-permute-done.23.refs_1_), channel_id=1, source_target_pairs={{0,1},{1,0},{2,3},{3,2},{4,5},{5,4},{6,7},{7,6},{8,9},{9,8},{10,11... | collective-permute-start | bytes 3145736 | tf_op jit(solution)/shard_map/ppermute | solution.py:511
  138.6 22.7 %collective-permute-start.28 = (bf16[4,512,256]{2,1,0:T(8,128)(2,1)S(1)}, bf16[4,512,256]{2,1,0:T(8,128)(2,1)}, u32[]{:S(2)}, u32[]{:S(2)}) collective-permute-start(bf16[4,512,256]{2,1,0:T(8,128)(2,1)S(1)} %collective-permute-done.24.refs_2_), channel_id=1, source_target_pairs={{0,1},{1,0},{2,3},{3,2},{4,5},{5,4},{6,7},{7,6},{8,9},{9,8},{10,11... | collective-permute-start | bytes 3145736 | tf_op jit(solution)/shard_map/ppermute | solution.py:511
  161.1 2.7 collective-permute-start.29
  211.3 14.6 %collective-permute-start.30 = (bf16[4,4,512,256]{3,2,1,0:T(8,128)(2,1)}, bf16[4,4,512,256]{3,2,1,0:T(8,128)(2,1)}, u32[]{:S(2)}, u32[]{:S(2)}) collective-permute-start(bf16[4,4,512,256]{3,2,1,0:T(8,128)(2,1)} %get-tuple-element.182), channel_id=1, source_target_pairs={{0,1},{1,0},{2,3},{3,2},{4,5},{5,4},{6,7},{7,6},{8,9},{9,8},{10,11... | collective-permute-start | bytes 12582920 | tf_op jit(solution)/shard_map/ppermute | solution.py:511
  225.6 26.0 %collective-permute-start.31 = (bf16[4,4,128,1024]{3,2,1,0:T(8,128)(2,1)}, bf16[4,4,128,1024]{3,2,1,0:T(8,128)(2,1)}, u32[]{:S(2)}, u32[]{:S(2)}) collective-permute-start(bf16[4,4,128,1024]{3,2,1,0:T(8,128)(2,1)} %get-tuple-element.191), channel_id=1, source_target_pairs={{0,1},{1,0},{2,3},{3,2},{4,5},{5,4},{6,7},{7,6},{8,9},{9,8},{10,11... | collective-permute-start | bytes 12582920 | tf_op jit(solution)/shard_map/ppermute | solution.py:511
  229.3 51.9 %collective-permute-start.32 = (bf16[2,4,512,256]{3,2,1,0:T(8,128)(2,1)}, bf16[2,4,512,256]{3,2,1,0:T(8,128)(2,1)}, u32[]{:S(2)}, u32[]{:S(2)}) collective-permute-start(bf16[2,4,512,256]{3,2,1,0:T(8,128)(2,1)} %add_leading.4), channel_id=1, source_target_pairs={{0,8},{1,17},{2,10},{3,19},{4,12},{5,21},{6,14},{7,23},{8,0},{9,25... | collective-permute-start | bytes 6291464 | tf_op jit(solution)/shard_map/ppermute | solution.py:511
  255.0 26.2 %collective-permute-start.33 = (bf16[2,4,128,1024]{3,2,1,0:T(8,128)(2,1)}, bf16[2,4,128,1024]{3,2,1,0:T(8,128)(2,1)S(1)}, u32[]{:S(2)}, u32[]{:S(2)}) collective-permute-start(bf16[2,4,128,1024]{3,2,1,0:T(8,128)(2,1)} %add_leading.5), channel_id=1, source_target_pairs={{0,8},{1,17},{2,10},{3,19},{4,12},{5,21},{6,14},{7,23},{8,0},{9,25... | collective-permute-start | bytes 6291464 | tf_op jit(solution)/shard_map/ppermute | solution.py:511
  288.3 15.1 %collective-permute-start.34 = (bf16[4,512,256]{2,1,0:T(8,128)(2,1)}, bf16[4,512,256]{2,1,0:T(8,128)(2,1)}, u32[]{:S(2)}, u32[]{:S(2)}) collective-permute-start(bf16[4,512,256]{2,1,0:T(8,128)(2,1)} %fusion.3), channel_id=1, source_target_pairs={{0,16},{1,9},{2,18},{3,11},{4,20},{5,13},{6,22},{7,15},{8,24},{9,1... | collective-permute-start | bytes 3145736 | tf_op jit(solution)/shard_map/ppermute | solution.py:511
  301.4 20.7 %collective-permute-start.37 = (bf16[4,4,128,640]{3,2,1,0:T(8,128)(2,1)}, bf16[4,4,128,640]{3,2,1,0:T(8,128)(2,1)S(1)}, u32[]{:S(2)}, u32[]{:S(2)}) collective-permute-start(bf16[4,4,128,640]{3,2,1,0:T(8,128)(2,1)} %get-tuple-element.205), channel_id=1, source_target_pairs={{0,1},{1,0},{2,3},{3,2},{4,5},{5,4},{6,7},{7,6},{8,9},{9,8},{10,11... | collective-permute-start | bytes 7864328 | tf_op jit(solution)/shard_map/ppermute | solution.py:511
  301.5 20.0 %collective-permute-start.36 = (bf16[4,128,1024]{2,1,0:T(8,128)(2,1)}, bf16[4,128,1024]{2,1,0:T(8,128)(2,1)}, u32[]{:S(2)}, u32[]{:S(2)}) collective-permute-start(bf16[4,128,1024]{2,1,0:T(8,128)(2,1)} %fusion.4), channel_id=1, source_target_pairs={{0,16},{1,9},{2,18},{3,11},{4,20},{5,13},{6,22},{7,15},{8,24},{9,1... | collective-permute-start | bytes 3145736 | tf_op jit(solution)/shard_map/ppermute | solution.py:511
  307.2 14.9 %collective-permute-start.35 = (bf16[2,512,256]{2,1,0:T(8,128)(2,1)S(1)}, bf16[2,512,256]{2,1,0:T(8,128)(2,1)S(1)}, u32[]{:S(2)}, u32[]{:S(2)}) collective-permute-start(bf16[2,512,256]{2,1,0:T(8,128)(2,1)S(1)} %pad_maximum_fusion.6), channel_id=1, source_target_pairs={{0,2},{1,5},{2,0},{3,7},{4,6},{5,1},{6,4},{7,3},{8,10},{9,13},{10,... | collective-permute-start | bytes 1572872 | tf_op jit(solution)/shard_map/ppermute | solution.py:511
  329.4 24.7 %copy-start.6 = (bf16[4,128,1024]{2,1,0:T(8,128)(2,1)}, bf16[4,128,1024]{2,1,0:T(8,128)(2,1)S(1)}, u32[]{:S(2)}) copy-start(bf16[4,128,1024]{2,1,0:T(8,128)(2,1)S(1)} %fusion) | copy-start | bytes 3145732
  329.5 22.3 %collective-permute-start.40 = (bf16[2,4,128,640]{3,2,1,0:T(8,128)(2,1)}, bf16[2,4,128,640]{3,2,1,0:T(8,128)(2,1)}, u32[]{:S(2)}, u32[]{:S(2)}) collective-permute-start(bf16[2,4,128,640]{3,2,1,0:T(8,128)(2,1)} %add_leading.6), channel_id=1, source_target_pairs={{0,8},{1,17},{2,10},{3,19},{4,12},{5,21},{6,14},{7,23},{8,0},{9,25... | collective-permute-start | bytes 3932168 | tf_op jit(solution)/shard_map/ppermute | solution.py:511
  331.7 20.0 %collective-permute-start.39 = (bf16[2,128,1024]{2,1,0:T(8,128)(2,1)}, bf16[2,128,1024]{2,1,0:T(8,128)(2,1)}, u32[]{:S(2)}, u32[]{:S(2)}) collective-permute-start(bf16[2,128,1024]{2,1,0:T(8,128)(2,1)} %pad_maximum_fusion.7), channel_id=1, source_target_pairs={{0,2},{1,5},{2,0},{3,7},{4,6},{5,1},{6,4},{7,3},{8,10},{9,13},{10,... | collective-permute-start | bytes 1572872 | tf_op jit(solution)/shard_map/ppermute | solution.py:511
  333.8 15.6 %collective-permute-start.38 = (bf16[512,256]{1,0:T(8,128)(2,1)}, bf16[512,256]{1,0:T(8,128)(2,1)S(1)}, u32[]{:S(2)}, u32[]{:S(2)}) collective-permute-start(bf16[512,256]{1,0:T(8,128)(2,1)} %fusion.11), channel_id=1, source_target_pairs={{0,4},{1,3},{2,6},{3,1},{4,0},{5,7},{6,2},{7,5},{8,12},{9,11},{10,... | collective-permute-start | bytes 786440 | tf_op jit(solution)/shard_map/ppermute | solution.py:511
  355.8 12.6 %collective-permute-start.42 = (bf16[4,128,640]{2,1,0:T(8,128)(2,1)}, bf16[4,128,640]{2,1,0:T(8,128)(2,1)}, u32[]{:S(2)}, u32[]{:S(2)}) collective-permute-start(bf16[4,128,640]{2,1,0:T(8,128)(2,1)} %fusion.6), channel_id=1, source_target_pairs={{0,16},{1,9},{2,18},{3,11},{4,20},{5,13},{6,22},{7,15},{8,24},{9,1... | collective-permute-start | bytes 1966088 | tf_op jit(solution)/shard_map/ppermute | solution.py:511
  357.2 11.2 %collective-permute-start.41 = (bf16[128,1024]{1,0:T(8,128)(2,1)}, bf16[128,1024]{1,0:T(8,128)(2,1)S(1)}, u32[]{:S(2)}, u32[]{:S(2)}) collective-permute-start(bf16[128,1024]{1,0:T(8,128)(2,1)} %fusion.12), channel_id=1, source_target_pairs={{0,4},{1,3},{2,6},{3,1},{4,0},{5,7},{6,2},{7,5},{8,12},{9,11},{10,... | collective-permute-start | bytes 786440 | tf_op jit(solution)/shard_map/ppermute | solution.py:511
  368.4 13.2 %collective-permute-start.43 = (bf16[4,4,144,384]{3,2,1,0:T(8,128)(2,1)}, bf16[4,4,144,384]{3,2,1,0:T(8,128)(2,1)}, u32[]{:S(2)}, u32[]{:S(2)}) collective-permute-start(bf16[4,4,144,384]{3,2,1,0:T(8,128)(2,1)} %get-tuple-element.225), channel_id=1, source_target_pairs={{0,1},{1,0},{2,3},{3,2},{4,5},{5,4},{6,7},{7,6},{8,9},{9,8},{10,11... | collective-permute-start | bytes 5308424 | tf_op jit(solution)/shard_map/ppermute | solution.py:511
  370.5 10.9 %collective-permute-start.44 = (bf16[2,128,640]{2,1,0:T(8,128)(2,1)S(1)}, bf16[2,128,640]{2,1,0:T(8,128)(2,1)S(1)}, u32[]{:S(2)}, u32[]{:S(2)}) collective-permute-start(bf16[2,128,640]{2,1,0:T(8,128)(2,1)S(1)} %pad_maximum_fusion.10), channel_id=1, source_target_pairs={{0,2},{1,5},{2,0},{3,7},{4,6},{5,1},{6,4},{7,3},{8,10},{9,13},{10,... | collective-permute-start | bytes 983048 | tf_op jit(solution)/shard_map/ppermute | solution.py:511
  372.3 9.2 %collective-permute-start.45 = (bf16[1024,256]{1,0:T(8,128)(2,1)S(1)}, bf16[1024,256]{1,0:T(8,128)(2,1)S(1)}, u32[]{:S(2)}, u32[]{:S(2)}) collective-permute-start(bf16[1024,256]{1,0:T(8,128)(2,1)S(1)} %slice_dynamic-update-slice_fusion.refs_0_), channel_id=1, source_target_pairs={{0,8},{1,17},{2,10},{3,19},{4,12},{5,21},{6,14},{7,23},{8,0},{9,25... | collective-permute-start | bytes 1572872 | tf_op jit(solution)/shard_map/ppermute | solution.py:511
  383.9 13.4 %collective-permute-start.46 = (bf16[2,4,144,384]{3,2,1,0:T(8,128)(2,1)}, bf16[2,4,144,384]{3,2,1,0:T(8,128)(2,1)}, u32[]{:S(2)}, u32[]{:S(2)}) collective-permute-start(bf16[2,4,144,384]{3,2,1,0:T(8,128)(2,1)} %add_leading.7), channel_id=1, source_target_pairs={{0,8},{1,17},{2,10},{3,19},{4,12},{5,21},{6,14},{7,23},{8,0},{9,25... | collective-permute-start | bytes 2654216 | tf_op jit(solution)/shard_map/ppermute | solution.py:511
  386.0 9.7 %collective-permute-start.47 = (bf16[128,640]{1,0:T(8,128)(2,1)S(1)}, bf16[128,640]{1,0:T(8,128)(2,1)S(1)}, u32[]{:S(2)}, u32[]{:S(2)}) collective-permute-start(bf16[128,640]{1,0:T(8,128)(2,1)S(1)} %fusion.16), channel_id=1, source_target_pairs={{0,4},{1,3},{2,6},{3,1},{4,0},{5,7},{6,2},{7,5},{8,12},{9,11},{10,... | collective-permute-start | bytes 491528 | tf_op jit(solution)/shard_map/ppermute | solution.py:511
  398.6 10.1 %collective-permute-start.48 = (bf16[4,144,384]{2,1,0:T(8,128)(2,1)S(1)}, bf16[4,144,384]{2,1,0:T(8,128)(2,1)S(1)}, u32[]{:S(2)}, u32[]{:S(2)}) collective-permute-start(bf16[4,144,384]{2,1,0:T(8,128)(2,1)S(1)} %fusion.9), channel_id=1, source_target_pairs={{0,16},{1,9},{2,18},{3,11},{4,20},{5,13},{6,22},{7,15},{8,24},{9,1... | collective-permute-start | bytes 1327112 | tf_op jit(solution)/shard_map/ppermute | solution.py:511
  400.5 7.2 %collective-permute-start.49 = (bf16[128,640]{1,0:T(8,128)(2,1)S(1)}, bf16[128,640]{1,0:T(8,128)(2,1)S(1)}, u32[]{:S(2)}, u32[]{:S(2)}) collective-permute-start(bf16[128,640]{1,0:T(8,128)(2,1)S(1)} %fusion.10.refs_0_), channel_id=1, source_target_pairs={{0,8},{1,17},{2,10},{3,19},{4,12},{5,21},{6,14},{7,23},{8,0},{9,25... | collective-permute-start | bytes 491528 | tf_op jit(solution)/shard_map/ppermute | solution.py:511
  411.9 16.2 %collective-permute-start.54 = (bf16[2,1024,256]{2,1,0:T(8,128)(2,1)}, bf16[2,1024,256]{2,1,0:T(8,128)(2,1)S(1)}, u32[]{:S(2)}, u32[]{:S(2)}) collective-permute-start(bf16[2,1024,256]{2,1,0:T(8,128)(2,1)} %pad_maximum_fusion.2), channel_id=1, source_target_pairs={{0,16},{1,9},{2,18},{3,11},{4,20},{5,13},{6,22},{7,15},{8,24},{9,1... | collective-permute-start | bytes 3145736 | tf_op jit(solution)/shard_map/ppermute | solution.py:511
  412.8 7.9 %collective-permute-start.51 = (bf16[144,384]{1,0:T(8,128)(2,1)S(1)}, bf16[144,384]{1,0:T(8,128)(2,1)S(1)}, u32[]{:S(2)}, u32[]{:S(2)}) collective-permute-start(bf16[144,384]{1,0:T(8,128)(2,1)S(1)} %get-tuple-element.259), channel_id=1, source_target_pairs={{0,6},{1,7},{2,4},{3,5},{4,2},{5,3},{6,0},{7,1},{8,14},{9,15},{10,... | collective-permute-start | bytes 331784 | tf_op jit(solution)/shard_map/ppermute | solution.py:511
  415.1 8.9 %collective-permute-start.52 = (bf16[144,384]{1,0:T(8,128)(2,1)S(1)}, bf16[144,384]{1,0:T(8,128)(2,1)S(1)}, u32[]{:S(2)}, u32[]{:S(2)}) collective-permute-start(bf16[144,384]{1,0:T(8,128)(2,1)S(1)} %get-tuple-element.258), channel_id=1, source_target_pairs={{0,4},{1,5},{2,6},{3,7},{4,0},{5,1},{6,2},{7,3},{8,12},{9,13},{10,... | collective-permute-start | bytes 331784 | tf_op jit(solution)/shard_map/ppermute | solution.py:511
  415.6 8.4 %collective-permute-start.53 = (bf16[144,384]{1,0:T(8,128)(2,1)S(1)}, bf16[144,384]{1,0:T(8,128)(2,1)S(1)}, u32[]{:S(2)}, u32[]{:S(2)}) collective-permute-start(bf16[144,384]{1,0:T(8,128)(2,1)S(1)} %get-tuple-element.257), channel_id=1, source_target_pairs={{0,2},{1,3},{2,0},{3,1},{4,6},{5,7},{6,4},{7,5},{8,10},{9,11},{10,... | collective-permute-start | bytes 331784 | tf_op jit(solution)/shard_map/ppermute | solution.py:511
  417.3 15.2 %collective-permute-start.50 = (bf16[2,128,640]{2,1,0:T(8,128)(2,1)S(1)}, bf16[2,128,640]{2,1,0:T(8,128)(2,1)S(1)}, u32[]{:S(2)}, u32[]{:S(2)}) collective-permute-start(bf16[2,128,640]{2,1,0:T(8,128)(2,1)S(1)} %pad_maximum_fusion.11), channel_id=1, source_target_pairs={{0,16},{1,9},{2,18},{3,11},{4,20},{5,13},{6,22},{7,15},{8,24},{9,1... | collective-permute-start | bytes 983048 | tf_op jit(solution)/shard_map/ppermute | solution.py:511
  424.0 8.6 %collective-permute-start.55 = (bf16[144,384]{1,0:T(8,128)(2,1)S(1)}, bf16[144,384]{1,0:T(8,128)(2,1)S(1)}, u32[]{:S(2)}, u32[]{:S(2)}) collective-permute-start(bf16[144,384]{1,0:T(8,128)(2,1)S(1)} %fusion.15.refs_4_), channel_id=1, source_target_pairs={{0,8},{1,9},{2,10},{3,11},{4,12},{5,13},{6,14},{7,15},{8,0},{9,1},... | collective-permute-start | bytes 331784 | tf_op jit(solution)/shard_map/ppermute | solution.py:511
  425.0 10.1 %collective-permute-start.56 = (bf16[144,384]{1,0:T(8,128)(2,1)S(1)}, bf16[144,384]{1,0:T(8,128)(2,1)S(1)}, u32[]{:S(2)}, u32[]{:S(2)}) collective-permute-start(bf16[144,384]{1,0:T(8,128)(2,1)S(1)} %fusion.15.refs_4_), channel_id=1, source_target_pairs={{0,16},{1,17},{2,18},{3,19},{4,20},{5,21},{6,22},{7,23},{8,24},{9,... | collective-permute-start | bytes 331784 | tf_op jit(solution)/shard_map/ppermute | solution.py:511
  426.1 9.1 %collective-permute-start.57 = (bf16[144,384]{1,0:T(8,128)(2,1)S(1)}, bf16[144,384]{1,0:T(8,128)(2,1)S(1)}, u32[]{:S(2)}, u32[]{:S(2)}) collective-permute-start(bf16[144,384]{1,0:T(8,128)(2,1)S(1)} %fusion.15.refs_4_), channel_id=1, source_target_pairs={{0,24},{1,25},{2,26},{3,27},{4,28},{5,29},{6,30},{7,31},{8,16},{9,... | collective-permute-start | bytes 331784 | tf_op jit(solution)/shard_map/ppermute | solution.py:511
  (22 other events, 103.5 us)

commit v2 on v1

--- a/solution.py
+++ b/solution.py
@@ -865,8 +865,9 @@
     def kernel(where, ready, weight, x_ref, bias_ref, hid_ref, slope_ref):
         ready()
         at = pl.ds(pl.multiple_of((where[2] ^ pl.program_id(0)) * cols, LANES), cols)
-        for tile in range(length // TILE):
-            here = pl.ds(tile * TILE, TILE)
+        size = min(512, length)
+        for tile in range(length // size):
+            here = pl.ds(tile * size, size)
             pre = mxu(x_ref[here, :], weight[:, at], NN) + bias_ref[:, at]
             share = 0.5 + 0.5 * lax.erf(pre * (1.0 / math.sqrt(2.0)))
             bell = jnp.exp(-0.5 * pre * pre) * (1.0 / math.sqrt(2.0 * math.pi))
@@ -1237,26 +1238,6 @@
     return total.astype(jnp.bfloat16)
 
 
-def add_leading(left, right):
-    _, chips, rows, cols = left.shape
-
-    def kernel(left_ref, right_ref, out_ref):
-        total = left_ref[...].astype(jnp.float32) + right_ref[...].astype(jnp.float32)
-        out_ref[...] = total.astype(jnp.bfloat16)
-
-    block = pl.BlockSpec((1, chips, rows, cols), lambda i: (i, 0, 0, 0))
-    return pl.pallas_call(
-        kernel,
-        grid=(2,),
-        in_specs=[block, block],
-        out_specs=block,
-        out_shape=shaped((2, chips, rows, cols), jnp.bfloat16),
-        compiler_params=params(60),
-        cost_estimate=cost(512 * chips * rows * cols),
-        name="add_leading",
-    )(left, right)
-
-
 class Reduction:
     def __init__(self, place, made):
         self.place = place
@@ -1265,7 +1246,7 @@
 
     def near(self):
         self.core = self.flying
-        leave = add_leading(self.made, self.core)
+        leave = add(self.made[:2], self.core[:2])
         self.flying = self.place.swap_grp(leave, 0)
         return leave
 
@@ -1276,37 +1257,39 @@
         return second
 
     def column(self):
-        mine = add(self.made[2], self.core[2], self.first[0], self.flying)
-        return mine, lambda chip: lax.dynamic_index_in_dim(mine, chip, 0, False)
+        terms = (self.made[2], self.core[2], self.first[0], self.flying)
+        return lambda chip: [lax.dynamic_index_in_dim(t, chip, 0, False) for t in terms]
 
     def along(self):
         place = self.place
-        mine, at = self.column()
-        self.mine = [at(place.slot_chip(slot)) for slot in range(4)]
-        both = jnp.stack([self.mine[1], self.mine[3]])
+        at = self.column()
+        self.mine = [at(place.slot_chip(slot)) for slot in (0, 2)]
+        both = jnp.stack([add(*at(place.slot_chip(slot))) for slot in (1, 3)])
         self.flying = place.swap_chip(both, 0)
         return both
 
     def along_far(self):
         self.first = self.flying
-        second = add(self.mine[2], self.first[1])
+        second = add(*self.mine[1], self.first[1])
         self.flying = self.place.swap_chip(second, 1)
         return second
 
     def share(self):
-        return add(self.mine[0], self.first[0], self.flying)
+        return add(*self.mine[0], self.first[0], self.flying)
 
     def along_direct(self):
         place = self.place
-        mine, at = self.column()
+        at = self.column()
         self.mine = at(place.chip)
+        sent = [add(*at(place.chip ^ k)) for k in range(place.chips - 1, 0, -1)]
         self.flying = tuple(
-            place.permute(at(place.chip ^ k), (2 * k, 2 * k)) for k in range(place.chips - 1, 0, -1)
+            place.permute(block, (2 * k, 2 * k))
+            for k, block in zip(range(place.chips - 1, 0, -1), sent)
         )
-        return mine
+        return sent
 
     def share_direct(self):
-        return add(self.mine, *self.flying)
+        return add(*self.mine, *self.flying)
 
 
 class Replication:
@@ -1570,8 +1553,8 @@
     all_a = Replication(place, r_a.share())
     meet(all_a.blocks[0], r_b, all_a)
     along = r_b.along_direct()
-    all_a.flying = after(all_a.flying, along)
-    all_ffn.flying = after(all_ffn.flying, along)
+    all_a.flying = after(all_a.flying, *along)
+    all_ffn.flying = after(all_ffn.flying, *along)
     pairs_made = (all_a.far(), all_ffn.far())
     meet(pairs_made, r_b)
     share_b = r_b.share_direct()

time: 443 us -> 449 us (1.014)
  local copies, waits for them, and re-layouts: 10.6 us -> 24.3 us
  Pallas kernels: 279 us -> 267 us
  other arithmetic: 38.9 us -> 50.4 us
  waiting for transfers between devices: 49.7 us -> 42.9 us
    slice x0 -> x12, local copies, waits for them, and re-layouts: none -> 16.4 us  [column(): terms = (self.made[2], self.core[2], self.first[0], self.flying)]
    pallas_call x4 -> x0, Pallas kernels: 11.8 us -> none  [add_leading(): pl.pallas_call(kernel, grid=(2,), in_specs=[block, block], out_specs=bloc...]
    convert_element_type x14 -> x18, other arithmetic: 27.3 us -> 38.5 us  [add(): return total.astype(jnp.bfloat16)]
    ppermute x58, waiting for transfers between devices: 49.7 us -> 42.9 us  [permute(): return lax.ppermute(array, AXES, pairs)]
  transfers between devices with their start and end apart: 58 -> 58, of which waited for: 24 -> 21; matrix products, arithmetic and copies ran while one was open for 4% -> 10% of each run, Pallas kernels for 51% -> 49%
where the time goes in v2:
time: 449 us; the launch traced here: 445 us
  Pallas kernels  267 us (59%)
  starting transfers between devices  58.5 us (13%)
  other arithmetic  50.4 us (11%)
  waiting for transfers between devices  42.9 us (10%)
  local copies, waits for them, and re-layouts  24.3 us (5%)
    pallas_call x4, Pallas kernels, weight_call(): pl.pallas_call(body, grid_spec=pltpu.PrefetchScalarGridSpec(num_scalar_pr...  76.3 us
    ppermute x58, starting transfers between devices, permute(): return lax.ppermute(array, AXES, pairs)  58.5 us
    pallas_call x3, Pallas kernels, attention_backward(): pl.pallas_call(body, grid=(pairs,), in_specs=[pair(0), pair(1), pair(2),...  51.2 us
    pallas_call x3, Pallas kernels, attention_forward(): pl.pallas_call(body, grid=(pairs,), in_specs=[pair(0), pair(1), pair(2),...  44.4 us
    ppermute x58, waiting for transfers between devices, permute(): return lax.ppermute(array, AXES, pairs)  42.9 us
    convert_element_type x18, other arithmetic, add(): return total.astype(jnp.bfloat16)  38.5 us
    pallas_call x2, Pallas kernels, weight_grad(): pl.pallas_call(functools.partial(weight_grad_kernel, rows=rows, groups=gr...  28 us
    pallas_call x2, Pallas kernels, attention_grads(): pl.pallas_call(functools.partial(attention_grads_kernel, rows=rows, group...  21.1 us
  transfers between devices with their start and end apart: 58, of which 21 were waited for; matrix products, arithmetic and copies ran while one was open for 10% of the time, Pallas kernels for 49%

profile of v2, /device:TPU:0, one launch (start us, length us, event | category | flops | bytes accessed | tf_op | source)
XLA Modules:
  0.0 444.7 jit_solution(6287575780028630721)
XLA Ops:
  0.6 3.1 collective-permute-start
  3.7 1.5 concatenate.29
  6.7 2.7 collective-permute-done
  10.4 2.5 collective-permute-start.2
  12.9 2.5 collective-permute-start.3
  16.4 4.3 collective-permute-done.3
  22.9 2.7 collective-permute-start.4
  25.6 1.6 collective-permute-start.7
  27.2 1.5 collective-permute-start.8
  29.3 3.3 collective-permute-start.5
  32.6 2.0 collective-permute-done.5
  35.5 2.9 collective-permute-start.6
  40.4 2.1 vectors.1
  42.4 2.4 collective-permute-done.7.refs_1_
  49.0 5.4 %collective-permute-done.6 = bf16[2,128,1280]{2,1,0:T(8,128)(2,1)} collective-permute-done((bf16[2,128,1280]{2,1,0:T(8,128)(2,1)}, bf16[2,128,1280]{2,1,0:T(8,128)(2,1)}, u32[]{:S(2)}, u32[]{:S(2)}) %collective-permute-start.6) | collective-permute-done | bytes 655392 | tf_op jit(solution)/shard_map/ppermute | solution.py:511
  57.0 1.5 collective-permute-start.15
  61.7 12.8 %qkv.1 = (bf16[1024,3072]{1,0:T(8,128)(2,1)}, bf16[1024,3072]{1,0:T(8,128)(2,1)}) custom-call(s32[3]{0:T(128)} %pad_add_fusion.where, bf16[4,128,768]{2,1,0:T(8,128)(2,1)} %copy-done.14, bf16[4,128,768]{2,1,0:T(8,128)(2,1)} %collective-permute-done.7.refs_1_, bf16[4,128,768]{2,1,0:T(8,128)(2,1)} %collective-permute-done.8.refs_2_, ...), custom_call_target="tpu_custom_call" | custom-call | flops 12884901888 | tf_op jit(solution)/shard_map/qkv/pallas_call | solution.py:657
  74.6 2.5 collective-permute-start.17
  77.1 16.2 %attn_fwd.3 = (bf16[1024,1024]{1,0:T(8,128)(2,1)}, bf16[16,1024,1024]{2,1,0:T(8,128)(2,1)}, f32[1024,1024]{1,0:T(8,128)}) custom-call(bf16[1024,3072]{1,0:T(8,128)(2,1)} %get-tuple-element.161.q_ref.k_ref.v_ref.refs_0_.refs_1_.refs_2_, bf16[1024,3072]{1,0:T(8,128)(2,1)} %get-tuple-element.161.q_ref.k_ref.v_ref.refs_0_.refs_1_.refs_2_, ...), custom_call_target="tpu_custom_call" | custom-call | flops 12884901888 | tf_op jit(solution)/shard_map/attn_fwd/pallas_call | solution.py:391
  95.5 16.2 %attn_fwd.4 = (bf16[1024,1024]{1,0:T(8,128)(2,1)}, bf16[16,1024,1024]{2,1,0:T(8,128)(2,1)}, f32[1024,1024]{1,0:T(8,128)}) custom-call(bf16[1024,3072]{1,0:T(8,128)(2,1)} %get-tuple-element.161.q_ref.k_ref.v_ref.refs_0_.refs_1_.refs_2_, ...), custom_call_target="tpu_custom_call", output_to_operand_aliasing={{0}: (5, {}), {1}: (6, {}), {2}: (7, {})} | custom-call | flops 12884901888 | tf_op jit(solution)/shard_map/attn_fwd/pallas_call | solution.py:391
  114.0 12.0 %attn_fwd.5 = (bf16[1024,1024]{1,0:T(8,128)(2,1)}, bf16[16,1024,1024]{2,1,0:T(8,128)(2,1)}, f32[1024,1024]{1,0:T(8,128)}) custom-call(bf16[1024,3072]{1,0:T(8,128)(2,1)} %get-tuple-element.161.q_ref.k_ref.v_ref.refs_0_.refs_1_.refs_2_, ...), custom_call_target="tpu_custom_call", output_to_operand_aliasing={{0}: (5, {}), {1}: (6, {}), {2}: (7, {})} | custom-call | flops 8589934592 | tf_op jit(solution)/shard_map/attn_fwd/pallas_call | solution.py:391
  127.1 9.6 %attn_out.1 = (f32[1024,1024]{1,0:T(8,128)}, f32[1024,128]{1,0:T(8,128)}, bf16[1024,1024]{1,0:T(8,128)(2,1)}, bf16[1024,1024]{1,0:T(8,128)(2,1)}) custom-call(s32[3]{0:T(128)} %pad_add_fusion.where, bf16[4,128,1280]{2,1,0:T(8,128)(2,1)} %copy-done.11, bf16[4,128,1280]{2,1,0:T(8,128)(2,1)} %collective-permute-done.15.refs_1_, ...), custom_call_target="tpu_custom_call" | custom-call | flops 4294967296 | tf_op jit(solution)/shard_map/attn_out/pallas_call | solution.py:657
  139.1 21.3 %feed_in.1 = (bf16[1024,4096]{1,0:T(8,128)(2,1)}, bf16[1024,4096]{1,0:T(8,128)(2,1)}, bf16[1024,4096]{1,0:T(8,128)(2,1)}) custom-call(s32[3]{0:T(128)} %pad_add_fusion.where, bf16[4,128,1280]{2,1,0:T(8,128)(2,1)} %copy-done.11, bf16[4,128,1280]{2,1,0:T(8,128)(2,1)} %collective-permute-done.15.refs_1_, bf16[4,128,1280]{2,1,0:T(8,128)(2,1)} %collective-permute-done.16.refs_2_, ...), custom_call_target="tpu_custom_call" | custom-call | flops 17179869184 | tf_op jit(solution)/shard_map/feed_in/pallas_call | solution.py:657
  160.5 2.6 collective-permute-done.29.refs_7_
  164.1 32.5 %feed_out.1 = (bf16[1024,1024]{1,0:T(8,128)(2,1)}, f32[1024,1024]{1,0:T(8,128)}, bf16[1024,1024]{1,0:T(8,128)(2,1)}, f32[8,1024]{1,0:T(8,128)}, bf16[1024,4096]{1,0:T(8,128)(2,1)}, /*index=5*/f32[1,4096]{1,0:T(1,128)}) custom-call(s32[3]{0:T(128)} %pad_add_fusion.where, bf16[4,512,256]{2,1,0:T(8,128)(2,1)} %copy-done.12, ...), custom_call_target="tpu_custom_call" | custom-call | flops 34359738368 | tf_op jit(solution)/shard_map/feed_out/pallas_call | solution.py:657
  196.7 13.9 %wgrad_out.1 = (bf16[4,4,512,256]{3,2,1,0:T(8,128)(2,1)}, bf16[4,4,512,256]{3,2,1,0:T(8,128)(2,1)}) custom-call(s32[3]{0:T(128)} %pad_add_fusion.where, bf16[1024,4096]{1,0:T(8,128)(2,1)} %get-tuple-element.170.refs_8_.left_ref, bf16[1024,1024]{1,0:T(8,128)(2,1)} %get-tuple-element.178.right_ref), custom_call_target="tpu_custom_call" | custom-call | flops 17179869184 | tf_op jit(solution)/shard_map/wgrad_out/pallas_call | solution.py:1215
  210.8 14.1 %wgrad_in.1 = (bf16[4,4,128,1024]{3,2,1,0:T(8,128)(2,1)}, bf16[4,4,128,1024]{3,2,1,0:T(8,128)(2,1)}) custom-call(s32[3]{0:T(128)} %pad_add_fusion.where, bf16[1024,1024]{1,0:T(8,128)(2,1)} %get-tuple-element.180.refs_8_.left_ref, bf16[1024,4096]{1,0:T(8,128)(2,1)} %get-tuple-element.184.right_ref.p_ref), custom_call_target="tpu_custom_call" | custom-call | flops 17179869184 | tf_op jit(solution)/shard_map/wgrad_in/pallas_call | solution.py:1215
  225.2 2.7 add_convert_fusion.1
  229.3 21.0 %feed_in_back.1 = (f32[1024,1024]{1,0:T(8,128)}, bf16[1024,1024]{1,0:T(8,128)(2,1)}, bf16[1024,1024]{1,0:T(8,128)(2,1)}, f32[8,1024]{1,0:T(8,128)}) custom-call(bf16[1024,4096]{1,0:T(8,128)(2,1)} %get-tuple-element.184.right_ref.p_ref, bf16[1024,4096]{1,0:T(8,128)(2,1)} %get-tuple-element.185.w_ref, f32[1024,1024]{1,0:T(8,128)} %get-tuple-element.186.g_ref, ...), custom_call_target="tpu_custom_call" | custom-call | flops 21474836480 | tf_op jit(solution)/shard_map/feed_in_back/pallas_call | solution.py:679
  250.3 4.7 %add_convert_fusion = bf16[2,4,128,1024]{3,2,1,0:T(8,128)(2,1)} fusion(bf16[4,4,128,1024]{3,2,1,0:T(8,128)(2,1)} %collective-permute-done.31, bf16[4,4,128,1024]{3,2,1,0:T(8,128)(2,1)} %get-tuple-element.181), kind=kLoop, calls=%fused_computation | loop fusion | flops 4194304 | bytes 6291456 | tf_op jit(solution)/shard_map/convert_element_type | solution.py:1238
  255.7 23.7 %attn_bwd.3 = (bf16[3,1024,512]{2,1,0:T(8,128)(2,1)}, f32[2,512]{1,0:T(2,128)}) custom-call(bf16[1024,3072]{1,0:T(8,128)(2,1)} %get-tuple-element.161.q_ref.k_ref.v_ref.refs_0_.refs_1_.refs_2_, bf16[1024,3072]{1,0:T(8,128)(2,1)} %get-tuple-element.161.q_ref.k_ref.v_ref.refs_0_.refs_1_.refs_2_, ...), custom_call_target="tpu_custom_call" | custom-call | flops 34359738368 | tf_op jit(solution)/shard_map/attn_bwd/pallas_call | solution.py:470
  279.4 1.9 collective-permute-done.33
  281.3 3.4 fusion.1
  284.7 3.2 fusion
  288.6 12.4 %wgrad_a.1 = (bf16[4,4,128,640]{3,2,1,0:T(8,128)(2,1)}, bf16[4,4,128,640]{3,2,1,0:T(8,128)(2,1)}) custom-call(s32[3]{0:T(128)} %pad_add_fusion.where, bf16[2,512,1024]{2,1,0:T(8,128)(2,1)} %copy-done.1, bf16[3,1024,512]{2,1,0:T(8,128)(2,1)} %get-tuple-element.196.refs_1_.refs_0_, bf16[1024,1024]{1,0:T(8,128)(2,1)} %get-tuple-element.164.refs_8_.refs_3_.refs_2_, ...), custom_call_target="tpu_custom_call" | custom-call | flops 10737418240 | tf_op jit(solution)/shard_map/wgrad_a/pallas_call | solution.py:1173
  302.3 1.7 slice.188
  305.2 1.7 slice.189
  308.2 1.5 collective-permute-start.36
  311.0 1.5 slice.203
  315.3 13.7 %attn_bwd.4 = (bf16[3,1024,512]{2,1,0:T(8,128)(2,1)}, f32[2,512]{1,0:T(2,128)}) custom-call(bf16[1024,3072]{1,0:T(8,128)(2,1)} %get-tuple-element.161.q_ref.k_ref.v_ref.refs_0_.refs_1_.refs_2_, bf16[1024,3072]{1,0:T(8,128)(2,1)} %get-tuple-element.161.q_ref.k_ref.v_ref.refs_0_.refs_1_.refs_2_, ...), custom_call_target="tpu_custom_call" | custom-call | flops 17179869184 | tf_op jit(solution)/shard_map/attn_bwd/pallas_call | solution.py:470
  329.4 3.1 add_convert_fusion.2
  336.5 2.1 fusion.8
  339.3 13.9 %attn_bwd.5 = (bf16[3,1024,512]{2,1,0:T(8,128)(2,1)}, f32[2,512]{1,0:T(2,128)}) custom-call(bf16[1024,3072]{1,0:T(8,128)(2,1)} %get-tuple-element.161.q_ref.k_ref.v_ref.refs_0_.refs_1_.refs_2_, bf16[1024,3072]{1,0:T(8,128)(2,1)} %get-tuple-element.161.q_ref.k_ref.v_ref.refs_0_.refs_1_.refs_2_, ...), custom_call_target="tpu_custom_call", output_to_operand_aliasing={{0}: (7, {}), {1}: (8, {})} | custom-call | flops 17179869184 | tf_op jit(solution)/shard_map/attn_bwd/pallas_call | solution.py:470
  353.2 2.0 slice.204
  355.2 1.5 collective-permute-done.39
  356.7 2.6 fusion.2
  359.2 1.9 fusion.7
  363.7 1.5 constant_dynamic-update-slice_fusion
  365.3 8.7 %wgrad_b.1 = (bf16[4,4,144,384]{3,2,1,0:T(8,128)(2,1)}, bf16[4,4,144,384]{3,2,1,0:T(8,128)(2,1)}) custom-call(s32[3]{0:T(128)} %pad_add_fusion.where, bf16[2,512,1024]{2,1,0:T(8,128)(2,1)} %copy-done.1, bf16[3,1024,512]{2,1,0:T(8,128)(2,1)} %get-tuple-element.223.refs_1_, f32[2,512]{1,0:T(2,128)} %get-tuple-element.197.refs_2_, ...), custom_call_target="tpu_custom_call" | custom-call | flops 6442450944 | tf_op jit(solution)/shard_map/wgrad_b/pallas_call | solution.py:1173
  380.0 8.2 %qkv_back.2.refs_3_ = f32[1024,1024]{1,0:T(8,128)} custom-call(bf16[1024,3072]{1,0:T(8,128)(2,1)} %get-tuple-element.176.w_ref, bf16[3,1024,512]{2,1,0:T(8,128)(2,1)} %get-tuple-element.196.refs_1_.refs_0_, bf16[3,1024,512]{2,1,0:T(8,128)(2,1)} %get-tuple-element.223.refs_1_, f32[1024,1024]{1,0:T(8,128)} %get-tuple-element.228.refs_2_), custom_call_target="tpu_custom_call" | custom-call | flops 6442450944 | tf_op jit(solution)/shard_map/qkv_back/pallas_call | solution.py:1014
  388.8 2.6 add_convert_fusion.5
  394.3 8.5 %qkv_back.3 = f32[1024,1024]{1,0:T(8,128)} custom-call(bf16[1024,3072]{1,0:T(8,128)(2,1)} %get-tuple-element.176.w_ref, bf16[3,1024,512]{2,1,0:T(8,128)(2,1)} %get-tuple-element.196.refs_1_.refs_0_, bf16[3,1024,512]{2,1,0:T(8,128)(2,1)} %get-tuple-element.223.refs_1_, f32[1024,1024]{1,0:T(8,128)} %get-tuple-element.228.refs_2_, ...), custom_call_target="tpu_custom_call", output_to_operand_aliasing={{}: (4, {})} | custom-call | flops 6442450944 | tf_op jit(solution)/shard_map/qkv_back/pallas_call | solution.py:1014
  402.9 1.8 collective-permute-done.46
  404.7 2.2 fusion.13
  413.3 2.2 collective-permute-done.49.refs_1_
  419.4 1.8 collective-permute-start.51
  421.3 2.6 collective-permute-start.53
  424.6 1.5 collective-permute-done.51
  426.2 3.1 collective-permute-done.52
  430.3 1.7 collective-permute-start.55
  431.9 1.5 collective-permute-start.56
  433.9 2.8 order_feed_forward.1
  436.7 3.3 collective-permute-done.50
  441.2 2.1 order_attention.1
  (180 shorter events, 71.2 us)
Async XLA Ops:
  0.6 8.7 %collective-permute-start = (bf16[128,768]{1,0:T(8,128)(2,1)}, bf16[128,768]{1,0:T(8,128)(2,1)S(1)}, u32[]{:S(2)}, u32[]{:S(2)}) collective-permute-start(bf16[128,768]{1,0:T(8,128)(2,1)} %param.21), channel_id=1, source_target_pairs={{0,2},{1,5},{2,0},{3,7},{4,6},{5,1},{6,4},{7,3},{8,10},{9,13},{10,... | collective-permute-start | bytes 589832 | tf_op jit(solution)/shard_map/ppermute | solution.py:511
  5.2 1.4 collective-permute-start.1
  9.3 36.0 %copy-start = (bf16[1,1024,1024]{2,1,0:T(8,128)(2,1)S(1)}, bf16[1,1024,1024]{2,1,0:T(8,128)(2,1)}, u32[]{:S(2)}) copy-start(bf16[1,1024,1024]{2,1,0:T(8,128)(2,1)} %param.17) | copy-start | bytes 6291460
  10.4 11.5 %collective-permute-start.2 = (bf16[2,128,768]{2,1,0:T(8,128)(2,1)S(1)}, bf16[2,128,768]{2,1,0:T(8,128)(2,1)S(1)}, u32[]{:S(2)}, u32[]{:S(2)}) collective-permute-start(bf16[2,128,768]{2,1,0:T(8,128)(2,1)S(1)} %pad_maximum_fusion.8), channel_id=1, source_target_pairs={{0,4},{1,3},{2,6},{3,1},{4,0},{5,7},{6,2},{7,5},{8,12},{9,11},{10,... | collective-permute-start | bytes 1179656 | tf_op jit(solution)/shard_map/ppermute | solution.py:511
  12.9 7.8 %collective-permute-start.3 = (bf16[2,16,128]{2,1,0:T(8,128)(2,1)S(1)}, bf16[2,16,128]{2,1,0:T(8,128)(2,1)S(1)}, u32[]{:S(2)}, u32[]{:S(2)}) collective-permute-start(bf16[2,16,128]{2,1,0:T(8,128)(2,1)S(1)} %get-tuple-element.275), channel_id=1, source_target_pairs={{0,2},{1,5},{2,0},{3,7},{4,6},{5,1},{6,4},{7,3},{8,10},{9,13},{10,... | collective-permute-start | bytes 24584 | tf_op jit(solution)/shard_map/ppermute | solution.py:511
  22.9 24.2 %copy-start.14 = (bf16[4,128,768]{2,1,0:T(8,128)(2,1)}, bf16[4,128,768]{2,1,0:T(8,128)(2,1)S(1)}, u32[]{:S(2)}) copy-start(bf16[4,128,768]{2,1,0:T(8,128)(2,1)S(1)} %pad_maximum_fusion.3.refs_0_) | copy-start | bytes 2359300
  22.9 11.7 %collective-permute-start.4 = (bf16[128,1280]{1,0:T(8,128)(2,1)S(1)}, bf16[128,1280]{1,0:T(8,128)(2,1)S(1)}, u32[]{:S(2)}, u32[]{:S(2)}) collective-permute-start(bf16[128,1280]{1,0:T(8,128)(2,1)S(1)} %pad_maximum_fusion.9), channel_id=1, source_target_pairs={{0,2},{1,5},{2,0},{3,7},{4,6},{5,1},{6,4},{7,3},{8,10},{9,13},{10,... | collective-permute-start | bytes 983048 | tf_op jit(solution)/shard_map/ppermute | solution.py:511
  25.6 19.2 %collective-permute-start.7 = (bf16[4,128,768]{2,1,0:T(8,128)(2,1)S(1)}, bf16[4,128,768]{2,1,0:T(8,128)(2,1)}, u32[]{:S(2)}, u32[]{:S(2)}) collective-permute-start(bf16[4,128,768]{2,1,0:T(8,128)(2,1)S(1)} %pad_maximum_fusion.3.refs_0_), channel_id=1, source_target_pairs={{0,8},{1,17},{2,10},{3,19},{4,12},{5,21},{6,14},{7,23},{8,0},{9,25... | collective-permute-start | bytes 2359304 | tf_op jit(solution)/shard_map/ppermute | solution.py:511
  27.2 17.6 %collective-permute-start.8 = (bf16[4,128,768]{2,1,0:T(8,128)(2,1)S(1)}, bf16[4,128,768]{2,1,0:T(8,128)(2,1)}, u32[]{:S(2)}, u32[]{:S(2)}) collective-permute-start(bf16[4,128,768]{2,1,0:T(8,128)(2,1)S(1)} %pad_maximum_fusion.3.refs_0_), channel_id=1, source_target_pairs={{0,16},{1,9},{2,18},{3,11},{4,20},{5,13},{6,22},{7,15},{8,24},{9,1... | collective-permute-start | bytes 2359304 | tf_op jit(solution)/shard_map/ppermute | solution.py:511
  29.3 5.3 %collective-permute-start.5 = (bf16[2,2,16,128]{3,2,1,0:T(8,128)(2,1)}, bf16[2,2,16,128]{3,2,1,0:T(8,128)(2,1)}, u32[]{:S(2)}, u32[]{:S(2)}) collective-permute-start(bf16[2,2,16,128]{3,2,1,0:T(8,128)(2,1)} %pad_maximum_fusion.13), channel_id=1, source_target_pairs={{0,4},{1,3},{2,6},{3,1},{4,0},{5,7},{6,2},{7,5},{8,12},{9,11},{10,... | collective-permute-start | bytes 49160 | tf_op jit(solution)/shard_map/ppermute | solution.py:511
  35.5 18.8 %collective-permute-start.6 = (bf16[2,128,1280]{2,1,0:T(8,128)(2,1)}, bf16[2,128,1280]{2,1,0:T(8,128)(2,1)}, u32[]{:S(2)}, u32[]{:S(2)}) collective-permute-start(bf16[2,128,1280]{2,1,0:T(8,128)(2,1)} %pad_maximum_fusion.4), channel_id=1, source_target_pairs={{0,4},{1,3},{2,6},{3,1},{4,0},{5,7},{6,2},{7,5},{8,12},{9,11},{10,... | collective-permute-start | bytes 1966088 | tf_op jit(solution)/shard_map/ppermute | solution.py:511
  44.8 12.2 %collective-permute-start.9 = (bf16[4,128,768]{2,1,0:T(8,128)(2,1)}, bf16[4,128,768]{2,1,0:T(8,128)(2,1)S(1)}, u32[]{:S(2)}, u32[]{:S(2)}) collective-permute-start(bf16[4,128,768]{2,1,0:T(8,128)(2,1)} %collective-permute-done.7.refs_1_), channel_id=1, source_target_pairs={{0,16},{1,9},{2,18},{3,11},{4,20},{5,13},{6,22},{7,15},{8,24},{9,1... | collective-permute-start | bytes 2359304 | tf_op jit(solution)/shard_map/ppermute | solution.py:511
  45.3 13.2 %collective-permute-start.10 = (bf16[4,128,768]{2,1,0:T(8,128)(2,1)S(1)}, bf16[4,128,768]{2,1,0:T(8,128)(2,1)S(1)}, u32[]{:S(2)}, u32[]{:S(2)}) collective-permute-start(bf16[4,128,768]{2,1,0:T(8,128)(2,1)S(1)} %pad_maximum_fusion.3.refs_0_), channel_id=1, source_target_pairs={{0,1},{1,0},{2,3},{3,2},{4,5},{5,4},{6,7},{7,6},{8,9},{9,8},{10,11... | collective-permute-start | bytes 2359304 | tf_op jit(solution)/shard_map/ppermute | solution.py:511
  48.5 10.6 %collective-permute-start.11 = (bf16[4,128,768]{2,1,0:T(8,128)(2,1)}, bf16[4,128,768]{2,1,0:T(8,128)(2,1)S(1)}, u32[]{:S(2)}, u32[]{:S(2)}) collective-permute-start(bf16[4,128,768]{2,1,0:T(8,128)(2,1)} %collective-permute-done.7.refs_1_), channel_id=1, source_target_pairs={{0,1},{1,0},{2,3},{3,2},{4,5},{5,4},{6,7},{7,6},{8,9},{9,8},{10,11... | collective-permute-start | bytes 2359304 | tf_op jit(solution)/shard_map/ppermute | solution.py:511
  49.0 11.0 %collective-permute-start.12 = (bf16[4,128,768]{2,1,0:T(8,128)(2,1)}, bf16[4,128,768]{2,1,0:T(8,128)(2,1)S(1)}, u32[]{:S(2)}, u32[]{:S(2)}) collective-permute-start(bf16[4,128,768]{2,1,0:T(8,128)(2,1)} %collective-permute-done.8.refs_2_), channel_id=1, source_target_pairs={{0,1},{1,0},{2,3},{3,2},{4,5},{5,4},{6,7},{7,6},{8,9},{9,8},{10,11... | collective-permute-start | bytes 2359304 | tf_op jit(solution)/shard_map/ppermute | solution.py:511
  55.6 21.5 %copy-start.11 = (bf16[4,128,1280]{2,1,0:T(8,128)(2,1)}, bf16[4,128,1280]{2,1,0:T(8,128)(2,1)S(1)}, u32[]{:S(2)}) copy-start(bf16[4,128,1280]{2,1,0:T(8,128)(2,1)S(1)} %pad_maximum_fusion.refs_0_) | copy-start | bytes 3932164
  57.0 2.9 collective-permute-start.13
  57.0 36.3 %collective-permute-start.15 = (bf16[4,128,1280]{2,1,0:T(8,128)(2,1)S(1)}, bf16[4,128,1280]{2,1,0:T(8,128)(2,1)}, u32[]{:S(2)}, u32[]{:S(2)}) collective-permute-start(bf16[4,128,1280]{2,1,0:T(8,128)(2,1)S(1)} %pad_maximum_fusion.refs_0_), channel_id=1, source_target_pairs={{0,8},{1,17},{2,10},{3,19},{4,12},{5,21},{6,14},{7,23},{8,0},{9,25... | collective-permute-start | bytes 3932168 | tf_op jit(solution)/shard_map/ppermute | solution.py:511
  58.5 34.8 %collective-permute-start.16 = (bf16[4,128,1280]{2,1,0:T(8,128)(2,1)S(1)}, bf16[4,128,1280]{2,1,0:T(8,128)(2,1)}, u32[]{:S(2)}, u32[]{:S(2)}) collective-permute-start(bf16[4,128,1280]{2,1,0:T(8,128)(2,1)S(1)} %pad_maximum_fusion.refs_0_), channel_id=1, source_target_pairs={{0,16},{1,9},{2,18},{3,11},{4,20},{5,13},{6,22},{7,15},{8,24},{9,1... | collective-permute-start | bytes 3932168 | tf_op jit(solution)/shard_map/ppermute | solution.py:511
  59.0 15.5 %collective-permute-start.14 = (bf16[512,256]{1,0:T(8,128)(2,1)S(1)}, bf16[512,256]{1,0:T(8,128)(2,1)S(1)}, u32[]{:S(2)}, u32[]{:S(2)}) collective-permute-start(bf16[512,256]{1,0:T(8,128)(2,1)S(1)} %copy-done.13), channel_id=1, source_target_pairs={{0,2},{1,5},{2,0},{3,7},{4,6},{5,1},{6,4},{7,3},{8,10},{9,13},{10,... | collective-permute-start | bytes 786440 | tf_op jit(solution)/shard_map/ppermute | solution.py:511
  74.6 18.7 %collective-permute-start.17 = (bf16[2,512,256]{2,1,0:T(8,128)(2,1)S(1)}, bf16[2,512,256]{2,1,0:T(8,128)(2,1)S(1)}, u32[]{:S(2)}, u32[]{:S(2)}) collective-permute-start(bf16[2,512,256]{2,1,0:T(8,128)(2,1)S(1)} %pad_maximum_fusion.5), channel_id=1, source_target_pairs={{0,4},{1,3},{2,6},{3,1},{4,0},{5,7},{6,2},{7,5},{8,12},{9,11},{10,... | collective-permute-start | bytes 1572872 | tf_op jit(solution)/shard_map/ppermute | solution.py:511
  77.1 35.5 %collective-permute-start.19 = (bf16[4,128,1280]{2,1,0:T(8,128)(2,1)S(1)}, bf16[4,128,1280]{2,1,0:T(8,128)(2,1)}, u32[]{:S(2)}, u32[]{:S(2)}) collective-permute-start(bf16[4,128,1280]{2,1,0:T(8,128)(2,1)S(1)} %pad_maximum_fusion.refs_0_), channel_id=1, source_target_pairs={{0,1},{1,0},{2,3},{3,2},{4,5},{5,4},{6,7},{7,6},{8,9},{9,8},{10,11... | collective-permute-start | bytes 3932168 | tf_op jit(solution)/shard_map/ppermute | solution.py:511
  93.3 18.3 %collective-permute-start.18 = (bf16[4,128,1280]{2,1,0:T(8,128)(2,1)}, bf16[4,128,1280]{2,1,0:T(8,128)(2,1)}, u32[]{:S(2)}, u32[]{:S(2)}) collective-permute-start(bf16[4,128,1280]{2,1,0:T(8,128)(2,1)} %collective-permute-done.15.refs_1_), channel_id=1, source_target_pairs={{0,16},{1,9},{2,18},{3,11},{4,20},{5,13},{6,22},{7,15},{8,24},{9,1... | collective-permute-start | bytes 3932168 | tf_op jit(solution)/shard_map/ppermute | solution.py:511
  94.8 31.2 %collective-permute-start.20 = (bf16[4,128,1280]{2,1,0:T(8,128)(2,1)}, bf16[4,128,1280]{2,1,0:T(8,128)(2,1)}, u32[]{:S(2)}, u32[]{:S(2)}) collective-permute-start(bf16[4,128,1280]{2,1,0:T(8,128)(2,1)} %collective-permute-done.15.refs_1_), channel_id=1, source_target_pairs={{0,1},{1,0},{2,3},{3,2},{4,5},{5,4},{6,7},{7,6},{8,9},{9,8},{10,11... | collective-permute-start | bytes 3932168 | tf_op jit(solution)/shard_map/ppermute | solution.py:511
  94.9 31.1 %copy-start.12 = (bf16[4,512,256]{2,1,0:T(8,128)(2,1)}, bf16[4,512,256]{2,1,0:T(8,128)(2,1)S(1)}, u32[]{:S(2)}) copy-start(bf16[4,512,256]{2,1,0:T(8,128)(2,1)S(1)} %pad_maximum_fusion.1.refs_0_) | copy-start | bytes 3145732
  94.9 31.2 %collective-permute-start.21 = (bf16[4,128,1280]{2,1,0:T(8,128)(2,1)}, bf16[4,128,1280]{2,1,0:T(8,128)(2,1)S(1)}, u32[]{:S(2)}, u32[]{:S(2)}) collective-permute-start(bf16[4,128,1280]{2,1,0:T(8,128)(2,1)} %collective-permute-done.16.refs_2_), channel_id=1, source_target_pairs={{0,1},{1,0},{2,3},{3,2},{4,5},{5,4},{6,7},{7,6},{8,9},{9,8},{10,11... | collective-permute-start | bytes 3932168 | tf_op jit(solution)/shard_map/ppermute | solution.py:511
  111.7 14.4 %collective-permute-start.22 = (bf16[4,128,1280]{2,1,0:T(8,128)(2,1)}, bf16[4,128,1280]{2,1,0:T(8,128)(2,1)}, u32[]{:S(2)}, u32[]{:S(2)}) collective-permute-start(bf16[4,128,1280]{2,1,0:T(8,128)(2,1)} %collective-permute-done.18.refs_3_), channel_id=1, source_target_pairs={{0,1},{1,0},{2,3},{3,2},{4,5},{5,4},{6,7},{7,6},{8,9},{9,8},{10,11... | collective-permute-start | bytes 3932168 | tf_op jit(solution)/shard_map/ppermute | solution.py:511
  112.1 26.1 %collective-permute-start.23 = (bf16[4,512,256]{2,1,0:T(8,128)(2,1)S(1)}, bf16[4,512,256]{2,1,0:T(8,128)(2,1)}, u32[]{:S(2)}, u32[]{:S(2)}) collective-permute-start(bf16[4,512,256]{2,1,0:T(8,128)(2,1)S(1)} %pad_maximum_fusion.1.refs_0_), channel_id=1, source_target_pairs={{0,8},{1,17},{2,10},{3,19},{4,12},{5,21},{6,14},{7,23},{8,0},{9,25... | collective-permute-start | bytes 3145736 | tf_op jit(solution)/shard_map/ppermute | solution.py:511
  112.6 25.5 %collective-permute-start.24 = (bf16[4,512,256]{2,1,0:T(8,128)(2,1)S(1)}, bf16[4,512,256]{2,1,0:T(8,128)(2,1)S(1)}, u32[]{:S(2)}, u32[]{:S(2)}) collective-permute-start(bf16[4,512,256]{2,1,0:T(8,128)(2,1)S(1)} %pad_maximum_fusion.1.refs_0_), channel_id=1, source_target_pairs={{0,16},{1,9},{2,18},{3,11},{4,20},{5,13},{6,22},{7,15},{8,24},{9,1... | collective-permute-start | bytes 3145736 | tf_op jit(solution)/shard_map/ppermute | solution.py:511
  126.0 34.5 %collective-permute-start.26 = (bf16[4,512,256]{2,1,0:T(8,128)(2,1)S(1)}, bf16[4,512,256]{2,1,0:T(8,128)(2,1)}, u32[]{:S(2)}, u32[]{:S(2)}) collective-permute-start(bf16[4,512,256]{2,1,0:T(8,128)(2,1)S(1)} %pad_maximum_fusion.1.refs_0_), channel_id=1, source_target_pairs={{0,1},{1,0},{2,3},{3,2},{4,5},{5,4},{6,7},{7,6},{8,9},{9,8},{10,11... | collective-permute-start | bytes 3145736 | tf_op jit(solution)/shard_map/ppermute | solution.py:511
  138.1 22.3 %copy-start.17 = (bf16[4,512,256]{2,1,0:T(8,128)(2,1)}, bf16[4,512,256]{2,1,0:T(8,128)(2,1)S(1)}, u32[]{:S(2)}) copy-start(bf16[4,512,256]{2,1,0:T(8,128)(2,1)S(1)} %collective-permute-done.24.refs_2_) | copy-start | bytes 3145732
  138.1 22.3 %collective-permute-start.25 = (bf16[4,512,256]{2,1,0:T(8,128)(2,1)}, bf16[4,512,256]{2,1,0:T(8,128)(2,1)S(1)}, u32[]{:S(2)}, u32[]{:S(2)}) collective-permute-start(bf16[4,512,256]{2,1,0:T(8,128)(2,1)} %collective-permute-done.23.refs_1_), channel_id=1, source_target_pairs={{0,16},{1,9},{2,18},{3,11},{4,20},{5,13},{6,22},{7,15},{8,24},{9,1... | collective-permute-start | bytes 3145736 | tf_op jit(solution)/shard_map/ppermute | solution.py:511
  138.5 22.0 %collective-permute-start.27 = (bf16[4,512,256]{2,1,0:T(8,128)(2,1)}, bf16[4,512,256]{2,1,0:T(8,128)(2,1)}, u32[]{:S(2)}, u32[]{:S(2)}) collective-permute-start(bf16[4,512,256]{2,1,0:T(8,128)(2,1)} %collective-permute-done.23.refs_1_), channel_id=1, source_target_pairs={{0,1},{1,0},{2,3},{3,2},{4,5},{5,4},{6,7},{7,6},{8,9},{9,8},{10,11... | collective-permute-start | bytes 3145736 | tf_op jit(solution)/shard_map/ppermute | solution.py:511
  138.6 22.0 %collective-permute-start.28 = (bf16[4,512,256]{2,1,0:T(8,128)(2,1)S(1)}, bf16[4,512,256]{2,1,0:T(8,128)(2,1)}, u32[]{:S(2)}, u32[]{:S(2)}) collective-permute-start(bf16[4,512,256]{2,1,0:T(8,128)(2,1)S(1)} %collective-permute-done.24.refs_2_), channel_id=1, source_target_pairs={{0,1},{1,0},{2,3},{3,2},{4,5},{5,4},{6,7},{7,6},{8,9},{9,8},{10,11... | collective-permute-start | bytes 3145736 | tf_op jit(solution)/shard_map/ppermute | solution.py:511
  160.4 2.7 collective-permute-start.29
  210.6 14.6 %collective-permute-start.30 = (bf16[4,4,512,256]{3,2,1,0:T(8,128)(2,1)}, bf16[4,4,512,256]{3,2,1,0:T(8,128)(2,1)}, u32[]{:S(2)}, u32[]{:S(2)}) collective-permute-start(bf16[4,4,512,256]{3,2,1,0:T(8,128)(2,1)} %get-tuple-element.182), channel_id=1, source_target_pairs={{0,1},{1,0},{2,3},{3,2},{4,5},{5,4},{6,7},{7,6},{8,9},{9,8},{10,11... | collective-permute-start | bytes 12582920 | tf_op jit(solution)/shard_map/ppermute | solution.py:511
  224.9 25.4 %collective-permute-start.31 = (bf16[4,4,128,1024]{3,2,1,0:T(8,128)(2,1)}, bf16[4,4,128,1024]{3,2,1,0:T(8,128)(2,1)}, u32[]{:S(2)}, u32[]{:S(2)}) collective-permute-start(bf16[4,4,128,1024]{3,2,1,0:T(8,128)(2,1)} %get-tuple-element.191), channel_id=1, source_target_pairs={{0,1},{1,0},{2,3},{3,2},{4,5},{5,4},{6,7},{7,6},{8,9},{9,8},{10,11... | collective-permute-start | bytes 12582920 | tf_op jit(solution)/shard_map/ppermute | solution.py:511
  227.9 53.4 %collective-permute-start.32 = (bf16[2,4,512,256]{3,2,1,0:T(8,128)(2,1)S(1)}, bf16[2,4,512,256]{3,2,1,0:T(8,128)(2,1)}, u32[]{:S(2)}, u32[]{:S(2)}) collective-permute-start(bf16[2,4,512,256]{3,2,1,0:T(8,128)(2,1)S(1)} %add_convert_fusion.1), channel_id=1, source_target_pairs={{0,8},{1,17},{2,10},{3,19},{4,12},{5,21},{6,14},{7,23},{8,0},{9,25... | collective-permute-start | bytes 6291464 | tf_op jit(solution)/shard_map/ppermute | solution.py:511
  254.9 26.4 %collective-permute-start.33 = (bf16[2,4,128,1024]{3,2,1,0:T(8,128)(2,1)}, bf16[2,4,128,1024]{3,2,1,0:T(8,128)(2,1)}, u32[]{:S(2)}, u32[]{:S(2)}) collective-permute-start(bf16[2,4,128,1024]{3,2,1,0:T(8,128)(2,1)} %add_convert_fusion), channel_id=1, source_target_pairs={{0,8},{1,17},{2,10},{3,19},{4,12},{5,21},{6,14},{7,23},{8,0},{9,25... | collective-permute-start | bytes 6291464 | tf_op jit(solution)/shard_map/ppermute | solution.py:511
  288.0 24.6 %collective-permute-start.34 = (bf16[4,512,256]{2,1,0:T(8,128)(2,1)}, bf16[4,512,256]{2,1,0:T(8,128)(2,1)}, u32[]{:S(2)}, u32[]{:S(2)}) collective-permute-start(bf16[4,512,256]{2,1,0:T(8,128)(2,1)} %fusion), channel_id=1, source_target_pairs={{0,16},{1,9},{2,18},{3,11},{4,20},{5,13},{6,22},{7,15},{8,24},{9,1... | collective-permute-start | bytes 3145736 | tf_op jit(solution)/shard_map/ppermute | solution.py:511
  300.9 28.5 %collective-permute-start.37 = (bf16[4,4,128,640]{3,2,1,0:T(8,128)(2,1)}, bf16[4,4,128,640]{3,2,1,0:T(8,128)(2,1)}, u32[]{:S(2)}, u32[]{:S(2)}) collective-permute-start(bf16[4,4,128,640]{3,2,1,0:T(8,128)(2,1)} %get-tuple-element.205), channel_id=1, source_target_pairs={{0,1},{1,0},{2,3},{3,2},{4,5},{5,4},{6,7},{7,6},{8,9},{9,8},{10,11... | collective-permute-start | bytes 7864328 | tf_op jit(solution)/shard_map/ppermute | solution.py:511
  308.2 20.7 %collective-permute-start.36 = (bf16[4,128,1024]{2,1,0:T(8,128)(2,1)}, bf16[4,128,1024]{2,1,0:T(8,128)(2,1)}, u32[]{:S(2)}, u32[]{:S(2)}) collective-permute-start(bf16[4,128,1024]{2,1,0:T(8,128)(2,1)} %fusion.1), channel_id=1, source_target_pairs={{0,16},{1,9},{2,18},{3,11},{4,20},{5,13},{6,22},{7,15},{8,24},{9,1... | collective-permute-start | bytes 3145736 | tf_op jit(solution)/shard_map/ppermute | solution.py:511
  311.0 48.2 %copy-start.4 = (bf16[1,4,128,1024]{3,2,1,0:T(8,128)(2,1)}, bf16[1,4,128,1024]{3,2,1,0:T(8,128)(2,1)S(1)}, u32[]{:S(2)}) copy-start(bf16[1,4,128,1024]{3,2,1,0:T(8,128)(2,1)S(1)} %slice.190) | copy-start | bytes 3145732
  314.7 14.7 %collective-permute-start.35 = (bf16[2,512,256]{2,1,0:T(8,128)(2,1)}, bf16[2,512,256]{2,1,0:T(8,128)(2,1)}, u32[]{:S(2)}, u32[]{:S(2)}) collective-permute-start(bf16[2,512,256]{2,1,0:T(8,128)(2,1)} %pad_maximum_fusion.6), channel_id=1, source_target_pairs={{0,2},{1,5},{2,0},{3,7},{4,6},{5,1},{6,4},{7,3},{8,10},{9,13},{10,... | collective-permute-start | bytes 1572872 | tf_op jit(solution)/shard_map/ppermute | solution.py:511
  332.5 24.1 %collective-permute-start.40 = (bf16[2,4,128,640]{3,2,1,0:T(8,128)(2,1)}, bf16[2,4,128,640]{3,2,1,0:T(8,128)(2,1)}, u32[]{:S(2)}, u32[]{:S(2)}) collective-permute-start(bf16[2,4,128,640]{3,2,1,0:T(8,128)(2,1)} %add_convert_fusion.2), channel_id=1, source_target_pairs={{0,8},{1,17},{2,10},{3,19},{4,12},{5,21},{6,14},{7,23},{8,0},{9,25... | collective-permute-start | bytes 3932168 | tf_op jit(solution)/shard_map/ppermute | solution.py:511
  336.1 20.5 %collective-permute-start.39 = (bf16[2,128,1024]{2,1,0:T(8,128)(2,1)}, bf16[2,128,1024]{2,1,0:T(8,128)(2,1)}, u32[]{:S(2)}, u32[]{:S(2)}) collective-permute-start(bf16[2,128,1024]{2,1,0:T(8,128)(2,1)} %pad_maximum_fusion.7), channel_id=1, source_target_pairs={{0,2},{1,5},{2,0},{3,7},{4,6},{5,1},{6,4},{7,3},{8,10},{9,13},{10,... | collective-permute-start | bytes 1572872 | tf_op jit(solution)/shard_map/ppermute | solution.py:511
  338.6 16.6 %collective-permute-start.38 = (bf16[512,256]{1,0:T(8,128)(2,1)}, bf16[512,256]{1,0:T(8,128)(2,1)S(1)}, u32[]{:S(2)}, u32[]{:S(2)}) collective-permute-start(bf16[512,256]{1,0:T(8,128)(2,1)} %fusion.8), channel_id=1, source_target_pairs={{0,4},{1,3},{2,6},{3,1},{4,0},{5,7},{6,2},{7,5},{8,12},{9,11},{10,... | collective-permute-start | bytes 786440 | tf_op jit(solution)/shard_map/ppermute | solution.py:511
  361.2 14.1 %collective-permute-start.42 = (bf16[4,128,640]{2,1,0:T(8,128)(2,1)}, bf16[4,128,640]{2,1,0:T(8,128)(2,1)}, u32[]{:S(2)}, u32[]{:S(2)}) collective-permute-start(bf16[4,128,640]{2,1,0:T(8,128)(2,1)} %fusion.2), channel_id=1, source_target_pairs={{0,16},{1,9},{2,18},{3,11},{4,20},{5,13},{6,22},{7,15},{8,24},{9,1... | collective-permute-start | bytes 1966088 | tf_op jit(solution)/shard_map/ppermute | solution.py:511
  362.5 12.8 %collective-permute-start.41 = (bf16[128,1024]{1,0:T(8,128)(2,1)}, bf16[128,1024]{1,0:T(8,128)(2,1)S(1)}, u32[]{:S(2)}, u32[]{:S(2)}) collective-permute-start(bf16[128,1024]{1,0:T(8,128)(2,1)} %fusion.7), channel_id=1, source_target_pairs={{0,4},{1,3},{2,6},{3,1},{4,0},{5,7},{6,2},{7,5},{8,12},{9,11},{10,... | collective-permute-start | bytes 786440 | tf_op jit(solution)/shard_map/ppermute | solution.py:511
  375.2 13.6 %collective-permute-start.43 = (bf16[4,4,144,384]{3,2,1,0:T(8,128)(2,1)}, bf16[4,4,144,384]{3,2,1,0:T(8,128)(2,1)}, u32[]{:S(2)}, u32[]{:S(2)}) collective-permute-start(bf16[4,4,144,384]{3,2,1,0:T(8,128)(2,1)} %get-tuple-element.225), channel_id=1, source_target_pairs={{0,1},{1,0},{2,3},{3,2},{4,5},{5,4},{6,7},{7,6},{8,9},{9,8},{10,11... | collective-permute-start | bytes 5308424 | tf_op jit(solution)/shard_map/ppermute | solution.py:511
  376.8 11.4 %collective-permute-start.44 = (bf16[2,128,640]{2,1,0:T(8,128)(2,1)S(1)}, bf16[2,128,640]{2,1,0:T(8,128)(2,1)}, u32[]{:S(2)}, u32[]{:S(2)}) collective-permute-start(bf16[2,128,640]{2,1,0:T(8,128)(2,1)S(1)} %pad_maximum_fusion.10), channel_id=1, source_target_pairs={{0,2},{1,5},{2,0},{3,7},{4,6},{5,1},{6,4},{7,3},{8,10},{9,13},{10,... | collective-permute-start | bytes 983048 | tf_op jit(solution)/shard_map/ppermute | solution.py:511
  379.5 9.2 %collective-permute-start.45 = (bf16[1024,256]{1,0:T(8,128)(2,1)S(1)}, bf16[1024,256]{1,0:T(8,128)(2,1)S(1)}, u32[]{:S(2)}, u32[]{:S(2)}) collective-permute-start(bf16[1024,256]{1,0:T(8,128)(2,1)S(1)} %slice_dynamic-update-slice_fusion.refs_0_), channel_id=1, source_target_pairs={{0,8},{1,17},{2,10},{3,19},{4,12},{5,21},{6,14},{7,23},{8,0},{9,25... | collective-permute-start | bytes 1572872 | tf_op jit(solution)/shard_map/ppermute | solution.py:511
  391.4 13.4 %collective-permute-start.46 = (bf16[2,4,144,384]{3,2,1,0:T(8,128)(2,1)}, bf16[2,4,144,384]{3,2,1,0:T(8,128)(2,1)}, u32[]{:S(2)}, u32[]{:S(2)}) collective-permute-start(bf16[2,4,144,384]{3,2,1,0:T(8,128)(2,1)} %add_convert_fusion.5), channel_id=1, source_target_pairs={{0,8},{1,17},{2,10},{3,19},{4,12},{5,21},{6,14},{7,23},{8,0},{9,25... | collective-permute-start | bytes 2654216 | tf_op jit(solution)/shard_map/ppermute | solution.py:511
  393.7 9.2 %collective-permute-start.47 = (bf16[128,640]{1,0:T(8,128)(2,1)S(1)}, bf16[128,640]{1,0:T(8,128)(2,1)S(1)}, u32[]{:S(2)}, u32[]{:S(2)}) collective-permute-start(bf16[128,640]{1,0:T(8,128)(2,1)S(1)} %fusion.16), channel_id=1, source_target_pairs={{0,4},{1,3},{2,6},{3,1},{4,0},{5,7},{6,2},{7,5},{8,12},{9,11},{10,... | collective-permute-start | bytes 491528 | tf_op jit(solution)/shard_map/ppermute | solution.py:511
  406.9 9.8 %collective-permute-start.48 = (bf16[4,144,384]{2,1,0:T(8,128)(2,1)}, bf16[4,144,384]{2,1,0:T(8,128)(2,1)}, u32[]{:S(2)}, u32[]{:S(2)}) collective-permute-start(bf16[4,144,384]{2,1,0:T(8,128)(2,1)} %fusion.13), channel_id=1, source_target_pairs={{0,16},{1,9},{2,18},{3,11},{4,20},{5,13},{6,22},{7,15},{8,24},{9,1... | collective-permute-start | bytes 1327112 | tf_op jit(solution)/shard_map/ppermute | solution.py:511
  409.0 6.5 %collective-permute-start.49 = (bf16[128,640]{1,0:T(8,128)(2,1)S(1)}, bf16[128,640]{1,0:T(8,128)(2,1)S(1)}, u32[]{:S(2)}, u32[]{:S(2)}) collective-permute-start(bf16[128,640]{1,0:T(8,128)(2,1)S(1)} %fusion.15.refs_0_), channel_id=1, source_target_pairs={{0,8},{1,17},{2,10},{3,19},{4,12},{5,21},{6,14},{7,23},{8,0},{9,25... | collective-permute-start | bytes 491528 | tf_op jit(solution)/shard_map/ppermute | solution.py:511
  418.1 15.8 %collective-permute-start.54 = (bf16[2,1024,256]{2,1,0:T(8,128)(2,1)S(1)}, bf16[2,1024,256]{2,1,0:T(8,128)(2,1)S(1)}, u32[]{:S(2)}, u32[]{:S(2)}) collective-permute-start(bf16[2,1024,256]{2,1,0:T(8,128)(2,1)S(1)} %pad_maximum_fusion.2), channel_id=1, source_target_pairs={{0,16},{1,9},{2,18},{3,11},{4,20},{5,13},{6,22},{7,15},{8,24},{9,1... | collective-permute-start | bytes 3145736 | tf_op jit(solution)/shard_map/ppermute | solution.py:511
  419.4 6.7 %collective-permute-start.51 = (bf16[144,384]{1,0:T(8,128)(2,1)S(1)}, bf16[144,384]{1,0:T(8,128)(2,1)S(1)}, u32[]{:S(2)}, u32[]{:S(2)}) collective-permute-start(bf16[144,384]{1,0:T(8,128)(2,1)S(1)} %get-tuple-element.257), channel_id=1, source_target_pairs={{0,6},{1,7},{2,4},{3,5},{4,2},{5,3},{6,0},{7,1},{8,14},{9,15},{10,... | collective-permute-start | bytes 331784 | tf_op jit(solution)/shard_map/ppermute | solution.py:511
  421.3 8.0 %collective-permute-start.52 = (bf16[144,384]{1,0:T(8,128)(2,1)S(1)}, bf16[144,384]{1,0:T(8,128)(2,1)S(1)}, u32[]{:S(2)}, u32[]{:S(2)}) collective-permute-start(bf16[144,384]{1,0:T(8,128)(2,1)S(1)} %get-tuple-element.256), channel_id=1, source_target_pairs={{0,4},{1,5},{2,6},{3,7},{4,0},{5,1},{6,2},{7,3},{8,12},{9,13},{10,... | collective-permute-start | bytes 331784 | tf_op jit(solution)/shard_map/ppermute | solution.py:511
  421.3 8.0 %collective-permute-start.53 = (bf16[144,384]{1,0:T(8,128)(2,1)S(1)}, bf16[144,384]{1,0:T(8,128)(2,1)S(1)}, u32[]{:S(2)}, u32[]{:S(2)}) collective-permute-start(bf16[144,384]{1,0:T(8,128)(2,1)S(1)} %get-tuple-element.255), channel_id=1, source_target_pairs={{0,2},{1,3},{2,0},{3,1},{4,6},{5,7},{6,4},{7,5},{8,10},{9,11},{10,... | collective-permute-start | bytes 331784 | tf_op jit(solution)/shard_map/ppermute | solution.py:511
  423.9 16.1 %collective-permute-start.50 = (bf16[2,128,640]{2,1,0:T(8,128)(2,1)S(1)}, bf16[2,128,640]{2,1,0:T(8,128)(2,1)S(1)}, u32[]{:S(2)}, u32[]{:S(2)}) collective-permute-start(bf16[2,128,640]{2,1,0:T(8,128)(2,1)S(1)} %pad_maximum_fusion.11), channel_id=1, source_target_pairs={{0,16},{1,9},{2,18},{3,11},{4,20},{5,13},{6,22},{7,15},{8,24},{9,1... | collective-permute-start | bytes 983048 | tf_op jit(solution)/shard_map/ppermute | solution.py:511
  430.3 9.8 %collective-permute-start.55 = (bf16[144,384]{1,0:T(8,128)(2,1)S(1)}, bf16[144,384]{1,0:T(8,128)(2,1)S(1)}, u32[]{:S(2)}, u32[]{:S(2)}) collective-permute-start(bf16[144,384]{1,0:T(8,128)(2,1)S(1)} %fusion.22.refs_4_), channel_id=1, source_target_pairs={{0,8},{1,9},{2,10},{3,11},{4,12},{5,13},{6,14},{7,15},{8,0},{9,1},... | collective-permute-start | bytes 331784 | tf_op jit(solution)/shard_map/ppermute | solution.py:511
  431.9 9.2 %collective-permute-start.56 = (bf16[144,384]{1,0:T(8,128)(2,1)S(1)}, bf16[144,384]{1,0:T(8,128)(2,1)S(1)}, u32[]{:S(2)}, u32[]{:S(2)}) collective-permute-start(bf16[144,384]{1,0:T(8,128)(2,1)S(1)} %fusion.22.refs_4_), channel_id=1, source_target_pairs={{0,16},{1,17},{2,18},{3,19},{4,20},{5,21},{6,22},{7,23},{8,24},{9,... | collective-permute-start | bytes 331784 | tf_op jit(solution)/shard_map/ppermute | solution.py:511
  433.5 7.7 %collective-permute-start.57 = (bf16[144,384]{1,0:T(8,128)(2,1)S(1)}, bf16[144,384]{1,0:T(8,128)(2,1)S(1)}, u32[]{:S(2)}, u32[]{:S(2)}) collective-permute-start(bf16[144,384]{1,0:T(8,128)(2,1)S(1)} %fusion.22.refs_4_), channel_id=1, source_target_pairs={{0,24},{1,25},{2,26},{3,27},{4,28},{5,29},{6,30},{7,31},{8,16},{9,... | collective-permute-start | bytes 331784 | tf_op jit(solution)/shard_map/ppermute | solution.py:511
  (19 other events, 84.3 us)

commit v3 on v1

--- a/solution.py
+++ b/solution.py
@@ -782,8 +782,9 @@
     def kernel(where, ready, weight, x_ref, bias_ref, scale_ref, out_ref):
         ready()
         at = pl.ds(pl.multiple_of((where[2] ^ pl.program_id(0)) * cols, LANES), cols)
-        for tile in range(length // TILE):
-            here = pl.ds(tile * TILE, TILE)
+        size = min(512, length)
+        for tile in range(length // size):
+            here = pl.ds(tile * size, size)
             mixed = mxu(x_ref[here, :], weight[:, at], NN) + bias_ref[:, at]
             mixed = mixed.astype(jnp.bfloat16).astype(jnp.float32) * scale_ref[:, at]
             out_ref[here, :] = mixed.astype(jnp.bfloat16)
@@ -865,8 +866,9 @@
     def kernel(where, ready, weight, x_ref, bias_ref, hid_ref, slope_ref):
         ready()
         at = pl.ds(pl.multiple_of((where[2] ^ pl.program_id(0)) * cols, LANES), cols)
-        for tile in range(length // TILE):
-            here = pl.ds(tile * TILE, TILE)
+        size = min(512, length)
+        for tile in range(length // size):
+            here = pl.ds(tile * size, size)
             pre = mxu(x_ref[here, :], weight[:, at], NN) + bias_ref[:, at]
             share = 0.5 + 0.5 * lax.erf(pre * (1.0 / math.sqrt(2.0)))
             bell = jnp.exp(-0.5 * pre * pre) * (1.0 / math.sqrt(2.0 * math.pi))
@@ -1237,26 +1239,6 @@
     return total.astype(jnp.bfloat16)
 
 
-def add_leading(left, right):
-    _, chips, rows, cols = left.shape
-
-    def kernel(left_ref, right_ref, out_ref):
-        total = left_ref[...].astype(jnp.float32) + right_ref[...].astype(jnp.float32)
-        out_ref[...] = total.astype(jnp.bfloat16)
-
-    block = pl.BlockSpec((1, chips, rows, cols), lambda i: (i, 0, 0, 0))
-    return pl.pallas_call(
-        kernel,
-        grid=(2,),
-        in_specs=[block, block],
-        out_specs=block,
-        out_shape=shaped((2, chips, rows, cols), jnp.bfloat16),
-        compiler_params=params(60),
-        cost_estimate=cost(512 * chips * rows * cols),
-        name="add_leading",
-    )(left, right)
-
-
 class Reduction:
     def __init__(self, place, made):
         self.place = place
@@ -1265,7 +1247,7 @@
 
     def near(self):
         self.core = self.flying
-        leave = add_leading(self.made, self.core)
+        leave = add(self.made[:2], self.core[:2])
         self.flying = self.place.swap_grp(leave, 0)
         return leave
 

time: 443 us -> 434 us (0.980)
  Pallas kernels: 279 us -> 267 us
    pallas_call x4 -> x0, Pallas kernels: 11.8 us -> none  [add_leading(): pl.pallas_call(kernel, grid=(2,), in_specs=[block, block], out_specs=bloc...]
    convert_element_type x14 -> x18, other arithmetic: 27.3 us -> 33.2 us  [add(): return total.astype(jnp.bfloat16)]
  transfers between devices with their start and end apart: 58 -> 58, of which waited for: 24 -> 23; matrix products, arithmetic and copies ran while one was open for 4% -> 5% of each run, Pallas kernels for 51% -> 51%
where the time goes in v3:
time: 434 us; the launch traced here: 430 us
  Pallas kernels  267 us (62%)
  starting transfers between devices  58.6 us (14%)
  waiting for transfers between devices  52.2 us (12%)
  other arithmetic  43.1 us (10%)
  local copies, waits for them, and re-layouts  8.15 us (2%)
    pallas_call x4, Pallas kernels, weight_call(): pl.pallas_call(body, grid_spec=pltpu.PrefetchScalarGridSpec(num_scalar_pr...  76.3 us
    ppermute x58, starting transfers between devices, permute(): return lax.ppermute(array, AXES, pairs)  58.6 us
    ppermute x58, waiting for transfers between devices, permute(): return lax.ppermute(array, AXES, pairs)  52.2 us
    pallas_call x3, Pallas kernels, attention_backward(): pl.pallas_call(body, grid=(pairs,), in_specs=[pair(0), pair(1), pair(2),...  51.3 us
    pallas_call x3, Pallas kernels, attention_forward(): pl.pallas_call(body, grid=(pairs,), in_specs=[pair(0), pair(1), pair(2),...  44.4 us
    convert_element_type x18, other arithmetic, add(): return total.astype(jnp.bfloat16)  33.2 us
    pallas_call x2, Pallas kernels, weight_grad(): pl.pallas_call(functools.partial(weight_grad_kernel, rows=rows, groups=gr...  28 us
    pallas_call x2, Pallas kernels, attention_grads(): pl.pallas_call(functools.partial(attention_grads_kernel, rows=rows, group...  21.1 us
  transfers between devices with their start and end apart: 58, of which 23 were waited for; matrix products, arithmetic and copies ran while one was open for 5% of the time, Pallas kernels for 51%

profile of v3, /device:TPU:0, one launch (start us, length us, event | category | flops | bytes accessed | tf_op | source)
XLA Modules:
  0.0 430.1 jit_solution(5570784237757652354)
XLA Ops:
  0.6 3.1 collective-permute-start
  3.7 1.5 concatenate.29
  6.7 2.7 collective-permute-done
  10.4 2.5 collective-permute-start.2
  12.9 2.5 collective-permute-start.3
  16.4 4.3 %collective-permute-done.3 = bf16[2,16,128]{2,1,0:T(8,128)(2,1)S(1)} collective-permute-done((bf16[2,16,128]{2,1,0:T(8,128)(2,1)S(1)}, bf16[2,16,128]{2,1,0:T(8,128)(2,1)S(1)}, u32[]{:S(2)}, u32[]{:S(2)}) %collective-permute-start.3) | collective-permute-done | bytes 8224 | tf_op jit(solution)/shard_map/ppermute | solution.py:511
  22.9 2.7 collective-permute-start.4
  25.6 1.6 collective-permute-start.7
  27.2 1.5 collective-permute-start.8
  29.3 3.3 collective-permute-start.5
  32.6 2.0 collective-permute-done.5
  35.5 2.9 collective-permute-start.6
  40.4 2.0 vectors.1
  42.4 2.4 collective-permute-done.7.refs_1_
  49.0 5.4 %collective-permute-done.6 = bf16[2,128,1280]{2,1,0:T(8,128)(2,1)} collective-permute-done((bf16[2,128,1280]{2,1,0:T(8,128)(2,1)}, bf16[2,128,1280]{2,1,0:T(8,128)(2,1)}, u32[]{:S(2)}, u32[]{:S(2)}) %collective-permute-start.6) | collective-permute-done | bytes 655392 | tf_op jit(solution)/shard_map/ppermute | solution.py:511
  57.0 1.5 collective-permute-start.15
  61.7 12.7 %qkv.1 = (bf16[1024,3072]{1,0:T(8,128)(2,1)}, bf16[1024,3072]{1,0:T(8,128)(2,1)}) custom-call(s32[3]{0:T(128)} %pad_add_fusion.where, bf16[4,128,768]{2,1,0:T(8,128)(2,1)} %copy-done.7, bf16[4,128,768]{2,1,0:T(8,128)(2,1)} %collective-permute-done.7.refs_1_, bf16[4,128,768]{2,1,0:T(8,128)(2,1)} %collective-permute-done.8.refs_2_, ...), custom_call_target="tpu_custom_call" | custom-call | flops 12884901888 | tf_op jit(solution)/shard_map/qkv/pallas_call | solution.py:657
  74.5 2.5 collective-permute-start.17
  77.1 16.2 %attn_fwd.3 = (bf16[1024,1024]{1,0:T(8,128)(2,1)}, bf16[16,1024,1024]{2,1,0:T(8,128)(2,1)}, f32[1024,1024]{1,0:T(8,128)}) custom-call(bf16[1024,3072]{1,0:T(8,128)(2,1)} %get-tuple-element.161.q_ref.k_ref.v_ref.refs_0_.refs_1_.refs_2_, bf16[1024,3072]{1,0:T(8,128)(2,1)} %get-tuple-element.161.q_ref.k_ref.v_ref.refs_0_.refs_1_.refs_2_, ...), custom_call_target="tpu_custom_call" | custom-call | flops 12884901888 | tf_op jit(solution)/shard_map/attn_fwd/pallas_call | solution.py:391
  93.3 1.5 collective-permute-start.18
  95.4 16.2 %attn_fwd.4 = (bf16[1024,1024]{1,0:T(8,128)(2,1)}, bf16[16,1024,1024]{2,1,0:T(8,128)(2,1)}, f32[1024,1024]{1,0:T(8,128)}) custom-call(bf16[1024,3072]{1,0:T(8,128)(2,1)} %get-tuple-element.161.q_ref.k_ref.v_ref.refs_0_.refs_1_.refs_2_, ...), custom_call_target="tpu_custom_call", output_to_operand_aliasing={{0}: (5, {}), {1}: (6, {}), {2}: (7, {})} | custom-call | flops 12884901888 | tf_op jit(solution)/shard_map/attn_fwd/pallas_call | solution.py:391
  113.9 12.0 %attn_fwd.5 = (bf16[1024,1024]{1,0:T(8,128)(2,1)}, bf16[16,1024,1024]{2,1,0:T(8,128)(2,1)}, f32[1024,1024]{1,0:T(8,128)}) custom-call(bf16[1024,3072]{1,0:T(8,128)(2,1)} %get-tuple-element.161.q_ref.k_ref.v_ref.refs_0_.refs_1_.refs_2_, ...), custom_call_target="tpu_custom_call", output_to_operand_aliasing={{0}: (5, {}), {1}: (6, {}), {2}: (7, {})} | custom-call | flops 8589934592 | tf_op jit(solution)/shard_map/attn_fwd/pallas_call | solution.py:391
  127.1 9.6 %attn_out.1 = (f32[1024,1024]{1,0:T(8,128)}, f32[1024,128]{1,0:T(8,128)}, bf16[1024,1024]{1,0:T(8,128)(2,1)}, bf16[1024,1024]{1,0:T(8,128)(2,1)}) custom-call(s32[3]{0:T(128)} %pad_add_fusion.where, bf16[4,128,1280]{2,1,0:T(8,128)(2,1)} %copy-done.4, bf16[4,128,1280]{2,1,0:T(8,128)(2,1)} %collective-permute-done.15.refs_1_, ...), custom_call_target="tpu_custom_call" | custom-call | flops 4294967296 | tf_op jit(solution)/shard_map/attn_out/pallas_call | solution.py:657
  139.0 21.3 %feed_in.1 = (bf16[1024,4096]{1,0:T(8,128)(2,1)}, bf16[1024,4096]{1,0:T(8,128)(2,1)}, bf16[1024,4096]{1,0:T(8,128)(2,1)}) custom-call(s32[3]{0:T(128)} %pad_add_fusion.where, bf16[4,128,1280]{2,1,0:T(8,128)(2,1)} %copy-done.4, bf16[4,128,1280]{2,1,0:T(8,128)(2,1)} %collective-permute-done.15.refs_1_, bf16[4,128,1280]{2,1,0:T(8,128)(2,1)} %collective-permute-done.16.refs_2_, ...), custom_call_target="tpu_custom_call" | custom-call | flops 17179869184 | tf_op jit(solution)/shard_map/feed_in/pallas_call | solution.py:657
  160.5 2.6 collective-permute-done.29.refs_7_
  164.1 32.5 %feed_out.1 = (bf16[1024,1024]{1,0:T(8,128)(2,1)}, f32[1024,1024]{1,0:T(8,128)}, bf16[1024,1024]{1,0:T(8,128)(2,1)}, f32[8,1024]{1,0:T(8,128)}, bf16[1024,4096]{1,0:T(8,128)(2,1)}, /*index=5*/f32[1,4096]{1,0:T(1,128)}) custom-call(s32[3]{0:T(128)} %pad_add_fusion.where, bf16[4,512,256]{2,1,0:T(8,128)(2,1)} %copy-done.5, ...), custom_call_target="tpu_custom_call" | custom-call | flops 34359738368 | tf_op jit(solution)/shard_map/feed_out/pallas_call | solution.py:657
  196.7 13.9 %wgrad_out.1 = (bf16[4,4,512,256]{3,2,1,0:T(8,128)(2,1)}, bf16[4,4,512,256]{3,2,1,0:T(8,128)(2,1)}) custom-call(s32[3]{0:T(128)} %pad_add_fusion.where, bf16[1024,4096]{1,0:T(8,128)(2,1)} %get-tuple-element.170.refs_8_.left_ref, bf16[1024,1024]{1,0:T(8,128)(2,1)} %get-tuple-element.178.right_ref), custom_call_target="tpu_custom_call" | custom-call | flops 17179869184 | tf_op jit(solution)/shard_map/wgrad_out/pallas_call | solution.py:1216
  210.8 14.1 %wgrad_in.1 = (bf16[4,4,128,1024]{3,2,1,0:T(8,128)(2,1)}, bf16[4,4,128,1024]{3,2,1,0:T(8,128)(2,1)}) custom-call(s32[3]{0:T(128)} %pad_add_fusion.where, bf16[1024,1024]{1,0:T(8,128)(2,1)} %get-tuple-element.180.refs_8_.left_ref, bf16[1024,4096]{1,0:T(8,128)(2,1)} %get-tuple-element.184.right_ref.p_ref), custom_call_target="tpu_custom_call" | custom-call | flops 17179869184 | tf_op jit(solution)/shard_map/wgrad_in/pallas_call | solution.py:1216
  225.2 2.7 add_convert_fusion.1
  229.3 21.0 %feed_in_back.1 = (f32[1024,1024]{1,0:T(8,128)}, bf16[1024,1024]{1,0:T(8,128)(2,1)}, bf16[1024,1024]{1,0:T(8,128)(2,1)}, f32[8,1024]{1,0:T(8,128)}) custom-call(bf16[1024,4096]{1,0:T(8,128)(2,1)} %get-tuple-element.184.right_ref.p_ref, bf16[1024,4096]{1,0:T(8,128)(2,1)} %get-tuple-element.185.w_ref, f32[1024,1024]{1,0:T(8,128)} %get-tuple-element.186.g_ref, ...), custom_call_target="tpu_custom_call" | custom-call | flops 21474836480 | tf_op jit(solution)/shard_map/feed_in_back/pallas_call | solution.py:679
  250.3 4.7 %add_convert_fusion = bf16[2,4,128,1024]{3,2,1,0:T(8,128)(2,1)} fusion(bf16[4,4,128,1024]{3,2,1,0:T(8,128)(2,1)} %collective-permute-done.31, bf16[4,4,128,1024]{3,2,1,0:T(8,128)(2,1)} %get-tuple-element.181), kind=kLoop, calls=%fused_computation | loop fusion | flops 4194304 | bytes 6291456 | tf_op jit(solution)/shard_map/convert_element_type | solution.py:1239
  255.7 23.7 %attn_bwd.3 = (bf16[3,1024,512]{2,1,0:T(8,128)(2,1)}, f32[2,512]{1,0:T(2,128)}) custom-call(bf16[1024,3072]{1,0:T(8,128)(2,1)} %get-tuple-element.161.q_ref.k_ref.v_ref.refs_0_.refs_1_.refs_2_, bf16[1024,3072]{1,0:T(8,128)(2,1)} %get-tuple-element.161.q_ref.k_ref.v_ref.refs_0_.refs_1_.refs_2_, ...), custom_call_target="tpu_custom_call" | custom-call | flops 34359738368 | tf_op jit(solution)/shard_map/attn_bwd/pallas_call | solution.py:470
  279.4 1.9 collective-permute-done.33
  281.3 3.5 fusion.4
  284.8 2.2 fusion.3
  287.6 12.4 %wgrad_a.1 = (bf16[4,4,128,640]{3,2,1,0:T(8,128)(2,1)}, bf16[4,4,128,640]{3,2,1,0:T(8,128)(2,1)}) custom-call(s32[3]{0:T(128)} %pad_add_fusion.where, bf16[2,512,1024]{2,1,0:T(8,128)(2,1)} %copy-done.1, bf16[3,1024,512]{2,1,0:T(8,128)(2,1)} %get-tuple-element.196.refs_1_.refs_0_, bf16[1024,1024]{1,0:T(8,128)(2,1)} %get-tuple-element.164.refs_8_.refs_3_.refs_2_, ...), custom_call_target="tpu_custom_call" | custom-call | flops 10737418240 | tf_op jit(solution)/shard_map/wgrad_a/pallas_call | solution.py:1174
  299.9 1.6 collective-permute-start.36
  301.9 2.4 fusion.1
  305.0 13.7 %attn_bwd.4 = (bf16[3,1024,512]{2,1,0:T(8,128)(2,1)}, f32[2,512]{1,0:T(2,128)}) custom-call(bf16[1024,3072]{1,0:T(8,128)(2,1)} %get-tuple-element.161.q_ref.k_ref.v_ref.refs_0_.refs_1_.refs_2_, bf16[1024,3072]{1,0:T(8,128)(2,1)} %get-tuple-element.161.q_ref.k_ref.v_ref.refs_0_.refs_1_.refs_2_, ...), custom_call_target="tpu_custom_call" | custom-call | flops 17179869184 | tf_op jit(solution)/shard_map/attn_bwd/pallas_call | solution.py:470
  319.1 3.3 add_convert_fusion.2
  322.4 3.1 fusion
  325.6 1.5 collective-permute-start.40
  329.0 13.9 %attn_bwd.5 = (bf16[3,1024,512]{2,1,0:T(8,128)(2,1)}, f32[2,512]{1,0:T(2,128)}) custom-call(bf16[1024,3072]{1,0:T(8,128)(2,1)} %get-tuple-element.161.q_ref.k_ref.v_ref.refs_0_.refs_1_.refs_2_, bf16[1024,3072]{1,0:T(8,128)(2,1)} %get-tuple-element.161.q_ref.k_ref.v_ref.refs_0_.refs_1_.refs_2_, ...), custom_call_target="tpu_custom_call", output_to_operand_aliasing={{0}: (7, {}), {1}: (8, {})} | custom-call | flops 17179869184 | tf_op jit(solution)/shard_map/attn_bwd/pallas_call | solution.py:470
  342.9 1.9 collective-permute-done.38
  344.8 2.1 collective-permute-done.39
  346.9 1.9 fusion.6
  350.2 1.5 collective-permute-start.41
  351.8 8.8 %wgrad_b.1 = (bf16[4,4,144,384]{3,2,1,0:T(8,128)(2,1)}, bf16[4,4,144,384]{3,2,1,0:T(8,128)(2,1)}) custom-call(s32[3]{0:T(128)} %pad_add_fusion.where, bf16[2,512,1024]{2,1,0:T(8,128)(2,1)} %copy-done.1, bf16[3,1024,512]{2,1,0:T(8,128)(2,1)} %get-tuple-element.223.refs_1_, f32[2,512]{1,0:T(2,128)} %get-tuple-element.197.refs_2_, ...), custom_call_target="tpu_custom_call" | custom-call | flops 6442450944 | tf_op jit(solution)/shard_map/wgrad_b/pallas_call | solution.py:1174
  360.6 2.1 fusion.2
  364.8 8.2 %qkv_back.2.refs_3_ = f32[1024,1024]{1,0:T(8,128)} custom-call(bf16[1024,3072]{1,0:T(8,128)(2,1)} %get-tuple-element.176.w_ref, bf16[3,1024,512]{2,1,0:T(8,128)(2,1)} %get-tuple-element.196.refs_1_.refs_0_, bf16[3,1024,512]{2,1,0:T(8,128)(2,1)} %get-tuple-element.223.refs_1_, f32[1024,1024]{1,0:T(8,128)} %get-tuple-element.228.refs_2_), custom_call_target="tpu_custom_call" | custom-call | flops 6442450944 | tf_op jit(solution)/shard_map/qkv_back/pallas_call | solution.py:1015
  373.7 2.6 add_convert_fusion.5
  378.9 8.2 %qkv_back.3 = f32[1024,1024]{1,0:T(8,128)} custom-call(bf16[1024,3072]{1,0:T(8,128)(2,1)} %get-tuple-element.176.w_ref, bf16[3,1024,512]{2,1,0:T(8,128)(2,1)} %get-tuple-element.196.refs_1_.refs_0_, bf16[3,1024,512]{2,1,0:T(8,128)(2,1)} %get-tuple-element.223.refs_1_, f32[1024,1024]{1,0:T(8,128)} %get-tuple-element.228.refs_2_, ...), custom_call_target="tpu_custom_call", output_to_operand_aliasing={{}: (4, {})} | custom-call | flops 6442450944 | tf_op jit(solution)/shard_map/qkv_back/pallas_call | solution.py:1015
  387.1 2.4 collective-permute-done.46
  392.9 6.2 %collective-permute-done.49.refs_1_ = bf16[128,640]{1,0:T(8,128)(2,1)S(1)} collective-permute-done((bf16[128,640]{1,0:T(8,128)(2,1)S(1)}, bf16[128,640]{1,0:T(8,128)(2,1)S(1)}, u32[]{:S(2)}, u32[]{:S(2)}) %collective-permute-start.49) | collective-permute-done | bytes 163872 | tf_op jit(solution)/shard_map/ppermute | solution.py:511
  399.1 1.9 collective-permute-done.48
  403.8 1.5 collective-permute-start.51
  406.1 2.2 collective-permute-start.53
  408.3 1.7 collective-permute-start.50
  410.0 1.7 collective-permute-done.51
  411.7 4.2 collective-permute-done.52
  416.4 1.7 collective-permute-start.56
  419.6 2.8 order_feed_forward.1
  422.4 3.1 collective-permute-done.50
  426.7 2.1 order_attention.1
  (166 shorter events, 51.5 us)
Async XLA Ops:
  0.6 8.7 %collective-permute-start = (bf16[128,768]{1,0:T(8,128)(2,1)}, bf16[128,768]{1,0:T(8,128)(2,1)S(1)}, u32[]{:S(2)}, u32[]{:S(2)}) collective-permute-start(bf16[128,768]{1,0:T(8,128)(2,1)} %param.21), channel_id=1, source_target_pairs={{0,2},{1,5},{2,0},{3,7},{4,6},{5,1},{6,4},{7,3},{8,10},{9,13},{10,... | collective-permute-start | bytes 589832 | tf_op jit(solution)/shard_map/ppermute | solution.py:511
  5.2 1.4 collective-permute-start.1
  9.3 36.0 %copy-start = (bf16[1,1024,1024]{2,1,0:T(8,128)(2,1)S(1)}, bf16[1,1024,1024]{2,1,0:T(8,128)(2,1)}, u32[]{:S(2)}) copy-start(bf16[1,1024,1024]{2,1,0:T(8,128)(2,1)} %param.17) | copy-start | bytes 6291460
  10.4 11.5 %collective-permute-start.2 = (bf16[2,128,768]{2,1,0:T(8,128)(2,1)S(1)}, bf16[2,128,768]{2,1,0:T(8,128)(2,1)S(1)}, u32[]{:S(2)}, u32[]{:S(2)}) collective-permute-start(bf16[2,128,768]{2,1,0:T(8,128)(2,1)S(1)} %pad_maximum_fusion.8), channel_id=1, source_target_pairs={{0,4},{1,3},{2,6},{3,1},{4,0},{5,7},{6,2},{7,5},{8,12},{9,11},{10,... | collective-permute-start | bytes 1179656 | tf_op jit(solution)/shard_map/ppermute | solution.py:511
  12.9 7.8 %collective-permute-start.3 = (bf16[2,16,128]{2,1,0:T(8,128)(2,1)S(1)}, bf16[2,16,128]{2,1,0:T(8,128)(2,1)S(1)}, u32[]{:S(2)}, u32[]{:S(2)}) collective-permute-start(bf16[2,16,128]{2,1,0:T(8,128)(2,1)S(1)} %get-tuple-element.275), channel_id=1, source_target_pairs={{0,2},{1,5},{2,0},{3,7},{4,6},{5,1},{6,4},{7,3},{8,10},{9,13},{10,... | collective-permute-start | bytes 24584 | tf_op jit(solution)/shard_map/ppermute | solution.py:511
  22.9 24.2 %copy-start.7 = (bf16[4,128,768]{2,1,0:T(8,128)(2,1)}, bf16[4,128,768]{2,1,0:T(8,128)(2,1)S(1)}, u32[]{:S(2)}) copy-start(bf16[4,128,768]{2,1,0:T(8,128)(2,1)S(1)} %pad_maximum_fusion.3.refs_0_) | copy-start | bytes 2359300
  22.9 11.7 %collective-permute-start.4 = (bf16[128,1280]{1,0:T(8,128)(2,1)S(1)}, bf16[128,1280]{1,0:T(8,128)(2,1)S(1)}, u32[]{:S(2)}, u32[]{:S(2)}) collective-permute-start(bf16[128,1280]{1,0:T(8,128)(2,1)S(1)} %pad_maximum_fusion.9), channel_id=1, source_target_pairs={{0,2},{1,5},{2,0},{3,7},{4,6},{5,1},{6,4},{7,3},{8,10},{9,13},{10,... | collective-permute-start | bytes 983048 | tf_op jit(solution)/shard_map/ppermute | solution.py:511
  25.6 19.2 %collective-permute-start.7 = (bf16[4,128,768]{2,1,0:T(8,128)(2,1)S(1)}, bf16[4,128,768]{2,1,0:T(8,128)(2,1)}, u32[]{:S(2)}, u32[]{:S(2)}) collective-permute-start(bf16[4,128,768]{2,1,0:T(8,128)(2,1)S(1)} %pad_maximum_fusion.3.refs_0_), channel_id=1, source_target_pairs={{0,8},{1,17},{2,10},{3,19},{4,12},{5,21},{6,14},{7,23},{8,0},{9,25... | collective-permute-start | bytes 2359304 | tf_op jit(solution)/shard_map/ppermute | solution.py:511
  27.2 17.6 %collective-permute-start.8 = (bf16[4,128,768]{2,1,0:T(8,128)(2,1)S(1)}, bf16[4,128,768]{2,1,0:T(8,128)(2,1)}, u32[]{:S(2)}, u32[]{:S(2)}) collective-permute-start(bf16[4,128,768]{2,1,0:T(8,128)(2,1)S(1)} %pad_maximum_fusion.3.refs_0_), channel_id=1, source_target_pairs={{0,16},{1,9},{2,18},{3,11},{4,20},{5,13},{6,22},{7,15},{8,24},{9,1... | collective-permute-start | bytes 2359304 | tf_op jit(solution)/shard_map/ppermute | solution.py:511
  29.3 5.3 %collective-permute-start.5 = (bf16[2,2,16,128]{3,2,1,0:T(8,128)(2,1)}, bf16[2,2,16,128]{3,2,1,0:T(8,128)(2,1)}, u32[]{:S(2)}, u32[]{:S(2)}) collective-permute-start(bf16[2,2,16,128]{3,2,1,0:T(8,128)(2,1)} %pad_maximum_fusion.13), channel_id=1, source_target_pairs={{0,4},{1,3},{2,6},{3,1},{4,0},{5,7},{6,2},{7,5},{8,12},{9,11},{10,... | collective-permute-start | bytes 49160 | tf_op jit(solution)/shard_map/ppermute | solution.py:511
  35.5 18.8 %collective-permute-start.6 = (bf16[2,128,1280]{2,1,0:T(8,128)(2,1)}, bf16[2,128,1280]{2,1,0:T(8,128)(2,1)}, u32[]{:S(2)}, u32[]{:S(2)}) collective-permute-start(bf16[2,128,1280]{2,1,0:T(8,128)(2,1)} %pad_maximum_fusion.4), channel_id=1, source_target_pairs={{0,4},{1,3},{2,6},{3,1},{4,0},{5,7},{6,2},{7,5},{8,12},{9,11},{10,... | collective-permute-start | bytes 1966088 | tf_op jit(solution)/shard_map/ppermute | solution.py:511
  44.8 12.2 %collective-permute-start.9 = (bf16[4,128,768]{2,1,0:T(8,128)(2,1)}, bf16[4,128,768]{2,1,0:T(8,128)(2,1)S(1)}, u32[]{:S(2)}, u32[]{:S(2)}) collective-permute-start(bf16[4,128,768]{2,1,0:T(8,128)(2,1)} %collective-permute-done.7.refs_1_), channel_id=1, source_target_pairs={{0,16},{1,9},{2,18},{3,11},{4,20},{5,13},{6,22},{7,15},{8,24},{9,1... | collective-permute-start | bytes 2359304 | tf_op jit(solution)/shard_map/ppermute | solution.py:511
  45.3 13.2 %collective-permute-start.10 = (bf16[4,128,768]{2,1,0:T(8,128)(2,1)S(1)}, bf16[4,128,768]{2,1,0:T(8,128)(2,1)S(1)}, u32[]{:S(2)}, u32[]{:S(2)}) collective-permute-start(bf16[4,128,768]{2,1,0:T(8,128)(2,1)S(1)} %pad_maximum_fusion.3.refs_0_), channel_id=1, source_target_pairs={{0,1},{1,0},{2,3},{3,2},{4,5},{5,4},{6,7},{7,6},{8,9},{9,8},{10,11... | collective-permute-start | bytes 2359304 | tf_op jit(solution)/shard_map/ppermute | solution.py:511
  48.5 10.6 %collective-permute-start.11 = (bf16[4,128,768]{2,1,0:T(8,128)(2,1)}, bf16[4,128,768]{2,1,0:T(8,128)(2,1)S(1)}, u32[]{:S(2)}, u32[]{:S(2)}) collective-permute-start(bf16[4,128,768]{2,1,0:T(8,128)(2,1)} %collective-permute-done.7.refs_1_), channel_id=1, source_target_pairs={{0,1},{1,0},{2,3},{3,2},{4,5},{5,4},{6,7},{7,6},{8,9},{9,8},{10,11... | collective-permute-start | bytes 2359304 | tf_op jit(solution)/shard_map/ppermute | solution.py:511
  49.0 11.0 %collective-permute-start.12 = (bf16[4,128,768]{2,1,0:T(8,128)(2,1)}, bf16[4,128,768]{2,1,0:T(8,128)(2,1)S(1)}, u32[]{:S(2)}, u32[]{:S(2)}) collective-permute-start(bf16[4,128,768]{2,1,0:T(8,128)(2,1)} %collective-permute-done.8.refs_2_), channel_id=1, source_target_pairs={{0,1},{1,0},{2,3},{3,2},{4,5},{5,4},{6,7},{7,6},{8,9},{9,8},{10,11... | collective-permute-start | bytes 2359304 | tf_op jit(solution)/shard_map/ppermute | solution.py:511
  55.6 21.5 %copy-start.4 = (bf16[4,128,1280]{2,1,0:T(8,128)(2,1)}, bf16[4,128,1280]{2,1,0:T(8,128)(2,1)S(1)}, u32[]{:S(2)}) copy-start(bf16[4,128,1280]{2,1,0:T(8,128)(2,1)S(1)} %pad_maximum_fusion.refs_0_) | copy-start | bytes 3932164
  57.0 2.9 collective-permute-start.13
  57.0 36.3 %collective-permute-start.15 = (bf16[4,128,1280]{2,1,0:T(8,128)(2,1)S(1)}, bf16[4,128,1280]{2,1,0:T(8,128)(2,1)}, u32[]{:S(2)}, u32[]{:S(2)}) collective-permute-start(bf16[4,128,1280]{2,1,0:T(8,128)(2,1)S(1)} %pad_maximum_fusion.refs_0_), channel_id=1, source_target_pairs={{0,8},{1,17},{2,10},{3,19},{4,12},{5,21},{6,14},{7,23},{8,0},{9,25... | collective-permute-start | bytes 3932168 | tf_op jit(solution)/shard_map/ppermute | solution.py:511
  58.5 34.8 %collective-permute-start.16 = (bf16[4,128,1280]{2,1,0:T(8,128)(2,1)S(1)}, bf16[4,128,1280]{2,1,0:T(8,128)(2,1)}, u32[]{:S(2)}, u32[]{:S(2)}) collective-permute-start(bf16[4,128,1280]{2,1,0:T(8,128)(2,1)S(1)} %pad_maximum_fusion.refs_0_), channel_id=1, source_target_pairs={{0,16},{1,9},{2,18},{3,11},{4,20},{5,13},{6,22},{7,15},{8,24},{9,1... | collective-permute-start | bytes 3932168 | tf_op jit(solution)/shard_map/ppermute | solution.py:511
  59.0 15.4 %collective-permute-start.14 = (bf16[512,256]{1,0:T(8,128)(2,1)S(1)}, bf16[512,256]{1,0:T(8,128)(2,1)S(1)}, u32[]{:S(2)}, u32[]{:S(2)}) collective-permute-start(bf16[512,256]{1,0:T(8,128)(2,1)S(1)} %copy-done.6), channel_id=1, source_target_pairs={{0,2},{1,5},{2,0},{3,7},{4,6},{5,1},{6,4},{7,3},{8,10},{9,13},{10,... | collective-permute-start | bytes 786440 | tf_op jit(solution)/shard_map/ppermute | solution.py:511
  74.5 18.7 %collective-permute-start.17 = (bf16[2,512,256]{2,1,0:T(8,128)(2,1)S(1)}, bf16[2,512,256]{2,1,0:T(8,128)(2,1)S(1)}, u32[]{:S(2)}, u32[]{:S(2)}) collective-permute-start(bf16[2,512,256]{2,1,0:T(8,128)(2,1)S(1)} %pad_maximum_fusion.5), channel_id=1, source_target_pairs={{0,4},{1,3},{2,6},{3,1},{4,0},{5,7},{6,2},{7,5},{8,12},{9,11},{10,... | collective-permute-start | bytes 1572872 | tf_op jit(solution)/shard_map/ppermute | solution.py:511
  77.0 35.5 %collective-permute-start.19 = (bf16[4,128,1280]{2,1,0:T(8,128)(2,1)S(1)}, bf16[4,128,1280]{2,1,0:T(8,128)(2,1)}, u32[]{:S(2)}, u32[]{:S(2)}) collective-permute-start(bf16[4,128,1280]{2,1,0:T(8,128)(2,1)S(1)} %pad_maximum_fusion.refs_0_), channel_id=1, source_target_pairs={{0,1},{1,0},{2,3},{3,2},{4,5},{5,4},{6,7},{7,6},{8,9},{9,8},{10,11... | collective-permute-start | bytes 3932168 | tf_op jit(solution)/shard_map/ppermute | solution.py:511
  93.3 18.4 %collective-permute-start.18 = (bf16[4,128,1280]{2,1,0:T(8,128)(2,1)}, bf16[4,128,1280]{2,1,0:T(8,128)(2,1)}, u32[]{:S(2)}, u32[]{:S(2)}) collective-permute-start(bf16[4,128,1280]{2,1,0:T(8,128)(2,1)} %collective-permute-done.15.refs_1_), channel_id=1, source_target_pairs={{0,16},{1,9},{2,18},{3,11},{4,20},{5,13},{6,22},{7,15},{8,24},{9,1... | collective-permute-start | bytes 3932168 | tf_op jit(solution)/shard_map/ppermute | solution.py:511
  94.8 31.2 %collective-permute-start.20 = (bf16[4,128,1280]{2,1,0:T(8,128)(2,1)}, bf16[4,128,1280]{2,1,0:T(8,128)(2,1)}, u32[]{:S(2)}, u32[]{:S(2)}) collective-permute-start(bf16[4,128,1280]{2,1,0:T(8,128)(2,1)} %collective-permute-done.15.refs_1_), channel_id=1, source_target_pairs={{0,1},{1,0},{2,3},{3,2},{4,5},{5,4},{6,7},{7,6},{8,9},{9,8},{10,11... | collective-permute-start | bytes 3932168 | tf_op jit(solution)/shard_map/ppermute | solution.py:511
  94.9 31.1 %copy-start.5 = (bf16[4,512,256]{2,1,0:T(8,128)(2,1)}, bf16[4,512,256]{2,1,0:T(8,128)(2,1)S(1)}, u32[]{:S(2)}) copy-start(bf16[4,512,256]{2,1,0:T(8,128)(2,1)S(1)} %pad_maximum_fusion.1.refs_0_) | copy-start | bytes 3145732
  94.9 31.2 %collective-permute-start.21 = (bf16[4,128,1280]{2,1,0:T(8,128)(2,1)}, bf16[4,128,1280]{2,1,0:T(8,128)(2,1)S(1)}, u32[]{:S(2)}, u32[]{:S(2)}) collective-permute-start(bf16[4,128,1280]{2,1,0:T(8,128)(2,1)} %collective-permute-done.16.refs_2_), channel_id=1, source_target_pairs={{0,1},{1,0},{2,3},{3,2},{4,5},{5,4},{6,7},{7,6},{8,9},{9,8},{10,11... | collective-permute-start | bytes 3932168 | tf_op jit(solution)/shard_map/ppermute | solution.py:511
  111.6 14.4 %collective-permute-start.22 = (bf16[4,128,1280]{2,1,0:T(8,128)(2,1)}, bf16[4,128,1280]{2,1,0:T(8,128)(2,1)}, u32[]{:S(2)}, u32[]{:S(2)}) collective-permute-start(bf16[4,128,1280]{2,1,0:T(8,128)(2,1)} %collective-permute-done.18.refs_3_), channel_id=1, source_target_pairs={{0,1},{1,0},{2,3},{3,2},{4,5},{5,4},{6,7},{7,6},{8,9},{9,8},{10,11... | collective-permute-start | bytes 3932168 | tf_op jit(solution)/shard_map/ppermute | solution.py:511
  112.0 26.1 %collective-permute-start.23 = (bf16[4,512,256]{2,1,0:T(8,128)(2,1)S(1)}, bf16[4,512,256]{2,1,0:T(8,128)(2,1)}, u32[]{:S(2)}, u32[]{:S(2)}) collective-permute-start(bf16[4,512,256]{2,1,0:T(8,128)(2,1)S(1)} %pad_maximum_fusion.1.refs_0_), channel_id=1, source_target_pairs={{0,8},{1,17},{2,10},{3,19},{4,12},{5,21},{6,14},{7,23},{8,0},{9,25... | collective-permute-start | bytes 3145736 | tf_op jit(solution)/shard_map/ppermute | solution.py:511
  112.6 25.5 %collective-permute-start.24 = (bf16[4,512,256]{2,1,0:T(8,128)(2,1)S(1)}, bf16[4,512,256]{2,1,0:T(8,128)(2,1)S(1)}, u32[]{:S(2)}, u32[]{:S(2)}) collective-permute-start(bf16[4,512,256]{2,1,0:T(8,128)(2,1)S(1)} %pad_maximum_fusion.1.refs_0_), channel_id=1, source_target_pairs={{0,16},{1,9},{2,18},{3,11},{4,20},{5,13},{6,22},{7,15},{8,24},{9,1... | collective-permute-start | bytes 3145736 | tf_op jit(solution)/shard_map/ppermute | solution.py:511
  125.9 34.5 %collective-permute-start.26 = (bf16[4,512,256]{2,1,0:T(8,128)(2,1)S(1)}, bf16[4,512,256]{2,1,0:T(8,128)(2,1)}, u32[]{:S(2)}, u32[]{:S(2)}) collective-permute-start(bf16[4,512,256]{2,1,0:T(8,128)(2,1)S(1)} %pad_maximum_fusion.1.refs_0_), channel_id=1, source_target_pairs={{0,1},{1,0},{2,3},{3,2},{4,5},{5,4},{6,7},{7,6},{8,9},{9,8},{10,11... | collective-permute-start | bytes 3145736 | tf_op jit(solution)/shard_map/ppermute | solution.py:511
  138.1 22.3 %copy-start.14 = (bf16[4,512,256]{2,1,0:T(8,128)(2,1)}, bf16[4,512,256]{2,1,0:T(8,128)(2,1)S(1)}, u32[]{:S(2)}) copy-start(bf16[4,512,256]{2,1,0:T(8,128)(2,1)S(1)} %collective-permute-done.24.refs_2_) | copy-start | bytes 3145732
  138.1 22.3 %collective-permute-start.25 = (bf16[4,512,256]{2,1,0:T(8,128)(2,1)}, bf16[4,512,256]{2,1,0:T(8,128)(2,1)S(1)}, u32[]{:S(2)}, u32[]{:S(2)}) collective-permute-start(bf16[4,512,256]{2,1,0:T(8,128)(2,1)} %collective-permute-done.23.refs_1_), channel_id=1, source_target_pairs={{0,16},{1,9},{2,18},{3,11},{4,20},{5,13},{6,22},{7,15},{8,24},{9,1... | collective-permute-start | bytes 3145736 | tf_op jit(solution)/shard_map/ppermute | solution.py:511
  138.5 22.0 %collective-permute-start.27 = (bf16[4,512,256]{2,1,0:T(8,128)(2,1)}, bf16[4,512,256]{2,1,0:T(8,128)(2,1)}, u32[]{:S(2)}, u32[]{:S(2)}) collective-permute-start(bf16[4,512,256]{2,1,0:T(8,128)(2,1)} %collective-permute-done.23.refs_1_), channel_id=1, source_target_pairs={{0,1},{1,0},{2,3},{3,2},{4,5},{5,4},{6,7},{7,6},{8,9},{9,8},{10,11... | collective-permute-start | bytes 3145736 | tf_op jit(solution)/shard_map/ppermute | solution.py:511
  138.5 22.0 %collective-permute-start.28 = (bf16[4,512,256]{2,1,0:T(8,128)(2,1)S(1)}, bf16[4,512,256]{2,1,0:T(8,128)(2,1)}, u32[]{:S(2)}, u32[]{:S(2)}) collective-permute-start(bf16[4,512,256]{2,1,0:T(8,128)(2,1)S(1)} %collective-permute-done.24.refs_2_), channel_id=1, source_target_pairs={{0,1},{1,0},{2,3},{3,2},{4,5},{5,4},{6,7},{7,6},{8,9},{9,8},{10,11... | collective-permute-start | bytes 3145736 | tf_op jit(solution)/shard_map/ppermute | solution.py:511
  160.4 2.7 collective-permute-start.29
  210.6 14.6 %collective-permute-start.30 = (bf16[4,4,512,256]{3,2,1,0:T(8,128)(2,1)}, bf16[4,4,512,256]{3,2,1,0:T(8,128)(2,1)}, u32[]{:S(2)}, u32[]{:S(2)}) collective-permute-start(bf16[4,4,512,256]{3,2,1,0:T(8,128)(2,1)} %get-tuple-element.182), channel_id=1, source_target_pairs={{0,1},{1,0},{2,3},{3,2},{4,5},{5,4},{6,7},{7,6},{8,9},{9,8},{10,11... | collective-permute-start | bytes 12582920 | tf_op jit(solution)/shard_map/ppermute | solution.py:511
  224.9 25.4 %collective-permute-start.31 = (bf16[4,4,128,1024]{3,2,1,0:T(8,128)(2,1)}, bf16[4,4,128,1024]{3,2,1,0:T(8,128)(2,1)}, u32[]{:S(2)}, u32[]{:S(2)}) collective-permute-start(bf16[4,4,128,1024]{3,2,1,0:T(8,128)(2,1)} %get-tuple-element.191), channel_id=1, source_target_pairs={{0,1},{1,0},{2,3},{3,2},{4,5},{5,4},{6,7},{7,6},{8,9},{9,8},{10,11... | collective-permute-start | bytes 12582920 | tf_op jit(solution)/shard_map/ppermute | solution.py:511
  227.9 53.4 %collective-permute-start.32 = (bf16[2,4,512,256]{3,2,1,0:T(8,128)(2,1)S(1)}, bf16[2,4,512,256]{3,2,1,0:T(8,128)(2,1)}, u32[]{:S(2)}, u32[]{:S(2)}) collective-permute-start(bf16[2,4,512,256]{3,2,1,0:T(8,128)(2,1)S(1)} %add_convert_fusion.1), channel_id=1, source_target_pairs={{0,8},{1,17},{2,10},{3,19},{4,12},{5,21},{6,14},{7,23},{8,0},{9,25... | collective-permute-start | bytes 6291464 | tf_op jit(solution)/shard_map/ppermute | solution.py:511
  255.0 26.4 %collective-permute-start.33 = (bf16[2,4,128,1024]{3,2,1,0:T(8,128)(2,1)}, bf16[2,4,128,1024]{3,2,1,0:T(8,128)(2,1)}, u32[]{:S(2)}, u32[]{:S(2)}) collective-permute-start(bf16[2,4,128,1024]{3,2,1,0:T(8,128)(2,1)} %add_convert_fusion), channel_id=1, source_target_pairs={{0,8},{1,17},{2,10},{3,19},{4,12},{5,21},{6,14},{7,23},{8,0},{9,25... | collective-permute-start | bytes 6291464 | tf_op jit(solution)/shard_map/ppermute | solution.py:511
  287.0 14.9 %collective-permute-start.34 = (bf16[4,512,256]{2,1,0:T(8,128)(2,1)S(1)}, bf16[4,512,256]{2,1,0:T(8,128)(2,1)S(1)}, u32[]{:S(2)}, u32[]{:S(2)}) collective-permute-start(bf16[4,512,256]{2,1,0:T(8,128)(2,1)S(1)} %fusion.3), channel_id=1, source_target_pairs={{0,16},{1,9},{2,18},{3,11},{4,20},{5,13},{6,22},{7,15},{8,24},{9,1... | collective-permute-start | bytes 3145736 | tf_op jit(solution)/shard_map/ppermute | solution.py:511
  299.9 19.2 %collective-permute-start.37 = (bf16[4,4,128,640]{3,2,1,0:T(8,128)(2,1)}, bf16[4,4,128,640]{3,2,1,0:T(8,128)(2,1)}, u32[]{:S(2)}, u32[]{:S(2)}) collective-permute-start(bf16[4,4,128,640]{3,2,1,0:T(8,128)(2,1)} %get-tuple-element.205), channel_id=1, source_target_pairs={{0,1},{1,0},{2,3},{3,2},{4,5},{5,4},{6,7},{7,6},{8,9},{9,8},{10,11... | collective-permute-start | bytes 7864328 | tf_op jit(solution)/shard_map/ppermute | solution.py:511
  299.9 18.7 %collective-permute-start.36 = (bf16[4,128,1024]{2,1,0:T(8,128)(2,1)}, bf16[4,128,1024]{2,1,0:T(8,128)(2,1)}, u32[]{:S(2)}, u32[]{:S(2)}) collective-permute-start(bf16[4,128,1024]{2,1,0:T(8,128)(2,1)} %fusion.4), channel_id=1, source_target_pairs={{0,16},{1,9},{2,18},{3,11},{4,20},{5,13},{6,22},{7,15},{8,24},{9,1... | collective-permute-start | bytes 3145736 | tf_op jit(solution)/shard_map/ppermute | solution.py:511
  304.4 14.7 %collective-permute-start.35 = (bf16[2,512,256]{2,1,0:T(8,128)(2,1)S(1)}, bf16[2,512,256]{2,1,0:T(8,128)(2,1)S(1)}, u32[]{:S(2)}, u32[]{:S(2)}) collective-permute-start(bf16[2,512,256]{2,1,0:T(8,128)(2,1)S(1)} %pad_maximum_fusion.6), channel_id=1, source_target_pairs={{0,2},{1,5},{2,0},{3,7},{4,6},{5,1},{6,4},{7,3},{8,10},{9,13},{10,... | collective-permute-start | bytes 1572872 | tf_op jit(solution)/shard_map/ppermute | solution.py:511
  325.6 21.3 %collective-permute-start.40 = (bf16[2,4,128,640]{3,2,1,0:T(8,128)(2,1)}, bf16[2,4,128,640]{3,2,1,0:T(8,128)(2,1)}, u32[]{:S(2)}, u32[]{:S(2)}) collective-permute-start(bf16[2,4,128,640]{3,2,1,0:T(8,128)(2,1)} %add_convert_fusion.2), channel_id=1, source_target_pairs={{0,8},{1,17},{2,10},{3,19},{4,12},{5,21},{6,14},{7,23},{8,0},{9,25... | collective-permute-start | bytes 3932168 | tf_op jit(solution)/shard_map/ppermute | solution.py:511
  327.1 19.8 %collective-permute-start.39 = (bf16[2,128,1024]{2,1,0:T(8,128)(2,1)S(1)}, bf16[2,128,1024]{2,1,0:T(8,128)(2,1)S(1)}, u32[]{:S(2)}, u32[]{:S(2)}) collective-permute-start(bf16[2,128,1024]{2,1,0:T(8,128)(2,1)S(1)} %pad_maximum_fusion.7), channel_id=1, source_target_pairs={{0,2},{1,5},{2,0},{3,7},{4,6},{5,1},{6,4},{7,3},{8,10},{9,13},{10,... | collective-permute-start | bytes 1572872 | tf_op jit(solution)/shard_map/ppermute | solution.py:511
  328.3 16.5 %collective-permute-start.38 = (bf16[512,256]{1,0:T(8,128)(2,1)}, bf16[512,256]{1,0:T(8,128)(2,1)S(1)}, u32[]{:S(2)}, u32[]{:S(2)}) collective-permute-start(bf16[512,256]{1,0:T(8,128)(2,1)} %fusion.11), channel_id=1, source_target_pairs={{0,4},{1,3},{2,6},{3,1},{4,0},{5,7},{6,2},{7,5},{8,12},{9,11},{10,... | collective-permute-start | bytes 786440 | tf_op jit(solution)/shard_map/ppermute | solution.py:511
  348.9 11.7 %collective-permute-start.42 = (bf16[4,128,640]{2,1,0:T(8,128)(2,1)S(1)}, bf16[4,128,640]{2,1,0:T(8,128)(2,1)}, u32[]{:S(2)}, u32[]{:S(2)}) collective-permute-start(bf16[4,128,640]{2,1,0:T(8,128)(2,1)S(1)} %fusion.6), channel_id=1, source_target_pairs={{0,16},{1,9},{2,18},{3,11},{4,20},{5,13},{6,22},{7,15},{8,24},{9,1... | collective-permute-start | bytes 1966088 | tf_op jit(solution)/shard_map/ppermute | solution.py:511
  350.2 10.3 %collective-permute-start.41 = (bf16[128,1024]{1,0:T(8,128)(2,1)S(1)}, bf16[128,1024]{1,0:T(8,128)(2,1)S(1)}, u32[]{:S(2)}, u32[]{:S(2)}) collective-permute-start(bf16[128,1024]{1,0:T(8,128)(2,1)S(1)} %fusion.12), channel_id=1, source_target_pairs={{0,4},{1,3},{2,6},{3,1},{4,0},{5,7},{6,2},{7,5},{8,12},{9,11},{10,... | collective-permute-start | bytes 786440 | tf_op jit(solution)/shard_map/ppermute | solution.py:511
  360.5 13.2 %collective-permute-start.43 = (bf16[4,4,144,384]{3,2,1,0:T(8,128)(2,1)}, bf16[4,4,144,384]{3,2,1,0:T(8,128)(2,1)}, u32[]{:S(2)}, u32[]{:S(2)}) collective-permute-start(bf16[4,4,144,384]{3,2,1,0:T(8,128)(2,1)} %get-tuple-element.225), channel_id=1, source_target_pairs={{0,1},{1,0},{2,3},{3,2},{4,5},{5,4},{6,7},{7,6},{8,9},{9,8},{10,11... | collective-permute-start | bytes 5308424 | tf_op jit(solution)/shard_map/ppermute | solution.py:511
  362.8 10.3 %collective-permute-start.44 = (bf16[2,128,640]{2,1,0:T(8,128)(2,1)S(1)}, bf16[2,128,640]{2,1,0:T(8,128)(2,1)S(1)}, u32[]{:S(2)}, u32[]{:S(2)}) collective-permute-start(bf16[2,128,640]{2,1,0:T(8,128)(2,1)S(1)} %pad_maximum_fusion.10), channel_id=1, source_target_pairs={{0,2},{1,5},{2,0},{3,7},{4,6},{5,1},{6,4},{7,3},{8,10},{9,13},{10,... | collective-permute-start | bytes 983048 | tf_op jit(solution)/shard_map/ppermute | solution.py:511
  364.5 9.2 %collective-permute-start.45 = (bf16[1024,256]{1,0:T(8,128)(2,1)S(1)}, bf16[1024,256]{1,0:T(8,128)(2,1)S(1)}, u32[]{:S(2)}, u32[]{:S(2)}) collective-permute-start(bf16[1024,256]{1,0:T(8,128)(2,1)S(1)} %slice_dynamic-update-slice_fusion.refs_0_), channel_id=1, source_target_pairs={{0,8},{1,17},{2,10},{3,19},{4,12},{5,21},{6,14},{7,23},{8,0},{9,25... | collective-permute-start | bytes 1572872 | tf_op jit(solution)/shard_map/ppermute | solution.py:511
  376.3 13.3 %collective-permute-start.46 = (bf16[2,4,144,384]{3,2,1,0:T(8,128)(2,1)}, bf16[2,4,144,384]{3,2,1,0:T(8,128)(2,1)S(1)}, u32[]{:S(2)}, u32[]{:S(2)}) collective-permute-start(bf16[2,4,144,384]{3,2,1,0:T(8,128)(2,1)} %add_convert_fusion.5), channel_id=1, source_target_pairs={{0,8},{1,17},{2,10},{3,19},{4,12},{5,21},{6,14},{7,23},{8,0},{9,25... | collective-permute-start | bytes 2654216 | tf_op jit(solution)/shard_map/ppermute | solution.py:511
  377.4 9.7 %collective-permute-start.47 = (bf16[128,640]{1,0:T(8,128)(2,1)S(1)}, bf16[128,640]{1,0:T(8,128)(2,1)S(1)}, u32[]{:S(2)}, u32[]{:S(2)}) collective-permute-start(bf16[128,640]{1,0:T(8,128)(2,1)S(1)} %fusion.16), channel_id=1, source_target_pairs={{0,4},{1,3},{2,6},{3,1},{4,0},{5,7},{6,2},{7,5},{8,12},{9,11},{10,... | collective-permute-start | bytes 491528 | tf_op jit(solution)/shard_map/ppermute | solution.py:511
  390.8 10.1 %collective-permute-start.48 = (bf16[4,144,384]{2,1,0:T(8,128)(2,1)S(1)}, bf16[4,144,384]{2,1,0:T(8,128)(2,1)S(1)}, u32[]{:S(2)}, u32[]{:S(2)}) collective-permute-start(bf16[4,144,384]{2,1,0:T(8,128)(2,1)S(1)} %fusion.9), channel_id=1, source_target_pairs={{0,16},{1,9},{2,18},{3,11},{4,20},{5,13},{6,22},{7,15},{8,24},{9,1... | collective-permute-start | bytes 1327112 | tf_op jit(solution)/shard_map/ppermute | solution.py:511
  391.9 7.2 %collective-permute-start.49 = (bf16[128,640]{1,0:T(8,128)(2,1)S(1)}, bf16[128,640]{1,0:T(8,128)(2,1)S(1)}, u32[]{:S(2)}, u32[]{:S(2)}) collective-permute-start(bf16[128,640]{1,0:T(8,128)(2,1)S(1)} %fusion.10.refs_0_), channel_id=1, source_target_pairs={{0,8},{1,17},{2,10},{3,19},{4,12},{5,21},{6,14},{7,23},{8,0},{9,25... | collective-permute-start | bytes 491528 | tf_op jit(solution)/shard_map/ppermute | solution.py:511
  403.4 16.2 %copy-start.3 = (s32[3]{0:T(128)S(1)}, s32[3]{0:T(128)}, u32[]{:S(2)}) copy-start(s32[3]{0:T(128)} %pad_add_fusion.where) | copy-start | bytes 40
  403.4 16.1 %collective-permute-start.54 = (bf16[2,1024,256]{2,1,0:T(8,128)(2,1)}, bf16[2,1024,256]{2,1,0:T(8,128)(2,1)S(1)}, u32[]{:S(2)}, u32[]{:S(2)}) collective-permute-start(bf16[2,1024,256]{2,1,0:T(8,128)(2,1)} %pad_maximum_fusion.2), channel_id=1, source_target_pairs={{0,16},{1,9},{2,18},{3,11},{4,20},{5,13},{6,22},{7,15},{8,24},{9,1... | collective-permute-start | bytes 3145736 | tf_op jit(solution)/shard_map/ppermute | solution.py:511
  403.8 7.8 %collective-permute-start.51 = (bf16[144,384]{1,0:T(8,128)(2,1)S(1)}, bf16[144,384]{1,0:T(8,128)(2,1)S(1)}, u32[]{:S(2)}, u32[]{:S(2)}) collective-permute-start(bf16[144,384]{1,0:T(8,128)(2,1)S(1)} %get-tuple-element.259), channel_id=1, source_target_pairs={{0,6},{1,7},{2,4},{3,5},{4,2},{5,3},{6,0},{7,1},{8,14},{9,15},{10,... | collective-permute-start | bytes 331784 | tf_op jit(solution)/shard_map/ppermute | solution.py:511
  405.3 10.5 %collective-permute-start.52 = (bf16[144,384]{1,0:T(8,128)(2,1)S(1)}, bf16[144,384]{1,0:T(8,128)(2,1)S(1)}, u32[]{:S(2)}, u32[]{:S(2)}) collective-permute-start(bf16[144,384]{1,0:T(8,128)(2,1)S(1)} %get-tuple-element.258), channel_id=1, source_target_pairs={{0,4},{1,5},{2,6},{3,7},{4,0},{5,1},{6,2},{7,3},{8,12},{9,13},{10,... | collective-permute-start | bytes 331784 | tf_op jit(solution)/shard_map/ppermute | solution.py:511
  406.1 9.7 %collective-permute-start.53 = (bf16[144,384]{1,0:T(8,128)(2,1)S(1)}, bf16[144,384]{1,0:T(8,128)(2,1)S(1)}, u32[]{:S(2)}, u32[]{:S(2)}) collective-permute-start(bf16[144,384]{1,0:T(8,128)(2,1)S(1)} %get-tuple-element.257), channel_id=1, source_target_pairs={{0,2},{1,3},{2,0},{3,1},{4,6},{5,7},{6,4},{7,5},{8,10},{9,11},{10,... | collective-permute-start | bytes 331784 | tf_op jit(solution)/shard_map/ppermute | solution.py:511
  408.3 17.1 %collective-permute-start.50 = (bf16[2,128,640]{2,1,0:T(8,128)(2,1)S(1)}, bf16[2,128,640]{2,1,0:T(8,128)(2,1)S(1)}, u32[]{:S(2)}, u32[]{:S(2)}) collective-permute-start(bf16[2,128,640]{2,1,0:T(8,128)(2,1)S(1)} %pad_maximum_fusion.11), channel_id=1, source_target_pairs={{0,16},{1,9},{2,18},{3,11},{4,20},{5,13},{6,22},{7,15},{8,24},{9,1... | collective-permute-start | bytes 983048 | tf_op jit(solution)/shard_map/ppermute | solution.py:511
  415.9 9.6 %collective-permute-start.55 = (bf16[144,384]{1,0:T(8,128)(2,1)S(1)}, bf16[144,384]{1,0:T(8,128)(2,1)S(1)}, u32[]{:S(2)}, u32[]{:S(2)}) collective-permute-start(bf16[144,384]{1,0:T(8,128)(2,1)S(1)} %fusion.15.refs_4_), channel_id=1, source_target_pairs={{0,8},{1,9},{2,10},{3,11},{4,12},{5,13},{6,14},{7,15},{8,0},{9,1},... | collective-permute-start | bytes 331784 | tf_op jit(solution)/shard_map/ppermute | solution.py:511
  416.4 10.3 %collective-permute-start.56 = (bf16[144,384]{1,0:T(8,128)(2,1)S(1)}, bf16[144,384]{1,0:T(8,128)(2,1)S(1)}, u32[]{:S(2)}, u32[]{:S(2)}) collective-permute-start(bf16[144,384]{1,0:T(8,128)(2,1)S(1)} %fusion.15.refs_4_), channel_id=1, source_target_pairs={{0,16},{1,17},{2,18},{3,19},{4,20},{5,21},{6,22},{7,23},{8,24},{9,... | collective-permute-start | bytes 331784 | tf_op jit(solution)/shard_map/ppermute | solution.py:511
  418.0 8.6 %collective-permute-start.57 = (bf16[144,384]{1,0:T(8,128)(2,1)S(1)}, bf16[144,384]{1,0:T(8,128)(2,1)S(1)}, u32[]{:S(2)}, u32[]{:S(2)}) collective-permute-start(bf16[144,384]{1,0:T(8,128)(2,1)S(1)} %fusion.15.refs_4_), channel_id=1, source_target_pairs={{0,24},{1,25},{2,26},{3,27},{4,28},{5,29},{6,30},{7,31},{8,16},{9,... | collective-permute-start | bytes 331784 | tf_op jit(solution)/shard_map/ppermute | solution.py:511
  (16 other events, 51.7 us)

commit v4 on v3

--- a/solution.py
+++ b/solution.py
@@ -367,11 +367,11 @@
             scores = jnp.where(allowed, scores, masked_score)
             powers = jnp.exp(scores - jnp.max(scores, 0, keepdims=True))
             scale = 1.0 / jnp.sum(powers, 0, keepdims=True)
-            scales.append(jnp.transpose(jnp.broadcast_to(scale, (LANES, rows))))
+            scales.append(jnp.broadcast_to(scale, (HD, rows)))
             powers = powers.astype(jnp.bfloat16)
             probs_ref[head, :, here] = powers
             outs.append(mxu(powers, values, TN))
-        scale = jnp.where(first, scales[0], scales[1])
+        scale = jnp.transpose(jnp.concatenate(scales))
         scale_ref[here, :] = scale
         out_ref[here, :] = (jnp.where(first, outs[0], outs[1]) * scale).astype(jnp.bfloat16)
 
@@ -423,7 +423,7 @@
     pick = (
         lax.broadcasted_iota(jnp.int32, (8, LANES), 0)
         == lax.broadcasted_iota(jnp.int32, (8, LANES), 1) // HD
-    ).astype(jnp.float32)
+    ).astype(jnp.bfloat16)
     q = q_ref[...]
     scaled = do_ref[...].astype(jnp.float32) * scale_ref[...]
     do = scaled.astype(jnp.bfloat16)
@@ -431,13 +431,10 @@
     values = v_ref[...]
     zero = jnp.zeros_like(values)
     head_values = (jnp.where(first, values, zero), jnp.where(first, zero, values))
-    dots = lax.dot_general(
-        pick,
-        scaled * o_ref[...].astype(jnp.float32),
-        NT,
-        precision=lax.Precision.HIGHEST,
-        preferred_element_type=jnp.float32,
-    )
+    products = scaled * o_ref[...].astype(jnp.float32)
+    high = products.astype(jnp.bfloat16)
+    low = (products - high.astype(jnp.float32)).astype(jnp.bfloat16)
+    dots = mxu(pick, high, NT) + mxu(pick, low, NT)
     query_parts, key_parts, value_parts = [], [], []
     for head in range(2):
         probs = probs_ref[head]

time: 434 us -> 434 us (level)
  transfers between devices with their start and end apart: 58 -> 58, of which waited for: 23 -> 24; matrix products, arithmetic and copies ran while one was open for 5% -> 5% of each run, Pallas kernels for 51% -> 50%
where the time goes in v4:
time: 434 us; the launch traced here: 430 us
  Pallas kernels  265 us (61%)
  starting transfers between devices  58.4 us (13%)
  waiting for transfers between devices  53.7 us (12%)
  other arithmetic  43.1 us (10%)
  local copies, waits for them, and re-layouts  8.15 us (2%)
    pallas_call x4, Pallas kernels, weight_call(): pl.pallas_call(body, grid_spec=pltpu.PrefetchScalarGridSpec(num_scalar_pr...  76.3 us
    ppermute x58, starting transfers between devices, permute(): return lax.ppermute(array, AXES, pairs)  58.4 us
    ppermute x58, waiting for transfers between devices, permute(): return lax.ppermute(array, AXES, pairs)  53.7 us
    pallas_call x3, Pallas kernels, attention_backward(): pl.pallas_call(body, grid=(pairs,), in_specs=[pair(0), pair(1), pair(2),...  49.3 us
    pallas_call x3, Pallas kernels, attention_forward(): pl.pallas_call(body, grid=(pairs,), in_specs=[pair(0), pair(1), pair(2),...  44.8 us
    convert_element_type x18, other arithmetic, add(): return total.astype(jnp.bfloat16)  33.2 us
    pallas_call x2, Pallas kernels, weight_grad(): pl.pallas_call(functools.partial(weight_grad_kernel, rows=rows, groups=gr...  28 us
    pallas_call x2, Pallas kernels, attention_grads(): pl.pallas_call(functools.partial(attention_grads_kernel, rows=rows, group...  21.1 us
  transfers between devices with their start and end apart: 58, of which 24 were waited for; matrix products, arithmetic and copies ran while one was open for 5% of the time, Pallas kernels for 50%

profile of v4, /device:TPU:0, one launch (start us, length us, event | category | flops | bytes accessed | tf_op | source)
XLA Modules:
  0.0 429.9 jit_solution(12010106921101880261)
XLA Ops:
  0.6 3.1 collective-permute-start
  3.7 1.5 concatenate.29
  6.7 2.7 collective-permute-done
  10.4 2.5 collective-permute-start.2
  12.9 2.5 collective-permute-start.3
  16.4 4.3 %collective-permute-done.3 = bf16[2,16,128]{2,1,0:T(8,128)(2,1)S(1)} collective-permute-done((bf16[2,16,128]{2,1,0:T(8,128)(2,1)S(1)}, bf16[2,16,128]{2,1,0:T(8,128)(2,1)S(1)}, u32[]{:S(2)}, u32[]{:S(2)}) %collective-permute-start.3) | collective-permute-done | bytes 8224 | tf_op jit(solution)/shard_map/ppermute | solution.py:508
  22.9 2.7 collective-permute-start.4
  25.6 1.6 collective-permute-start.7
  27.2 1.5 collective-permute-start.8
  29.3 3.3 collective-permute-start.5
  32.6 2.0 collective-permute-done.5
  35.5 2.9 collective-permute-start.6
  40.4 2.0 vectors.1
  42.4 2.4 collective-permute-done.7.refs_1_
  49.0 5.4 %collective-permute-done.6 = bf16[2,128,1280]{2,1,0:T(8,128)(2,1)} collective-permute-done((bf16[2,128,1280]{2,1,0:T(8,128)(2,1)}, bf16[2,128,1280]{2,1,0:T(8,128)(2,1)}, u32[]{:S(2)}, u32[]{:S(2)}) %collective-permute-start.6) | collective-permute-done | bytes 655392 | tf_op jit(solution)/shard_map/ppermute | solution.py:508
  55.6 1.4 collective-permute-done.9.refs_3_
  57.0 1.5 collective-permute-start.15
  61.7 12.7 %qkv.1 = (bf16[1024,3072]{1,0:T(8,128)(2,1)}, bf16[1024,3072]{1,0:T(8,128)(2,1)}) custom-call(s32[3]{0:T(128)} %pad_add_fusion.where, bf16[4,128,768]{2,1,0:T(8,128)(2,1)} %copy-done.7, bf16[4,128,768]{2,1,0:T(8,128)(2,1)} %collective-permute-done.7.refs_1_, bf16[4,128,768]{2,1,0:T(8,128)(2,1)} %collective-permute-done.8.refs_2_, ...), custom_call_target="tpu_custom_call" | custom-call | flops 12884901888 | tf_op jit(solution)/shard_map/qkv/pallas_call | solution.py:654
  74.5 2.5 collective-permute-start.17
  77.1 16.4 %attn_fwd.3 = (bf16[1024,1024]{1,0:T(8,128)(2,1)}, bf16[16,1024,1024]{2,1,0:T(8,128)(2,1)}, f32[1024,1024]{1,0:T(8,128)}) custom-call(bf16[1024,3072]{1,0:T(8,128)(2,1)} %get-tuple-element.161.q_ref.k_ref.v_ref.refs_0_.refs_1_.refs_2_, bf16[1024,3072]{1,0:T(8,128)(2,1)} %get-tuple-element.161.q_ref.k_ref.v_ref.refs_0_.refs_1_.refs_2_, ...), custom_call_target="tpu_custom_call" | custom-call | flops 12884901888 | tf_op jit(solution)/shard_map/attn_fwd/pallas_call | solution.py:391
  93.4 1.5 collective-permute-start.18
  95.6 16.3 %attn_fwd.4 = (bf16[1024,1024]{1,0:T(8,128)(2,1)}, bf16[16,1024,1024]{2,1,0:T(8,128)(2,1)}, f32[1024,1024]{1,0:T(8,128)}) custom-call(bf16[1024,3072]{1,0:T(8,128)(2,1)} %get-tuple-element.161.q_ref.k_ref.v_ref.refs_0_.refs_1_.refs_2_, ...), custom_call_target="tpu_custom_call", output_to_operand_aliasing={{0}: (5, {}), {1}: (6, {}), {2}: (7, {})} | custom-call | flops 12884901888 | tf_op jit(solution)/shard_map/attn_fwd/pallas_call | solution.py:391
  114.2 12.1 %attn_fwd.5 = (bf16[1024,1024]{1,0:T(8,128)(2,1)}, bf16[16,1024,1024]{2,1,0:T(8,128)(2,1)}, f32[1024,1024]{1,0:T(8,128)}) custom-call(bf16[1024,3072]{1,0:T(8,128)(2,1)} %get-tuple-element.161.q_ref.k_ref.v_ref.refs_0_.refs_1_.refs_2_, ...), custom_call_target="tpu_custom_call", output_to_operand_aliasing={{0}: (5, {}), {1}: (6, {}), {2}: (7, {})} | custom-call | flops 8589934592 | tf_op jit(solution)/shard_map/attn_fwd/pallas_call | solution.py:391
  127.5 9.6 %attn_out.1 = (f32[1024,1024]{1,0:T(8,128)}, f32[1024,128]{1,0:T(8,128)}, bf16[1024,1024]{1,0:T(8,128)(2,1)}, bf16[1024,1024]{1,0:T(8,128)(2,1)}) custom-call(s32[3]{0:T(128)} %pad_add_fusion.where, bf16[4,128,1280]{2,1,0:T(8,128)(2,1)} %copy-done.4, bf16[4,128,1280]{2,1,0:T(8,128)(2,1)} %collective-permute-done.15.refs_1_, ...), custom_call_target="tpu_custom_call" | custom-call | flops 4294967296 | tf_op jit(solution)/shard_map/attn_out/pallas_call | solution.py:654
  139.3 21.3 %feed_in.1 = (bf16[1024,4096]{1,0:T(8,128)(2,1)}, bf16[1024,4096]{1,0:T(8,128)(2,1)}, bf16[1024,4096]{1,0:T(8,128)(2,1)}) custom-call(s32[3]{0:T(128)} %pad_add_fusion.where, bf16[4,128,1280]{2,1,0:T(8,128)(2,1)} %copy-done.4, bf16[4,128,1280]{2,1,0:T(8,128)(2,1)} %collective-permute-done.15.refs_1_, bf16[4,128,1280]{2,1,0:T(8,128)(2,1)} %collective-permute-done.16.refs_2_, ...), custom_call_target="tpu_custom_call" | custom-call | flops 17179869184 | tf_op jit(solution)/shard_map/feed_in/pallas_call | solution.py:654
  160.8 2.6 collective-permute-done.29.refs_7_
  164.4 32.5 %feed_out.1 = (bf16[1024,1024]{1,0:T(8,128)(2,1)}, f32[1024,1024]{1,0:T(8,128)}, bf16[1024,1024]{1,0:T(8,128)(2,1)}, f32[8,1024]{1,0:T(8,128)}, bf16[1024,4096]{1,0:T(8,128)(2,1)}, /*index=5*/f32[1,4096]{1,0:T(1,128)}) custom-call(s32[3]{0:T(128)} %pad_add_fusion.where, bf16[4,512,256]{2,1,0:T(8,128)(2,1)} %copy-done.5, ...), custom_call_target="tpu_custom_call" | custom-call | flops 34359738368 | tf_op jit(solution)/shard_map/feed_out/pallas_call | solution.py:654
  197.0 13.9 %wgrad_out.1 = (bf16[4,4,512,256]{3,2,1,0:T(8,128)(2,1)}, bf16[4,4,512,256]{3,2,1,0:T(8,128)(2,1)}) custom-call(s32[3]{0:T(128)} %pad_add_fusion.where, bf16[1024,4096]{1,0:T(8,128)(2,1)} %get-tuple-element.170.refs_8_.left_ref, bf16[1024,1024]{1,0:T(8,128)(2,1)} %get-tuple-element.178.right_ref), custom_call_target="tpu_custom_call" | custom-call | flops 17179869184 | tf_op jit(solution)/shard_map/wgrad_out/pallas_call | solution.py:1213
  211.1 14.1 %wgrad_in.1 = (bf16[4,4,128,1024]{3,2,1,0:T(8,128)(2,1)}, bf16[4,4,128,1024]{3,2,1,0:T(8,128)(2,1)}) custom-call(s32[3]{0:T(128)} %pad_add_fusion.where, bf16[1024,1024]{1,0:T(8,128)(2,1)} %get-tuple-element.180.refs_8_.left_ref, bf16[1024,4096]{1,0:T(8,128)(2,1)} %get-tuple-element.184.right_ref.p_ref), custom_call_target="tpu_custom_call" | custom-call | flops 17179869184 | tf_op jit(solution)/shard_map/wgrad_in/pallas_call | solution.py:1213
  225.5 2.7 add_convert_fusion.1
  229.6 21.0 %feed_in_back.1 = (f32[1024,1024]{1,0:T(8,128)}, bf16[1024,1024]{1,0:T(8,128)(2,1)}, bf16[1024,1024]{1,0:T(8,128)(2,1)}, f32[8,1024]{1,0:T(8,128)}) custom-call(bf16[1024,4096]{1,0:T(8,128)(2,1)} %get-tuple-element.184.right_ref.p_ref, bf16[1024,4096]{1,0:T(8,128)(2,1)} %get-tuple-element.185.w_ref, f32[1024,1024]{1,0:T(8,128)} %get-tuple-element.186.g_ref, ...), custom_call_target="tpu_custom_call" | custom-call | flops 21474836480 | tf_op jit(solution)/shard_map/feed_in_back/pallas_call | solution.py:676
  250.6 4.7 %add_convert_fusion = bf16[2,4,128,1024]{3,2,1,0:T(8,128)(2,1)} fusion(bf16[4,4,128,1024]{3,2,1,0:T(8,128)(2,1)} %collective-permute-done.31, bf16[4,4,128,1024]{3,2,1,0:T(8,128)(2,1)} %get-tuple-element.181), kind=kLoop, calls=%fused_computation | loop fusion | flops 4194304 | bytes 6291456 | tf_op jit(solution)/shard_map/convert_element_type | solution.py:1236
  256.0 22.7 %attn_bwd.3 = (bf16[3,1024,512]{2,1,0:T(8,128)(2,1)}, f32[2,512]{1,0:T(2,128)}) custom-call(bf16[1024,3072]{1,0:T(8,128)(2,1)} %get-tuple-element.161.q_ref.k_ref.v_ref.refs_0_.refs_1_.refs_2_, bf16[1024,3072]{1,0:T(8,128)(2,1)} %get-tuple-element.161.q_ref.k_ref.v_ref.refs_0_.refs_1_.refs_2_, ...), custom_call_target="tpu_custom_call" | custom-call | flops 34359738368 | tf_op jit(solution)/shard_map/attn_bwd/pallas_call | solution.py:467
  278.7 2.9 collective-permute-done.33
  281.6 3.5 fusion.4
  285.1 2.2 fusion.3
  287.9 12.4 %wgrad_a.1 = (bf16[4,4,128,640]{3,2,1,0:T(8,128)(2,1)}, bf16[4,4,128,640]{3,2,1,0:T(8,128)(2,1)}) custom-call(s32[3]{0:T(128)} %pad_add_fusion.where, bf16[2,512,1024]{2,1,0:T(8,128)(2,1)} %copy-done.1, bf16[3,1024,512]{2,1,0:T(8,128)(2,1)} %get-tuple-element.196.refs_1_.refs_0_, bf16[1024,1024]{1,0:T(8,128)(2,1)} %get-tuple-element.164.refs_8_.refs_3_.refs_2_, ...), custom_call_target="tpu_custom_call" | custom-call | flops 10737418240 | tf_op jit(solution)/shard_map/wgrad_a/pallas_call | solution.py:1171
  300.2 1.6 collective-permute-start.36
  302.2 2.4 fusion.1
  305.3 13.2 %attn_bwd.4 = (bf16[3,1024,512]{2,1,0:T(8,128)(2,1)}, f32[2,512]{1,0:T(2,128)}) custom-call(bf16[1024,3072]{1,0:T(8,128)(2,1)} %get-tuple-element.161.q_ref.k_ref.v_ref.refs_0_.refs_1_.refs_2_, bf16[1024,3072]{1,0:T(8,128)(2,1)} %get-tuple-element.161.q_ref.k_ref.v_ref.refs_0_.refs_1_.refs_2_, ...), custom_call_target="tpu_custom_call" | custom-call | flops 17179869184 | tf_op jit(solution)/shard_map/attn_bwd/pallas_call | solution.py:467
  319.5 3.3 add_convert_fusion.2
  322.8 3.1 fusion
  328.5 13.4 %attn_bwd.5 = (bf16[3,1024,512]{2,1,0:T(8,128)(2,1)}, f32[2,512]{1,0:T(2,128)}) custom-call(bf16[1024,3072]{1,0:T(8,128)(2,1)} %get-tuple-element.161.q_ref.k_ref.v_ref.refs_0_.refs_1_.refs_2_, bf16[1024,3072]{1,0:T(8,128)(2,1)} %get-tuple-element.161.q_ref.k_ref.v_ref.refs_0_.refs_1_.refs_2_, ...), custom_call_target="tpu_custom_call", output_to_operand_aliasing={{0}: (7, {}), {1}: (8, {})} | custom-call | flops 17179869184 | tf_op jit(solution)/shard_map/attn_bwd/pallas_call | solution.py:467
  342.0 2.6 collective-permute-done.38
  344.6 2.0 collective-permute-done.39
  346.6 1.9 fusion.6
  348.6 2.0 collective-permute-start.42
  351.4 8.7 %wgrad_b.1 = (bf16[4,4,144,384]{3,2,1,0:T(8,128)(2,1)}, bf16[4,4,144,384]{3,2,1,0:T(8,128)(2,1)}) custom-call(s32[3]{0:T(128)} %pad_add_fusion.where, bf16[2,512,1024]{2,1,0:T(8,128)(2,1)} %copy-done.1, bf16[3,1024,512]{2,1,0:T(8,128)(2,1)} %get-tuple-element.223.refs_1_, f32[2,512]{1,0:T(2,128)} %get-tuple-element.197.refs_2_, ...), custom_call_target="tpu_custom_call" | custom-call | flops 6442450944 | tf_op jit(solution)/shard_map/wgrad_b/pallas_call | solution.py:1171
  360.2 2.1 fusion.2
  364.7 8.2 %qkv_back.2.refs_3_ = f32[1024,1024]{1,0:T(8,128)} custom-call(bf16[1024,3072]{1,0:T(8,128)(2,1)} %get-tuple-element.176.w_ref, bf16[3,1024,512]{2,1,0:T(8,128)(2,1)} %get-tuple-element.196.refs_1_.refs_0_, bf16[3,1024,512]{2,1,0:T(8,128)(2,1)} %get-tuple-element.223.refs_1_, f32[1024,1024]{1,0:T(8,128)} %get-tuple-element.228.refs_2_), custom_call_target="tpu_custom_call" | custom-call | flops 6442450944 | tf_op jit(solution)/shard_map/qkv_back/pallas_call | solution.py:1012
  373.5 2.6 add_convert_fusion.5
  377.2 1.8 collective-permute-start.47
  378.9 8.2 %qkv_back.3 = f32[1024,1024]{1,0:T(8,128)} custom-call(bf16[1024,3072]{1,0:T(8,128)(2,1)} %get-tuple-element.176.w_ref, bf16[3,1024,512]{2,1,0:T(8,128)(2,1)} %get-tuple-element.196.refs_1_.refs_0_, bf16[3,1024,512]{2,1,0:T(8,128)(2,1)} %get-tuple-element.223.refs_1_, f32[1024,1024]{1,0:T(8,128)} %get-tuple-element.228.refs_2_, ...), custom_call_target="tpu_custom_call", output_to_operand_aliasing={{}: (4, {})} | custom-call | flops 6442450944 | tf_op jit(solution)/shard_map/qkv_back/pallas_call | solution.py:1012
  387.2 2.1 collective-permute-done.46
  392.7 6.2 %collective-permute-done.49.refs_1_ = bf16[128,640]{1,0:T(8,128)(2,1)S(1)} collective-permute-done((bf16[128,640]{1,0:T(8,128)(2,1)S(1)}, bf16[128,640]{1,0:T(8,128)(2,1)S(1)}, u32[]{:S(2)}, u32[]{:S(2)}) %collective-permute-start.49) | collective-permute-done | bytes 163872 | tf_op jit(solution)/shard_map/ppermute | solution.py:508
  398.9 1.8 collective-permute-done.48
  404.1 1.6 collective-permute-start.51
  406.2 2.4 collective-permute-start.53
  409.8 2.2 collective-permute-done.51
  412.0 3.5 collective-permute-done.52
  416.3 1.4 collective-permute-start.56
  419.4 2.8 order_feed_forward.1
  423.5 2.9 collective-permute-done.56.refs_6_
  426.4 2.1 order_attention.1
  (166 shorter events, 51.4 us)
Async XLA Ops:
  0.6 8.7 %collective-permute-start = (bf16[128,768]{1,0:T(8,128)(2,1)}, bf16[128,768]{1,0:T(8,128)(2,1)S(1)}, u32[]{:S(2)}, u32[]{:S(2)}) collective-permute-start(bf16[128,768]{1,0:T(8,128)(2,1)} %param.21), channel_id=1, source_target_pairs={{0,2},{1,5},{2,0},{3,7},{4,6},{5,1},{6,4},{7,3},{8,10},{9,13},{10,... | collective-permute-start | bytes 589832 | tf_op jit(solution)/shard_map/ppermute | solution.py:508
  5.2 1.4 collective-permute-start.1
  9.3 36.0 %copy-start = (bf16[1,1024,1024]{2,1,0:T(8,128)(2,1)S(1)}, bf16[1,1024,1024]{2,1,0:T(8,128)(2,1)}, u32[]{:S(2)}) copy-start(bf16[1,1024,1024]{2,1,0:T(8,128)(2,1)} %param.17) | copy-start | bytes 6291460
  10.4 11.5 %collective-permute-start.2 = (bf16[2,128,768]{2,1,0:T(8,128)(2,1)S(1)}, bf16[2,128,768]{2,1,0:T(8,128)(2,1)S(1)}, u32[]{:S(2)}, u32[]{:S(2)}) collective-permute-start(bf16[2,128,768]{2,1,0:T(8,128)(2,1)S(1)} %pad_maximum_fusion.8), channel_id=1, source_target_pairs={{0,4},{1,3},{2,6},{3,1},{4,0},{5,7},{6,2},{7,5},{8,12},{9,11},{10,... | collective-permute-start | bytes 1179656 | tf_op jit(solution)/shard_map/ppermute | solution.py:508
  12.9 7.8 %collective-permute-start.3 = (bf16[2,16,128]{2,1,0:T(8,128)(2,1)S(1)}, bf16[2,16,128]{2,1,0:T(8,128)(2,1)S(1)}, u32[]{:S(2)}, u32[]{:S(2)}) collective-permute-start(bf16[2,16,128]{2,1,0:T(8,128)(2,1)S(1)} %get-tuple-element.275), channel_id=1, source_target_pairs={{0,2},{1,5},{2,0},{3,7},{4,6},{5,1},{6,4},{7,3},{8,10},{9,13},{10,... | collective-permute-start | bytes 24584 | tf_op jit(solution)/shard_map/ppermute | solution.py:508
  22.9 24.2 %copy-start.7 = (bf16[4,128,768]{2,1,0:T(8,128)(2,1)}, bf16[4,128,768]{2,1,0:T(8,128)(2,1)S(1)}, u32[]{:S(2)}) copy-start(bf16[4,128,768]{2,1,0:T(8,128)(2,1)S(1)} %pad_maximum_fusion.3.refs_0_) | copy-start | bytes 2359300
  22.9 11.7 %collective-permute-start.4 = (bf16[128,1280]{1,0:T(8,128)(2,1)S(1)}, bf16[128,1280]{1,0:T(8,128)(2,1)S(1)}, u32[]{:S(2)}, u32[]{:S(2)}) collective-permute-start(bf16[128,1280]{1,0:T(8,128)(2,1)S(1)} %pad_maximum_fusion.9), channel_id=1, source_target_pairs={{0,2},{1,5},{2,0},{3,7},{4,6},{5,1},{6,4},{7,3},{8,10},{9,13},{10,... | collective-permute-start | bytes 983048 | tf_op jit(solution)/shard_map/ppermute | solution.py:508
  25.6 19.2 %collective-permute-start.7 = (bf16[4,128,768]{2,1,0:T(8,128)(2,1)S(1)}, bf16[4,128,768]{2,1,0:T(8,128)(2,1)}, u32[]{:S(2)}, u32[]{:S(2)}) collective-permute-start(bf16[4,128,768]{2,1,0:T(8,128)(2,1)S(1)} %pad_maximum_fusion.3.refs_0_), channel_id=1, source_target_pairs={{0,8},{1,17},{2,10},{3,19},{4,12},{5,21},{6,14},{7,23},{8,0},{9,25... | collective-permute-start | bytes 2359304 | tf_op jit(solution)/shard_map/ppermute | solution.py:508
  27.2 17.6 %collective-permute-start.8 = (bf16[4,128,768]{2,1,0:T(8,128)(2,1)S(1)}, bf16[4,128,768]{2,1,0:T(8,128)(2,1)}, u32[]{:S(2)}, u32[]{:S(2)}) collective-permute-start(bf16[4,128,768]{2,1,0:T(8,128)(2,1)S(1)} %pad_maximum_fusion.3.refs_0_), channel_id=1, source_target_pairs={{0,16},{1,9},{2,18},{3,11},{4,20},{5,13},{6,22},{7,15},{8,24},{9,1... | collective-permute-start | bytes 2359304 | tf_op jit(solution)/shard_map/ppermute | solution.py:508
  29.3 5.3 %collective-permute-start.5 = (bf16[2,2,16,128]{3,2,1,0:T(8,128)(2,1)}, bf16[2,2,16,128]{3,2,1,0:T(8,128)(2,1)}, u32[]{:S(2)}, u32[]{:S(2)}) collective-permute-start(bf16[2,2,16,128]{3,2,1,0:T(8,128)(2,1)} %pad_maximum_fusion.13), channel_id=1, source_target_pairs={{0,4},{1,3},{2,6},{3,1},{4,0},{5,7},{6,2},{7,5},{8,12},{9,11},{10,... | collective-permute-start | bytes 49160 | tf_op jit(solution)/shard_map/ppermute | solution.py:508
  35.5 18.8 %collective-permute-start.6 = (bf16[2,128,1280]{2,1,0:T(8,128)(2,1)}, bf16[2,128,1280]{2,1,0:T(8,128)(2,1)}, u32[]{:S(2)}, u32[]{:S(2)}) collective-permute-start(bf16[2,128,1280]{2,1,0:T(8,128)(2,1)} %pad_maximum_fusion.4), channel_id=1, source_target_pairs={{0,4},{1,3},{2,6},{3,1},{4,0},{5,7},{6,2},{7,5},{8,12},{9,11},{10,... | collective-permute-start | bytes 1966088 | tf_op jit(solution)/shard_map/ppermute | solution.py:508
  44.8 12.2 %collective-permute-start.9 = (bf16[4,128,768]{2,1,0:T(8,128)(2,1)}, bf16[4,128,768]{2,1,0:T(8,128)(2,1)S(1)}, u32[]{:S(2)}, u32[]{:S(2)}) collective-permute-start(bf16[4,128,768]{2,1,0:T(8,128)(2,1)} %collective-permute-done.7.refs_1_), channel_id=1, source_target_pairs={{0,16},{1,9},{2,18},{3,11},{4,20},{5,13},{6,22},{7,15},{8,24},{9,1... | collective-permute-start | bytes 2359304 | tf_op jit(solution)/shard_map/ppermute | solution.py:508
  45.3 13.2 %collective-permute-start.10 = (bf16[4,128,768]{2,1,0:T(8,128)(2,1)S(1)}, bf16[4,128,768]{2,1,0:T(8,128)(2,1)S(1)}, u32[]{:S(2)}, u32[]{:S(2)}) collective-permute-start(bf16[4,128,768]{2,1,0:T(8,128)(2,1)S(1)} %pad_maximum_fusion.3.refs_0_), channel_id=1, source_target_pairs={{0,1},{1,0},{2,3},{3,2},{4,5},{5,4},{6,7},{7,6},{8,9},{9,8},{10,11... | collective-permute-start | bytes 2359304 | tf_op jit(solution)/shard_map/ppermute | solution.py:508
  48.5 10.6 %collective-permute-start.11 = (bf16[4,128,768]{2,1,0:T(8,128)(2,1)}, bf16[4,128,768]{2,1,0:T(8,128)(2,1)S(1)}, u32[]{:S(2)}, u32[]{:S(2)}) collective-permute-start(bf16[4,128,768]{2,1,0:T(8,128)(2,1)} %collective-permute-done.7.refs_1_), channel_id=1, source_target_pairs={{0,1},{1,0},{2,3},{3,2},{4,5},{5,4},{6,7},{7,6},{8,9},{9,8},{10,11... | collective-permute-start | bytes 2359304 | tf_op jit(solution)/shard_map/ppermute | solution.py:508
  49.0 11.0 %collective-permute-start.12 = (bf16[4,128,768]{2,1,0:T(8,128)(2,1)}, bf16[4,128,768]{2,1,0:T(8,128)(2,1)S(1)}, u32[]{:S(2)}, u32[]{:S(2)}) collective-permute-start(bf16[4,128,768]{2,1,0:T(8,128)(2,1)} %collective-permute-done.8.refs_2_), channel_id=1, source_target_pairs={{0,1},{1,0},{2,3},{3,2},{4,5},{5,4},{6,7},{7,6},{8,9},{9,8},{10,11... | collective-permute-start | bytes 2359304 | tf_op jit(solution)/shard_map/ppermute | solution.py:508
  55.6 21.5 %copy-start.4 = (bf16[4,128,1280]{2,1,0:T(8,128)(2,1)}, bf16[4,128,1280]{2,1,0:T(8,128)(2,1)S(1)}, u32[]{:S(2)}) copy-start(bf16[4,128,1280]{2,1,0:T(8,128)(2,1)S(1)} %pad_maximum_fusion.refs_0_) | copy-start | bytes 3932164
  57.0 2.9 collective-permute-start.13
  57.0 36.4 %collective-permute-start.15 = (bf16[4,128,1280]{2,1,0:T(8,128)(2,1)S(1)}, bf16[4,128,1280]{2,1,0:T(8,128)(2,1)}, u32[]{:S(2)}, u32[]{:S(2)}) collective-permute-start(bf16[4,128,1280]{2,1,0:T(8,128)(2,1)S(1)} %pad_maximum_fusion.refs_0_), channel_id=1, source_target_pairs={{0,8},{1,17},{2,10},{3,19},{4,12},{5,21},{6,14},{7,23},{8,0},{9,25... | collective-permute-start | bytes 3932168 | tf_op jit(solution)/shard_map/ppermute | solution.py:508
  58.5 34.9 %collective-permute-start.16 = (bf16[4,128,1280]{2,1,0:T(8,128)(2,1)S(1)}, bf16[4,128,1280]{2,1,0:T(8,128)(2,1)}, u32[]{:S(2)}, u32[]{:S(2)}) collective-permute-start(bf16[4,128,1280]{2,1,0:T(8,128)(2,1)S(1)} %pad_maximum_fusion.refs_0_), channel_id=1, source_target_pairs={{0,16},{1,9},{2,18},{3,11},{4,20},{5,13},{6,22},{7,15},{8,24},{9,1... | collective-permute-start | bytes 3932168 | tf_op jit(solution)/shard_map/ppermute | solution.py:508
  59.0 15.4 %collective-permute-start.14 = (bf16[512,256]{1,0:T(8,128)(2,1)S(1)}, bf16[512,256]{1,0:T(8,128)(2,1)S(1)}, u32[]{:S(2)}, u32[]{:S(2)}) collective-permute-start(bf16[512,256]{1,0:T(8,128)(2,1)S(1)} %copy-done.6), channel_id=1, source_target_pairs={{0,2},{1,5},{2,0},{3,7},{4,6},{5,1},{6,4},{7,3},{8,10},{9,13},{10,... | collective-permute-start | bytes 786440 | tf_op jit(solution)/shard_map/ppermute | solution.py:508
  74.5 18.9 %collective-permute-start.17 = (bf16[2,512,256]{2,1,0:T(8,128)(2,1)S(1)}, bf16[2,512,256]{2,1,0:T(8,128)(2,1)S(1)}, u32[]{:S(2)}, u32[]{:S(2)}) collective-permute-start(bf16[2,512,256]{2,1,0:T(8,128)(2,1)S(1)} %pad_maximum_fusion.5), channel_id=1, source_target_pairs={{0,4},{1,3},{2,6},{3,1},{4,0},{5,7},{6,2},{7,5},{8,12},{9,11},{10,... | collective-permute-start | bytes 1572872 | tf_op jit(solution)/shard_map/ppermute | solution.py:508
  77.0 35.8 %collective-permute-start.19 = (bf16[4,128,1280]{2,1,0:T(8,128)(2,1)S(1)}, bf16[4,128,1280]{2,1,0:T(8,128)(2,1)}, u32[]{:S(2)}, u32[]{:S(2)}) collective-permute-start(bf16[4,128,1280]{2,1,0:T(8,128)(2,1)S(1)} %pad_maximum_fusion.refs_0_), channel_id=1, source_target_pairs={{0,1},{1,0},{2,3},{3,2},{4,5},{5,4},{6,7},{7,6},{8,9},{9,8},{10,11... | collective-permute-start | bytes 3932168 | tf_op jit(solution)/shard_map/ppermute | solution.py:508
  93.4 18.5 %collective-permute-start.18 = (bf16[4,128,1280]{2,1,0:T(8,128)(2,1)}, bf16[4,128,1280]{2,1,0:T(8,128)(2,1)}, u32[]{:S(2)}, u32[]{:S(2)}) collective-permute-start(bf16[4,128,1280]{2,1,0:T(8,128)(2,1)} %collective-permute-done.15.refs_1_), channel_id=1, source_target_pairs={{0,16},{1,9},{2,18},{3,11},{4,20},{5,13},{6,22},{7,15},{8,24},{9,1... | collective-permute-start | bytes 3932168 | tf_op jit(solution)/shard_map/ppermute | solution.py:508
  94.9 31.4 %collective-permute-start.20 = (bf16[4,128,1280]{2,1,0:T(8,128)(2,1)}, bf16[4,128,1280]{2,1,0:T(8,128)(2,1)}, u32[]{:S(2)}, u32[]{:S(2)}) collective-permute-start(bf16[4,128,1280]{2,1,0:T(8,128)(2,1)} %collective-permute-done.15.refs_1_), channel_id=1, source_target_pairs={{0,1},{1,0},{2,3},{3,2},{4,5},{5,4},{6,7},{7,6},{8,9},{9,8},{10,11... | collective-permute-start | bytes 3932168 | tf_op jit(solution)/shard_map/ppermute | solution.py:508
  95.0 31.3 %copy-start.5 = (bf16[4,512,256]{2,1,0:T(8,128)(2,1)}, bf16[4,512,256]{2,1,0:T(8,128)(2,1)S(1)}, u32[]{:S(2)}) copy-start(bf16[4,512,256]{2,1,0:T(8,128)(2,1)S(1)} %pad_maximum_fusion.1.refs_0_) | copy-start | bytes 3145732
  95.0 31.4 %collective-permute-start.21 = (bf16[4,128,1280]{2,1,0:T(8,128)(2,1)}, bf16[4,128,1280]{2,1,0:T(8,128)(2,1)S(1)}, u32[]{:S(2)}, u32[]{:S(2)}) collective-permute-start(bf16[4,128,1280]{2,1,0:T(8,128)(2,1)} %collective-permute-done.16.refs_2_), channel_id=1, source_target_pairs={{0,1},{1,0},{2,3},{3,2},{4,5},{5,4},{6,7},{7,6},{8,9},{9,8},{10,11... | collective-permute-start | bytes 3932168 | tf_op jit(solution)/shard_map/ppermute | solution.py:508
  111.9 14.5 %collective-permute-start.22 = (bf16[4,128,1280]{2,1,0:T(8,128)(2,1)}, bf16[4,128,1280]{2,1,0:T(8,128)(2,1)}, u32[]{:S(2)}, u32[]{:S(2)}) collective-permute-start(bf16[4,128,1280]{2,1,0:T(8,128)(2,1)} %collective-permute-done.18.refs_3_), channel_id=1, source_target_pairs={{0,1},{1,0},{2,3},{3,2},{4,5},{5,4},{6,7},{7,6},{8,9},{9,8},{10,11... | collective-permute-start | bytes 3932168 | tf_op jit(solution)/shard_map/ppermute | solution.py:508
  112.3 25.9 %collective-permute-start.23 = (bf16[4,512,256]{2,1,0:T(8,128)(2,1)S(1)}, bf16[4,512,256]{2,1,0:T(8,128)(2,1)}, u32[]{:S(2)}, u32[]{:S(2)}) collective-permute-start(bf16[4,512,256]{2,1,0:T(8,128)(2,1)S(1)} %pad_maximum_fusion.1.refs_0_), channel_id=1, source_target_pairs={{0,8},{1,17},{2,10},{3,19},{4,12},{5,21},{6,14},{7,23},{8,0},{9,25... | collective-permute-start | bytes 3145736 | tf_op jit(solution)/shard_map/ppermute | solution.py:508
  112.9 25.4 %collective-permute-start.24 = (bf16[4,512,256]{2,1,0:T(8,128)(2,1)S(1)}, bf16[4,512,256]{2,1,0:T(8,128)(2,1)S(1)}, u32[]{:S(2)}, u32[]{:S(2)}) collective-permute-start(bf16[4,512,256]{2,1,0:T(8,128)(2,1)S(1)} %pad_maximum_fusion.1.refs_0_), channel_id=1, source_target_pairs={{0,16},{1,9},{2,18},{3,11},{4,20},{5,13},{6,22},{7,15},{8,24},{9,1... | collective-permute-start | bytes 3145736 | tf_op jit(solution)/shard_map/ppermute | solution.py:508
  126.3 34.5 %collective-permute-start.26 = (bf16[4,512,256]{2,1,0:T(8,128)(2,1)S(1)}, bf16[4,512,256]{2,1,0:T(8,128)(2,1)}, u32[]{:S(2)}, u32[]{:S(2)}) collective-permute-start(bf16[4,512,256]{2,1,0:T(8,128)(2,1)S(1)} %pad_maximum_fusion.1.refs_0_), channel_id=1, source_target_pairs={{0,1},{1,0},{2,3},{3,2},{4,5},{5,4},{6,7},{7,6},{8,9},{9,8},{10,11... | collective-permute-start | bytes 3145736 | tf_op jit(solution)/shard_map/ppermute | solution.py:508
  138.2 22.4 %copy-start.14 = (bf16[4,512,256]{2,1,0:T(8,128)(2,1)}, bf16[4,512,256]{2,1,0:T(8,128)(2,1)S(1)}, u32[]{:S(2)}) copy-start(bf16[4,512,256]{2,1,0:T(8,128)(2,1)S(1)} %collective-permute-done.24.refs_2_) | copy-start | bytes 3145732
  138.2 22.4 %collective-permute-start.25 = (bf16[4,512,256]{2,1,0:T(8,128)(2,1)}, bf16[4,512,256]{2,1,0:T(8,128)(2,1)S(1)}, u32[]{:S(2)}, u32[]{:S(2)}) collective-permute-start(bf16[4,512,256]{2,1,0:T(8,128)(2,1)} %collective-permute-done.23.refs_1_), channel_id=1, source_target_pairs={{0,16},{1,9},{2,18},{3,11},{4,20},{5,13},{6,22},{7,15},{8,24},{9,1... | collective-permute-start | bytes 3145736 | tf_op jit(solution)/shard_map/ppermute | solution.py:508
  138.8 22.0 %collective-permute-start.27 = (bf16[4,512,256]{2,1,0:T(8,128)(2,1)}, bf16[4,512,256]{2,1,0:T(8,128)(2,1)}, u32[]{:S(2)}, u32[]{:S(2)}) collective-permute-start(bf16[4,512,256]{2,1,0:T(8,128)(2,1)} %collective-permute-done.23.refs_1_), channel_id=1, source_target_pairs={{0,1},{1,0},{2,3},{3,2},{4,5},{5,4},{6,7},{7,6},{8,9},{9,8},{10,11... | collective-permute-start | bytes 3145736 | tf_op jit(solution)/shard_map/ppermute | solution.py:508
  138.8 22.0 %collective-permute-start.28 = (bf16[4,512,256]{2,1,0:T(8,128)(2,1)S(1)}, bf16[4,512,256]{2,1,0:T(8,128)(2,1)}, u32[]{:S(2)}, u32[]{:S(2)}) collective-permute-start(bf16[4,512,256]{2,1,0:T(8,128)(2,1)S(1)} %collective-permute-done.24.refs_2_), channel_id=1, source_target_pairs={{0,1},{1,0},{2,3},{3,2},{4,5},{5,4},{6,7},{7,6},{8,9},{9,8},{10,11... | collective-permute-start | bytes 3145736 | tf_op jit(solution)/shard_map/ppermute | solution.py:508
  160.7 2.7 collective-permute-start.29
  210.9 14.6 %collective-permute-start.30 = (bf16[4,4,512,256]{3,2,1,0:T(8,128)(2,1)}, bf16[4,4,512,256]{3,2,1,0:T(8,128)(2,1)}, u32[]{:S(2)}, u32[]{:S(2)}) collective-permute-start(bf16[4,4,512,256]{3,2,1,0:T(8,128)(2,1)} %get-tuple-element.182), channel_id=1, source_target_pairs={{0,1},{1,0},{2,3},{3,2},{4,5},{5,4},{6,7},{7,6},{8,9},{9,8},{10,11... | collective-permute-start | bytes 12582920 | tf_op jit(solution)/shard_map/ppermute | solution.py:508
  225.2 25.4 %collective-permute-start.31 = (bf16[4,4,128,1024]{3,2,1,0:T(8,128)(2,1)}, bf16[4,4,128,1024]{3,2,1,0:T(8,128)(2,1)}, u32[]{:S(2)}, u32[]{:S(2)}) collective-permute-start(bf16[4,4,128,1024]{3,2,1,0:T(8,128)(2,1)} %get-tuple-element.191), channel_id=1, source_target_pairs={{0,1},{1,0},{2,3},{3,2},{4,5},{5,4},{6,7},{7,6},{8,9},{9,8},{10,11... | collective-permute-start | bytes 12582920 | tf_op jit(solution)/shard_map/ppermute | solution.py:508
  228.2 53.4 %collective-permute-start.32 = (bf16[2,4,512,256]{3,2,1,0:T(8,128)(2,1)S(1)}, bf16[2,4,512,256]{3,2,1,0:T(8,128)(2,1)}, u32[]{:S(2)}, u32[]{:S(2)}) collective-permute-start(bf16[2,4,512,256]{3,2,1,0:T(8,128)(2,1)S(1)} %add_convert_fusion.1), channel_id=1, source_target_pairs={{0,8},{1,17},{2,10},{3,19},{4,12},{5,21},{6,14},{7,23},{8,0},{9,25... | collective-permute-start | bytes 6291464 | tf_op jit(solution)/shard_map/ppermute | solution.py:508
  255.3 26.4 %collective-permute-start.33 = (bf16[2,4,128,1024]{3,2,1,0:T(8,128)(2,1)}, bf16[2,4,128,1024]{3,2,1,0:T(8,128)(2,1)}, u32[]{:S(2)}, u32[]{:S(2)}) collective-permute-start(bf16[2,4,128,1024]{3,2,1,0:T(8,128)(2,1)} %add_convert_fusion), channel_id=1, source_target_pairs={{0,8},{1,17},{2,10},{3,19},{4,12},{5,21},{6,14},{7,23},{8,0},{9,25... | collective-permute-start | bytes 6291464 | tf_op jit(solution)/shard_map/ppermute | solution.py:508
  287.3 14.9 %collective-permute-start.34 = (bf16[4,512,256]{2,1,0:T(8,128)(2,1)S(1)}, bf16[4,512,256]{2,1,0:T(8,128)(2,1)S(1)}, u32[]{:S(2)}, u32[]{:S(2)}) collective-permute-start(bf16[4,512,256]{2,1,0:T(8,128)(2,1)S(1)} %fusion.3), channel_id=1, source_target_pairs={{0,16},{1,9},{2,18},{3,11},{4,20},{5,13},{6,22},{7,15},{8,24},{9,1... | collective-permute-start | bytes 3145736 | tf_op jit(solution)/shard_map/ppermute | solution.py:508
  300.2 19.3 %collective-permute-start.37 = (bf16[4,4,128,640]{3,2,1,0:T(8,128)(2,1)}, bf16[4,4,128,640]{3,2,1,0:T(8,128)(2,1)}, u32[]{:S(2)}, u32[]{:S(2)}) collective-permute-start(bf16[4,4,128,640]{3,2,1,0:T(8,128)(2,1)} %get-tuple-element.205), channel_id=1, source_target_pairs={{0,1},{1,0},{2,3},{3,2},{4,5},{5,4},{6,7},{7,6},{8,9},{9,8},{10,11... | collective-permute-start | bytes 7864328 | tf_op jit(solution)/shard_map/ppermute | solution.py:508
  300.2 18.2 %collective-permute-start.36 = (bf16[4,128,1024]{2,1,0:T(8,128)(2,1)}, bf16[4,128,1024]{2,1,0:T(8,128)(2,1)}, u32[]{:S(2)}, u32[]{:S(2)}) collective-permute-start(bf16[4,128,1024]{2,1,0:T(8,128)(2,1)} %fusion.4), channel_id=1, source_target_pairs={{0,16},{1,9},{2,18},{3,11},{4,20},{5,13},{6,22},{7,15},{8,24},{9,1... | collective-permute-start | bytes 3145736 | tf_op jit(solution)/shard_map/ppermute | solution.py:508
  304.7 14.9 %collective-permute-start.35 = (bf16[2,512,256]{2,1,0:T(8,128)(2,1)S(1)}, bf16[2,512,256]{2,1,0:T(8,128)(2,1)S(1)}, u32[]{:S(2)}, u32[]{:S(2)}) collective-permute-start(bf16[2,512,256]{2,1,0:T(8,128)(2,1)S(1)} %pad_maximum_fusion.6), channel_id=1, source_target_pairs={{0,2},{1,5},{2,0},{3,7},{4,6},{5,1},{6,4},{7,3},{8,10},{9,13},{10,... | collective-permute-start | bytes 1572872 | tf_op jit(solution)/shard_map/ppermute | solution.py:508
  326.0 20.6 %collective-permute-start.40 = (bf16[2,4,128,640]{3,2,1,0:T(8,128)(2,1)}, bf16[2,4,128,640]{3,2,1,0:T(8,128)(2,1)}, u32[]{:S(2)}, u32[]{:S(2)}) collective-permute-start(bf16[2,4,128,640]{3,2,1,0:T(8,128)(2,1)} %add_convert_fusion.2), channel_id=1, source_target_pairs={{0,8},{1,17},{2,10},{3,19},{4,12},{5,21},{6,14},{7,23},{8,0},{9,25... | collective-permute-start | bytes 3932168 | tf_op jit(solution)/shard_map/ppermute | solution.py:508
  326.7 19.9 %collective-permute-start.39 = (bf16[2,128,1024]{2,1,0:T(8,128)(2,1)S(1)}, bf16[2,128,1024]{2,1,0:T(8,128)(2,1)S(1)}, u32[]{:S(2)}, u32[]{:S(2)}) collective-permute-start(bf16[2,128,1024]{2,1,0:T(8,128)(2,1)S(1)} %pad_maximum_fusion.7), channel_id=1, source_target_pairs={{0,2},{1,5},{2,0},{3,7},{4,6},{5,1},{6,4},{7,3},{8,10},{9,13},{10,... | collective-permute-start | bytes 1572872 | tf_op jit(solution)/shard_map/ppermute | solution.py:508
  328.1 16.5 %collective-permute-start.38 = (bf16[512,256]{1,0:T(8,128)(2,1)}, bf16[512,256]{1,0:T(8,128)(2,1)S(1)}, u32[]{:S(2)}, u32[]{:S(2)}) collective-permute-start(bf16[512,256]{1,0:T(8,128)(2,1)} %fusion.11), channel_id=1, source_target_pairs={{0,4},{1,3},{2,6},{3,1},{4,0},{5,7},{6,2},{7,5},{8,12},{9,11},{10,... | collective-permute-start | bytes 786440 | tf_op jit(solution)/shard_map/ppermute | solution.py:508
  348.6 11.6 %collective-permute-start.42 = (bf16[4,128,640]{2,1,0:T(8,128)(2,1)S(1)}, bf16[4,128,640]{2,1,0:T(8,128)(2,1)}, u32[]{:S(2)}, u32[]{:S(2)}) collective-permute-start(bf16[4,128,640]{2,1,0:T(8,128)(2,1)S(1)} %fusion.6), channel_id=1, source_target_pairs={{0,16},{1,9},{2,18},{3,11},{4,20},{5,13},{6,22},{7,15},{8,24},{9,1... | collective-permute-start | bytes 1966088 | tf_op jit(solution)/shard_map/ppermute | solution.py:508
  350.6 9.6 %collective-permute-start.41 = (bf16[128,1024]{1,0:T(8,128)(2,1)S(1)}, bf16[128,1024]{1,0:T(8,128)(2,1)S(1)}, u32[]{:S(2)}, u32[]{:S(2)}) collective-permute-start(bf16[128,1024]{1,0:T(8,128)(2,1)S(1)} %fusion.12), channel_id=1, source_target_pairs={{0,4},{1,3},{2,6},{3,1},{4,0},{5,7},{6,2},{7,5},{8,12},{9,11},{10,... | collective-permute-start | bytes 786440 | tf_op jit(solution)/shard_map/ppermute | solution.py:508
  360.2 13.3 %collective-permute-start.43 = (bf16[4,4,144,384]{3,2,1,0:T(8,128)(2,1)}, bf16[4,4,144,384]{3,2,1,0:T(8,128)(2,1)}, u32[]{:S(2)}, u32[]{:S(2)}) collective-permute-start(bf16[4,4,144,384]{3,2,1,0:T(8,128)(2,1)} %get-tuple-element.225), channel_id=1, source_target_pairs={{0,1},{1,0},{2,3},{3,2},{4,5},{5,4},{6,7},{7,6},{8,9},{9,8},{10,11... | collective-permute-start | bytes 5308424 | tf_op jit(solution)/shard_map/ppermute | solution.py:508
  362.4 10.5 %collective-permute-start.44 = (bf16[2,128,640]{2,1,0:T(8,128)(2,1)S(1)}, bf16[2,128,640]{2,1,0:T(8,128)(2,1)S(1)}, u32[]{:S(2)}, u32[]{:S(2)}) collective-permute-start(bf16[2,128,640]{2,1,0:T(8,128)(2,1)S(1)} %pad_maximum_fusion.10), channel_id=1, source_target_pairs={{0,2},{1,5},{2,0},{3,7},{4,6},{5,1},{6,4},{7,3},{8,10},{9,13},{10,... | collective-permute-start | bytes 983048 | tf_op jit(solution)/shard_map/ppermute | solution.py:508
  364.2 9.2 %collective-permute-start.45 = (bf16[1024,256]{1,0:T(8,128)(2,1)S(1)}, bf16[1024,256]{1,0:T(8,128)(2,1)S(1)}, u32[]{:S(2)}, u32[]{:S(2)}) collective-permute-start(bf16[1024,256]{1,0:T(8,128)(2,1)S(1)} %slice_dynamic-update-slice_fusion.refs_0_), channel_id=1, source_target_pairs={{0,8},{1,17},{2,10},{3,19},{4,12},{5,21},{6,14},{7,23},{8,0},{9,25... | collective-permute-start | bytes 1572872 | tf_op jit(solution)/shard_map/ppermute | solution.py:508
  376.0 13.3 %collective-permute-start.46 = (bf16[2,4,144,384]{3,2,1,0:T(8,128)(2,1)}, bf16[2,4,144,384]{3,2,1,0:T(8,128)(2,1)S(1)}, u32[]{:S(2)}, u32[]{:S(2)}) collective-permute-start(bf16[2,4,144,384]{3,2,1,0:T(8,128)(2,1)} %add_convert_fusion.5), channel_id=1, source_target_pairs={{0,8},{1,17},{2,10},{3,19},{4,12},{5,21},{6,14},{7,23},{8,0},{9,25... | collective-permute-start | bytes 2654216 | tf_op jit(solution)/shard_map/ppermute | solution.py:508
  377.2 10.0 %collective-permute-start.47 = (bf16[128,640]{1,0:T(8,128)(2,1)S(1)}, bf16[128,640]{1,0:T(8,128)(2,1)S(1)}, u32[]{:S(2)}, u32[]{:S(2)}) collective-permute-start(bf16[128,640]{1,0:T(8,128)(2,1)S(1)} %fusion.16), channel_id=1, source_target_pairs={{0,4},{1,3},{2,6},{3,1},{4,0},{5,7},{6,2},{7,5},{8,12},{9,11},{10,... | collective-permute-start | bytes 491528 | tf_op jit(solution)/shard_map/ppermute | solution.py:508
  390.6 10.1 %collective-permute-start.48 = (bf16[4,144,384]{2,1,0:T(8,128)(2,1)S(1)}, bf16[4,144,384]{2,1,0:T(8,128)(2,1)S(1)}, u32[]{:S(2)}, u32[]{:S(2)}) collective-permute-start(bf16[4,144,384]{2,1,0:T(8,128)(2,1)S(1)} %fusion.9), channel_id=1, source_target_pairs={{0,16},{1,9},{2,18},{3,11},{4,20},{5,13},{6,22},{7,15},{8,24},{9,1... | collective-permute-start | bytes 1327112 | tf_op jit(solution)/shard_map/ppermute | solution.py:508
  391.7 7.2 %collective-permute-start.49 = (bf16[128,640]{1,0:T(8,128)(2,1)S(1)}, bf16[128,640]{1,0:T(8,128)(2,1)S(1)}, u32[]{:S(2)}, u32[]{:S(2)}) collective-permute-start(bf16[128,640]{1,0:T(8,128)(2,1)S(1)} %fusion.10.refs_0_), channel_id=1, source_target_pairs={{0,8},{1,17},{2,10},{3,19},{4,12},{5,21},{6,14},{7,23},{8,0},{9,25... | collective-permute-start | bytes 491528 | tf_op jit(solution)/shard_map/ppermute | solution.py:508
  403.1 16.3 %copy-start.3 = (s32[3]{0:T(128)S(1)}, s32[3]{0:T(128)}, u32[]{:S(2)}) copy-start(s32[3]{0:T(128)} %pad_add_fusion.where) | copy-start | bytes 40
  403.1 16.2 %collective-permute-start.54 = (bf16[2,1024,256]{2,1,0:T(8,128)(2,1)}, bf16[2,1024,256]{2,1,0:T(8,128)(2,1)S(1)}, u32[]{:S(2)}, u32[]{:S(2)}) collective-permute-start(bf16[2,1024,256]{2,1,0:T(8,128)(2,1)} %pad_maximum_fusion.2), channel_id=1, source_target_pairs={{0,16},{1,9},{2,18},{3,11},{4,20},{5,13},{6,22},{7,15},{8,24},{9,1... | collective-permute-start | bytes 3145736 | tf_op jit(solution)/shard_map/ppermute | solution.py:508
  404.1 7.9 %collective-permute-start.51 = (bf16[144,384]{1,0:T(8,128)(2,1)S(1)}, bf16[144,384]{1,0:T(8,128)(2,1)S(1)}, u32[]{:S(2)}, u32[]{:S(2)}) collective-permute-start(bf16[144,384]{1,0:T(8,128)(2,1)S(1)} %get-tuple-element.259), channel_id=1, source_target_pairs={{0,6},{1,7},{2,4},{3,5},{4,2},{5,3},{6,0},{7,1},{8,14},{9,15},{10,... | collective-permute-start | bytes 331784 | tf_op jit(solution)/shard_map/ppermute | solution.py:508
  405.7 9.8 %collective-permute-start.52 = (bf16[144,384]{1,0:T(8,128)(2,1)S(1)}, bf16[144,384]{1,0:T(8,128)(2,1)S(1)}, u32[]{:S(2)}, u32[]{:S(2)}) collective-permute-start(bf16[144,384]{1,0:T(8,128)(2,1)S(1)} %get-tuple-element.258), channel_id=1, source_target_pairs={{0,4},{1,5},{2,6},{3,7},{4,0},{5,1},{6,2},{7,3},{8,12},{9,13},{10,... | collective-permute-start | bytes 331784 | tf_op jit(solution)/shard_map/ppermute | solution.py:508
  406.2 9.3 %collective-permute-start.53 = (bf16[144,384]{1,0:T(8,128)(2,1)S(1)}, bf16[144,384]{1,0:T(8,128)(2,1)S(1)}, u32[]{:S(2)}, u32[]{:S(2)}) collective-permute-start(bf16[144,384]{1,0:T(8,128)(2,1)S(1)} %get-tuple-element.257), channel_id=1, source_target_pairs={{0,2},{1,3},{2,0},{3,1},{4,6},{5,7},{6,4},{7,5},{8,10},{9,11},{10,... | collective-permute-start | bytes 331784 | tf_op jit(solution)/shard_map/ppermute | solution.py:508
  408.6 14.9 %collective-permute-start.50 = (bf16[2,128,640]{2,1,0:T(8,128)(2,1)S(1)}, bf16[2,128,640]{2,1,0:T(8,128)(2,1)S(1)}, u32[]{:S(2)}, u32[]{:S(2)}) collective-permute-start(bf16[2,128,640]{2,1,0:T(8,128)(2,1)S(1)} %pad_maximum_fusion.11), channel_id=1, source_target_pairs={{0,16},{1,9},{2,18},{3,11},{4,20},{5,13},{6,22},{7,15},{8,24},{9,1... | collective-permute-start | bytes 983048 | tf_op jit(solution)/shard_map/ppermute | solution.py:508
  415.5 8.0 %collective-permute-start.55 = (bf16[144,384]{1,0:T(8,128)(2,1)S(1)}, bf16[144,384]{1,0:T(8,128)(2,1)S(1)}, u32[]{:S(2)}, u32[]{:S(2)}) collective-permute-start(bf16[144,384]{1,0:T(8,128)(2,1)S(1)} %fusion.15.refs_4_), channel_id=1, source_target_pairs={{0,8},{1,9},{2,10},{3,11},{4,12},{5,13},{6,14},{7,15},{8,0},{9,1},... | collective-permute-start | bytes 331784 | tf_op jit(solution)/shard_map/ppermute | solution.py:508
  416.3 10.1 %collective-permute-start.56 = (bf16[144,384]{1,0:T(8,128)(2,1)S(1)}, bf16[144,384]{1,0:T(8,128)(2,1)S(1)}, u32[]{:S(2)}, u32[]{:S(2)}) collective-permute-start(bf16[144,384]{1,0:T(8,128)(2,1)S(1)} %fusion.15.refs_4_), channel_id=1, source_target_pairs={{0,16},{1,17},{2,18},{3,19},{4,20},{5,21},{6,22},{7,23},{8,24},{9,... | collective-permute-start | bytes 331784 | tf_op jit(solution)/shard_map/ppermute | solution.py:508
  417.7 8.7 %collective-permute-start.57 = (bf16[144,384]{1,0:T(8,128)(2,1)S(1)}, bf16[144,384]{1,0:T(8,128)(2,1)S(1)}, u32[]{:S(2)}, u32[]{:S(2)}) collective-permute-start(bf16[144,384]{1,0:T(8,128)(2,1)S(1)} %fusion.15.refs_4_), channel_id=1, source_target_pairs={{0,24},{1,25},{2,26},{3,27},{4,28},{5,29},{6,30},{7,31},{8,16},{9,... | collective-permute-start | bytes 331784 | tf_op jit(solution)/shard_map/ppermute | solution.py:508
  (16 other events, 52.4 us)

commit v5 on v4

--- a/solution.py
+++ b/solution.py
@@ -1520,16 +1520,15 @@
     meet(r_a.made, r_out)
     step = r_out.along()
     part = back((r_a.made, step), half, quarter, 0)
-    meet(part[1], r_out, r_in, r_a)
-    steps = (r_out.along_far(), r_in.along(), r_a.near())
+    meet(part[1], r_in, r_a)
+    steps = (r_in.along(), r_a.near())
     low_b, late_b = back(steps, half + quarter, quarter, quarter, part)
     meet(late_b, r_out, r_in, r_a)
     sums = (late_a, late_b, first_sums, second_sums, bias_in_grad)
-    share_out = r_out.share()
-    steps = (r_in.along_far(), r_a.middle(), share_out)
+    steps = (r_out.along_far(), r_in.along_far(), r_a.middle())
     r_b = Reduction(place, attention_grads(place, after(turned, *steps), low_b, sums, "b"))
-    meet(r_b.made, r_in, r_a)
-    share_in = r_in.share()
+    meet(r_b.made, r_out, r_in, r_a)
+    share_out, share_in = r_out.share(), r_in.share()
     inner = share_in.shape[1] // groups
     joined = jnp.concatenate(
         [share_out] + [share_in[:, n * inner : (n + 1) * inner] for n in range(groups)]

time: 434 us -> 439 us (1.012)
  transfers between devices with their start and end apart: 58 -> 58, of which waited for: 24 -> 23; matrix products, arithmetic and copies ran while one was open for 5% -> 7% of each run, Pallas kernels for 50% -> 50%
where the time goes in v5:
time: 439 us; the launch traced here: 435 us
  Pallas kernels  265 us (60%)
  starting transfers between devices  60.1 us (14%)
  waiting for transfers between devices  52.4 us (12%)
  other arithmetic  46.6 us (11%)
  local copies, waits for them, and re-layouts  9.12 us (2%)
    pallas_call x4, Pallas kernels, weight_call(): pl.pallas_call(body, grid_spec=pltpu.PrefetchScalarGridSpec(num_scalar_pr...  76.2 us
    ppermute x58, starting transfers between devices, permute(): return lax.ppermute(array, AXES, pairs)  60.1 us
    ppermute x58, waiting for transfers between devices, permute(): return lax.ppermute(array, AXES, pairs)  52.4 us
    pallas_call x3, Pallas kernels, attention_backward(): pl.pallas_call(body, grid=(pairs,), in_specs=[pair(0), pair(1), pair(2),...  49.3 us
    pallas_call x3, Pallas kernels, attention_forward(): pl.pallas_call(body, grid=(pairs,), in_specs=[pair(0), pair(1), pair(2),...  44.8 us
    convert_element_type x18, other arithmetic, add(): return total.astype(jnp.bfloat16)  34.1 us
    pallas_call x2, Pallas kernels, weight_grad(): pl.pallas_call(functools.partial(weight_grad_kernel, rows=rows, groups=gr...  28.1 us
    pallas_call x2, Pallas kernels, attention_grads(): pl.pallas_call(functools.partial(attention_grads_kernel, rows=rows, group...  21.1 us
  transfers between devices with their start and end apart: 58, of which 23 were waited for; matrix products, arithmetic and copies ran while one was open for 7% of the time, Pallas kernels for 50%

profile of v5, /device:TPU:0, one launch (start us, length us, event | category | flops | bytes accessed | tf_op | source)
XLA Modules:
  0.0 434.8 jit_solution(14630491255695594612)
XLA Ops:
  0.6 3.1 collective-permute-start
  3.7 1.5 concatenate.29
  6.7 2.7 collective-permute-done
  10.4 2.5 collective-permute-start.2
  12.9 2.5 collective-permute-start.3
  16.4 4.3 collective-permute-done.3
  22.9 2.7 collective-permute-start.4
  25.6 1.6 collective-permute-start.7
  27.2 1.5 collective-permute-start.8
  29.3 3.3 collective-permute-start.5
  32.6 2.0 collective-permute-done.5
  35.5 2.9 collective-permute-start.6
  40.4 2.1 vectors.1
  42.4 2.4 collective-permute-done.7.refs_1_
  49.0 5.4 %collective-permute-done.6 = bf16[2,128,1280]{2,1,0:T(8,128)(2,1)} collective-permute-done((bf16[2,128,1280]{2,1,0:T(8,128)(2,1)}, bf16[2,128,1280]{2,1,0:T(8,128)(2,1)}, u32[]{:S(2)}, u32[]{:S(2)}) %collective-permute-start.6) | collective-permute-done | bytes 655392 | tf_op jit(solution)/shard_map/ppermute | solution.py:508
  57.0 1.5 collective-permute-start.15
  61.7 12.8 %qkv.1 = (bf16[1024,3072]{1,0:T(8,128)(2,1)}, bf16[1024,3072]{1,0:T(8,128)(2,1)}) custom-call(s32[3]{0:T(128)} %pad_add_fusion.where, bf16[4,128,768]{2,1,0:T(8,128)(2,1)} %copy-done.8, bf16[4,128,768]{2,1,0:T(8,128)(2,1)} %collective-permute-done.7.refs_1_, bf16[4,128,768]{2,1,0:T(8,128)(2,1)} %collective-permute-done.8.refs_2_, ...), custom_call_target="tpu_custom_call" | custom-call | flops 12884901888 | tf_op jit(solution)/shard_map/qkv/pallas_call | solution.py:654
  74.6 2.5 collective-permute-start.17
  77.1 16.4 %attn_fwd.3 = (bf16[1024,1024]{1,0:T(8,128)(2,1)}, bf16[16,1024,1024]{2,1,0:T(8,128)(2,1)}, f32[1024,1024]{1,0:T(8,128)}) custom-call(bf16[1024,3072]{1,0:T(8,128)(2,1)} %get-tuple-element.161.q_ref.k_ref.v_ref.refs_0_.refs_1_.refs_2_, bf16[1024,3072]{1,0:T(8,128)(2,1)} %get-tuple-element.161.q_ref.k_ref.v_ref.refs_0_.refs_1_.refs_2_, ...), custom_call_target="tpu_custom_call" | custom-call | flops 12884901888 | tf_op jit(solution)/shard_map/attn_fwd/pallas_call | solution.py:391
  95.6 16.3 %attn_fwd.4 = (bf16[1024,1024]{1,0:T(8,128)(2,1)}, bf16[16,1024,1024]{2,1,0:T(8,128)(2,1)}, f32[1024,1024]{1,0:T(8,128)}) custom-call(bf16[1024,3072]{1,0:T(8,128)(2,1)} %get-tuple-element.161.q_ref.k_ref.v_ref.refs_0_.refs_1_.refs_2_, ...), custom_call_target="tpu_custom_call", output_to_operand_aliasing={{0}: (5, {}), {1}: (6, {}), {2}: (7, {})} | custom-call | flops 12884901888 | tf_op jit(solution)/shard_map/attn_fwd/pallas_call | solution.py:391
  114.2 12.1 %attn_fwd.5 = (bf16[1024,1024]{1,0:T(8,128)(2,1)}, bf16[16,1024,1024]{2,1,0:T(8,128)(2,1)}, f32[1024,1024]{1,0:T(8,128)}) custom-call(bf16[1024,3072]{1,0:T(8,128)(2,1)} %get-tuple-element.161.q_ref.k_ref.v_ref.refs_0_.refs_1_.refs_2_, ...), custom_call_target="tpu_custom_call", output_to_operand_aliasing={{0}: (5, {}), {1}: (6, {}), {2}: (7, {})} | custom-call | flops 8589934592 | tf_op jit(solution)/shard_map/attn_fwd/pallas_call | solution.py:391
  127.5 9.6 %attn_out.1 = (f32[1024,1024]{1,0:T(8,128)}, f32[1024,128]{1,0:T(8,128)}, bf16[1024,1024]{1,0:T(8,128)(2,1)}, bf16[1024,1024]{1,0:T(8,128)(2,1)}) custom-call(s32[3]{0:T(128)} %pad_add_fusion.where, bf16[4,128,1280]{2,1,0:T(8,128)(2,1)} %copy-done.4, bf16[4,128,1280]{2,1,0:T(8,128)(2,1)} %collective-permute-done.15.refs_1_, ...), custom_call_target="tpu_custom_call" | custom-call | flops 4294967296 | tf_op jit(solution)/shard_map/attn_out/pallas_call | solution.py:654
  139.3 21.3 %feed_in.1 = (bf16[1024,4096]{1,0:T(8,128)(2,1)}, bf16[1024,4096]{1,0:T(8,128)(2,1)}, bf16[1024,4096]{1,0:T(8,128)(2,1)}) custom-call(s32[3]{0:T(128)} %pad_add_fusion.where, bf16[4,128,1280]{2,1,0:T(8,128)(2,1)} %copy-done.4, bf16[4,128,1280]{2,1,0:T(8,128)(2,1)} %collective-permute-done.15.refs_1_, bf16[4,128,1280]{2,1,0:T(8,128)(2,1)} %collective-permute-done.16.refs_2_, ...), custom_call_target="tpu_custom_call" | custom-call | flops 17179869184 | tf_op jit(solution)/shard_map/feed_in/pallas_call | solution.py:654
  160.7 2.6 collective-permute-done.29.refs_7_
  164.3 32.5 %feed_out.1 = (bf16[1024,1024]{1,0:T(8,128)(2,1)}, f32[1024,1024]{1,0:T(8,128)}, bf16[1024,1024]{1,0:T(8,128)(2,1)}, f32[8,1024]{1,0:T(8,128)}, bf16[1024,4096]{1,0:T(8,128)(2,1)}, /*index=5*/f32[1,4096]{1,0:T(1,128)}) custom-call(s32[3]{0:T(128)} %pad_add_fusion.where, bf16[4,512,256]{2,1,0:T(8,128)(2,1)} %copy-done.6, ...), custom_call_target="tpu_custom_call" | custom-call | flops 34359738368 | tf_op jit(solution)/shard_map/feed_out/pallas_call | solution.py:654
  196.9 14.0 %wgrad_out.1 = (bf16[4,4,512,256]{3,2,1,0:T(8,128)(2,1)}, bf16[4,4,512,256]{3,2,1,0:T(8,128)(2,1)}) custom-call(s32[3]{0:T(128)} %pad_add_fusion.where, bf16[1024,4096]{1,0:T(8,128)(2,1)} %get-tuple-element.170.refs_8_.left_ref, bf16[1024,1024]{1,0:T(8,128)(2,1)} %get-tuple-element.178.right_ref), custom_call_target="tpu_custom_call" | custom-call | flops 17179869184 | tf_op jit(solution)/shard_map/wgrad_out/pallas_call | solution.py:1213
  211.0 14.1 %wgrad_in.1 = (bf16[4,4,128,1024]{3,2,1,0:T(8,128)(2,1)}, bf16[4,4,128,1024]{3,2,1,0:T(8,128)(2,1)}) custom-call(s32[3]{0:T(128)} %pad_add_fusion.where, bf16[1024,1024]{1,0:T(8,128)(2,1)} %get-tuple-element.180.refs_8_.left_ref, bf16[1024,4096]{1,0:T(8,128)(2,1)} %get-tuple-element.184.right_ref.p_ref), custom_call_target="tpu_custom_call" | custom-call | flops 17179869184 | tf_op jit(solution)/shard_map/wgrad_in/pallas_call | solution.py:1213
  225.5 2.7 add_convert_fusion.1
  229.6 21.0 %feed_in_back.1 = (f32[1024,1024]{1,0:T(8,128)}, bf16[1024,1024]{1,0:T(8,128)(2,1)}, bf16[1024,1024]{1,0:T(8,128)(2,1)}, f32[8,1024]{1,0:T(8,128)}) custom-call(bf16[1024,4096]{1,0:T(8,128)(2,1)} %get-tuple-element.184.right_ref.p_ref, bf16[1024,4096]{1,0:T(8,128)(2,1)} %get-tuple-element.185.w_ref, f32[1024,1024]{1,0:T(8,128)} %get-tuple-element.186.g_ref, ...), custom_call_target="tpu_custom_call" | custom-call | flops 21474836480 | tf_op jit(solution)/shard_map/feed_in_back/pallas_call | solution.py:676
  250.6 4.7 %add_convert_fusion = bf16[2,4,128,1024]{3,2,1,0:T(8,128)(2,1)} fusion(bf16[4,4,128,1024]{3,2,1,0:T(8,128)(2,1)} %collective-permute-done.31, bf16[4,4,128,1024]{3,2,1,0:T(8,128)(2,1)} %get-tuple-element.181), kind=kLoop, calls=%fused_computation | loop fusion | flops 4194304 | bytes 6291456 | tf_op jit(solution)/shard_map/convert_element_type | solution.py:1236
  256.0 22.7 %attn_bwd.3 = (bf16[3,1024,512]{2,1,0:T(8,128)(2,1)}, f32[2,512]{1,0:T(2,128)}) custom-call(bf16[1024,3072]{1,0:T(8,128)(2,1)} %get-tuple-element.161.q_ref.k_ref.v_ref.refs_0_.refs_1_.refs_2_, bf16[1024,3072]{1,0:T(8,128)(2,1)} %get-tuple-element.161.q_ref.k_ref.v_ref.refs_0_.refs_1_.refs_2_, ...), custom_call_target="tpu_custom_call" | custom-call | flops 34359738368 | tf_op jit(solution)/shard_map/attn_bwd/pallas_call | solution.py:467
  278.7 2.9 collective-permute-done.33
  281.6 3.5 fusion.4
  285.1 2.2 fusion.3
  288.0 12.3 %wgrad_a.1 = (bf16[4,4,128,640]{3,2,1,0:T(8,128)(2,1)}, bf16[4,4,128,640]{3,2,1,0:T(8,128)(2,1)}) custom-call(s32[3]{0:T(128)} %pad_add_fusion.where, bf16[2,512,1024]{2,1,0:T(8,128)(2,1)} %copy-done.1, bf16[3,1024,512]{2,1,0:T(8,128)(2,1)} %get-tuple-element.196.refs_1_.refs_0_, bf16[1024,1024]{1,0:T(8,128)(2,1)} %get-tuple-element.164.refs_8_.refs_3_.refs_2_, ...), custom_call_target="tpu_custom_call" | custom-call | flops 10737418240 | tf_op jit(solution)/shard_map/wgrad_a/pallas_call | solution.py:1171
  302.2 2.4 fusion
  306.2 13.2 %attn_bwd.4 = (bf16[3,1024,512]{2,1,0:T(8,128)(2,1)}, f32[2,512]{1,0:T(2,128)}) custom-call(bf16[1024,3072]{1,0:T(8,128)(2,1)} %get-tuple-element.161.q_ref.k_ref.v_ref.refs_0_.refs_1_.refs_2_, bf16[1024,3072]{1,0:T(8,128)(2,1)} %get-tuple-element.161.q_ref.k_ref.v_ref.refs_0_.refs_1_.refs_2_, ...), custom_call_target="tpu_custom_call" | custom-call | flops 17179869184 | tf_op jit(solution)/shard_map/attn_bwd/pallas_call | solution.py:467
  320.4 3.1 add_convert_fusion.2
  323.5 3.1 fusion.1
  326.6 1.6 collective-permute-start.39
  329.5 13.4 %attn_bwd.5 = (bf16[3,1024,512]{2,1,0:T(8,128)(2,1)}, f32[2,512]{1,0:T(2,128)}) custom-call(bf16[1024,3072]{1,0:T(8,128)(2,1)} %get-tuple-element.161.q_ref.k_ref.v_ref.refs_0_.refs_1_.refs_2_, bf16[1024,3072]{1,0:T(8,128)(2,1)} %get-tuple-element.161.q_ref.k_ref.v_ref.refs_0_.refs_1_.refs_2_, ...), custom_call_target="tpu_custom_call", output_to_operand_aliasing={{0}: (7, {}), {1}: (8, {})} | custom-call | flops 17179869184 | tf_op jit(solution)/shard_map/attn_bwd/pallas_call | solution.py:467
  343.0 1.5 collective-permute-done.39
  344.5 1.6 fusion.6
  348.3 1.7 fusion.11
  350.2 2.7 collective-permute-start.40
  352.9 8.7 %wgrad_b.1 = (bf16[4,4,144,384]{3,2,1,0:T(8,128)(2,1)}, bf16[4,4,144,384]{3,2,1,0:T(8,128)(2,1)}) custom-call(s32[3]{0:T(128)} %pad_add_fusion.where, bf16[2,512,1024]{2,1,0:T(8,128)(2,1)} %copy-done.1, bf16[3,1024,512]{2,1,0:T(8,128)(2,1)} %get-tuple-element.223.refs_1_, f32[2,512]{1,0:T(2,128)} %get-tuple-element.197.refs_2_, ...), custom_call_target="tpu_custom_call" | custom-call | flops 6442450944 | tf_op jit(solution)/shard_map/wgrad_b/pallas_call | solution.py:1171
  361.7 4.3 collective-permute-done.40
  366.0 1.9 fusion.2
  370.9 8.2 %qkv_back.2.refs_3_ = f32[1024,1024]{1,0:T(8,128)} custom-call(bf16[1024,3072]{1,0:T(8,128)(2,1)} %get-tuple-element.176.w_ref, bf16[3,1024,512]{2,1,0:T(8,128)(2,1)} %get-tuple-element.196.refs_1_.refs_0_, bf16[3,1024,512]{2,1,0:T(8,128)(2,1)} %get-tuple-element.223.refs_1_, f32[1024,1024]{1,0:T(8,128)} %get-tuple-element.228.refs_2_), custom_call_target="tpu_custom_call" | custom-call | flops 6442450944 | tf_op jit(solution)/shard_map/qkv_back/pallas_call | solution.py:1012
  379.6 2.6 add_convert_fusion.5
  383.3 1.6 collective-permute-start.47
  385.0 8.2 %qkv_back.3 = f32[1024,1024]{1,0:T(8,128)} custom-call(bf16[1024,3072]{1,0:T(8,128)(2,1)} %get-tuple-element.176.w_ref, bf16[3,1024,512]{2,1,0:T(8,128)(2,1)} %get-tuple-element.196.refs_1_.refs_0_, bf16[3,1024,512]{2,1,0:T(8,128)(2,1)} %get-tuple-element.223.refs_1_, f32[1024,1024]{1,0:T(8,128)} %get-tuple-element.228.refs_2_, ...), custom_call_target="tpu_custom_call", output_to_operand_aliasing={{}: (4, {})} | custom-call | flops 6442450944 | tf_op jit(solution)/shard_map/qkv_back/pallas_call | solution.py:1012
  393.2 2.7 collective-permute-done.46
  397.2 2.0 collective-permute-start.48
  399.6 5.0 %collective-permute-done.49.refs_1_ = bf16[128,640]{1,0:T(8,128)(2,1)S(1)} collective-permute-done((bf16[128,640]{1,0:T(8,128)(2,1)S(1)}, bf16[128,640]{1,0:T(8,128)(2,1)S(1)}, u32[]{:S(2)}, u32[]{:S(2)}) %collective-permute-start.49) | collective-permute-done | bytes 163872 | tf_op jit(solution)/shard_map/ppermute | solution.py:508
  408.0 1.9 collective-permute-start.54
  410.1 4.1 collective-permute-start.52
  414.7 2.0 collective-permute-done.51
  416.7 3.5 collective-permute-done.52
  421.7 2.1 collective-permute-start.57
  423.8 1.6 collective-permute-done.54
  425.5 2.8 order_feed_forward.1
  428.3 1.8 collective-permute-done.50
  431.3 2.1 order_attention.1
  (164 shorter events, 53.8 us)
Async XLA Ops:
  0.6 8.7 %collective-permute-start = (bf16[128,768]{1,0:T(8,128)(2,1)}, bf16[128,768]{1,0:T(8,128)(2,1)S(1)}, u32[]{:S(2)}, u32[]{:S(2)}) collective-permute-start(bf16[128,768]{1,0:T(8,128)(2,1)} %param.21), channel_id=1, source_target_pairs={{0,2},{1,5},{2,0},{3,7},{4,6},{5,1},{6,4},{7,3},{8,10},{9,13},{10,... | collective-permute-start | bytes 589832 | tf_op jit(solution)/shard_map/ppermute | solution.py:508
  5.2 1.4 collective-permute-start.1
  9.3 36.0 %copy-start = (bf16[1,1024,1024]{2,1,0:T(8,128)(2,1)S(1)}, bf16[1,1024,1024]{2,1,0:T(8,128)(2,1)}, u32[]{:S(2)}) copy-start(bf16[1,1024,1024]{2,1,0:T(8,128)(2,1)} %param.17) | copy-start | bytes 6291460
  10.4 11.5 %collective-permute-start.2 = (bf16[2,128,768]{2,1,0:T(8,128)(2,1)S(1)}, bf16[2,128,768]{2,1,0:T(8,128)(2,1)S(1)}, u32[]{:S(2)}, u32[]{:S(2)}) collective-permute-start(bf16[2,128,768]{2,1,0:T(8,128)(2,1)S(1)} %pad_maximum_fusion.8), channel_id=1, source_target_pairs={{0,4},{1,3},{2,6},{3,1},{4,0},{5,7},{6,2},{7,5},{8,12},{9,11},{10,... | collective-permute-start | bytes 1179656 | tf_op jit(solution)/shard_map/ppermute | solution.py:508
  12.9 7.8 %collective-permute-start.3 = (bf16[2,16,128]{2,1,0:T(8,128)(2,1)S(1)}, bf16[2,16,128]{2,1,0:T(8,128)(2,1)S(1)}, u32[]{:S(2)}, u32[]{:S(2)}) collective-permute-start(bf16[2,16,128]{2,1,0:T(8,128)(2,1)S(1)} %get-tuple-element.273), channel_id=1, source_target_pairs={{0,2},{1,5},{2,0},{3,7},{4,6},{5,1},{6,4},{7,3},{8,10},{9,13},{10,... | collective-permute-start | bytes 24584 | tf_op jit(solution)/shard_map/ppermute | solution.py:508
  22.9 24.2 %copy-start.8 = (bf16[4,128,768]{2,1,0:T(8,128)(2,1)}, bf16[4,128,768]{2,1,0:T(8,128)(2,1)S(1)}, u32[]{:S(2)}) copy-start(bf16[4,128,768]{2,1,0:T(8,128)(2,1)S(1)} %pad_maximum_fusion.3.refs_0_) | copy-start | bytes 2359300
  22.9 11.7 %collective-permute-start.4 = (bf16[128,1280]{1,0:T(8,128)(2,1)S(1)}, bf16[128,1280]{1,0:T(8,128)(2,1)S(1)}, u32[]{:S(2)}, u32[]{:S(2)}) collective-permute-start(bf16[128,1280]{1,0:T(8,128)(2,1)S(1)} %pad_maximum_fusion.9), channel_id=1, source_target_pairs={{0,2},{1,5},{2,0},{3,7},{4,6},{5,1},{6,4},{7,3},{8,10},{9,13},{10,... | collective-permute-start | bytes 983048 | tf_op jit(solution)/shard_map/ppermute | solution.py:508
  25.6 19.2 %collective-permute-start.7 = (bf16[4,128,768]{2,1,0:T(8,128)(2,1)S(1)}, bf16[4,128,768]{2,1,0:T(8,128)(2,1)}, u32[]{:S(2)}, u32[]{:S(2)}) collective-permute-start(bf16[4,128,768]{2,1,0:T(8,128)(2,1)S(1)} %pad_maximum_fusion.3.refs_0_), channel_id=1, source_target_pairs={{0,8},{1,17},{2,10},{3,19},{4,12},{5,21},{6,14},{7,23},{8,0},{9,25... | collective-permute-start | bytes 2359304 | tf_op jit(solution)/shard_map/ppermute | solution.py:508
  27.2 17.6 %collective-permute-start.8 = (bf16[4,128,768]{2,1,0:T(8,128)(2,1)S(1)}, bf16[4,128,768]{2,1,0:T(8,128)(2,1)}, u32[]{:S(2)}, u32[]{:S(2)}) collective-permute-start(bf16[4,128,768]{2,1,0:T(8,128)(2,1)S(1)} %pad_maximum_fusion.3.refs_0_), channel_id=1, source_target_pairs={{0,16},{1,9},{2,18},{3,11},{4,20},{5,13},{6,22},{7,15},{8,24},{9,1... | collective-permute-start | bytes 2359304 | tf_op jit(solution)/shard_map/ppermute | solution.py:508
  29.3 5.3 %collective-permute-start.5 = (bf16[2,2,16,128]{3,2,1,0:T(8,128)(2,1)}, bf16[2,2,16,128]{3,2,1,0:T(8,128)(2,1)}, u32[]{:S(2)}, u32[]{:S(2)}) collective-permute-start(bf16[2,2,16,128]{3,2,1,0:T(8,128)(2,1)} %pad_maximum_fusion.13), channel_id=1, source_target_pairs={{0,4},{1,3},{2,6},{3,1},{4,0},{5,7},{6,2},{7,5},{8,12},{9,11},{10,... | collective-permute-start | bytes 49160 | tf_op jit(solution)/shard_map/ppermute | solution.py:508
  35.5 18.8 %collective-permute-start.6 = (bf16[2,128,1280]{2,1,0:T(8,128)(2,1)}, bf16[2,128,1280]{2,1,0:T(8,128)(2,1)}, u32[]{:S(2)}, u32[]{:S(2)}) collective-permute-start(bf16[2,128,1280]{2,1,0:T(8,128)(2,1)} %pad_maximum_fusion.4), channel_id=1, source_target_pairs={{0,4},{1,3},{2,6},{3,1},{4,0},{5,7},{6,2},{7,5},{8,12},{9,11},{10,... | collective-permute-start | bytes 1966088 | tf_op jit(solution)/shard_map/ppermute | solution.py:508
  44.8 12.2 %collective-permute-start.9 = (bf16[4,128,768]{2,1,0:T(8,128)(2,1)}, bf16[4,128,768]{2,1,0:T(8,128)(2,1)S(1)}, u32[]{:S(2)}, u32[]{:S(2)}) collective-permute-start(bf16[4,128,768]{2,1,0:T(8,128)(2,1)} %collective-permute-done.7.refs_1_), channel_id=1, source_target_pairs={{0,16},{1,9},{2,18},{3,11},{4,20},{5,13},{6,22},{7,15},{8,24},{9,1... | collective-permute-start | bytes 2359304 | tf_op jit(solution)/shard_map/ppermute | solution.py:508
  45.3 13.2 %collective-permute-start.10 = (bf16[4,128,768]{2,1,0:T(8,128)(2,1)S(1)}, bf16[4,128,768]{2,1,0:T(8,128)(2,1)S(1)}, u32[]{:S(2)}, u32[]{:S(2)}) collective-permute-start(bf16[4,128,768]{2,1,0:T(8,128)(2,1)S(1)} %pad_maximum_fusion.3.refs_0_), channel_id=1, source_target_pairs={{0,1},{1,0},{2,3},{3,2},{4,5},{5,4},{6,7},{7,6},{8,9},{9,8},{10,11... | collective-permute-start | bytes 2359304 | tf_op jit(solution)/shard_map/ppermute | solution.py:508
  48.5 10.6 %collective-permute-start.11 = (bf16[4,128,768]{2,1,0:T(8,128)(2,1)}, bf16[4,128,768]{2,1,0:T(8,128)(2,1)S(1)}, u32[]{:S(2)}, u32[]{:S(2)}) collective-permute-start(bf16[4,128,768]{2,1,0:T(8,128)(2,1)} %collective-permute-done.7.refs_1_), channel_id=1, source_target_pairs={{0,1},{1,0},{2,3},{3,2},{4,5},{5,4},{6,7},{7,6},{8,9},{9,8},{10,11... | collective-permute-start | bytes 2359304 | tf_op jit(solution)/shard_map/ppermute | solution.py:508
  49.0 11.0 %collective-permute-start.12 = (bf16[4,128,768]{2,1,0:T(8,128)(2,1)}, bf16[4,128,768]{2,1,0:T(8,128)(2,1)S(1)}, u32[]{:S(2)}, u32[]{:S(2)}) collective-permute-start(bf16[4,128,768]{2,1,0:T(8,128)(2,1)} %collective-permute-done.8.refs_2_), channel_id=1, source_target_pairs={{0,1},{1,0},{2,3},{3,2},{4,5},{5,4},{6,7},{7,6},{8,9},{9,8},{10,11... | collective-permute-start | bytes 2359304 | tf_op jit(solution)/shard_map/ppermute | solution.py:508
  55.6 21.5 %copy-start.4 = (bf16[4,128,1280]{2,1,0:T(8,128)(2,1)}, bf16[4,128,1280]{2,1,0:T(8,128)(2,1)S(1)}, u32[]{:S(2)}) copy-start(bf16[4,128,1280]{2,1,0:T(8,128)(2,1)S(1)} %pad_maximum_fusion.refs_0_) | copy-start | bytes 3932164
  57.0 2.9 collective-permute-start.13
  57.0 36.4 %collective-permute-start.15 = (bf16[4,128,1280]{2,1,0:T(8,128)(2,1)S(1)}, bf16[4,128,1280]{2,1,0:T(8,128)(2,1)}, u32[]{:S(2)}, u32[]{:S(2)}) collective-permute-start(bf16[4,128,1280]{2,1,0:T(8,128)(2,1)S(1)} %pad_maximum_fusion.refs_0_), channel_id=1, source_target_pairs={{0,8},{1,17},{2,10},{3,19},{4,12},{5,21},{6,14},{7,23},{8,0},{9,25... | collective-permute-start | bytes 3932168 | tf_op jit(solution)/shard_map/ppermute | solution.py:508
  58.5 34.9 %collective-permute-start.16 = (bf16[4,128,1280]{2,1,0:T(8,128)(2,1)S(1)}, bf16[4,128,1280]{2,1,0:T(8,128)(2,1)}, u32[]{:S(2)}, u32[]{:S(2)}) collective-permute-start(bf16[4,128,1280]{2,1,0:T(8,128)(2,1)S(1)} %pad_maximum_fusion.refs_0_), channel_id=1, source_target_pairs={{0,16},{1,9},{2,18},{3,11},{4,20},{5,13},{6,22},{7,15},{8,24},{9,1... | collective-permute-start | bytes 3932168 | tf_op jit(solution)/shard_map/ppermute | solution.py:508
  59.0 15.5 %collective-permute-start.14 = (bf16[512,256]{1,0:T(8,128)(2,1)S(1)}, bf16[512,256]{1,0:T(8,128)(2,1)S(1)}, u32[]{:S(2)}, u32[]{:S(2)}) collective-permute-start(bf16[512,256]{1,0:T(8,128)(2,1)S(1)} %copy-done.7), channel_id=1, source_target_pairs={{0,2},{1,5},{2,0},{3,7},{4,6},{5,1},{6,4},{7,3},{8,10},{9,13},{10,... | collective-permute-start | bytes 786440 | tf_op jit(solution)/shard_map/ppermute | solution.py:508
  74.6 18.9 %collective-permute-start.17 = (bf16[2,512,256]{2,1,0:T(8,128)(2,1)S(1)}, bf16[2,512,256]{2,1,0:T(8,128)(2,1)S(1)}, u32[]{:S(2)}, u32[]{:S(2)}) collective-permute-start(bf16[2,512,256]{2,1,0:T(8,128)(2,1)S(1)} %pad_maximum_fusion.5), channel_id=1, source_target_pairs={{0,4},{1,3},{2,6},{3,1},{4,0},{5,7},{6,2},{7,5},{8,12},{9,11},{10,... | collective-permute-start | bytes 1572872 | tf_op jit(solution)/shard_map/ppermute | solution.py:508
  77.1 35.8 %collective-permute-start.19 = (bf16[4,128,1280]{2,1,0:T(8,128)(2,1)S(1)}, bf16[4,128,1280]{2,1,0:T(8,128)(2,1)}, u32[]{:S(2)}, u32[]{:S(2)}) collective-permute-start(bf16[4,128,1280]{2,1,0:T(8,128)(2,1)S(1)} %pad_maximum_fusion.refs_0_), channel_id=1, source_target_pairs={{0,1},{1,0},{2,3},{3,2},{4,5},{5,4},{6,7},{7,6},{8,9},{9,8},{10,11... | collective-permute-start | bytes 3932168 | tf_op jit(solution)/shard_map/ppermute | solution.py:508
  93.4 18.5 %collective-permute-start.18 = (bf16[4,128,1280]{2,1,0:T(8,128)(2,1)}, bf16[4,128,1280]{2,1,0:T(8,128)(2,1)}, u32[]{:S(2)}, u32[]{:S(2)}) collective-permute-start(bf16[4,128,1280]{2,1,0:T(8,128)(2,1)} %collective-permute-done.15.refs_1_), channel_id=1, source_target_pairs={{0,16},{1,9},{2,18},{3,11},{4,20},{5,13},{6,22},{7,15},{8,24},{9,1... | collective-permute-start | bytes 3932168 | tf_op jit(solution)/shard_map/ppermute | solution.py:508
  94.9 31.4 %collective-permute-start.20 = (bf16[4,128,1280]{2,1,0:T(8,128)(2,1)}, bf16[4,128,1280]{2,1,0:T(8,128)(2,1)}, u32[]{:S(2)}, u32[]{:S(2)}) collective-permute-start(bf16[4,128,1280]{2,1,0:T(8,128)(2,1)} %collective-permute-done.15.refs_1_), channel_id=1, source_target_pairs={{0,1},{1,0},{2,3},{3,2},{4,5},{5,4},{6,7},{7,6},{8,9},{9,8},{10,11... | collective-permute-start | bytes 3932168 | tf_op jit(solution)/shard_map/ppermute | solution.py:508
  95.0 31.3 %copy-start.6 = (bf16[4,512,256]{2,1,0:T(8,128)(2,1)}, bf16[4,512,256]{2,1,0:T(8,128)(2,1)S(1)}, u32[]{:S(2)}) copy-start(bf16[4,512,256]{2,1,0:T(8,128)(2,1)S(1)} %pad_maximum_fusion.1.refs_0_) | copy-start | bytes 3145732
  95.0 31.4 %collective-permute-start.21 = (bf16[4,128,1280]{2,1,0:T(8,128)(2,1)}, bf16[4,128,1280]{2,1,0:T(8,128)(2,1)S(1)}, u32[]{:S(2)}, u32[]{:S(2)}) collective-permute-start(bf16[4,128,1280]{2,1,0:T(8,128)(2,1)} %collective-permute-done.16.refs_2_), channel_id=1, source_target_pairs={{0,1},{1,0},{2,3},{3,2},{4,5},{5,4},{6,7},{7,6},{8,9},{9,8},{10,11... | collective-permute-start | bytes 3932168 | tf_op jit(solution)/shard_map/ppermute | solution.py:508
  111.9 14.5 %collective-permute-start.22 = (bf16[4,128,1280]{2,1,0:T(8,128)(2,1)}, bf16[4,128,1280]{2,1,0:T(8,128)(2,1)}, u32[]{:S(2)}, u32[]{:S(2)}) collective-permute-start(bf16[4,128,1280]{2,1,0:T(8,128)(2,1)} %collective-permute-done.18.refs_3_), channel_id=1, source_target_pairs={{0,1},{1,0},{2,3},{3,2},{4,5},{5,4},{6,7},{7,6},{8,9},{9,8},{10,11... | collective-permute-start | bytes 3932168 | tf_op jit(solution)/shard_map/ppermute | solution.py:508
  112.3 25.9 %collective-permute-start.23 = (bf16[4,512,256]{2,1,0:T(8,128)(2,1)S(1)}, bf16[4,512,256]{2,1,0:T(8,128)(2,1)}, u32[]{:S(2)}, u32[]{:S(2)}) collective-permute-start(bf16[4,512,256]{2,1,0:T(8,128)(2,1)S(1)} %pad_maximum_fusion.1.refs_0_), channel_id=1, source_target_pairs={{0,8},{1,17},{2,10},{3,19},{4,12},{5,21},{6,14},{7,23},{8,0},{9,25... | collective-permute-start | bytes 3145736 | tf_op jit(solution)/shard_map/ppermute | solution.py:508
  112.8 25.4 %collective-permute-start.24 = (bf16[4,512,256]{2,1,0:T(8,128)(2,1)S(1)}, bf16[4,512,256]{2,1,0:T(8,128)(2,1)S(1)}, u32[]{:S(2)}, u32[]{:S(2)}) collective-permute-start(bf16[4,512,256]{2,1,0:T(8,128)(2,1)S(1)} %pad_maximum_fusion.1.refs_0_), channel_id=1, source_target_pairs={{0,16},{1,9},{2,18},{3,11},{4,20},{5,13},{6,22},{7,15},{8,24},{9,1... | collective-permute-start | bytes 3145736 | tf_op jit(solution)/shard_map/ppermute | solution.py:508
  126.3 34.4 %collective-permute-start.26 = (bf16[4,512,256]{2,1,0:T(8,128)(2,1)S(1)}, bf16[4,512,256]{2,1,0:T(8,128)(2,1)}, u32[]{:S(2)}, u32[]{:S(2)}) collective-permute-start(bf16[4,512,256]{2,1,0:T(8,128)(2,1)S(1)} %pad_maximum_fusion.1.refs_0_), channel_id=1, source_target_pairs={{0,1},{1,0},{2,3},{3,2},{4,5},{5,4},{6,7},{7,6},{8,9},{9,8},{10,11... | collective-permute-start | bytes 3145736 | tf_op jit(solution)/shard_map/ppermute | solution.py:508
  138.2 22.4 %copy-start.13 = (bf16[4,512,256]{2,1,0:T(8,128)(2,1)}, bf16[4,512,256]{2,1,0:T(8,128)(2,1)S(1)}, u32[]{:S(2)}) copy-start(bf16[4,512,256]{2,1,0:T(8,128)(2,1)S(1)} %collective-permute-done.24.refs_2_) | copy-start | bytes 3145732
  138.2 22.4 %collective-permute-start.25 = (bf16[4,512,256]{2,1,0:T(8,128)(2,1)}, bf16[4,512,256]{2,1,0:T(8,128)(2,1)S(1)}, u32[]{:S(2)}, u32[]{:S(2)}) collective-permute-start(bf16[4,512,256]{2,1,0:T(8,128)(2,1)} %collective-permute-done.23.refs_1_), channel_id=1, source_target_pairs={{0,16},{1,9},{2,18},{3,11},{4,20},{5,13},{6,22},{7,15},{8,24},{9,1... | collective-permute-start | bytes 3145736 | tf_op jit(solution)/shard_map/ppermute | solution.py:508
  138.8 22.0 %collective-permute-start.27 = (bf16[4,512,256]{2,1,0:T(8,128)(2,1)}, bf16[4,512,256]{2,1,0:T(8,128)(2,1)}, u32[]{:S(2)}, u32[]{:S(2)}) collective-permute-start(bf16[4,512,256]{2,1,0:T(8,128)(2,1)} %collective-permute-done.23.refs_1_), channel_id=1, source_target_pairs={{0,1},{1,0},{2,3},{3,2},{4,5},{5,4},{6,7},{7,6},{8,9},{9,8},{10,11... | collective-permute-start | bytes 3145736 | tf_op jit(solution)/shard_map/ppermute | solution.py:508
  138.8 22.0 %collective-permute-start.28 = (bf16[4,512,256]{2,1,0:T(8,128)(2,1)S(1)}, bf16[4,512,256]{2,1,0:T(8,128)(2,1)}, u32[]{:S(2)}, u32[]{:S(2)}) collective-permute-start(bf16[4,512,256]{2,1,0:T(8,128)(2,1)S(1)} %collective-permute-done.24.refs_2_), channel_id=1, source_target_pairs={{0,1},{1,0},{2,3},{3,2},{4,5},{5,4},{6,7},{7,6},{8,9},{9,8},{10,11... | collective-permute-start | bytes 3145736 | tf_op jit(solution)/shard_map/ppermute | solution.py:508
  160.6 2.7 collective-permute-start.29
  210.9 14.6 %collective-permute-start.30 = (bf16[4,4,512,256]{3,2,1,0:T(8,128)(2,1)}, bf16[4,4,512,256]{3,2,1,0:T(8,128)(2,1)}, u32[]{:S(2)}, u32[]{:S(2)}) collective-permute-start(bf16[4,4,512,256]{3,2,1,0:T(8,128)(2,1)} %get-tuple-element.182), channel_id=1, source_target_pairs={{0,1},{1,0},{2,3},{3,2},{4,5},{5,4},{6,7},{7,6},{8,9},{9,8},{10,11... | collective-permute-start | bytes 12582920 | tf_op jit(solution)/shard_map/ppermute | solution.py:508
  225.1 25.5 %collective-permute-start.31 = (bf16[4,4,128,1024]{3,2,1,0:T(8,128)(2,1)}, bf16[4,4,128,1024]{3,2,1,0:T(8,128)(2,1)}, u32[]{:S(2)}, u32[]{:S(2)}) collective-permute-start(bf16[4,4,128,1024]{3,2,1,0:T(8,128)(2,1)} %get-tuple-element.191), channel_id=1, source_target_pairs={{0,1},{1,0},{2,3},{3,2},{4,5},{5,4},{6,7},{7,6},{8,9},{9,8},{10,11... | collective-permute-start | bytes 12582920 | tf_op jit(solution)/shard_map/ppermute | solution.py:508
  228.2 53.4 %collective-permute-start.32 = (bf16[2,4,512,256]{3,2,1,0:T(8,128)(2,1)S(1)}, bf16[2,4,512,256]{3,2,1,0:T(8,128)(2,1)}, u32[]{:S(2)}, u32[]{:S(2)}) collective-permute-start(bf16[2,4,512,256]{3,2,1,0:T(8,128)(2,1)S(1)} %add_convert_fusion.1), channel_id=1, source_target_pairs={{0,8},{1,17},{2,10},{3,19},{4,12},{5,21},{6,14},{7,23},{8,0},{9,25... | collective-permute-start | bytes 6291464 | tf_op jit(solution)/shard_map/ppermute | solution.py:508
  255.3 26.4 %collective-permute-start.33 = (bf16[2,4,128,1024]{3,2,1,0:T(8,128)(2,1)}, bf16[2,4,128,1024]{3,2,1,0:T(8,128)(2,1)}, u32[]{:S(2)}, u32[]{:S(2)}) collective-permute-start(bf16[2,4,128,1024]{3,2,1,0:T(8,128)(2,1)} %add_convert_fusion), channel_id=1, source_target_pairs={{0,8},{1,17},{2,10},{3,19},{4,12},{5,21},{6,14},{7,23},{8,0},{9,25... | collective-permute-start | bytes 6291464 | tf_op jit(solution)/shard_map/ppermute | solution.py:508
  287.3 14.9 %collective-permute-start.34 = (bf16[4,512,256]{2,1,0:T(8,128)(2,1)S(1)}, bf16[4,512,256]{2,1,0:T(8,128)(2,1)S(1)}, u32[]{:S(2)}, u32[]{:S(2)}) collective-permute-start(bf16[4,512,256]{2,1,0:T(8,128)(2,1)S(1)} %fusion.3), channel_id=1, source_target_pairs={{0,16},{1,9},{2,18},{3,11},{4,20},{5,13},{6,22},{7,15},{8,24},{9,1... | collective-permute-start | bytes 3145736 | tf_op jit(solution)/shard_map/ppermute | solution.py:508
  300.4 19.0 %collective-permute-start.36 = (bf16[4,4,128,640]{3,2,1,0:T(8,128)(2,1)}, bf16[4,4,128,640]{3,2,1,0:T(8,128)(2,1)}, u32[]{:S(2)}, u32[]{:S(2)}) collective-permute-start(bf16[4,4,128,640]{3,2,1,0:T(8,128)(2,1)} %get-tuple-element.205), channel_id=1, source_target_pairs={{0,1},{1,0},{2,3},{3,2},{4,5},{5,4},{6,7},{7,6},{8,9},{9,8},{10,11... | collective-permute-start | bytes 7864328 | tf_op jit(solution)/shard_map/ppermute | solution.py:508
  300.4 19.0 %collective-permute-start.35 = (bf16[4,128,1024]{2,1,0:T(8,128)(2,1)}, bf16[4,128,1024]{2,1,0:T(8,128)(2,1)S(1)}, u32[]{:S(2)}, u32[]{:S(2)}) collective-permute-start(bf16[4,128,1024]{2,1,0:T(8,128)(2,1)} %fusion.4), channel_id=1, source_target_pairs={{0,16},{1,9},{2,18},{3,11},{4,20},{5,13},{6,22},{7,15},{8,24},{9,1... | collective-permute-start | bytes 3145736 | tf_op jit(solution)/shard_map/ppermute | solution.py:508
  305.5 37.5 %collective-permute-start.37 = (bf16[2,512,256]{2,1,0:T(8,128)(2,1)}, bf16[2,512,256]{2,1,0:T(8,128)(2,1)}, u32[]{:S(2)}, u32[]{:S(2)}) collective-permute-start(bf16[2,512,256]{2,1,0:T(8,128)(2,1)} %pad_maximum_fusion.6), channel_id=1, source_target_pairs={{0,2},{1,5},{2,0},{3,7},{4,6},{5,1},{6,4},{7,3},{8,10},{9,13},{10,... | collective-permute-start | bytes 1572872 | tf_op jit(solution)/shard_map/ppermute | solution.py:508
  326.6 17.9 %collective-permute-start.39 = (bf16[2,4,128,640]{3,2,1,0:T(8,128)(2,1)}, bf16[2,4,128,640]{3,2,1,0:T(8,128)(2,1)S(1)}, u32[]{:S(2)}, u32[]{:S(2)}) collective-permute-start(bf16[2,4,128,640]{3,2,1,0:T(8,128)(2,1)} %add_convert_fusion.2), channel_id=1, source_target_pairs={{0,8},{1,17},{2,10},{3,19},{4,12},{5,21},{6,14},{7,23},{8,0},{9,25... | collective-permute-start | bytes 3932168 | tf_op jit(solution)/shard_map/ppermute | solution.py:508
  329.1 13.9 %collective-permute-start.38 = (bf16[2,128,1024]{2,1,0:T(8,128)(2,1)}, bf16[2,128,1024]{2,1,0:T(8,128)(2,1)S(1)}, u32[]{:S(2)}, u32[]{:S(2)}) collective-permute-start(bf16[2,128,1024]{2,1,0:T(8,128)(2,1)} %pad_maximum_fusion.7), channel_id=1, source_target_pairs={{0,2},{1,5},{2,0},{3,7},{4,6},{5,1},{6,4},{7,3},{8,10},{9,13},{10,... | collective-permute-start | bytes 1572872 | tf_op jit(solution)/shard_map/ppermute | solution.py:508
  346.1 19.9 %collective-permute-start.42 = (bf16[4,128,640]{2,1,0:T(8,128)(2,1)S(1)}, bf16[4,128,640]{2,1,0:T(8,128)(2,1)}, u32[]{:S(2)}, u32[]{:S(2)}) collective-permute-start(bf16[4,128,640]{2,1,0:T(8,128)(2,1)S(1)} %fusion.6), channel_id=1, source_target_pairs={{0,16},{1,9},{2,18},{3,11},{4,20},{5,13},{6,22},{7,15},{8,24},{9,1... | collective-permute-start | bytes 1966088 | tf_op jit(solution)/shard_map/ppermute | solution.py:508
  350.0 11.7 %collective-permute-start.41 = (bf16[128,1024]{1,0:T(8,128)(2,1)}, bf16[128,1024]{1,0:T(8,128)(2,1)}, u32[]{:S(2)}, u32[]{:S(2)}) collective-permute-start(bf16[128,1024]{1,0:T(8,128)(2,1)} %fusion.12), channel_id=1, source_target_pairs={{0,4},{1,3},{2,6},{3,1},{4,0},{5,7},{6,2},{7,5},{8,12},{9,11},{10,... | collective-permute-start | bytes 786440 | tf_op jit(solution)/shard_map/ppermute | solution.py:508
  350.2 15.8 %collective-permute-start.40 = (bf16[512,256]{1,0:T(8,128)(2,1)}, bf16[512,256]{1,0:T(8,128)(2,1)}, u32[]{:S(2)}, u32[]{:S(2)}) collective-permute-start(bf16[512,256]{1,0:T(8,128)(2,1)} %fusion.11), channel_id=1, source_target_pairs={{0,4},{1,3},{2,6},{3,1},{4,0},{5,7},{6,2},{7,5},{8,12},{9,11},{10,... | collective-permute-start | bytes 786440 | tf_op jit(solution)/shard_map/ppermute | solution.py:508
  361.7 17.9 %collective-permute-start.43 = (bf16[4,4,144,384]{3,2,1,0:T(8,128)(2,1)}, bf16[4,4,144,384]{3,2,1,0:T(8,128)(2,1)}, u32[]{:S(2)}, u32[]{:S(2)}) collective-permute-start(bf16[4,4,144,384]{3,2,1,0:T(8,128)(2,1)} %get-tuple-element.225), channel_id=1, source_target_pairs={{0,1},{1,0},{2,3},{3,2},{4,5},{5,4},{6,7},{7,6},{8,9},{9,8},{10,11... | collective-permute-start | bytes 5308424 | tf_op jit(solution)/shard_map/ppermute | solution.py:508
  368.0 11.2 %collective-permute-start.44 = (bf16[2,128,640]{2,1,0:T(8,128)(2,1)S(1)}, bf16[2,128,640]{2,1,0:T(8,128)(2,1)S(1)}, u32[]{:S(2)}, u32[]{:S(2)}) collective-permute-start(bf16[2,128,640]{2,1,0:T(8,128)(2,1)S(1)} %pad_maximum_fusion.10), channel_id=1, source_target_pairs={{0,2},{1,5},{2,0},{3,7},{4,6},{5,1},{6,4},{7,3},{8,10},{9,13},{10,... | collective-permute-start | bytes 983048 | tf_op jit(solution)/shard_map/ppermute | solution.py:508
  370.4 9.2 %collective-permute-start.45 = (bf16[1024,256]{1,0:T(8,128)(2,1)S(1)}, bf16[1024,256]{1,0:T(8,128)(2,1)S(1)}, u32[]{:S(2)}, u32[]{:S(2)}) collective-permute-start(bf16[1024,256]{1,0:T(8,128)(2,1)S(1)} %slice_dynamic-update-slice_fusion.refs_0_), channel_id=1, source_target_pairs={{0,8},{1,17},{2,10},{3,19},{4,12},{5,21},{6,14},{7,23},{8,0},{9,25... | collective-permute-start | bytes 1572872 | tf_op jit(solution)/shard_map/ppermute | solution.py:508
  382.2 13.7 %collective-permute-start.46 = (bf16[2,4,144,384]{3,2,1,0:T(8,128)(2,1)}, bf16[2,4,144,384]{3,2,1,0:T(8,128)(2,1)S(1)}, u32[]{:S(2)}, u32[]{:S(2)}) collective-permute-start(bf16[2,4,144,384]{3,2,1,0:T(8,128)(2,1)} %add_convert_fusion.5), channel_id=1, source_target_pairs={{0,8},{1,17},{2,10},{3,19},{4,12},{5,21},{6,14},{7,23},{8,0},{9,25... | collective-permute-start | bytes 2654216 | tf_op jit(solution)/shard_map/ppermute | solution.py:508
  383.3 9.9 %collective-permute-start.47 = (bf16[128,640]{1,0:T(8,128)(2,1)S(1)}, bf16[128,640]{1,0:T(8,128)(2,1)S(1)}, u32[]{:S(2)}, u32[]{:S(2)}) collective-permute-start(bf16[128,640]{1,0:T(8,128)(2,1)S(1)} %fusion.17), channel_id=1, source_target_pairs={{0,4},{1,3},{2,6},{3,1},{4,0},{5,7},{6,2},{7,5},{8,12},{9,11},{10,... | collective-permute-start | bytes 491528 | tf_op jit(solution)/shard_map/ppermute | solution.py:508
  397.2 8.4 %collective-permute-start.48 = (bf16[4,144,384]{2,1,0:T(8,128)(2,1)S(1)}, bf16[4,144,384]{2,1,0:T(8,128)(2,1)S(1)}, u32[]{:S(2)}, u32[]{:S(2)}) collective-permute-start(bf16[4,144,384]{2,1,0:T(8,128)(2,1)S(1)} %fusion.9), channel_id=1, source_target_pairs={{0,16},{1,9},{2,18},{3,11},{4,20},{5,13},{6,22},{7,15},{8,24},{9,1... | collective-permute-start | bytes 1327112 | tf_op jit(solution)/shard_map/ppermute | solution.py:508
  399.3 5.4 %collective-permute-start.49 = (bf16[128,640]{1,0:T(8,128)(2,1)S(1)}, bf16[128,640]{1,0:T(8,128)(2,1)S(1)}, u32[]{:S(2)}, u32[]{:S(2)}) collective-permute-start(bf16[128,640]{1,0:T(8,128)(2,1)S(1)} %fusion.10.refs_0_), channel_id=1, source_target_pairs={{0,8},{1,17},{2,10},{3,19},{4,12},{5,21},{6,14},{7,23},{8,0},{9,25... | collective-permute-start | bytes 491528 | tf_op jit(solution)/shard_map/ppermute | solution.py:508
  408.0 17.5 %copy-start.3 = (s32[3]{0:T(128)S(1)}, s32[3]{0:T(128)}, u32[]{:S(2)}) copy-start(s32[3]{0:T(128)} %pad_add_fusion.where) | copy-start | bytes 40
  408.0 17.4 %collective-permute-start.54 = (bf16[2,1024,256]{2,1,0:T(8,128)(2,1)}, bf16[2,1024,256]{2,1,0:T(8,128)(2,1)S(1)}, u32[]{:S(2)}, u32[]{:S(2)}) collective-permute-start(bf16[2,1024,256]{2,1,0:T(8,128)(2,1)} %pad_maximum_fusion.2), channel_id=1, source_target_pairs={{0,16},{1,9},{2,18},{3,11},{4,20},{5,13},{6,22},{7,15},{8,24},{9,1... | collective-permute-start | bytes 3145736 | tf_op jit(solution)/shard_map/ppermute | solution.py:508
  410.0 6.7 %collective-permute-start.51 = (bf16[144,384]{1,0:T(8,128)(2,1)S(1)}, bf16[144,384]{1,0:T(8,128)(2,1)S(1)}, u32[]{:S(2)}, u32[]{:S(2)}) collective-permute-start(bf16[144,384]{1,0:T(8,128)(2,1)S(1)} %get-tuple-element.257), channel_id=1, source_target_pairs={{0,6},{1,7},{2,4},{3,5},{4,2},{5,3},{6,0},{7,1},{8,14},{9,15},{10,... | collective-permute-start | bytes 331784 | tf_op jit(solution)/shard_map/ppermute | solution.py:508
  410.1 10.1 %collective-permute-start.52 = (bf16[144,384]{1,0:T(8,128)(2,1)S(1)}, bf16[144,384]{1,0:T(8,128)(2,1)S(1)}, u32[]{:S(2)}, u32[]{:S(2)}) collective-permute-start(bf16[144,384]{1,0:T(8,128)(2,1)S(1)} %get-tuple-element.256), channel_id=1, source_target_pairs={{0,4},{1,5},{2,6},{3,7},{4,0},{5,1},{6,2},{7,3},{8,12},{9,13},{10,... | collective-permute-start | bytes 331784 | tf_op jit(solution)/shard_map/ppermute | solution.py:508
  414.1 6.0 %collective-permute-start.53 = (bf16[144,384]{1,0:T(8,128)(2,1)S(1)}, bf16[144,384]{1,0:T(8,128)(2,1)S(1)}, u32[]{:S(2)}, u32[]{:S(2)}) collective-permute-start(bf16[144,384]{1,0:T(8,128)(2,1)S(1)} %get-tuple-element.255), channel_id=1, source_target_pairs={{0,2},{1,3},{2,0},{3,1},{4,6},{5,7},{6,4},{7,5},{8,10},{9,11},{10,... | collective-permute-start | bytes 331784 | tf_op jit(solution)/shard_map/ppermute | solution.py:508
  414.5 15.6 %collective-permute-start.50 = (bf16[2,128,640]{2,1,0:T(8,128)(2,1)S(1)}, bf16[2,128,640]{2,1,0:T(8,128)(2,1)S(1)}, u32[]{:S(2)}, u32[]{:S(2)}) collective-permute-start(bf16[2,128,640]{2,1,0:T(8,128)(2,1)S(1)} %pad_maximum_fusion.11), channel_id=1, source_target_pairs={{0,16},{1,9},{2,18},{3,11},{4,20},{5,13},{6,22},{7,15},{8,24},{9,1... | collective-permute-start | bytes 983048 | tf_op jit(solution)/shard_map/ppermute | solution.py:508
  420.2 9.9 %collective-permute-start.55 = (bf16[144,384]{1,0:T(8,128)(2,1)S(1)}, bf16[144,384]{1,0:T(8,128)(2,1)S(1)}, u32[]{:S(2)}, u32[]{:S(2)}) collective-permute-start(bf16[144,384]{1,0:T(8,128)(2,1)S(1)} %fusion.16.refs_4_), channel_id=1, source_target_pairs={{0,8},{1,9},{2,10},{3,11},{4,12},{5,13},{6,14},{7,15},{8,0},{9,1},... | collective-permute-start | bytes 331784 | tf_op jit(solution)/shard_map/ppermute | solution.py:508
  420.6 10.7 %collective-permute-start.56 = (bf16[144,384]{1,0:T(8,128)(2,1)S(1)}, bf16[144,384]{1,0:T(8,128)(2,1)S(1)}, u32[]{:S(2)}, u32[]{:S(2)}) collective-permute-start(bf16[144,384]{1,0:T(8,128)(2,1)S(1)} %fusion.16.refs_4_), channel_id=1, source_target_pairs={{0,16},{1,17},{2,18},{3,19},{4,20},{5,21},{6,22},{7,23},{8,24},{9,... | collective-permute-start | bytes 331784 | tf_op jit(solution)/shard_map/ppermute | solution.py:508
  421.7 9.6 %collective-permute-start.57 = (bf16[144,384]{1,0:T(8,128)(2,1)S(1)}, bf16[144,384]{1,0:T(8,128)(2,1)S(1)}, u32[]{:S(2)}, u32[]{:S(2)}) collective-permute-start(bf16[144,384]{1,0:T(8,128)(2,1)S(1)} %fusion.16.refs_4_), channel_id=1, source_target_pairs={{0,24},{1,25},{2,26},{3,27},{4,28},{5,29},{6,30},{7,31},{8,16},{9,... | collective-permute-start | bytes 331784 | tf_op jit(solution)/shard_map/ppermute | solution.py:508
  (15 other events, 33.8 us)

commit v6 on v4

--- a/solution.py
+++ b/solution.py
@@ -1512,8 +1512,10 @@
         )
 
     low_a, late_a = back((step,), 0, half, 0)
-    meet(late_a, r_out, r_in)
-    steps = (r_out.middle(), r_in.middle())
+    meet(late_a, r_out)
+    step = r_out.middle()
+    meet(step, r_in)
+    steps = (step, r_in.middle())
     r_a = Reduction(
         place, attention_grads(place, after(turned, *steps), low_a, (contexts, attn_low), "a")
     )

time: 434 us -> 431 us (level)
  waiting for transfers between devices: 53.7 us -> 49.2 us
    ppermute x58, waiting for transfers between devices: 53.7 us -> 49.2 us  [permute(): return lax.ppermute(array, AXES, pairs)]
  transfers between devices with their start and end apart: 58 -> 58, of which waited for: 24 -> 21; matrix products, arithmetic and copies ran while one was open for 5% -> 6% of each run, Pallas kernels for 50% -> 51%
where the time goes in v6:
time: 431 us; the launch traced here: 427 us
  Pallas kernels  265 us (61%)
  starting transfers between devices  60.2 us (14%)
  waiting for transfers between devices  49.2 us (11%)
  other arithmetic  43 us (10%)
  local copies, waits for them, and re-layouts  8.15 us (2%)
    pallas_call x4, Pallas kernels, weight_call(): pl.pallas_call(body, grid_spec=pltpu.PrefetchScalarGridSpec(num_scalar_pr...  76.3 us
    ppermute x58, starting transfers between devices, permute(): return lax.ppermute(array, AXES, pairs)  60.2 us
    pallas_call x3, Pallas kernels, attention_backward(): pl.pallas_call(body, grid=(pairs,), in_specs=[pair(0), pair(1), pair(2),...  49.3 us
    ppermute x58, waiting for transfers between devices, permute(): return lax.ppermute(array, AXES, pairs)  49.2 us
    pallas_call x3, Pallas kernels, attention_forward(): pl.pallas_call(body, grid=(pairs,), in_specs=[pair(0), pair(1), pair(2),...  44.8 us
    convert_element_type x18, other arithmetic, add(): return total.astype(jnp.bfloat16)  33.2 us
    pallas_call x2, Pallas kernels, weight_grad(): pl.pallas_call(functools.partial(weight_grad_kernel, rows=rows, groups=gr...  28 us
    pallas_call x2, Pallas kernels, attention_grads(): pl.pallas_call(functools.partial(attention_grads_kernel, rows=rows, group...  21.1 us
  transfers between devices with their start and end apart: 58, of which 21 were waited for; matrix products, arithmetic and copies ran while one was open for 6% of the time, Pallas kernels for 51%

profile of v6, /device:TPU:0, one launch (start us, length us, event | category | flops | bytes accessed | tf_op | source)
XLA Modules:
  0.0 427.2 jit_solution(6154243172460171642)
XLA Ops:
  0.6 3.1 collective-permute-start
  3.7 1.5 concatenate.29
  6.7 2.7 collective-permute-done
  10.4 2.5 collective-permute-start.2
  12.9 2.5 collective-permute-start.3
  16.4 4.3 %collective-permute-done.3 = bf16[2,16,128]{2,1,0:T(8,128)(2,1)S(1)} collective-permute-done((bf16[2,16,128]{2,1,0:T(8,128)(2,1)S(1)}, bf16[2,16,128]{2,1,0:T(8,128)(2,1)S(1)}, u32[]{:S(2)}, u32[]{:S(2)}) %collective-permute-start.3) | collective-permute-done | bytes 8224 | tf_op jit(solution)/shard_map/ppermute | solution.py:508
  22.9 2.7 collective-permute-start.4
  25.6 1.6 collective-permute-start.7
  27.2 1.5 collective-permute-start.8
  29.3 3.3 collective-permute-start.5
  32.6 2.0 collective-permute-done.5
  35.5 2.9 collective-permute-start.6
  40.4 2.0 vectors.1
  42.4 2.4 collective-permute-done.7.refs_1_
  49.0 5.4 %collective-permute-done.6 = bf16[2,128,1280]{2,1,0:T(8,128)(2,1)} collective-permute-done((bf16[2,128,1280]{2,1,0:T(8,128)(2,1)}, bf16[2,128,1280]{2,1,0:T(8,128)(2,1)}, u32[]{:S(2)}, u32[]{:S(2)}) %collective-permute-start.6) | collective-permute-done | bytes 655392 | tf_op jit(solution)/shard_map/ppermute | solution.py:508
  57.0 1.5 collective-permute-start.15
  61.7 12.7 %qkv.1 = (bf16[1024,3072]{1,0:T(8,128)(2,1)}, bf16[1024,3072]{1,0:T(8,128)(2,1)}) custom-call(s32[3]{0:T(128)} %pad_add_fusion.where, bf16[4,128,768]{2,1,0:T(8,128)(2,1)} %copy-done.7, bf16[4,128,768]{2,1,0:T(8,128)(2,1)} %collective-permute-done.7.refs_1_, bf16[4,128,768]{2,1,0:T(8,128)(2,1)} %collective-permute-done.8.refs_2_, ...), custom_call_target="tpu_custom_call" | custom-call | flops 12884901888 | tf_op jit(solution)/shard_map/qkv/pallas_call | solution.py:654
  74.5 2.5 collective-permute-start.17
  77.1 16.4 %attn_fwd.3 = (bf16[1024,1024]{1,0:T(8,128)(2,1)}, bf16[16,1024,1024]{2,1,0:T(8,128)(2,1)}, f32[1024,1024]{1,0:T(8,128)}) custom-call(bf16[1024,3072]{1,0:T(8,128)(2,1)} %get-tuple-element.161.q_ref.k_ref.v_ref.refs_0_.refs_1_.refs_2_, bf16[1024,3072]{1,0:T(8,128)(2,1)} %get-tuple-element.161.q_ref.k_ref.v_ref.refs_0_.refs_1_.refs_2_, ...), custom_call_target="tpu_custom_call" | custom-call | flops 12884901888 | tf_op jit(solution)/shard_map/attn_fwd/pallas_call | solution.py:391
  93.4 1.5 collective-permute-start.18
  95.6 16.3 %attn_fwd.4 = (bf16[1024,1024]{1,0:T(8,128)(2,1)}, bf16[16,1024,1024]{2,1,0:T(8,128)(2,1)}, f32[1024,1024]{1,0:T(8,128)}) custom-call(bf16[1024,3072]{1,0:T(8,128)(2,1)} %get-tuple-element.161.q_ref.k_ref.v_ref.refs_0_.refs_1_.refs_2_, ...), custom_call_target="tpu_custom_call", output_to_operand_aliasing={{0}: (5, {}), {1}: (6, {}), {2}: (7, {})} | custom-call | flops 12884901888 | tf_op jit(solution)/shard_map/attn_fwd/pallas_call | solution.py:391
  114.2 12.1 %attn_fwd.5 = (bf16[1024,1024]{1,0:T(8,128)(2,1)}, bf16[16,1024,1024]{2,1,0:T(8,128)(2,1)}, f32[1024,1024]{1,0:T(8,128)}) custom-call(bf16[1024,3072]{1,0:T(8,128)(2,1)} %get-tuple-element.161.q_ref.k_ref.v_ref.refs_0_.refs_1_.refs_2_, ...), custom_call_target="tpu_custom_call", output_to_operand_aliasing={{0}: (5, {}), {1}: (6, {}), {2}: (7, {})} | custom-call | flops 8589934592 | tf_op jit(solution)/shard_map/attn_fwd/pallas_call | solution.py:391
  127.5 9.6 %attn_out.1 = (f32[1024,1024]{1,0:T(8,128)}, f32[1024,128]{1,0:T(8,128)}, bf16[1024,1024]{1,0:T(8,128)(2,1)}, bf16[1024,1024]{1,0:T(8,128)(2,1)}) custom-call(s32[3]{0:T(128)} %pad_add_fusion.where, bf16[4,128,1280]{2,1,0:T(8,128)(2,1)} %copy-done.4, bf16[4,128,1280]{2,1,0:T(8,128)(2,1)} %collective-permute-done.15.refs_1_, ...), custom_call_target="tpu_custom_call" | custom-call | flops 4294967296 | tf_op jit(solution)/shard_map/attn_out/pallas_call | solution.py:654
  139.3 21.3 %feed_in.1 = (bf16[1024,4096]{1,0:T(8,128)(2,1)}, bf16[1024,4096]{1,0:T(8,128)(2,1)}, bf16[1024,4096]{1,0:T(8,128)(2,1)}) custom-call(s32[3]{0:T(128)} %pad_add_fusion.where, bf16[4,128,1280]{2,1,0:T(8,128)(2,1)} %copy-done.4, bf16[4,128,1280]{2,1,0:T(8,128)(2,1)} %collective-permute-done.15.refs_1_, bf16[4,128,1280]{2,1,0:T(8,128)(2,1)} %collective-permute-done.16.refs_2_, ...), custom_call_target="tpu_custom_call" | custom-call | flops 17179869184 | tf_op jit(solution)/shard_map/feed_in/pallas_call | solution.py:654
  160.8 2.6 collective-permute-done.29.refs_7_
  164.4 32.5 %feed_out.1 = (bf16[1024,1024]{1,0:T(8,128)(2,1)}, f32[1024,1024]{1,0:T(8,128)}, bf16[1024,1024]{1,0:T(8,128)(2,1)}, f32[8,1024]{1,0:T(8,128)}, bf16[1024,4096]{1,0:T(8,128)(2,1)}, /*index=5*/f32[1,4096]{1,0:T(1,128)}) custom-call(s32[3]{0:T(128)} %pad_add_fusion.where, bf16[4,512,256]{2,1,0:T(8,128)(2,1)} %copy-done.5, ...), custom_call_target="tpu_custom_call" | custom-call | flops 34359738368 | tf_op jit(solution)/shard_map/feed_out/pallas_call | solution.py:654
  197.0 13.9 %wgrad_out.1 = (bf16[4,4,512,256]{3,2,1,0:T(8,128)(2,1)}, bf16[4,4,512,256]{3,2,1,0:T(8,128)(2,1)}) custom-call(s32[3]{0:T(128)} %pad_add_fusion.where, bf16[1024,4096]{1,0:T(8,128)(2,1)} %get-tuple-element.170.refs_8_.left_ref, bf16[1024,1024]{1,0:T(8,128)(2,1)} %get-tuple-element.178.right_ref), custom_call_target="tpu_custom_call" | custom-call | flops 17179869184 | tf_op jit(solution)/shard_map/wgrad_out/pallas_call | solution.py:1213
  211.1 14.1 %wgrad_in.1 = (bf16[4,4,128,1024]{3,2,1,0:T(8,128)(2,1)}, bf16[4,4,128,1024]{3,2,1,0:T(8,128)(2,1)}) custom-call(s32[3]{0:T(128)} %pad_add_fusion.where, bf16[1024,1024]{1,0:T(8,128)(2,1)} %get-tuple-element.180.refs_8_.left_ref, bf16[1024,4096]{1,0:T(8,128)(2,1)} %get-tuple-element.184.right_ref.p_ref), custom_call_target="tpu_custom_call" | custom-call | flops 17179869184 | tf_op jit(solution)/shard_map/wgrad_in/pallas_call | solution.py:1213
  225.5 2.7 add_convert_fusion.1
  229.6 21.0 %feed_in_back.1 = (f32[1024,1024]{1,0:T(8,128)}, bf16[1024,1024]{1,0:T(8,128)(2,1)}, bf16[1024,1024]{1,0:T(8,128)(2,1)}, f32[8,1024]{1,0:T(8,128)}) custom-call(bf16[1024,4096]{1,0:T(8,128)(2,1)} %get-tuple-element.184.right_ref.p_ref, bf16[1024,4096]{1,0:T(8,128)(2,1)} %get-tuple-element.185.w_ref, f32[1024,1024]{1,0:T(8,128)} %get-tuple-element.186.g_ref, ...), custom_call_target="tpu_custom_call" | custom-call | flops 21474836480 | tf_op jit(solution)/shard_map/feed_in_back/pallas_call | solution.py:676
  250.6 4.7 %add_convert_fusion = bf16[2,4,128,1024]{3,2,1,0:T(8,128)(2,1)} fusion(bf16[4,4,128,1024]{3,2,1,0:T(8,128)(2,1)} %collective-permute-done.31, bf16[4,4,128,1024]{3,2,1,0:T(8,128)(2,1)} %get-tuple-element.181), kind=kLoop, calls=%fused_computation | loop fusion | flops 4194304 | bytes 6291456 | tf_op jit(solution)/shard_map/convert_element_type | solution.py:1236
  256.0 22.7 %attn_bwd.3 = (bf16[3,1024,512]{2,1,0:T(8,128)(2,1)}, f32[2,512]{1,0:T(2,128)}) custom-call(bf16[1024,3072]{1,0:T(8,128)(2,1)} %get-tuple-element.161.q_ref.k_ref.v_ref.refs_0_.refs_1_.refs_2_, bf16[1024,3072]{1,0:T(8,128)(2,1)} %get-tuple-element.161.q_ref.k_ref.v_ref.refs_0_.refs_1_.refs_2_, ...), custom_call_target="tpu_custom_call" | custom-call | flops 34359738368 | tf_op jit(solution)/shard_map/attn_bwd/pallas_call | solution.py:467
  278.7 2.2 fusion.3
  281.0 1.5 collective-permute-start.34
  282.4 3.5 fusion.4
  285.9 12.4 %wgrad_a.1 = (bf16[4,4,128,640]{3,2,1,0:T(8,128)(2,1)}, bf16[4,4,128,640]{3,2,1,0:T(8,128)(2,1)}) custom-call(s32[3]{0:T(128)} %pad_add_fusion.where, bf16[2,512,1024]{2,1,0:T(8,128)(2,1)} %copy-done.1, bf16[3,1024,512]{2,1,0:T(8,128)(2,1)} %get-tuple-element.196.refs_1_.refs_0_, bf16[1024,1024]{1,0:T(8,128)(2,1)} %get-tuple-element.164.refs_8_.refs_3_.refs_2_, ...), custom_call_target="tpu_custom_call" | custom-call | flops 10737418240 | tf_op jit(solution)/shard_map/wgrad_a/pallas_call | solution.py:1171
  298.9 2.4 fusion.1
  301.4 1.6 collective-permute-start.35
  303.0 13.2 %attn_bwd.4 = (bf16[3,1024,512]{2,1,0:T(8,128)(2,1)}, f32[2,512]{1,0:T(2,128)}) custom-call(bf16[1024,3072]{1,0:T(8,128)(2,1)} %get-tuple-element.161.q_ref.k_ref.v_ref.refs_0_.refs_1_.refs_2_, bf16[1024,3072]{1,0:T(8,128)(2,1)} %get-tuple-element.161.q_ref.k_ref.v_ref.refs_0_.refs_1_.refs_2_, ...), custom_call_target="tpu_custom_call" | custom-call | flops 17179869184 | tf_op jit(solution)/shard_map/attn_bwd/pallas_call | solution.py:467
  316.2 3.3 add_convert_fusion.2
  319.5 3.1 fusion
  326.3 13.4 %attn_bwd.5 = (bf16[3,1024,512]{2,1,0:T(8,128)(2,1)}, f32[2,512]{1,0:T(2,128)}) custom-call(bf16[1024,3072]{1,0:T(8,128)(2,1)} %get-tuple-element.161.q_ref.k_ref.v_ref.refs_0_.refs_1_.refs_2_, bf16[1024,3072]{1,0:T(8,128)(2,1)} %get-tuple-element.161.q_ref.k_ref.v_ref.refs_0_.refs_1_.refs_2_, ...), custom_call_target="tpu_custom_call", output_to_operand_aliasing={{0}: (7, {}), {1}: (8, {})} | custom-call | flops 17179869184 | tf_op jit(solution)/shard_map/attn_bwd/pallas_call | solution.py:467
  339.7 2.6 collective-permute-done.38
  342.3 2.1 collective-permute-done.39
  344.3 1.9 fusion.6
  348.2 8.8 %wgrad_b.1 = (bf16[4,4,144,384]{3,2,1,0:T(8,128)(2,1)}, bf16[4,4,144,384]{3,2,1,0:T(8,128)(2,1)}) custom-call(s32[3]{0:T(128)} %pad_add_fusion.where, bf16[2,512,1024]{2,1,0:T(8,128)(2,1)} %copy-done.1, bf16[3,1024,512]{2,1,0:T(8,128)(2,1)} %get-tuple-element.223.refs_1_, f32[2,512]{1,0:T(2,128)} %get-tuple-element.197.refs_2_, ...), custom_call_target="tpu_custom_call" | custom-call | flops 6442450944 | tf_op jit(solution)/shard_map/wgrad_b/pallas_call | solution.py:1171
  357.1 2.1 fusion.2
  360.8 1.9 collective-permute-start.45
  362.7 8.2 %qkv_back.2.refs_3_ = f32[1024,1024]{1,0:T(8,128)} custom-call(bf16[1024,3072]{1,0:T(8,128)(2,1)} %get-tuple-element.176.w_ref, bf16[3,1024,512]{2,1,0:T(8,128)(2,1)} %get-tuple-element.196.refs_1_.refs_0_, bf16[3,1024,512]{2,1,0:T(8,128)(2,1)} %get-tuple-element.223.refs_1_, f32[1024,1024]{1,0:T(8,128)} %get-tuple-element.228.refs_2_), custom_call_target="tpu_custom_call" | custom-call | flops 6442450944 | tf_op jit(solution)/shard_map/qkv_back/pallas_call | solution.py:1012
  370.9 2.6 add_convert_fusion.5
  374.5 1.6 collective-permute-start.47
  376.1 8.2 %qkv_back.3 = f32[1024,1024]{1,0:T(8,128)} custom-call(bf16[1024,3072]{1,0:T(8,128)(2,1)} %get-tuple-element.176.w_ref, bf16[3,1024,512]{2,1,0:T(8,128)(2,1)} %get-tuple-element.196.refs_1_.refs_0_, bf16[3,1024,512]{2,1,0:T(8,128)(2,1)} %get-tuple-element.223.refs_1_, f32[1024,1024]{1,0:T(8,128)} %get-tuple-element.228.refs_2_, ...), custom_call_target="tpu_custom_call", output_to_operand_aliasing={{}: (4, {})} | custom-call | flops 6442450944 | tf_op jit(solution)/shard_map/qkv_back/pallas_call | solution.py:1012
  384.3 2.4 collective-permute-done.46
  390.0 6.0 %collective-permute-done.49.refs_1_ = bf16[128,640]{1,0:T(8,128)(2,1)S(1)} collective-permute-done((bf16[128,640]{1,0:T(8,128)(2,1)S(1)}, bf16[128,640]{1,0:T(8,128)(2,1)S(1)}, u32[]{:S(2)}, u32[]{:S(2)}) %collective-permute-start.49) | collective-permute-done | bytes 163872 | tf_op jit(solution)/shard_map/ppermute | solution.py:508
  396.1 1.9 collective-permute-done.48
  401.3 1.8 collective-permute-start.51
  403.7 2.1 collective-permute-start.53
  407.1 2.1 collective-permute-done.51
  409.2 3.2 collective-permute-done.52
  412.5 1.5 collective-permute-start.55
  414.6 1.5 collective-permute-start.57
  416.2 2.8 order_feed_forward.1
  419.0 3.5 collective-permute-done.50
  423.7 2.1 order_attention.1
  (166 shorter events, 49.9 us)
Async XLA Ops:
  0.6 8.7 %collective-permute-start = (bf16[128,768]{1,0:T(8,128)(2,1)}, bf16[128,768]{1,0:T(8,128)(2,1)S(1)}, u32[]{:S(2)}, u32[]{:S(2)}) collective-permute-start(bf16[128,768]{1,0:T(8,128)(2,1)} %param.21), channel_id=1, source_target_pairs={{0,2},{1,5},{2,0},{3,7},{4,6},{5,1},{6,4},{7,3},{8,10},{9,13},{10,... | collective-permute-start | bytes 589832 | tf_op jit(solution)/shard_map/ppermute | solution.py:508
  5.2 1.4 collective-permute-start.1
  9.3 36.0 %copy-start = (bf16[1,1024,1024]{2,1,0:T(8,128)(2,1)S(1)}, bf16[1,1024,1024]{2,1,0:T(8,128)(2,1)}, u32[]{:S(2)}) copy-start(bf16[1,1024,1024]{2,1,0:T(8,128)(2,1)} %param.17) | copy-start | bytes 6291460
  10.4 11.5 %collective-permute-start.2 = (bf16[2,128,768]{2,1,0:T(8,128)(2,1)S(1)}, bf16[2,128,768]{2,1,0:T(8,128)(2,1)S(1)}, u32[]{:S(2)}, u32[]{:S(2)}) collective-permute-start(bf16[2,128,768]{2,1,0:T(8,128)(2,1)S(1)} %pad_maximum_fusion.8), channel_id=1, source_target_pairs={{0,4},{1,3},{2,6},{3,1},{4,0},{5,7},{6,2},{7,5},{8,12},{9,11},{10,... | collective-permute-start | bytes 1179656 | tf_op jit(solution)/shard_map/ppermute | solution.py:508
  12.9 7.8 %collective-permute-start.3 = (bf16[2,16,128]{2,1,0:T(8,128)(2,1)S(1)}, bf16[2,16,128]{2,1,0:T(8,128)(2,1)S(1)}, u32[]{:S(2)}, u32[]{:S(2)}) collective-permute-start(bf16[2,16,128]{2,1,0:T(8,128)(2,1)S(1)} %get-tuple-element.275), channel_id=1, source_target_pairs={{0,2},{1,5},{2,0},{3,7},{4,6},{5,1},{6,4},{7,3},{8,10},{9,13},{10,... | collective-permute-start | bytes 24584 | tf_op jit(solution)/shard_map/ppermute | solution.py:508
  22.9 24.2 %copy-start.7 = (bf16[4,128,768]{2,1,0:T(8,128)(2,1)}, bf16[4,128,768]{2,1,0:T(8,128)(2,1)S(1)}, u32[]{:S(2)}) copy-start(bf16[4,128,768]{2,1,0:T(8,128)(2,1)S(1)} %pad_maximum_fusion.3.refs_0_) | copy-start | bytes 2359300
  22.9 11.7 %collective-permute-start.4 = (bf16[128,1280]{1,0:T(8,128)(2,1)S(1)}, bf16[128,1280]{1,0:T(8,128)(2,1)S(1)}, u32[]{:S(2)}, u32[]{:S(2)}) collective-permute-start(bf16[128,1280]{1,0:T(8,128)(2,1)S(1)} %pad_maximum_fusion.9), channel_id=1, source_target_pairs={{0,2},{1,5},{2,0},{3,7},{4,6},{5,1},{6,4},{7,3},{8,10},{9,13},{10,... | collective-permute-start | bytes 983048 | tf_op jit(solution)/shard_map/ppermute | solution.py:508
  25.6 19.2 %collective-permute-start.7 = (bf16[4,128,768]{2,1,0:T(8,128)(2,1)S(1)}, bf16[4,128,768]{2,1,0:T(8,128)(2,1)}, u32[]{:S(2)}, u32[]{:S(2)}) collective-permute-start(bf16[4,128,768]{2,1,0:T(8,128)(2,1)S(1)} %pad_maximum_fusion.3.refs_0_), channel_id=1, source_target_pairs={{0,8},{1,17},{2,10},{3,19},{4,12},{5,21},{6,14},{7,23},{8,0},{9,25... | collective-permute-start | bytes 2359304 | tf_op jit(solution)/shard_map/ppermute | solution.py:508
  27.2 17.6 %collective-permute-start.8 = (bf16[4,128,768]{2,1,0:T(8,128)(2,1)S(1)}, bf16[4,128,768]{2,1,0:T(8,128)(2,1)}, u32[]{:S(2)}, u32[]{:S(2)}) collective-permute-start(bf16[4,128,768]{2,1,0:T(8,128)(2,1)S(1)} %pad_maximum_fusion.3.refs_0_), channel_id=1, source_target_pairs={{0,16},{1,9},{2,18},{3,11},{4,20},{5,13},{6,22},{7,15},{8,24},{9,1... | collective-permute-start | bytes 2359304 | tf_op jit(solution)/shard_map/ppermute | solution.py:508
  29.3 5.3 %collective-permute-start.5 = (bf16[2,2,16,128]{3,2,1,0:T(8,128)(2,1)}, bf16[2,2,16,128]{3,2,1,0:T(8,128)(2,1)}, u32[]{:S(2)}, u32[]{:S(2)}) collective-permute-start(bf16[2,2,16,128]{3,2,1,0:T(8,128)(2,1)} %pad_maximum_fusion.13), channel_id=1, source_target_pairs={{0,4},{1,3},{2,6},{3,1},{4,0},{5,7},{6,2},{7,5},{8,12},{9,11},{10,... | collective-permute-start | bytes 49160 | tf_op jit(solution)/shard_map/ppermute | solution.py:508
  35.5 18.8 %collective-permute-start.6 = (bf16[2,128,1280]{2,1,0:T(8,128)(2,1)}, bf16[2,128,1280]{2,1,0:T(8,128)(2,1)}, u32[]{:S(2)}, u32[]{:S(2)}) collective-permute-start(bf16[2,128,1280]{2,1,0:T(8,128)(2,1)} %pad_maximum_fusion.4), channel_id=1, source_target_pairs={{0,4},{1,3},{2,6},{3,1},{4,0},{5,7},{6,2},{7,5},{8,12},{9,11},{10,... | collective-permute-start | bytes 1966088 | tf_op jit(solution)/shard_map/ppermute | solution.py:508
  44.8 12.2 %collective-permute-start.9 = (bf16[4,128,768]{2,1,0:T(8,128)(2,1)}, bf16[4,128,768]{2,1,0:T(8,128)(2,1)S(1)}, u32[]{:S(2)}, u32[]{:S(2)}) collective-permute-start(bf16[4,128,768]{2,1,0:T(8,128)(2,1)} %collective-permute-done.7.refs_1_), channel_id=1, source_target_pairs={{0,16},{1,9},{2,18},{3,11},{4,20},{5,13},{6,22},{7,15},{8,24},{9,1... | collective-permute-start | bytes 2359304 | tf_op jit(solution)/shard_map/ppermute | solution.py:508
  45.3 13.2 %collective-permute-start.10 = (bf16[4,128,768]{2,1,0:T(8,128)(2,1)S(1)}, bf16[4,128,768]{2,1,0:T(8,128)(2,1)S(1)}, u32[]{:S(2)}, u32[]{:S(2)}) collective-permute-start(bf16[4,128,768]{2,1,0:T(8,128)(2,1)S(1)} %pad_maximum_fusion.3.refs_0_), channel_id=1, source_target_pairs={{0,1},{1,0},{2,3},{3,2},{4,5},{5,4},{6,7},{7,6},{8,9},{9,8},{10,11... | collective-permute-start | bytes 2359304 | tf_op jit(solution)/shard_map/ppermute | solution.py:508
  48.5 10.6 %collective-permute-start.11 = (bf16[4,128,768]{2,1,0:T(8,128)(2,1)}, bf16[4,128,768]{2,1,0:T(8,128)(2,1)S(1)}, u32[]{:S(2)}, u32[]{:S(2)}) collective-permute-start(bf16[4,128,768]{2,1,0:T(8,128)(2,1)} %collective-permute-done.7.refs_1_), channel_id=1, source_target_pairs={{0,1},{1,0},{2,3},{3,2},{4,5},{5,4},{6,7},{7,6},{8,9},{9,8},{10,11... | collective-permute-start | bytes 2359304 | tf_op jit(solution)/shard_map/ppermute | solution.py:508
  49.0 11.0 %collective-permute-start.12 = (bf16[4,128,768]{2,1,0:T(8,128)(2,1)}, bf16[4,128,768]{2,1,0:T(8,128)(2,1)S(1)}, u32[]{:S(2)}, u32[]{:S(2)}) collective-permute-start(bf16[4,128,768]{2,1,0:T(8,128)(2,1)} %collective-permute-done.8.refs_2_), channel_id=1, source_target_pairs={{0,1},{1,0},{2,3},{3,2},{4,5},{5,4},{6,7},{7,6},{8,9},{9,8},{10,11... | collective-permute-start | bytes 2359304 | tf_op jit(solution)/shard_map/ppermute | solution.py:508
  55.6 21.5 %copy-start.4 = (bf16[4,128,1280]{2,1,0:T(8,128)(2,1)}, bf16[4,128,1280]{2,1,0:T(8,128)(2,1)S(1)}, u32[]{:S(2)}) copy-start(bf16[4,128,1280]{2,1,0:T(8,128)(2,1)S(1)} %pad_maximum_fusion.refs_0_) | copy-start | bytes 3932164
  57.0 2.9 collective-permute-start.13
  57.0 36.4 %collective-permute-start.15 = (bf16[4,128,1280]{2,1,0:T(8,128)(2,1)S(1)}, bf16[4,128,1280]{2,1,0:T(8,128)(2,1)}, u32[]{:S(2)}, u32[]{:S(2)}) collective-permute-start(bf16[4,128,1280]{2,1,0:T(8,128)(2,1)S(1)} %pad_maximum_fusion.refs_0_), channel_id=1, source_target_pairs={{0,8},{1,17},{2,10},{3,19},{4,12},{5,21},{6,14},{7,23},{8,0},{9,25... | collective-permute-start | bytes 3932168 | tf_op jit(solution)/shard_map/ppermute | solution.py:508
  58.5 34.9 %collective-permute-start.16 = (bf16[4,128,1280]{2,1,0:T(8,128)(2,1)S(1)}, bf16[4,128,1280]{2,1,0:T(8,128)(2,1)}, u32[]{:S(2)}, u32[]{:S(2)}) collective-permute-start(bf16[4,128,1280]{2,1,0:T(8,128)(2,1)S(1)} %pad_maximum_fusion.refs_0_), channel_id=1, source_target_pairs={{0,16},{1,9},{2,18},{3,11},{4,20},{5,13},{6,22},{7,15},{8,24},{9,1... | collective-permute-start | bytes 3932168 | tf_op jit(solution)/shard_map/ppermute | solution.py:508
  59.0 15.4 %collective-permute-start.14 = (bf16[512,256]{1,0:T(8,128)(2,1)S(1)}, bf16[512,256]{1,0:T(8,128)(2,1)S(1)}, u32[]{:S(2)}, u32[]{:S(2)}) collective-permute-start(bf16[512,256]{1,0:T(8,128)(2,1)S(1)} %copy-done.6), channel_id=1, source_target_pairs={{0,2},{1,5},{2,0},{3,7},{4,6},{5,1},{6,4},{7,3},{8,10},{9,13},{10,... | collective-permute-start | bytes 786440 | tf_op jit(solution)/shard_map/ppermute | solution.py:508
  74.5 18.9 %collective-permute-start.17 = (bf16[2,512,256]{2,1,0:T(8,128)(2,1)S(1)}, bf16[2,512,256]{2,1,0:T(8,128)(2,1)S(1)}, u32[]{:S(2)}, u32[]{:S(2)}) collective-permute-start(bf16[2,512,256]{2,1,0:T(8,128)(2,1)S(1)} %pad_maximum_fusion.5), channel_id=1, source_target_pairs={{0,4},{1,3},{2,6},{3,1},{4,0},{5,7},{6,2},{7,5},{8,12},{9,11},{10,... | collective-permute-start | bytes 1572872 | tf_op jit(solution)/shard_map/ppermute | solution.py:508
  77.0 35.8 %collective-permute-start.19 = (bf16[4,128,1280]{2,1,0:T(8,128)(2,1)S(1)}, bf16[4,128,1280]{2,1,0:T(8,128)(2,1)}, u32[]{:S(2)}, u32[]{:S(2)}) collective-permute-start(bf16[4,128,1280]{2,1,0:T(8,128)(2,1)S(1)} %pad_maximum_fusion.refs_0_), channel_id=1, source_target_pairs={{0,1},{1,0},{2,3},{3,2},{4,5},{5,4},{6,7},{7,6},{8,9},{9,8},{10,11... | collective-permute-start | bytes 3932168 | tf_op jit(solution)/shard_map/ppermute | solution.py:508
  93.4 18.5 %collective-permute-start.18 = (bf16[4,128,1280]{2,1,0:T(8,128)(2,1)}, bf16[4,128,1280]{2,1,0:T(8,128)(2,1)}, u32[]{:S(2)}, u32[]{:S(2)}) collective-permute-start(bf16[4,128,1280]{2,1,0:T(8,128)(2,1)} %collective-permute-done.15.refs_1_), channel_id=1, source_target_pairs={{0,16},{1,9},{2,18},{3,11},{4,20},{5,13},{6,22},{7,15},{8,24},{9,1... | collective-permute-start | bytes 3932168 | tf_op jit(solution)/shard_map/ppermute | solution.py:508
  94.9 31.4 %collective-permute-start.20 = (bf16[4,128,1280]{2,1,0:T(8,128)(2,1)}, bf16[4,128,1280]{2,1,0:T(8,128)(2,1)}, u32[]{:S(2)}, u32[]{:S(2)}) collective-permute-start(bf16[4,128,1280]{2,1,0:T(8,128)(2,1)} %collective-permute-done.15.refs_1_), channel_id=1, source_target_pairs={{0,1},{1,0},{2,3},{3,2},{4,5},{5,4},{6,7},{7,6},{8,9},{9,8},{10,11... | collective-permute-start | bytes 3932168 | tf_op jit(solution)/shard_map/ppermute | solution.py:508
  95.0 31.3 %copy-start.5 = (bf16[4,512,256]{2,1,0:T(8,128)(2,1)}, bf16[4,512,256]{2,1,0:T(8,128)(2,1)S(1)}, u32[]{:S(2)}) copy-start(bf16[4,512,256]{2,1,0:T(8,128)(2,1)S(1)} %pad_maximum_fusion.1.refs_0_) | copy-start | bytes 3145732
  95.0 31.4 %collective-permute-start.21 = (bf16[4,128,1280]{2,1,0:T(8,128)(2,1)}, bf16[4,128,1280]{2,1,0:T(8,128)(2,1)S(1)}, u32[]{:S(2)}, u32[]{:S(2)}) collective-permute-start(bf16[4,128,1280]{2,1,0:T(8,128)(2,1)} %collective-permute-done.16.refs_2_), channel_id=1, source_target_pairs={{0,1},{1,0},{2,3},{3,2},{4,5},{5,4},{6,7},{7,6},{8,9},{9,8},{10,11... | collective-permute-start | bytes 3932168 | tf_op jit(solution)/shard_map/ppermute | solution.py:508
  111.9 14.5 %collective-permute-start.22 = (bf16[4,128,1280]{2,1,0:T(8,128)(2,1)}, bf16[4,128,1280]{2,1,0:T(8,128)(2,1)}, u32[]{:S(2)}, u32[]{:S(2)}) collective-permute-start(bf16[4,128,1280]{2,1,0:T(8,128)(2,1)} %collective-permute-done.18.refs_3_), channel_id=1, source_target_pairs={{0,1},{1,0},{2,3},{3,2},{4,5},{5,4},{6,7},{7,6},{8,9},{9,8},{10,11... | collective-permute-start | bytes 3932168 | tf_op jit(solution)/shard_map/ppermute | solution.py:508
  112.3 25.9 %collective-permute-start.23 = (bf16[4,512,256]{2,1,0:T(8,128)(2,1)S(1)}, bf16[4,512,256]{2,1,0:T(8,128)(2,1)}, u32[]{:S(2)}, u32[]{:S(2)}) collective-permute-start(bf16[4,512,256]{2,1,0:T(8,128)(2,1)S(1)} %pad_maximum_fusion.1.refs_0_), channel_id=1, source_target_pairs={{0,8},{1,17},{2,10},{3,19},{4,12},{5,21},{6,14},{7,23},{8,0},{9,25... | collective-permute-start | bytes 3145736 | tf_op jit(solution)/shard_map/ppermute | solution.py:508
  112.9 25.4 %collective-permute-start.24 = (bf16[4,512,256]{2,1,0:T(8,128)(2,1)S(1)}, bf16[4,512,256]{2,1,0:T(8,128)(2,1)S(1)}, u32[]{:S(2)}, u32[]{:S(2)}) collective-permute-start(bf16[4,512,256]{2,1,0:T(8,128)(2,1)S(1)} %pad_maximum_fusion.1.refs_0_), channel_id=1, source_target_pairs={{0,16},{1,9},{2,18},{3,11},{4,20},{5,13},{6,22},{7,15},{8,24},{9,1... | collective-permute-start | bytes 3145736 | tf_op jit(solution)/shard_map/ppermute | solution.py:508
  126.3 34.5 %collective-permute-start.26 = (bf16[4,512,256]{2,1,0:T(8,128)(2,1)S(1)}, bf16[4,512,256]{2,1,0:T(8,128)(2,1)}, u32[]{:S(2)}, u32[]{:S(2)}) collective-permute-start(bf16[4,512,256]{2,1,0:T(8,128)(2,1)S(1)} %pad_maximum_fusion.1.refs_0_), channel_id=1, source_target_pairs={{0,1},{1,0},{2,3},{3,2},{4,5},{5,4},{6,7},{7,6},{8,9},{9,8},{10,11... | collective-permute-start | bytes 3145736 | tf_op jit(solution)/shard_map/ppermute | solution.py:508
  138.2 22.4 %copy-start.14 = (bf16[4,512,256]{2,1,0:T(8,128)(2,1)}, bf16[4,512,256]{2,1,0:T(8,128)(2,1)S(1)}, u32[]{:S(2)}) copy-start(bf16[4,512,256]{2,1,0:T(8,128)(2,1)S(1)} %collective-permute-done.24.refs_2_) | copy-start | bytes 3145732
  138.2 22.4 %collective-permute-start.25 = (bf16[4,512,256]{2,1,0:T(8,128)(2,1)}, bf16[4,512,256]{2,1,0:T(8,128)(2,1)S(1)}, u32[]{:S(2)}, u32[]{:S(2)}) collective-permute-start(bf16[4,512,256]{2,1,0:T(8,128)(2,1)} %collective-permute-done.23.refs_1_), channel_id=1, source_target_pairs={{0,16},{1,9},{2,18},{3,11},{4,20},{5,13},{6,22},{7,15},{8,24},{9,1... | collective-permute-start | bytes 3145736 | tf_op jit(solution)/shard_map/ppermute | solution.py:508
  138.8 22.0 %collective-permute-start.27 = (bf16[4,512,256]{2,1,0:T(8,128)(2,1)}, bf16[4,512,256]{2,1,0:T(8,128)(2,1)}, u32[]{:S(2)}, u32[]{:S(2)}) collective-permute-start(bf16[4,512,256]{2,1,0:T(8,128)(2,1)} %collective-permute-done.23.refs_1_), channel_id=1, source_target_pairs={{0,1},{1,0},{2,3},{3,2},{4,5},{5,4},{6,7},{7,6},{8,9},{9,8},{10,11... | collective-permute-start | bytes 3145736 | tf_op jit(solution)/shard_map/ppermute | solution.py:508
  138.8 22.0 %collective-permute-start.28 = (bf16[4,512,256]{2,1,0:T(8,128)(2,1)S(1)}, bf16[4,512,256]{2,1,0:T(8,128)(2,1)}, u32[]{:S(2)}, u32[]{:S(2)}) collective-permute-start(bf16[4,512,256]{2,1,0:T(8,128)(2,1)S(1)} %collective-permute-done.24.refs_2_), channel_id=1, source_target_pairs={{0,1},{1,0},{2,3},{3,2},{4,5},{5,4},{6,7},{7,6},{8,9},{9,8},{10,11... | collective-permute-start | bytes 3145736 | tf_op jit(solution)/shard_map/ppermute | solution.py:508
  160.7 2.7 collective-permute-start.29
  210.9 14.6 %collective-permute-start.30 = (bf16[4,4,512,256]{3,2,1,0:T(8,128)(2,1)}, bf16[4,4,512,256]{3,2,1,0:T(8,128)(2,1)}, u32[]{:S(2)}, u32[]{:S(2)}) collective-permute-start(bf16[4,4,512,256]{3,2,1,0:T(8,128)(2,1)} %get-tuple-element.182), channel_id=1, source_target_pairs={{0,1},{1,0},{2,3},{3,2},{4,5},{5,4},{6,7},{7,6},{8,9},{9,8},{10,11... | collective-permute-start | bytes 12582920 | tf_op jit(solution)/shard_map/ppermute | solution.py:508
  225.2 25.4 %collective-permute-start.31 = (bf16[4,4,128,1024]{3,2,1,0:T(8,128)(2,1)}, bf16[4,4,128,1024]{3,2,1,0:T(8,128)(2,1)}, u32[]{:S(2)}, u32[]{:S(2)}) collective-permute-start(bf16[4,4,128,1024]{3,2,1,0:T(8,128)(2,1)} %get-tuple-element.191), channel_id=1, source_target_pairs={{0,1},{1,0},{2,3},{3,2},{4,5},{5,4},{6,7},{7,6},{8,9},{9,8},{10,11... | collective-permute-start | bytes 12582920 | tf_op jit(solution)/shard_map/ppermute | solution.py:508
  228.2 50.5 %collective-permute-start.32 = (bf16[2,4,512,256]{3,2,1,0:T(8,128)(2,1)S(1)}, bf16[2,4,512,256]{3,2,1,0:T(8,128)(2,1)}, u32[]{:S(2)}, u32[]{:S(2)}) collective-permute-start(bf16[2,4,512,256]{3,2,1,0:T(8,128)(2,1)S(1)} %add_convert_fusion.1), channel_id=1, source_target_pairs={{0,8},{1,17},{2,10},{3,19},{4,12},{5,21},{6,14},{7,23},{8,0},{9,25... | collective-permute-start | bytes 6291464 | tf_op jit(solution)/shard_map/ppermute | solution.py:508
  255.3 27.2 %collective-permute-start.33 = (bf16[2,4,128,1024]{3,2,1,0:T(8,128)(2,1)}, bf16[2,4,128,1024]{3,2,1,0:T(8,128)(2,1)}, u32[]{:S(2)}, u32[]{:S(2)}) collective-permute-start(bf16[2,4,128,1024]{3,2,1,0:T(8,128)(2,1)} %add_convert_fusion), channel_id=1, source_target_pairs={{0,8},{1,17},{2,10},{3,19},{4,12},{5,21},{6,14},{7,23},{8,0},{9,25... | collective-permute-start | bytes 6291464 | tf_op jit(solution)/shard_map/ppermute | solution.py:508
  281.0 17.9 %collective-permute-start.34 = (bf16[4,512,256]{2,1,0:T(8,128)(2,1)S(1)}, bf16[4,512,256]{2,1,0:T(8,128)(2,1)S(1)}, u32[]{:S(2)}, u32[]{:S(2)}) collective-permute-start(bf16[4,512,256]{2,1,0:T(8,128)(2,1)S(1)} %fusion.3), channel_id=1, source_target_pairs={{0,16},{1,9},{2,18},{3,11},{4,20},{5,13},{6,22},{7,15},{8,24},{9,1... | collective-permute-start | bytes 3145736 | tf_op jit(solution)/shard_map/ppermute | solution.py:508
  298.3 17.9 %collective-permute-start.37 = (bf16[4,4,128,640]{3,2,1,0:T(8,128)(2,1)}, bf16[4,4,128,640]{3,2,1,0:T(8,128)(2,1)}, u32[]{:S(2)}, u32[]{:S(2)}) collective-permute-start(bf16[4,4,128,640]{3,2,1,0:T(8,128)(2,1)} %get-tuple-element.205), channel_id=1, source_target_pairs={{0,1},{1,0},{2,3},{3,2},{4,5},{5,4},{6,7},{7,6},{8,9},{9,8},{10,11... | collective-permute-start | bytes 7864328 | tf_op jit(solution)/shard_map/ppermute | solution.py:508
  298.3 17.9 %collective-permute-start.36 = (bf16[4,128,1024]{2,1,0:T(8,128)(2,1)}, bf16[4,128,1024]{2,1,0:T(8,128)(2,1)}, u32[]{:S(2)}, u32[]{:S(2)}) collective-permute-start(bf16[4,128,1024]{2,1,0:T(8,128)(2,1)} %fusion.4), channel_id=1, source_target_pairs={{0,16},{1,9},{2,18},{3,11},{4,20},{5,13},{6,22},{7,15},{8,24},{9,1... | collective-permute-start | bytes 3145736 | tf_op jit(solution)/shard_map/ppermute | solution.py:508
  301.4 14.8 %collective-permute-start.35 = (bf16[2,512,256]{2,1,0:T(8,128)(2,1)S(1)}, bf16[2,512,256]{2,1,0:T(8,128)(2,1)S(1)}, u32[]{:S(2)}, u32[]{:S(2)}) collective-permute-start(bf16[2,512,256]{2,1,0:T(8,128)(2,1)S(1)} %pad_maximum_fusion.6), channel_id=1, source_target_pairs={{0,2},{1,5},{2,0},{3,7},{4,6},{5,1},{6,4},{7,3},{8,10},{9,13},{10,... | collective-permute-start | bytes 1572872 | tf_op jit(solution)/shard_map/ppermute | solution.py:508
  322.6 21.7 %collective-permute-start.40 = (bf16[2,4,128,640]{3,2,1,0:T(8,128)(2,1)}, bf16[2,4,128,640]{3,2,1,0:T(8,128)(2,1)}, u32[]{:S(2)}, u32[]{:S(2)}) collective-permute-start(bf16[2,4,128,640]{3,2,1,0:T(8,128)(2,1)} %add_convert_fusion.2), channel_id=1, source_target_pairs={{0,8},{1,17},{2,10},{3,19},{4,12},{5,21},{6,14},{7,23},{8,0},{9,25... | collective-permute-start | bytes 3932168 | tf_op jit(solution)/shard_map/ppermute | solution.py:508
  323.9 20.5 %collective-permute-start.39 = (bf16[2,128,1024]{2,1,0:T(8,128)(2,1)S(1)}, bf16[2,128,1024]{2,1,0:T(8,128)(2,1)S(1)}, u32[]{:S(2)}, u32[]{:S(2)}) collective-permute-start(bf16[2,128,1024]{2,1,0:T(8,128)(2,1)S(1)} %pad_maximum_fusion.7), channel_id=1, source_target_pairs={{0,2},{1,5},{2,0},{3,7},{4,6},{5,1},{6,4},{7,3},{8,10},{9,13},{10,... | collective-permute-start | bytes 1572872 | tf_op jit(solution)/shard_map/ppermute | solution.py:508
  325.4 16.9 %collective-permute-start.38 = (bf16[512,256]{1,0:T(8,128)(2,1)}, bf16[512,256]{1,0:T(8,128)(2,1)S(1)}, u32[]{:S(2)}, u32[]{:S(2)}) collective-permute-start(bf16[512,256]{1,0:T(8,128)(2,1)} %fusion.11), channel_id=1, source_target_pairs={{0,4},{1,3},{2,6},{3,1},{4,0},{5,7},{6,2},{7,5},{8,12},{9,11},{10,... | collective-permute-start | bytes 786440 | tf_op jit(solution)/shard_map/ppermute | solution.py:508
  346.3 10.8 %collective-permute-start.42 = (bf16[4,128,640]{2,1,0:T(8,128)(2,1)S(1)}, bf16[4,128,640]{2,1,0:T(8,128)(2,1)}, u32[]{:S(2)}, u32[]{:S(2)}) collective-permute-start(bf16[4,128,640]{2,1,0:T(8,128)(2,1)S(1)} %fusion.6), channel_id=1, source_target_pairs={{0,16},{1,9},{2,18},{3,11},{4,20},{5,13},{6,22},{7,15},{8,24},{9,1... | collective-permute-start | bytes 1966088 | tf_op jit(solution)/shard_map/ppermute | solution.py:508
  346.9 10.1 %collective-permute-start.41 = (bf16[128,1024]{1,0:T(8,128)(2,1)S(1)}, bf16[128,1024]{1,0:T(8,128)(2,1)S(1)}, u32[]{:S(2)}, u32[]{:S(2)}) collective-permute-start(bf16[128,1024]{1,0:T(8,128)(2,1)S(1)} %fusion.12), channel_id=1, source_target_pairs={{0,4},{1,3},{2,6},{3,1},{4,0},{5,7},{6,2},{7,5},{8,12},{9,11},{10,... | collective-permute-start | bytes 786440 | tf_op jit(solution)/shard_map/ppermute | solution.py:508
  356.9 14.0 %collective-permute-start.43 = (bf16[4,4,144,384]{3,2,1,0:T(8,128)(2,1)}, bf16[4,4,144,384]{3,2,1,0:T(8,128)(2,1)}, u32[]{:S(2)}, u32[]{:S(2)}) collective-permute-start(bf16[4,4,144,384]{3,2,1,0:T(8,128)(2,1)} %get-tuple-element.225), channel_id=1, source_target_pairs={{0,1},{1,0},{2,3},{3,2},{4,5},{5,4},{6,7},{7,6},{8,9},{9,8},{10,11... | collective-permute-start | bytes 5308424 | tf_op jit(solution)/shard_map/ppermute | solution.py:508
  359.3 11.7 %collective-permute-start.44 = (bf16[2,128,640]{2,1,0:T(8,128)(2,1)S(1)}, bf16[2,128,640]{2,1,0:T(8,128)(2,1)S(1)}, u32[]{:S(2)}, u32[]{:S(2)}) collective-permute-start(bf16[2,128,640]{2,1,0:T(8,128)(2,1)S(1)} %pad_maximum_fusion.10), channel_id=1, source_target_pairs={{0,2},{1,5},{2,0},{3,7},{4,6},{5,1},{6,4},{7,3},{8,10},{9,13},{10,... | collective-permute-start | bytes 983048 | tf_op jit(solution)/shard_map/ppermute | solution.py:508
  360.8 10.1 %collective-permute-start.45 = (bf16[1024,256]{1,0:T(8,128)(2,1)S(1)}, bf16[1024,256]{1,0:T(8,128)(2,1)S(1)}, u32[]{:S(2)}, u32[]{:S(2)}) collective-permute-start(bf16[1024,256]{1,0:T(8,128)(2,1)S(1)} %slice_dynamic-update-slice_fusion.refs_0_), channel_id=1, source_target_pairs={{0,8},{1,17},{2,10},{3,19},{4,12},{5,21},{6,14},{7,23},{8,0},{9,25... | collective-permute-start | bytes 1572872 | tf_op jit(solution)/shard_map/ppermute | solution.py:508
  373.5 13.3 %collective-permute-start.46 = (bf16[2,4,144,384]{3,2,1,0:T(8,128)(2,1)}, bf16[2,4,144,384]{3,2,1,0:T(8,128)(2,1)S(1)}, u32[]{:S(2)}, u32[]{:S(2)}) collective-permute-start(bf16[2,4,144,384]{3,2,1,0:T(8,128)(2,1)} %add_convert_fusion.5), channel_id=1, source_target_pairs={{0,8},{1,17},{2,10},{3,19},{4,12},{5,21},{6,14},{7,23},{8,0},{9,25... | collective-permute-start | bytes 2654216 | tf_op jit(solution)/shard_map/ppermute | solution.py:508
  374.5 9.8 %collective-permute-start.47 = (bf16[128,640]{1,0:T(8,128)(2,1)S(1)}, bf16[128,640]{1,0:T(8,128)(2,1)S(1)}, u32[]{:S(2)}, u32[]{:S(2)}) collective-permute-start(bf16[128,640]{1,0:T(8,128)(2,1)S(1)} %fusion.16), channel_id=1, source_target_pairs={{0,4},{1,3},{2,6},{3,1},{4,0},{5,7},{6,2},{7,5},{8,12},{9,11},{10,... | collective-permute-start | bytes 491528 | tf_op jit(solution)/shard_map/ppermute | solution.py:508
  388.1 9.9 %collective-permute-start.48 = (bf16[4,144,384]{2,1,0:T(8,128)(2,1)S(1)}, bf16[4,144,384]{2,1,0:T(8,128)(2,1)S(1)}, u32[]{:S(2)}, u32[]{:S(2)}) collective-permute-start(bf16[4,144,384]{2,1,0:T(8,128)(2,1)S(1)} %fusion.9), channel_id=1, source_target_pairs={{0,16},{1,9},{2,18},{3,11},{4,20},{5,13},{6,22},{7,15},{8,24},{9,1... | collective-permute-start | bytes 1327112 | tf_op jit(solution)/shard_map/ppermute | solution.py:508
  388.9 7.2 %collective-permute-start.49 = (bf16[128,640]{1,0:T(8,128)(2,1)S(1)}, bf16[128,640]{1,0:T(8,128)(2,1)S(1)}, u32[]{:S(2)}, u32[]{:S(2)}) collective-permute-start(bf16[128,640]{1,0:T(8,128)(2,1)S(1)} %fusion.10.refs_0_), channel_id=1, source_target_pairs={{0,8},{1,17},{2,10},{3,19},{4,12},{5,21},{6,14},{7,23},{8,0},{9,25... | collective-permute-start | bytes 491528 | tf_op jit(solution)/shard_map/ppermute | solution.py:508
  400.4 15.7 %copy-start.3 = (s32[3]{0:T(128)S(1)}, s32[3]{0:T(128)}, u32[]{:S(2)}) copy-start(s32[3]{0:T(128)} %pad_add_fusion.where) | copy-start | bytes 40
  400.4 15.6 %collective-permute-start.54 = (bf16[2,1024,256]{2,1,0:T(8,128)(2,1)}, bf16[2,1024,256]{2,1,0:T(8,128)(2,1)S(1)}, u32[]{:S(2)}, u32[]{:S(2)}) collective-permute-start(bf16[2,1024,256]{2,1,0:T(8,128)(2,1)} %pad_maximum_fusion.2), channel_id=1, source_target_pairs={{0,16},{1,9},{2,18},{3,11},{4,20},{5,13},{6,22},{7,15},{8,24},{9,1... | collective-permute-start | bytes 3145736 | tf_op jit(solution)/shard_map/ppermute | solution.py:508
  401.3 7.9 %collective-permute-start.51 = (bf16[144,384]{1,0:T(8,128)(2,1)S(1)}, bf16[144,384]{1,0:T(8,128)(2,1)S(1)}, u32[]{:S(2)}, u32[]{:S(2)}) collective-permute-start(bf16[144,384]{1,0:T(8,128)(2,1)S(1)} %get-tuple-element.259), channel_id=1, source_target_pairs={{0,6},{1,7},{2,4},{3,5},{4,2},{5,3},{6,0},{7,1},{8,14},{9,15},{10,... | collective-permute-start | bytes 331784 | tf_op jit(solution)/shard_map/ppermute | solution.py:508
  403.1 9.3 %collective-permute-start.52 = (bf16[144,384]{1,0:T(8,128)(2,1)S(1)}, bf16[144,384]{1,0:T(8,128)(2,1)S(1)}, u32[]{:S(2)}, u32[]{:S(2)}) collective-permute-start(bf16[144,384]{1,0:T(8,128)(2,1)S(1)} %get-tuple-element.258), channel_id=1, source_target_pairs={{0,4},{1,5},{2,6},{3,7},{4,0},{5,1},{6,2},{7,3},{8,12},{9,13},{10,... | collective-permute-start | bytes 331784 | tf_op jit(solution)/shard_map/ppermute | solution.py:508
  403.7 8.7 %collective-permute-start.53 = (bf16[144,384]{1,0:T(8,128)(2,1)S(1)}, bf16[144,384]{1,0:T(8,128)(2,1)S(1)}, u32[]{:S(2)}, u32[]{:S(2)}) collective-permute-start(bf16[144,384]{1,0:T(8,128)(2,1)S(1)} %get-tuple-element.257), channel_id=1, source_target_pairs={{0,2},{1,3},{2,0},{3,1},{4,6},{5,7},{6,4},{7,5},{8,10},{9,11},{10,... | collective-permute-start | bytes 331784 | tf_op jit(solution)/shard_map/ppermute | solution.py:508
  405.8 16.7 %collective-permute-start.50 = (bf16[2,128,640]{2,1,0:T(8,128)(2,1)S(1)}, bf16[2,128,640]{2,1,0:T(8,128)(2,1)S(1)}, u32[]{:S(2)}, u32[]{:S(2)}) collective-permute-start(bf16[2,128,640]{2,1,0:T(8,128)(2,1)S(1)} %pad_maximum_fusion.11), channel_id=1, source_target_pairs={{0,16},{1,9},{2,18},{3,11},{4,20},{5,13},{6,22},{7,15},{8,24},{9,1... | collective-permute-start | bytes 983048 | tf_op jit(solution)/shard_map/ppermute | solution.py:508
  412.5 10.1 %collective-permute-start.55 = (bf16[144,384]{1,0:T(8,128)(2,1)S(1)}, bf16[144,384]{1,0:T(8,128)(2,1)S(1)}, u32[]{:S(2)}, u32[]{:S(2)}) collective-permute-start(bf16[144,384]{1,0:T(8,128)(2,1)S(1)} %fusion.15.refs_4_), channel_id=1, source_target_pairs={{0,8},{1,9},{2,10},{3,11},{4,12},{5,13},{6,14},{7,15},{8,0},{9,1},... | collective-permute-start | bytes 331784 | tf_op jit(solution)/shard_map/ppermute | solution.py:508
  414.0 9.7 %collective-permute-start.56 = (bf16[144,384]{1,0:T(8,128)(2,1)S(1)}, bf16[144,384]{1,0:T(8,128)(2,1)S(1)}, u32[]{:S(2)}, u32[]{:S(2)}) collective-permute-start(bf16[144,384]{1,0:T(8,128)(2,1)S(1)} %fusion.15.refs_4_), channel_id=1, source_target_pairs={{0,16},{1,17},{2,18},{3,19},{4,20},{5,21},{6,22},{7,23},{8,24},{9,... | collective-permute-start | bytes 331784 | tf_op jit(solution)/shard_map/ppermute | solution.py:508
  414.6 9.1 %collective-permute-start.57 = (bf16[144,384]{1,0:T(8,128)(2,1)S(1)}, bf16[144,384]{1,0:T(8,128)(2,1)S(1)}, u32[]{:S(2)}, u32[]{:S(2)}) collective-permute-start(bf16[144,384]{1,0:T(8,128)(2,1)S(1)} %fusion.15.refs_4_), channel_id=1, source_target_pairs={{0,24},{1,25},{2,26},{3,27},{4,28},{5,29},{6,30},{7,31},{8,16},{9,... | collective-permute-start | bytes 331784 | tf_op jit(solution)/shard_map/ppermute | solution.py:508
  (16 other events, 50.4 us)

commit v7 on v6

--- a/solution.py
+++ b/solution.py
@@ -1525,10 +1525,12 @@
     meet(part[1], r_out, r_in, r_a)
     steps = (r_out.along_far(), r_in.along(), r_a.near())
     low_b, late_b = back(steps, half + quarter, quarter, quarter, part)
-    meet(late_b, r_out, r_in, r_a)
+    meet(late_b, r_a)
+    middle = r_a.middle()
+    meet(middle, r_out, r_in)
     sums = (late_a, late_b, first_sums, second_sums, bias_in_grad)
     share_out = r_out.share()
-    steps = (r_in.along_far(), r_a.middle(), share_out)
+    steps = (r_in.along_far(), middle, share_out)
     r_b = Reduction(place, attention_grads(place, after(turned, *steps), low_b, sums, "b"))
     meet(r_b.made, r_in, r_a)
     share_in = r_in.share()

time: 431 us -> 429 us (level)
  transfers between devices with their start and end apart: 58 -> 58, of which waited for: 21 -> 19; matrix products, arithmetic and copies ran while one was open for 6% -> 7% of each run, Pallas kernels for 51% -> 51%
where the time goes in v7:
time: 429 us; the launch traced here: 425 us
  Pallas kernels  265 us (62%)
  starting transfers between devices  60.8 us (14%)
  waiting for transfers between devices  46 us (11%)
  other arithmetic  42.9 us (10%)
  local copies, waits for them, and re-layouts  8.87 us (2%)
    pallas_call x4, Pallas kernels, weight_call(): pl.pallas_call(body, grid_spec=pltpu.PrefetchScalarGridSpec(num_scalar_pr...  76.3 us
    ppermute x58, starting transfers between devices, permute(): return lax.ppermute(array, AXES, pairs)  60.8 us
    pallas_call x3, Pallas kernels, attention_backward(): pl.pallas_call(body, grid=(pairs,), in_specs=[pair(0), pair(1), pair(2),...  49.3 us
    ppermute x58, waiting for transfers between devices, permute(): return lax.ppermute(array, AXES, pairs)  46 us
    pallas_call x3, Pallas kernels, attention_forward(): pl.pallas_call(body, grid=(pairs,), in_specs=[pair(0), pair(1), pair(2),...  44.8 us
    convert_element_type x18, other arithmetic, add(): return total.astype(jnp.bfloat16)  33 us
    pallas_call x2, Pallas kernels, weight_grad(): pl.pallas_call(functools.partial(weight_grad_kernel, rows=rows, groups=gr...  28 us
    pallas_call x2, Pallas kernels, attention_grads(): pl.pallas_call(functools.partial(attention_grads_kernel, rows=rows, group...  21.1 us
  transfers between devices with their start and end apart: 58, of which 19 were waited for; matrix products, arithmetic and copies ran while one was open for 7% of the time, Pallas kernels for 51%

profile of v7, /device:TPU:0, one launch (start us, length us, event | category | flops | bytes accessed | tf_op | source)
XLA Modules:
  0.0 425.1 jit_solution(7995748156562035590)
XLA Ops:
  0.6 3.1 collective-permute-start
  3.7 1.5 concatenate.29
  6.7 2.7 collective-permute-done
  10.4 2.5 collective-permute-start.2
  12.9 2.5 collective-permute-start.3
  16.4 4.3 %collective-permute-done.3 = bf16[2,16,128]{2,1,0:T(8,128)(2,1)S(1)} collective-permute-done((bf16[2,16,128]{2,1,0:T(8,128)(2,1)S(1)}, bf16[2,16,128]{2,1,0:T(8,128)(2,1)S(1)}, u32[]{:S(2)}, u32[]{:S(2)}) %collective-permute-start.3) | collective-permute-done | bytes 8224 | tf_op jit(solution)/shard_map/ppermute | solution.py:508
  22.9 2.7 collective-permute-start.4
  25.6 1.6 collective-permute-start.7
  27.2 1.5 collective-permute-start.8
  29.3 3.3 collective-permute-start.5
  32.6 2.0 collective-permute-done.5
  35.5 2.9 collective-permute-start.6
  40.4 2.0 vectors.1
  42.4 2.4 collective-permute-done.7.refs_1_
  49.0 5.4 %collective-permute-done.6 = bf16[2,128,1280]{2,1,0:T(8,128)(2,1)} collective-permute-done((bf16[2,128,1280]{2,1,0:T(8,128)(2,1)}, bf16[2,128,1280]{2,1,0:T(8,128)(2,1)}, u32[]{:S(2)}, u32[]{:S(2)}) %collective-permute-start.6) | collective-permute-done | bytes 655392 | tf_op jit(solution)/shard_map/ppermute | solution.py:508
  55.6 1.4 collective-permute-done.9.refs_3_
  57.0 1.5 collective-permute-start.15
  61.7 12.7 %qkv.1 = (bf16[1024,3072]{1,0:T(8,128)(2,1)}, bf16[1024,3072]{1,0:T(8,128)(2,1)}) custom-call(s32[3]{0:T(128)} %pad_add_fusion.where, bf16[4,128,768]{2,1,0:T(8,128)(2,1)} %copy-done.7, bf16[4,128,768]{2,1,0:T(8,128)(2,1)} %collective-permute-done.7.refs_1_, bf16[4,128,768]{2,1,0:T(8,128)(2,1)} %collective-permute-done.8.refs_2_, ...), custom_call_target="tpu_custom_call" | custom-call | flops 12884901888 | tf_op jit(solution)/shard_map/qkv/pallas_call | solution.py:654
  74.5 2.5 collective-permute-start.17
  77.1 16.4 %attn_fwd.3 = (bf16[1024,1024]{1,0:T(8,128)(2,1)}, bf16[16,1024,1024]{2,1,0:T(8,128)(2,1)}, f32[1024,1024]{1,0:T(8,128)}) custom-call(bf16[1024,3072]{1,0:T(8,128)(2,1)} %get-tuple-element.161.q_ref.k_ref.v_ref.refs_0_.refs_1_.refs_2_, bf16[1024,3072]{1,0:T(8,128)(2,1)} %get-tuple-element.161.q_ref.k_ref.v_ref.refs_0_.refs_1_.refs_2_, ...), custom_call_target="tpu_custom_call" | custom-call | flops 12884901888 | tf_op jit(solution)/shard_map/attn_fwd/pallas_call | solution.py:391
  93.4 1.5 collective-permute-start.18
  95.6 16.3 %attn_fwd.4 = (bf16[1024,1024]{1,0:T(8,128)(2,1)}, bf16[16,1024,1024]{2,1,0:T(8,128)(2,1)}, f32[1024,1024]{1,0:T(8,128)}) custom-call(bf16[1024,3072]{1,0:T(8,128)(2,1)} %get-tuple-element.161.q_ref.k_ref.v_ref.refs_0_.refs_1_.refs_2_, ...), custom_call_target="tpu_custom_call", output_to_operand_aliasing={{0}: (5, {}), {1}: (6, {}), {2}: (7, {})} | custom-call | flops 12884901888 | tf_op jit(solution)/shard_map/attn_fwd/pallas_call | solution.py:391
  112.9 1.4 collective-permute-start.24
  114.2 12.1 %attn_fwd.5 = (bf16[1024,1024]{1,0:T(8,128)(2,1)}, bf16[16,1024,1024]{2,1,0:T(8,128)(2,1)}, f32[1024,1024]{1,0:T(8,128)}) custom-call(bf16[1024,3072]{1,0:T(8,128)(2,1)} %get-tuple-element.161.q_ref.k_ref.v_ref.refs_0_.refs_1_.refs_2_, ...), custom_call_target="tpu_custom_call", output_to_operand_aliasing={{0}: (5, {}), {1}: (6, {}), {2}: (7, {})} | custom-call | flops 8589934592 | tf_op jit(solution)/shard_map/attn_fwd/pallas_call | solution.py:391
  127.5 9.6 %attn_out.1 = (f32[1024,1024]{1,0:T(8,128)}, f32[1024,128]{1,0:T(8,128)}, bf16[1024,1024]{1,0:T(8,128)(2,1)}, bf16[1024,1024]{1,0:T(8,128)(2,1)}) custom-call(s32[3]{0:T(128)} %pad_add_fusion.where, bf16[4,128,1280]{2,1,0:T(8,128)(2,1)} %copy-done.4, bf16[4,128,1280]{2,1,0:T(8,128)(2,1)} %collective-permute-done.15.refs_1_, ...), custom_call_target="tpu_custom_call" | custom-call | flops 4294967296 | tf_op jit(solution)/shard_map/attn_out/pallas_call | solution.py:654
  139.3 21.3 %feed_in.1 = (bf16[1024,4096]{1,0:T(8,128)(2,1)}, bf16[1024,4096]{1,0:T(8,128)(2,1)}, bf16[1024,4096]{1,0:T(8,128)(2,1)}) custom-call(s32[3]{0:T(128)} %pad_add_fusion.where, bf16[4,128,1280]{2,1,0:T(8,128)(2,1)} %copy-done.4, bf16[4,128,1280]{2,1,0:T(8,128)(2,1)} %collective-permute-done.15.refs_1_, bf16[4,128,1280]{2,1,0:T(8,128)(2,1)} %collective-permute-done.16.refs_2_, ...), custom_call_target="tpu_custom_call" | custom-call | flops 17179869184 | tf_op jit(solution)/shard_map/feed_in/pallas_call | solution.py:654
  160.8 2.6 collective-permute-done.29.refs_7_
  164.4 32.5 %feed_out.1 = (bf16[1024,1024]{1,0:T(8,128)(2,1)}, f32[1024,1024]{1,0:T(8,128)}, bf16[1024,1024]{1,0:T(8,128)(2,1)}, f32[8,1024]{1,0:T(8,128)}, bf16[1024,4096]{1,0:T(8,128)(2,1)}, /*index=5*/f32[1,4096]{1,0:T(1,128)}) custom-call(s32[3]{0:T(128)} %pad_add_fusion.where, bf16[4,512,256]{2,1,0:T(8,128)(2,1)} %copy-done.5, ...), custom_call_target="tpu_custom_call" | custom-call | flops 34359738368 | tf_op jit(solution)/shard_map/feed_out/pallas_call | solution.py:654
  197.0 13.9 %wgrad_out.1 = (bf16[4,4,512,256]{3,2,1,0:T(8,128)(2,1)}, bf16[4,4,512,256]{3,2,1,0:T(8,128)(2,1)}) custom-call(s32[3]{0:T(128)} %pad_add_fusion.where, bf16[1024,4096]{1,0:T(8,128)(2,1)} %get-tuple-element.170.refs_8_.left_ref, bf16[1024,1024]{1,0:T(8,128)(2,1)} %get-tuple-element.178.right_ref), custom_call_target="tpu_custom_call" | custom-call | flops 17179869184 | tf_op jit(solution)/shard_map/wgrad_out/pallas_call | solution.py:1213
  211.1 14.1 %wgrad_in.1 = (bf16[4,4,128,1024]{3,2,1,0:T(8,128)(2,1)}, bf16[4,4,128,1024]{3,2,1,0:T(8,128)(2,1)}) custom-call(s32[3]{0:T(128)} %pad_add_fusion.where, bf16[1024,1024]{1,0:T(8,128)(2,1)} %get-tuple-element.180.refs_8_.left_ref, bf16[1024,4096]{1,0:T(8,128)(2,1)} %get-tuple-element.184.right_ref.p_ref), custom_call_target="tpu_custom_call" | custom-call | flops 17179869184 | tf_op jit(solution)/shard_map/wgrad_in/pallas_call | solution.py:1213
  225.5 2.7 add_convert_fusion.1
  229.6 21.0 %feed_in_back.1 = (f32[1024,1024]{1,0:T(8,128)}, bf16[1024,1024]{1,0:T(8,128)(2,1)}, bf16[1024,1024]{1,0:T(8,128)(2,1)}, f32[8,1024]{1,0:T(8,128)}) custom-call(bf16[1024,4096]{1,0:T(8,128)(2,1)} %get-tuple-element.184.right_ref.p_ref, bf16[1024,4096]{1,0:T(8,128)(2,1)} %get-tuple-element.185.w_ref, f32[1024,1024]{1,0:T(8,128)} %get-tuple-element.186.g_ref, ...), custom_call_target="tpu_custom_call" | custom-call | flops 21474836480 | tf_op jit(solution)/shard_map/feed_in_back/pallas_call | solution.py:676
  250.6 4.7 %add_convert_fusion = bf16[2,4,128,1024]{3,2,1,0:T(8,128)(2,1)} fusion(bf16[4,4,128,1024]{3,2,1,0:T(8,128)(2,1)} %collective-permute-done.31, bf16[4,4,128,1024]{3,2,1,0:T(8,128)(2,1)} %get-tuple-element.181), kind=kLoop, calls=%fused_computation | loop fusion | flops 4194304 | bytes 6291456 | tf_op jit(solution)/shard_map/convert_element_type | solution.py:1236
  256.0 22.7 %attn_bwd.3 = (bf16[3,1024,512]{2,1,0:T(8,128)(2,1)}, f32[2,512]{1,0:T(2,128)}) custom-call(bf16[1024,3072]{1,0:T(8,128)(2,1)} %get-tuple-element.161.q_ref.k_ref.v_ref.refs_0_.refs_1_.refs_2_, bf16[1024,3072]{1,0:T(8,128)(2,1)} %get-tuple-element.161.q_ref.k_ref.v_ref.refs_0_.refs_1_.refs_2_, ...), custom_call_target="tpu_custom_call" | custom-call | flops 34359738368 | tf_op jit(solution)/shard_map/attn_bwd/pallas_call | solution.py:467
  278.7 2.2 fusion.3
  281.0 1.5 collective-permute-start.34
  282.4 3.5 fusion.4
  285.9 12.4 %wgrad_a.1 = (bf16[4,4,128,640]{3,2,1,0:T(8,128)(2,1)}, bf16[4,4,128,640]{3,2,1,0:T(8,128)(2,1)}) custom-call(s32[3]{0:T(128)} %pad_add_fusion.where, bf16[2,512,1024]{2,1,0:T(8,128)(2,1)} %copy-done.1, bf16[3,1024,512]{2,1,0:T(8,128)(2,1)} %get-tuple-element.196.refs_1_.refs_0_, bf16[1024,1024]{1,0:T(8,128)(2,1)} %get-tuple-element.164.refs_8_.refs_3_.refs_2_, ...), custom_call_target="tpu_custom_call" | custom-call | flops 10737418240 | tf_op jit(solution)/shard_map/wgrad_a/pallas_call | solution.py:1171
  298.9 2.4 fusion.1
  301.4 1.6 collective-permute-start.35
  303.0 13.2 %attn_bwd.4 = (bf16[3,1024,512]{2,1,0:T(8,128)(2,1)}, f32[2,512]{1,0:T(2,128)}) custom-call(bf16[1024,3072]{1,0:T(8,128)(2,1)} %get-tuple-element.161.q_ref.k_ref.v_ref.refs_0_.refs_1_.refs_2_, bf16[1024,3072]{1,0:T(8,128)(2,1)} %get-tuple-element.161.q_ref.k_ref.v_ref.refs_0_.refs_1_.refs_2_, ...), custom_call_target="tpu_custom_call" | custom-call | flops 17179869184 | tf_op jit(solution)/shard_map/attn_bwd/pallas_call | solution.py:467
  316.2 3.3 add_convert_fusion.2
  319.5 3.1 fusion
  326.3 13.4 %attn_bwd.5 = (bf16[3,1024,512]{2,1,0:T(8,128)(2,1)}, f32[2,512]{1,0:T(2,128)}) custom-call(bf16[1024,3072]{1,0:T(8,128)(2,1)} %get-tuple-element.161.q_ref.k_ref.v_ref.refs_0_.refs_1_.refs_2_, bf16[1024,3072]{1,0:T(8,128)(2,1)} %get-tuple-element.161.q_ref.k_ref.v_ref.refs_0_.refs_1_.refs_2_, ...), custom_call_target="tpu_custom_call", output_to_operand_aliasing={{0}: (7, {}), {1}: (8, {})} | custom-call | flops 17179869184 | tf_op jit(solution)/shard_map/attn_bwd/pallas_call | solution.py:467
  340.6 1.7 fusion.6
  342.3 1.4 collective-permute-start.42
  346.4 8.7 %wgrad_b.1 = (bf16[4,4,144,384]{3,2,1,0:T(8,128)(2,1)}, bf16[4,4,144,384]{3,2,1,0:T(8,128)(2,1)}) custom-call(s32[3]{0:T(128)} %pad_add_fusion.where, bf16[2,512,1024]{2,1,0:T(8,128)(2,1)} %copy-done.1, bf16[3,1024,512]{2,1,0:T(8,128)(2,1)} %get-tuple-element.223.refs_1_, f32[2,512]{1,0:T(2,128)} %get-tuple-element.197.refs_2_, ...), custom_call_target="tpu_custom_call" | custom-call | flops 6442450944 | tf_op jit(solution)/shard_map/wgrad_b/pallas_call | solution.py:1171
  355.2 2.1 fusion.2
  360.4 8.2 %qkv_back.2.refs_3_ = f32[1024,1024]{1,0:T(8,128)} custom-call(bf16[1024,3072]{1,0:T(8,128)(2,1)} %get-tuple-element.176.w_ref, bf16[3,1024,512]{2,1,0:T(8,128)(2,1)} %get-tuple-element.196.refs_1_.refs_0_, bf16[3,1024,512]{2,1,0:T(8,128)(2,1)} %get-tuple-element.223.refs_1_, f32[1024,1024]{1,0:T(8,128)} %get-tuple-element.228.refs_2_), custom_call_target="tpu_custom_call" | custom-call | flops 6442450944 | tf_op jit(solution)/shard_map/qkv_back/pallas_call | solution.py:1012
  368.7 2.6 add_convert_fusion.5
  372.2 1.6 collective-permute-start.47
  373.7 8.2 %qkv_back.3 = f32[1024,1024]{1,0:T(8,128)} custom-call(bf16[1024,3072]{1,0:T(8,128)(2,1)} %get-tuple-element.176.w_ref, bf16[3,1024,512]{2,1,0:T(8,128)(2,1)} %get-tuple-element.196.refs_1_.refs_0_, bf16[3,1024,512]{2,1,0:T(8,128)(2,1)} %get-tuple-element.223.refs_1_, f32[1024,1024]{1,0:T(8,128)} %get-tuple-element.228.refs_2_, ...), custom_call_target="tpu_custom_call", output_to_operand_aliasing={{}: (4, {})} | custom-call | flops 6442450944 | tf_op jit(solution)/shard_map/qkv_back/pallas_call | solution.py:1012
  382.0 2.5 collective-permute-done.46
  387.9 6.2 %collective-permute-done.49.refs_1_ = bf16[128,640]{1,0:T(8,128)(2,1)S(1)} collective-permute-done((bf16[128,640]{1,0:T(8,128)(2,1)S(1)}, bf16[128,640]{1,0:T(8,128)(2,1)S(1)}, u32[]{:S(2)}, u32[]{:S(2)}) %collective-permute-start.49) | collective-permute-done | bytes 163872 | tf_op jit(solution)/shard_map/ppermute | solution.py:508
  394.1 1.8 collective-permute-done.48
  399.2 1.6 collective-permute-start.51
  400.9 2.7 collective-permute-start.53
  405.0 2.1 collective-permute-done.51
  407.1 3.7 collective-permute-done.52
  412.7 1.7 collective-permute-start.57
  414.5 2.8 order_feed_forward.1
  417.3 1.5 collective-permute-done.50
  418.8 2.7 collective-permute-done.56.refs_6_
  421.6 2.1 order_attention.1
  (166 shorter events, 49.8 us)
Async XLA Ops:
  0.6 8.7 %collective-permute-start = (bf16[128,768]{1,0:T(8,128)(2,1)}, bf16[128,768]{1,0:T(8,128)(2,1)S(1)}, u32[]{:S(2)}, u32[]{:S(2)}) collective-permute-start(bf16[128,768]{1,0:T(8,128)(2,1)} %param.21), channel_id=1, source_target_pairs={{0,2},{1,5},{2,0},{3,7},{4,6},{5,1},{6,4},{7,3},{8,10},{9,13},{10,... | collective-permute-start | bytes 589832 | tf_op jit(solution)/shard_map/ppermute | solution.py:508
  5.2 1.4 collective-permute-start.1
  9.3 36.0 %copy-start = (bf16[1,1024,1024]{2,1,0:T(8,128)(2,1)S(1)}, bf16[1,1024,1024]{2,1,0:T(8,128)(2,1)}, u32[]{:S(2)}) copy-start(bf16[1,1024,1024]{2,1,0:T(8,128)(2,1)} %param.17) | copy-start | bytes 6291460
  10.4 11.5 %collective-permute-start.2 = (bf16[2,128,768]{2,1,0:T(8,128)(2,1)S(1)}, bf16[2,128,768]{2,1,0:T(8,128)(2,1)S(1)}, u32[]{:S(2)}, u32[]{:S(2)}) collective-permute-start(bf16[2,128,768]{2,1,0:T(8,128)(2,1)S(1)} %pad_maximum_fusion.8), channel_id=1, source_target_pairs={{0,4},{1,3},{2,6},{3,1},{4,0},{5,7},{6,2},{7,5},{8,12},{9,11},{10,... | collective-permute-start | bytes 1179656 | tf_op jit(solution)/shard_map/ppermute | solution.py:508
  12.9 7.8 %collective-permute-start.3 = (bf16[2,16,128]{2,1,0:T(8,128)(2,1)S(1)}, bf16[2,16,128]{2,1,0:T(8,128)(2,1)S(1)}, u32[]{:S(2)}, u32[]{:S(2)}) collective-permute-start(bf16[2,16,128]{2,1,0:T(8,128)(2,1)S(1)} %get-tuple-element.275), channel_id=1, source_target_pairs={{0,2},{1,5},{2,0},{3,7},{4,6},{5,1},{6,4},{7,3},{8,10},{9,13},{10,... | collective-permute-start | bytes 24584 | tf_op jit(solution)/shard_map/ppermute | solution.py:508
  22.9 24.2 %copy-start.7 = (bf16[4,128,768]{2,1,0:T(8,128)(2,1)}, bf16[4,128,768]{2,1,0:T(8,128)(2,1)S(1)}, u32[]{:S(2)}) copy-start(bf16[4,128,768]{2,1,0:T(8,128)(2,1)S(1)} %pad_maximum_fusion.3.refs_0_) | copy-start | bytes 2359300
  22.9 11.7 %collective-permute-start.4 = (bf16[128,1280]{1,0:T(8,128)(2,1)S(1)}, bf16[128,1280]{1,0:T(8,128)(2,1)S(1)}, u32[]{:S(2)}, u32[]{:S(2)}) collective-permute-start(bf16[128,1280]{1,0:T(8,128)(2,1)S(1)} %pad_maximum_fusion.9), channel_id=1, source_target_pairs={{0,2},{1,5},{2,0},{3,7},{4,6},{5,1},{6,4},{7,3},{8,10},{9,13},{10,... | collective-permute-start | bytes 983048 | tf_op jit(solution)/shard_map/ppermute | solution.py:508
  25.6 19.2 %collective-permute-start.7 = (bf16[4,128,768]{2,1,0:T(8,128)(2,1)S(1)}, bf16[4,128,768]{2,1,0:T(8,128)(2,1)}, u32[]{:S(2)}, u32[]{:S(2)}) collective-permute-start(bf16[4,128,768]{2,1,0:T(8,128)(2,1)S(1)} %pad_maximum_fusion.3.refs_0_), channel_id=1, source_target_pairs={{0,8},{1,17},{2,10},{3,19},{4,12},{5,21},{6,14},{7,23},{8,0},{9,25... | collective-permute-start | bytes 2359304 | tf_op jit(solution)/shard_map/ppermute | solution.py:508
  27.2 17.6 %collective-permute-start.8 = (bf16[4,128,768]{2,1,0:T(8,128)(2,1)S(1)}, bf16[4,128,768]{2,1,0:T(8,128)(2,1)}, u32[]{:S(2)}, u32[]{:S(2)}) collective-permute-start(bf16[4,128,768]{2,1,0:T(8,128)(2,1)S(1)} %pad_maximum_fusion.3.refs_0_), channel_id=1, source_target_pairs={{0,16},{1,9},{2,18},{3,11},{4,20},{5,13},{6,22},{7,15},{8,24},{9,1... | collective-permute-start | bytes 2359304 | tf_op jit(solution)/shard_map/ppermute | solution.py:508
  29.3 5.3 %collective-permute-start.5 = (bf16[2,2,16,128]{3,2,1,0:T(8,128)(2,1)}, bf16[2,2,16,128]{3,2,1,0:T(8,128)(2,1)}, u32[]{:S(2)}, u32[]{:S(2)}) collective-permute-start(bf16[2,2,16,128]{3,2,1,0:T(8,128)(2,1)} %pad_maximum_fusion.13), channel_id=1, source_target_pairs={{0,4},{1,3},{2,6},{3,1},{4,0},{5,7},{6,2},{7,5},{8,12},{9,11},{10,... | collective-permute-start | bytes 49160 | tf_op jit(solution)/shard_map/ppermute | solution.py:508
  35.5 18.8 %collective-permute-start.6 = (bf16[2,128,1280]{2,1,0:T(8,128)(2,1)}, bf16[2,128,1280]{2,1,0:T(8,128)(2,1)}, u32[]{:S(2)}, u32[]{:S(2)}) collective-permute-start(bf16[2,128,1280]{2,1,0:T(8,128)(2,1)} %pad_maximum_fusion.4), channel_id=1, source_target_pairs={{0,4},{1,3},{2,6},{3,1},{4,0},{5,7},{6,2},{7,5},{8,12},{9,11},{10,... | collective-permute-start | bytes 1966088 | tf_op jit(solution)/shard_map/ppermute | solution.py:508
  44.8 12.2 %collective-permute-start.9 = (bf16[4,128,768]{2,1,0:T(8,128)(2,1)}, bf16[4,128,768]{2,1,0:T(8,128)(2,1)S(1)}, u32[]{:S(2)}, u32[]{:S(2)}) collective-permute-start(bf16[4,128,768]{2,1,0:T(8,128)(2,1)} %collective-permute-done.7.refs_1_), channel_id=1, source_target_pairs={{0,16},{1,9},{2,18},{3,11},{4,20},{5,13},{6,22},{7,15},{8,24},{9,1... | collective-permute-start | bytes 2359304 | tf_op jit(solution)/shard_map/ppermute | solution.py:508
  45.3 13.2 %collective-permute-start.10 = (bf16[4,128,768]{2,1,0:T(8,128)(2,1)S(1)}, bf16[4,128,768]{2,1,0:T(8,128)(2,1)S(1)}, u32[]{:S(2)}, u32[]{:S(2)}) collective-permute-start(bf16[4,128,768]{2,1,0:T(8,128)(2,1)S(1)} %pad_maximum_fusion.3.refs_0_), channel_id=1, source_target_pairs={{0,1},{1,0},{2,3},{3,2},{4,5},{5,4},{6,7},{7,6},{8,9},{9,8},{10,11... | collective-permute-start | bytes 2359304 | tf_op jit(solution)/shard_map/ppermute | solution.py:508
  48.5 10.6 %collective-permute-start.11 = (bf16[4,128,768]{2,1,0:T(8,128)(2,1)}, bf16[4,128,768]{2,1,0:T(8,128)(2,1)S(1)}, u32[]{:S(2)}, u32[]{:S(2)}) collective-permute-start(bf16[4,128,768]{2,1,0:T(8,128)(2,1)} %collective-permute-done.7.refs_1_), channel_id=1, source_target_pairs={{0,1},{1,0},{2,3},{3,2},{4,5},{5,4},{6,7},{7,6},{8,9},{9,8},{10,11... | collective-permute-start | bytes 2359304 | tf_op jit(solution)/shard_map/ppermute | solution.py:508
  49.0 11.0 %collective-permute-start.12 = (bf16[4,128,768]{2,1,0:T(8,128)(2,1)}, bf16[4,128,768]{2,1,0:T(8,128)(2,1)S(1)}, u32[]{:S(2)}, u32[]{:S(2)}) collective-permute-start(bf16[4,128,768]{2,1,0:T(8,128)(2,1)} %collective-permute-done.8.refs_2_), channel_id=1, source_target_pairs={{0,1},{1,0},{2,3},{3,2},{4,5},{5,4},{6,7},{7,6},{8,9},{9,8},{10,11... | collective-permute-start | bytes 2359304 | tf_op jit(solution)/shard_map/ppermute | solution.py:508
  55.6 21.5 %copy-start.4 = (bf16[4,128,1280]{2,1,0:T(8,128)(2,1)}, bf16[4,128,1280]{2,1,0:T(8,128)(2,1)S(1)}, u32[]{:S(2)}) copy-start(bf16[4,128,1280]{2,1,0:T(8,128)(2,1)S(1)} %pad_maximum_fusion.refs_0_) | copy-start | bytes 3932164
  57.0 2.9 collective-permute-start.13
  57.0 36.4 %collective-permute-start.15 = (bf16[4,128,1280]{2,1,0:T(8,128)(2,1)S(1)}, bf16[4,128,1280]{2,1,0:T(8,128)(2,1)}, u32[]{:S(2)}, u32[]{:S(2)}) collective-permute-start(bf16[4,128,1280]{2,1,0:T(8,128)(2,1)S(1)} %pad_maximum_fusion.refs_0_), channel_id=1, source_target_pairs={{0,8},{1,17},{2,10},{3,19},{4,12},{5,21},{6,14},{7,23},{8,0},{9,25... | collective-permute-start | bytes 3932168 | tf_op jit(solution)/shard_map/ppermute | solution.py:508
  58.5 34.9 %collective-permute-start.16 = (bf16[4,128,1280]{2,1,0:T(8,128)(2,1)S(1)}, bf16[4,128,1280]{2,1,0:T(8,128)(2,1)}, u32[]{:S(2)}, u32[]{:S(2)}) collective-permute-start(bf16[4,128,1280]{2,1,0:T(8,128)(2,1)S(1)} %pad_maximum_fusion.refs_0_), channel_id=1, source_target_pairs={{0,16},{1,9},{2,18},{3,11},{4,20},{5,13},{6,22},{7,15},{8,24},{9,1... | collective-permute-start | bytes 3932168 | tf_op jit(solution)/shard_map/ppermute | solution.py:508
  59.0 15.4 %collective-permute-start.14 = (bf16[512,256]{1,0:T(8,128)(2,1)S(1)}, bf16[512,256]{1,0:T(8,128)(2,1)S(1)}, u32[]{:S(2)}, u32[]{:S(2)}) collective-permute-start(bf16[512,256]{1,0:T(8,128)(2,1)S(1)} %copy-done.6), channel_id=1, source_target_pairs={{0,2},{1,5},{2,0},{3,7},{4,6},{5,1},{6,4},{7,3},{8,10},{9,13},{10,... | collective-permute-start | bytes 786440 | tf_op jit(solution)/shard_map/ppermute | solution.py:508
  74.5 18.9 %collective-permute-start.17 = (bf16[2,512,256]{2,1,0:T(8,128)(2,1)S(1)}, bf16[2,512,256]{2,1,0:T(8,128)(2,1)S(1)}, u32[]{:S(2)}, u32[]{:S(2)}) collective-permute-start(bf16[2,512,256]{2,1,0:T(8,128)(2,1)S(1)} %pad_maximum_fusion.5), channel_id=1, source_target_pairs={{0,4},{1,3},{2,6},{3,1},{4,0},{5,7},{6,2},{7,5},{8,12},{9,11},{10,... | collective-permute-start | bytes 1572872 | tf_op jit(solution)/shard_map/ppermute | solution.py:508
  77.0 35.8 %collective-permute-start.19 = (bf16[4,128,1280]{2,1,0:T(8,128)(2,1)S(1)}, bf16[4,128,1280]{2,1,0:T(8,128)(2,1)}, u32[]{:S(2)}, u32[]{:S(2)}) collective-permute-start(bf16[4,128,1280]{2,1,0:T(8,128)(2,1)S(1)} %pad_maximum_fusion.refs_0_), channel_id=1, source_target_pairs={{0,1},{1,0},{2,3},{3,2},{4,5},{5,4},{6,7},{7,6},{8,9},{9,8},{10,11... | collective-permute-start | bytes 3932168 | tf_op jit(solution)/shard_map/ppermute | solution.py:508
  93.4 18.5 %collective-permute-start.18 = (bf16[4,128,1280]{2,1,0:T(8,128)(2,1)}, bf16[4,128,1280]{2,1,0:T(8,128)(2,1)}, u32[]{:S(2)}, u32[]{:S(2)}) collective-permute-start(bf16[4,128,1280]{2,1,0:T(8,128)(2,1)} %collective-permute-done.15.refs_1_), channel_id=1, source_target_pairs={{0,16},{1,9},{2,18},{3,11},{4,20},{5,13},{6,22},{7,15},{8,24},{9,1... | collective-permute-start | bytes 3932168 | tf_op jit(solution)/shard_map/ppermute | solution.py:508
  94.9 31.4 %collective-permute-start.20 = (bf16[4,128,1280]{2,1,0:T(8,128)(2,1)}, bf16[4,128,1280]{2,1,0:T(8,128)(2,1)}, u32[]{:S(2)}, u32[]{:S(2)}) collective-permute-start(bf16[4,128,1280]{2,1,0:T(8,128)(2,1)} %collective-permute-done.15.refs_1_), channel_id=1, source_target_pairs={{0,1},{1,0},{2,3},{3,2},{4,5},{5,4},{6,7},{7,6},{8,9},{9,8},{10,11... | collective-permute-start | bytes 3932168 | tf_op jit(solution)/shard_map/ppermute | solution.py:508
  95.0 31.3 %copy-start.5 = (bf16[4,512,256]{2,1,0:T(8,128)(2,1)}, bf16[4,512,256]{2,1,0:T(8,128)(2,1)S(1)}, u32[]{:S(2)}) copy-start(bf16[4,512,256]{2,1,0:T(8,128)(2,1)S(1)} %pad_maximum_fusion.1.refs_0_) | copy-start | bytes 3145732
  95.0 31.4 %collective-permute-start.21 = (bf16[4,128,1280]{2,1,0:T(8,128)(2,1)}, bf16[4,128,1280]{2,1,0:T(8,128)(2,1)S(1)}, u32[]{:S(2)}, u32[]{:S(2)}) collective-permute-start(bf16[4,128,1280]{2,1,0:T(8,128)(2,1)} %collective-permute-done.16.refs_2_), channel_id=1, source_target_pairs={{0,1},{1,0},{2,3},{3,2},{4,5},{5,4},{6,7},{7,6},{8,9},{9,8},{10,11... | collective-permute-start | bytes 3932168 | tf_op jit(solution)/shard_map/ppermute | solution.py:508
  111.9 14.5 %collective-permute-start.22 = (bf16[4,128,1280]{2,1,0:T(8,128)(2,1)}, bf16[4,128,1280]{2,1,0:T(8,128)(2,1)}, u32[]{:S(2)}, u32[]{:S(2)}) collective-permute-start(bf16[4,128,1280]{2,1,0:T(8,128)(2,1)} %collective-permute-done.18.refs_3_), channel_id=1, source_target_pairs={{0,1},{1,0},{2,3},{3,2},{4,5},{5,4},{6,7},{7,6},{8,9},{9,8},{10,11... | collective-permute-start | bytes 3932168 | tf_op jit(solution)/shard_map/ppermute | solution.py:508
  112.3 25.9 %collective-permute-start.23 = (bf16[4,512,256]{2,1,0:T(8,128)(2,1)S(1)}, bf16[4,512,256]{2,1,0:T(8,128)(2,1)}, u32[]{:S(2)}, u32[]{:S(2)}) collective-permute-start(bf16[4,512,256]{2,1,0:T(8,128)(2,1)S(1)} %pad_maximum_fusion.1.refs_0_), channel_id=1, source_target_pairs={{0,8},{1,17},{2,10},{3,19},{4,12},{5,21},{6,14},{7,23},{8,0},{9,25... | collective-permute-start | bytes 3145736 | tf_op jit(solution)/shard_map/ppermute | solution.py:508
  112.9 25.4 %collective-permute-start.24 = (bf16[4,512,256]{2,1,0:T(8,128)(2,1)S(1)}, bf16[4,512,256]{2,1,0:T(8,128)(2,1)S(1)}, u32[]{:S(2)}, u32[]{:S(2)}) collective-permute-start(bf16[4,512,256]{2,1,0:T(8,128)(2,1)S(1)} %pad_maximum_fusion.1.refs_0_), channel_id=1, source_target_pairs={{0,16},{1,9},{2,18},{3,11},{4,20},{5,13},{6,22},{7,15},{8,24},{9,1... | collective-permute-start | bytes 3145736 | tf_op jit(solution)/shard_map/ppermute | solution.py:508
  126.3 34.5 %collective-permute-start.26 = (bf16[4,512,256]{2,1,0:T(8,128)(2,1)S(1)}, bf16[4,512,256]{2,1,0:T(8,128)(2,1)}, u32[]{:S(2)}, u32[]{:S(2)}) collective-permute-start(bf16[4,512,256]{2,1,0:T(8,128)(2,1)S(1)} %pad_maximum_fusion.1.refs_0_), channel_id=1, source_target_pairs={{0,1},{1,0},{2,3},{3,2},{4,5},{5,4},{6,7},{7,6},{8,9},{9,8},{10,11... | collective-permute-start | bytes 3145736 | tf_op jit(solution)/shard_map/ppermute | solution.py:508
  138.2 22.4 %copy-start.14 = (bf16[4,512,256]{2,1,0:T(8,128)(2,1)}, bf16[4,512,256]{2,1,0:T(8,128)(2,1)S(1)}, u32[]{:S(2)}) copy-start(bf16[4,512,256]{2,1,0:T(8,128)(2,1)S(1)} %collective-permute-done.24.refs_2_) | copy-start | bytes 3145732
  138.2 22.4 %collective-permute-start.25 = (bf16[4,512,256]{2,1,0:T(8,128)(2,1)}, bf16[4,512,256]{2,1,0:T(8,128)(2,1)S(1)}, u32[]{:S(2)}, u32[]{:S(2)}) collective-permute-start(bf16[4,512,256]{2,1,0:T(8,128)(2,1)} %collective-permute-done.23.refs_1_), channel_id=1, source_target_pairs={{0,16},{1,9},{2,18},{3,11},{4,20},{5,13},{6,22},{7,15},{8,24},{9,1... | collective-permute-start | bytes 3145736 | tf_op jit(solution)/shard_map/ppermute | solution.py:508
  138.8 22.0 %collective-permute-start.27 = (bf16[4,512,256]{2,1,0:T(8,128)(2,1)}, bf16[4,512,256]{2,1,0:T(8,128)(2,1)}, u32[]{:S(2)}, u32[]{:S(2)}) collective-permute-start(bf16[4,512,256]{2,1,0:T(8,128)(2,1)} %collective-permute-done.23.refs_1_), channel_id=1, source_target_pairs={{0,1},{1,0},{2,3},{3,2},{4,5},{5,4},{6,7},{7,6},{8,9},{9,8},{10,11... | collective-permute-start | bytes 3145736 | tf_op jit(solution)/shard_map/ppermute | solution.py:508
  138.8 22.0 %collective-permute-start.28 = (bf16[4,512,256]{2,1,0:T(8,128)(2,1)S(1)}, bf16[4,512,256]{2,1,0:T(8,128)(2,1)}, u32[]{:S(2)}, u32[]{:S(2)}) collective-permute-start(bf16[4,512,256]{2,1,0:T(8,128)(2,1)S(1)} %collective-permute-done.24.refs_2_), channel_id=1, source_target_pairs={{0,1},{1,0},{2,3},{3,2},{4,5},{5,4},{6,7},{7,6},{8,9},{9,8},{10,11... | collective-permute-start | bytes 3145736 | tf_op jit(solution)/shard_map/ppermute | solution.py:508
  160.7 2.7 collective-permute-start.29
  210.9 14.6 %collective-permute-start.30 = (bf16[4,4,512,256]{3,2,1,0:T(8,128)(2,1)}, bf16[4,4,512,256]{3,2,1,0:T(8,128)(2,1)}, u32[]{:S(2)}, u32[]{:S(2)}) collective-permute-start(bf16[4,4,512,256]{3,2,1,0:T(8,128)(2,1)} %get-tuple-element.182), channel_id=1, source_target_pairs={{0,1},{1,0},{2,3},{3,2},{4,5},{5,4},{6,7},{7,6},{8,9},{9,8},{10,11... | collective-permute-start | bytes 12582920 | tf_op jit(solution)/shard_map/ppermute | solution.py:508
  225.2 25.4 %collective-permute-start.31 = (bf16[4,4,128,1024]{3,2,1,0:T(8,128)(2,1)}, bf16[4,4,128,1024]{3,2,1,0:T(8,128)(2,1)}, u32[]{:S(2)}, u32[]{:S(2)}) collective-permute-start(bf16[4,4,128,1024]{3,2,1,0:T(8,128)(2,1)} %get-tuple-element.191), channel_id=1, source_target_pairs={{0,1},{1,0},{2,3},{3,2},{4,5},{5,4},{6,7},{7,6},{8,9},{9,8},{10,11... | collective-permute-start | bytes 12582920 | tf_op jit(solution)/shard_map/ppermute | solution.py:508
  228.2 50.5 %collective-permute-start.32 = (bf16[2,4,512,256]{3,2,1,0:T(8,128)(2,1)S(1)}, bf16[2,4,512,256]{3,2,1,0:T(8,128)(2,1)}, u32[]{:S(2)}, u32[]{:S(2)}) collective-permute-start(bf16[2,4,512,256]{3,2,1,0:T(8,128)(2,1)S(1)} %add_convert_fusion.1), channel_id=1, source_target_pairs={{0,8},{1,17},{2,10},{3,19},{4,12},{5,21},{6,14},{7,23},{8,0},{9,25... | collective-permute-start | bytes 6291464 | tf_op jit(solution)/shard_map/ppermute | solution.py:508
  255.3 27.2 %collective-permute-start.33 = (bf16[2,4,128,1024]{3,2,1,0:T(8,128)(2,1)}, bf16[2,4,128,1024]{3,2,1,0:T(8,128)(2,1)}, u32[]{:S(2)}, u32[]{:S(2)}) collective-permute-start(bf16[2,4,128,1024]{3,2,1,0:T(8,128)(2,1)} %add_convert_fusion), channel_id=1, source_target_pairs={{0,8},{1,17},{2,10},{3,19},{4,12},{5,21},{6,14},{7,23},{8,0},{9,25... | collective-permute-start | bytes 6291464 | tf_op jit(solution)/shard_map/ppermute | solution.py:508
  281.0 17.9 %collective-permute-start.34 = (bf16[4,512,256]{2,1,0:T(8,128)(2,1)S(1)}, bf16[4,512,256]{2,1,0:T(8,128)(2,1)S(1)}, u32[]{:S(2)}, u32[]{:S(2)}) collective-permute-start(bf16[4,512,256]{2,1,0:T(8,128)(2,1)S(1)} %fusion.3), channel_id=1, source_target_pairs={{0,16},{1,9},{2,18},{3,11},{4,20},{5,13},{6,22},{7,15},{8,24},{9,1... | collective-permute-start | bytes 3145736 | tf_op jit(solution)/shard_map/ppermute | solution.py:508
  298.3 17.9 %collective-permute-start.37 = (bf16[4,4,128,640]{3,2,1,0:T(8,128)(2,1)}, bf16[4,4,128,640]{3,2,1,0:T(8,128)(2,1)}, u32[]{:S(2)}, u32[]{:S(2)}) collective-permute-start(bf16[4,4,128,640]{3,2,1,0:T(8,128)(2,1)} %get-tuple-element.205), channel_id=1, source_target_pairs={{0,1},{1,0},{2,3},{3,2},{4,5},{5,4},{6,7},{7,6},{8,9},{9,8},{10,11... | collective-permute-start | bytes 7864328 | tf_op jit(solution)/shard_map/ppermute | solution.py:508
  298.3 17.9 %collective-permute-start.36 = (bf16[4,128,1024]{2,1,0:T(8,128)(2,1)}, bf16[4,128,1024]{2,1,0:T(8,128)(2,1)}, u32[]{:S(2)}, u32[]{:S(2)}) collective-permute-start(bf16[4,128,1024]{2,1,0:T(8,128)(2,1)} %fusion.4), channel_id=1, source_target_pairs={{0,16},{1,9},{2,18},{3,11},{4,20},{5,13},{6,22},{7,15},{8,24},{9,1... | collective-permute-start | bytes 3145736 | tf_op jit(solution)/shard_map/ppermute | solution.py:508
  301.4 14.8 %collective-permute-start.35 = (bf16[2,512,256]{2,1,0:T(8,128)(2,1)S(1)}, bf16[2,512,256]{2,1,0:T(8,128)(2,1)S(1)}, u32[]{:S(2)}, u32[]{:S(2)}) collective-permute-start(bf16[2,512,256]{2,1,0:T(8,128)(2,1)S(1)} %pad_maximum_fusion.6), channel_id=1, source_target_pairs={{0,2},{1,5},{2,0},{3,7},{4,6},{5,1},{6,4},{7,3},{8,10},{9,13},{10,... | collective-permute-start | bytes 1572872 | tf_op jit(solution)/shard_map/ppermute | solution.py:508
  322.6 18.0 %collective-permute-start.38 = (bf16[2,4,128,640]{3,2,1,0:T(8,128)(2,1)}, bf16[2,4,128,640]{3,2,1,0:T(8,128)(2,1)}, u32[]{:S(2)}, u32[]{:S(2)}) collective-permute-start(bf16[2,4,128,640]{3,2,1,0:T(8,128)(2,1)} %add_convert_fusion.2), channel_id=1, source_target_pairs={{0,8},{1,17},{2,10},{3,19},{4,12},{5,21},{6,14},{7,23},{8,0},{9,25... | collective-permute-start | bytes 3932168 | tf_op jit(solution)/shard_map/ppermute | solution.py:508
  323.9 20.5 %collective-permute-start.40 = (bf16[2,128,1024]{2,1,0:T(8,128)(2,1)S(1)}, bf16[2,128,1024]{2,1,0:T(8,128)(2,1)S(1)}, u32[]{:S(2)}, u32[]{:S(2)}) collective-permute-start(bf16[2,128,1024]{2,1,0:T(8,128)(2,1)S(1)} %pad_maximum_fusion.7), channel_id=1, source_target_pairs={{0,2},{1,5},{2,0},{3,7},{4,6},{5,1},{6,4},{7,3},{8,10},{9,13},{10,... | collective-permute-start | bytes 1572872 | tf_op jit(solution)/shard_map/ppermute | solution.py:508
  325.4 18.4 %collective-permute-start.39 = (bf16[512,256]{1,0:T(8,128)(2,1)}, bf16[512,256]{1,0:T(8,128)(2,1)S(1)}, u32[]{:S(2)}, u32[]{:S(2)}) collective-permute-start(bf16[512,256]{1,0:T(8,128)(2,1)} %fusion.11), channel_id=1, source_target_pairs={{0,4},{1,3},{2,6},{3,1},{4,0},{5,7},{6,2},{7,5},{8,12},{9,11},{10,... | collective-permute-start | bytes 786440 | tf_op jit(solution)/shard_map/ppermute | solution.py:508
  342.3 12.9 %collective-permute-start.42 = (bf16[4,128,640]{2,1,0:T(8,128)(2,1)S(1)}, bf16[4,128,640]{2,1,0:T(8,128)(2,1)}, u32[]{:S(2)}, u32[]{:S(2)}) collective-permute-start(bf16[4,128,640]{2,1,0:T(8,128)(2,1)S(1)} %fusion.6), channel_id=1, source_target_pairs={{0,16},{1,9},{2,18},{3,11},{4,20},{5,13},{6,22},{7,15},{8,24},{9,1... | collective-permute-start | bytes 1966088 | tf_op jit(solution)/shard_map/ppermute | solution.py:508
  345.1 10.1 %collective-permute-start.41 = (bf16[128,1024]{1,0:T(8,128)(2,1)S(1)}, bf16[128,1024]{1,0:T(8,128)(2,1)S(1)}, u32[]{:S(2)}, u32[]{:S(2)}) collective-permute-start(bf16[128,1024]{1,0:T(8,128)(2,1)S(1)} %fusion.12), channel_id=1, source_target_pairs={{0,4},{1,3},{2,6},{3,1},{4,0},{5,7},{6,2},{7,5},{8,12},{9,11},{10,... | collective-permute-start | bytes 786440 | tf_op jit(solution)/shard_map/ppermute | solution.py:508
  355.2 13.5 %collective-permute-start.43 = (bf16[4,4,144,384]{3,2,1,0:T(8,128)(2,1)}, bf16[4,4,144,384]{3,2,1,0:T(8,128)(2,1)}, u32[]{:S(2)}, u32[]{:S(2)}) collective-permute-start(bf16[4,4,144,384]{3,2,1,0:T(8,128)(2,1)} %get-tuple-element.225), channel_id=1, source_target_pairs={{0,1},{1,0},{2,3},{3,2},{4,5},{5,4},{6,7},{7,6},{8,9},{9,8},{10,11... | collective-permute-start | bytes 5308424 | tf_op jit(solution)/shard_map/ppermute | solution.py:508
  357.4 11.2 %collective-permute-start.44 = (bf16[2,128,640]{2,1,0:T(8,128)(2,1)S(1)}, bf16[2,128,640]{2,1,0:T(8,128)(2,1)S(1)}, u32[]{:S(2)}, u32[]{:S(2)}) collective-permute-start(bf16[2,128,640]{2,1,0:T(8,128)(2,1)S(1)} %pad_maximum_fusion.10), channel_id=1, source_target_pairs={{0,2},{1,5},{2,0},{3,7},{4,6},{5,1},{6,4},{7,3},{8,10},{9,13},{10,... | collective-permute-start | bytes 983048 | tf_op jit(solution)/shard_map/ppermute | solution.py:508
  359.1 9.6 %collective-permute-start.45 = (bf16[1024,256]{1,0:T(8,128)(2,1)S(1)}, bf16[1024,256]{1,0:T(8,128)(2,1)S(1)}, u32[]{:S(2)}, u32[]{:S(2)}) collective-permute-start(bf16[1024,256]{1,0:T(8,128)(2,1)S(1)} %slice_dynamic-update-slice_fusion.refs_0_), channel_id=1, source_target_pairs={{0,8},{1,17},{2,10},{3,19},{4,12},{5,21},{6,14},{7,23},{8,0},{9,25... | collective-permute-start | bytes 1572872 | tf_op jit(solution)/shard_map/ppermute | solution.py:508
  371.2 13.3 %collective-permute-start.46 = (bf16[2,4,144,384]{3,2,1,0:T(8,128)(2,1)}, bf16[2,4,144,384]{3,2,1,0:T(8,128)(2,1)S(1)}, u32[]{:S(2)}, u32[]{:S(2)}) collective-permute-start(bf16[2,4,144,384]{3,2,1,0:T(8,128)(2,1)} %add_convert_fusion.5), channel_id=1, source_target_pairs={{0,8},{1,17},{2,10},{3,19},{4,12},{5,21},{6,14},{7,23},{8,0},{9,25... | collective-permute-start | bytes 2654216 | tf_op jit(solution)/shard_map/ppermute | solution.py:508
  372.2 9.8 %collective-permute-start.47 = (bf16[128,640]{1,0:T(8,128)(2,1)S(1)}, bf16[128,640]{1,0:T(8,128)(2,1)S(1)}, u32[]{:S(2)}, u32[]{:S(2)}) collective-permute-start(bf16[128,640]{1,0:T(8,128)(2,1)S(1)} %fusion.16), channel_id=1, source_target_pairs={{0,4},{1,3},{2,6},{3,1},{4,0},{5,7},{6,2},{7,5},{8,12},{9,11},{10,... | collective-permute-start | bytes 491528 | tf_op jit(solution)/shard_map/ppermute | solution.py:508
  385.8 10.1 %collective-permute-start.48 = (bf16[4,144,384]{2,1,0:T(8,128)(2,1)S(1)}, bf16[4,144,384]{2,1,0:T(8,128)(2,1)S(1)}, u32[]{:S(2)}, u32[]{:S(2)}) collective-permute-start(bf16[4,144,384]{2,1,0:T(8,128)(2,1)S(1)} %fusion.9), channel_id=1, source_target_pairs={{0,16},{1,9},{2,18},{3,11},{4,20},{5,13},{6,22},{7,15},{8,24},{9,1... | collective-permute-start | bytes 1327112 | tf_op jit(solution)/shard_map/ppermute | solution.py:508
  386.9 7.2 %collective-permute-start.49 = (bf16[128,640]{1,0:T(8,128)(2,1)S(1)}, bf16[128,640]{1,0:T(8,128)(2,1)S(1)}, u32[]{:S(2)}, u32[]{:S(2)}) collective-permute-start(bf16[128,640]{1,0:T(8,128)(2,1)S(1)} %fusion.10.refs_0_), channel_id=1, source_target_pairs={{0,8},{1,17},{2,10},{3,19},{4,12},{5,21},{6,14},{7,23},{8,0},{9,25... | collective-permute-start | bytes 491528 | tf_op jit(solution)/shard_map/ppermute | solution.py:508
  398.3 16.2 %copy-start.3 = (s32[3]{0:T(128)S(1)}, s32[3]{0:T(128)}, u32[]{:S(2)}) copy-start(s32[3]{0:T(128)} %pad_add_fusion.where) | copy-start | bytes 40
  398.3 16.1 %collective-permute-start.54 = (bf16[2,1024,256]{2,1,0:T(8,128)(2,1)}, bf16[2,1024,256]{2,1,0:T(8,128)(2,1)S(1)}, u32[]{:S(2)}, u32[]{:S(2)}) collective-permute-start(bf16[2,1024,256]{2,1,0:T(8,128)(2,1)} %pad_maximum_fusion.2), channel_id=1, source_target_pairs={{0,16},{1,9},{2,18},{3,11},{4,20},{5,13},{6,22},{7,15},{8,24},{9,1... | collective-permute-start | bytes 3145736 | tf_op jit(solution)/shard_map/ppermute | solution.py:508
  399.2 7.9 %collective-permute-start.51 = (bf16[144,384]{1,0:T(8,128)(2,1)S(1)}, bf16[144,384]{1,0:T(8,128)(2,1)S(1)}, u32[]{:S(2)}, u32[]{:S(2)}) collective-permute-start(bf16[144,384]{1,0:T(8,128)(2,1)S(1)} %get-tuple-element.259), channel_id=1, source_target_pairs={{0,6},{1,7},{2,4},{3,5},{4,2},{5,3},{6,0},{7,1},{8,14},{9,15},{10,... | collective-permute-start | bytes 331784 | tf_op jit(solution)/shard_map/ppermute | solution.py:508
  400.8 10.0 %collective-permute-start.52 = (bf16[144,384]{1,0:T(8,128)(2,1)S(1)}, bf16[144,384]{1,0:T(8,128)(2,1)S(1)}, u32[]{:S(2)}, u32[]{:S(2)}) collective-permute-start(bf16[144,384]{1,0:T(8,128)(2,1)S(1)} %get-tuple-element.258), channel_id=1, source_target_pairs={{0,4},{1,5},{2,6},{3,7},{4,0},{5,1},{6,2},{7,3},{8,12},{9,13},{10,... | collective-permute-start | bytes 331784 | tf_op jit(solution)/shard_map/ppermute | solution.py:508
  400.9 9.8 %collective-permute-start.53 = (bf16[144,384]{1,0:T(8,128)(2,1)S(1)}, bf16[144,384]{1,0:T(8,128)(2,1)S(1)}, u32[]{:S(2)}, u32[]{:S(2)}) collective-permute-start(bf16[144,384]{1,0:T(8,128)(2,1)S(1)} %get-tuple-element.257), channel_id=1, source_target_pairs={{0,2},{1,3},{2,0},{3,1},{4,6},{5,7},{6,4},{7,5},{8,10},{9,11},{10,... | collective-permute-start | bytes 331784 | tf_op jit(solution)/shard_map/ppermute | solution.py:508
  403.7 15.1 %collective-permute-start.50 = (bf16[2,128,640]{2,1,0:T(8,128)(2,1)S(1)}, bf16[2,128,640]{2,1,0:T(8,128)(2,1)S(1)}, u32[]{:S(2)}, u32[]{:S(2)}) collective-permute-start(bf16[2,128,640]{2,1,0:T(8,128)(2,1)S(1)} %pad_maximum_fusion.11), channel_id=1, source_target_pairs={{0,16},{1,9},{2,18},{3,11},{4,20},{5,13},{6,22},{7,15},{8,24},{9,1... | collective-permute-start | bytes 983048 | tf_op jit(solution)/shard_map/ppermute | solution.py:508
  410.8 8.0 %collective-permute-start.55 = (bf16[144,384]{1,0:T(8,128)(2,1)S(1)}, bf16[144,384]{1,0:T(8,128)(2,1)S(1)}, u32[]{:S(2)}, u32[]{:S(2)}) collective-permute-start(bf16[144,384]{1,0:T(8,128)(2,1)S(1)} %fusion.15.refs_4_), channel_id=1, source_target_pairs={{0,8},{1,9},{2,10},{3,11},{4,12},{5,13},{6,14},{7,15},{8,0},{9,1},... | collective-permute-start | bytes 331784 | tf_op jit(solution)/shard_map/ppermute | solution.py:508
  411.4 10.2 %collective-permute-start.56 = (bf16[144,384]{1,0:T(8,128)(2,1)S(1)}, bf16[144,384]{1,0:T(8,128)(2,1)S(1)}, u32[]{:S(2)}, u32[]{:S(2)}) collective-permute-start(bf16[144,384]{1,0:T(8,128)(2,1)S(1)} %fusion.15.refs_4_), channel_id=1, source_target_pairs={{0,16},{1,17},{2,18},{3,19},{4,20},{5,21},{6,22},{7,23},{8,24},{9,... | collective-permute-start | bytes 331784 | tf_op jit(solution)/shard_map/ppermute | solution.py:508
  412.7 8.9 %collective-permute-start.57 = (bf16[144,384]{1,0:T(8,128)(2,1)S(1)}, bf16[144,384]{1,0:T(8,128)(2,1)S(1)}, u32[]{:S(2)}, u32[]{:S(2)}) collective-permute-start(bf16[144,384]{1,0:T(8,128)(2,1)S(1)} %fusion.15.refs_4_), channel_id=1, source_target_pairs={{0,24},{1,25},{2,26},{3,27},{4,28},{5,29},{6,30},{7,31},{8,16},{9,... | collective-permute-start | bytes 331784 | tf_op jit(solution)/shard_map/ppermute | solution.py:508
  (16 other events, 47.0 us)
